TPU v7x, 32 devices: a whole 2x2x4 slice. The times are simulated.
32 devices in a mesh: dp: 8 (over z, y), seq: 4 (over x, core).
Axes of the slice: x: 2, y: 2, z: 4, core: 2. Of those that a mesh axis runs over, the one named last changes fastest.
Arguments:
- tokens: bfloat16 [16, 2048, 768], P('dp', 'seq'), may hold values from -6 to 6
- cotangent: bfloat16 [16, 2048, 768], P('dp', 'seq'), may hold values from -6 to 6
- lengths: int32 [16], P('dp'), may hold values from 256 to 2048, as said below
- patch_mask: int32 [16, 2048], P('dp'), may hold values 0 or 1
- owners: int32 [48], replicated, may hold values from 0 to 7, as said below
- master: float32 [48, 384, 384], P('dp'), may hold values from -1 to 1
- moment_one: float32 [48, 384, 384], P('dp'), may hold values from -64 to 64
- moment_two: float32 [48, 384, 384], P('dp'), may hold values from 8.192 to 32.768
- left_stats: float32 [48, 384, 384], P('dp'), may hold values from -32768 to 12582912, as said below
- right_stats: float32 [48, 384, 384], P('dp'), may hold values from -32768 to 12582912, as said below
- left_basis: float32 [48, 384, 384], P('dp'), may hold values from -1 to 1, as said below
- right_basis: float32 [48, 384, 384], P('dp'), may hold values from -1 to 1, as said below
- vec_params: float32 [12, 768], replicated, may hold values from -2 to 2
- vec_one: float32 [12, 768], replicated, may hold values from -64 to 64
- vec_two: float32 [12, 768], replicated, may hold values from 8.192 to 32.768
Outputs:
- output: bfloat16 [16, 2048, 768], P('dp', 'seq')
- d_tokens: bfloat16 [16, 2048, 768], P('dp', 'seq')
- grad_blocks: float32 [48, 384, 384], P('dp')
- master_new: float32 [48, 384, 384], P('dp')
- moment_one_new: float32 [48, 384, 384], P('dp')
- moment_two_new: float32 [48, 384, 384], P('dp')
- left_new: float32 [48, 384, 384], P('dp')
- right_new: float32 [48, 384, 384], P('dp')
- left_basis_new: float32 [48, 384, 384], P('dp')
- right_basis_new: float32 [48, 384, 384], P('dp')
- vec_one_new: float32 [12, 768], replicated
- vec_two_new: float32 [12, 768], replicated
- vec_new: float32 [12, 768], replicated
Inputs may be any that keep to these rules, and one draw needn't show every extreme that they name: `lengths`: in each group of 2 sequences of one index of dp, one has length 2048. `owners`: at most 6 blocks share an owner, and some owner has exactly 6. `left_stats`: symmetric positive definite. `right_stats`: symmetric positive definite. `left_basis`: each block orthogonal. `right_basis`: each block orthogonal.
All inputs are finite; a program needn't handle non-finite values. No bound on the sum of `patch_mask` on one device may be relied on, other than what follows from the above.
Results may differ from a plain program's by a relative error of at most 0.014.
The roundings to bfloat16 on the way count: a program that leaves them out, or rounds other values in their place, can miss the bound.
Values may be sent and summed in bfloat16 or wider, within the bound.
No kernel may reach another device: no remote copies, remote signals or barrier semaphores. Data moves between devices by JAX's collectives and lax.ppermute only.
A program may use at most 320 MiB of HBM per device.

v0:
```python
import jax
import jax.numpy as jnp
from jax import lax
from jax.sharding import PartitionSpec as P

D = 768
HD = 64
FF = 3072
BLK = 384
STEP = 10


PRECISE = lax.Precision.HIGHEST
NORM_EPS = 1e-06
NEG_FILL = -1000000000.0
BETA_ONE = 0.9
BETA_TWO = 0.999
BETA_STAT = 0.95
RATE_MATRIX = 0.1
RATE_VECTOR = 0.3
DECAY_RATE = 0.01
ADAM_EPS = 1e-08


def layer_norm(inputs, norm_gain, norm_shift):
    center = inputs - jnp.mean(inputs, axis=-1, keepdims=True)
    spread = jnp.mean(center * center, axis=-1, keepdims=True)
    return center * lax.rsqrt(spread + NORM_EPS) * norm_gain + norm_shift


def exact_gelu(inputs):
    return jax.nn.gelu(inputs, approximate=False)


def block_layout(owners, owner_count, slot_count):
    block_count = owners.shape[0]
    block_ids = jnp.arange(block_count, dtype=jnp.int32)
    earlier = (owners[:, None] == owners[None, :]) & (block_ids[None, :] < block_ids[:, None])
    slot_ids = jnp.sum(earlier.astype(jnp.int32), axis=1)
    places = owners * slot_count + slot_ids
    place_ids = jnp.arange(owner_count * slot_count, dtype=jnp.int32)
    matched = places[None, :] == place_ids[:, None]
    missing = 1 - jnp.any(matched, axis=1).astype(jnp.int32)
    sources = jnp.sum(jnp.where(matched, block_ids[None, :], 0), axis=1) + block_count * missing
    return (places, sources)


def tile_matrix(tiles, row_tiles, col_tiles):
    return (
        tiles.reshape(row_tiles, col_tiles, BLK, BLK)
        .transpose(0, 2, 1, 3)
        .reshape(row_tiles * BLK, col_tiles * BLK)
    )


def assemble(blocks):
    across = D // BLK
    wide = FF // BLK
    end_qkv = across * 3 * across
    end_out = end_qkv + across * across
    end_up = end_out + across * wide
    return (
        tile_matrix(blocks[:end_qkv], across, 3 * across),
        tile_matrix(blocks[end_qkv:end_out], across, across),
        tile_matrix(blocks[end_out:end_up], across, wide),
        tile_matrix(blocks[end_up:], wide, across),
    )


def split_blocks(matrices):
    pieces = []
    for matrix in matrices:
        row_tiles = matrix.shape[0] // BLK
        col_tiles = matrix.shape[1] // BLK
        pieces.append(
            matrix.reshape(row_tiles, BLK, col_tiles, BLK)
            .transpose(0, 2, 1, 3)
            .reshape(row_tiles * col_tiles, BLK, BLK)
        )
    return jnp.concatenate(pieces, axis=0)


def key_valid(lengths, patch_mask):
    positions = jnp.arange(patch_mask.shape[-1], dtype=jnp.int32)
    return (positions[None, :] < lengths[:, None]) & ((patch_mask == 1) | (positions[None, :] == 0))


def orthonormal(matrix):
    gram_matrix = jnp.matmul(matrix.T, matrix, precision=PRECISE)
    factor = jnp.linalg.cholesky(gram_matrix)
    return lax.linalg.triangular_solve(
        factor, matrix, left_side=False, lower=True, transpose_a=True
    )


def soap_update(packed):
    gradient, weight, first_mom, second_mom, left_mat, right_mat, left_rot, right_rot = packed
    rotated = jnp.matmul(
        jnp.matmul(left_rot.T, gradient, precision=PRECISE), right_rot, precision=PRECISE
    )
    first_mom = BETA_ONE * first_mom + (1.0 - BETA_ONE) * rotated
    second_mom = BETA_TWO * second_mom + (1.0 - BETA_TWO) * rotated * rotated
    scaled = (
        first_mom
        / (1.0 - BETA_ONE**STEP)
        / (jnp.sqrt(second_mom / (1.0 - BETA_TWO**STEP)) + ADAM_EPS)
    )
    back_rotated = jnp.matmul(
        jnp.matmul(left_rot, scaled, precision=PRECISE), right_rot.T, precision=PRECISE
    )
    weight = weight - RATE_MATRIX * (back_rotated + DECAY_RATE * weight)
    left_mat = BETA_STAT * left_mat + (1.0 - BETA_STAT) * jnp.matmul(
        gradient, gradient.T, precision=PRECISE
    )
    right_mat = BETA_STAT * right_mat + (1.0 - BETA_STAT) * jnp.matmul(
        gradient.T, gradient, precision=PRECISE
    )
    left_rot = orthonormal(jnp.matmul(left_mat, left_rot, precision=PRECISE))
    right_rot = orthonormal(jnp.matmul(right_mat, right_rot, precision=PRECISE))
    return (weight, first_mom, second_mom, left_mat, right_mat, left_rot, right_rot)


def adam_vectors(gradient, params, first_mom, second_mom):
    first_mom = BETA_ONE * first_mom + (1.0 - BETA_ONE) * gradient
    second_mom = BETA_TWO * second_mom + (1.0 - BETA_TWO) * gradient * gradient
    step_size = (
        first_mom
        / (1.0 - BETA_ONE**STEP)
        / (jnp.sqrt(second_mom / (1.0 - BETA_TWO**STEP)) + ADAM_EPS)
    )
    return (first_mom, second_mom, params - RATE_VECTOR * step_size)


def column_sum(matrix):
    ones_row = jnp.ones((1, matrix.shape[0]), matrix.dtype)
    return jnp.dot(ones_row, matrix, preferred_element_type=jnp.float32)[0]


def attention_forward(heads_in, live_keys):
    full_len = heads_in.shape[1]
    head_count = heads_in.shape[3]
    head_size = heads_in.shape[4]
    block_rows = min(512, full_len)
    block_count = full_len // block_rows
    scale = head_size ** (-0.5)

    def one_sequence(packed):
        query, keys_all, values_all, live_row = packed

        def one_block(query_blk):
            logits = (
                jnp.einsum("qhd,khd->hqk", query_blk, keys_all, preferred_element_type=jnp.float32)
                * scale
            )
            logits = jnp.where(live_row[None, None, :], logits, NEG_FILL)
            row_top = jnp.max(logits, axis=-1, keepdims=True)
            expo = jnp.exp(logits - row_top)
            row_total = jnp.sum(expo, axis=-1, keepdims=True)
            probs_low = (expo / row_total).astype(jnp.bfloat16)
            attended = jnp.einsum(
                "hqk,khd->qhd", probs_low, values_all, preferred_element_type=jnp.float32
            )
            return (
                attended.astype(jnp.bfloat16).reshape(block_rows, head_count * head_size),
                (row_top + jnp.log(row_total))[:, :, 0],
            )

        outs, log_totals = lax.map(
            one_block, query.reshape(block_count, block_rows, head_count, head_size)
        )
        return (
            outs.reshape(full_len, head_count * head_size),
            log_totals.transpose(1, 0, 2).reshape(head_count, full_len),
        )

    return lax.map(
        one_sequence, (heads_in[:, :, 0], heads_in[:, :, 1], heads_in[:, :, 2], live_keys)
    )


def attention_backward(heads_in, log_totals, d_heads, live_keys):
    full_len = heads_in.shape[1]
    head_count = heads_in.shape[3]
    head_size = heads_in.shape[4]
    block_rows = min(512, full_len)
    block_count = full_len // block_rows
    scale = head_size ** (-0.5)

    def one_sequence(packed):
        query, keys_all, values_all, log_row, d_seq, live_row = packed

        def one_block(carry, block_in):
            query_blk, total_blk, d_blk = block_in
            logits = (
                jnp.einsum("qhd,khd->hqk", query_blk, keys_all, preferred_element_type=jnp.float32)
                * scale
            )
            logits = jnp.where(live_row[None, None, :], logits, NEG_FILL)
            probs = jnp.exp(logits - total_blk[:, :, None])
            d_probs = jnp.einsum(
                "qhd,khd->hqk", d_blk, values_all, preferred_element_type=jnp.float32
            )
            delta = jnp.sum(probs * d_probs, axis=-1, keepdims=True)
            d_logits = (probs * (d_probs - delta)).astype(jnp.bfloat16)
            d_query = (
                jnp.einsum("hqk,khd->qhd", d_logits, keys_all, preferred_element_type=jnp.float32)
                * scale
            )
            d_key = (
                carry[0]
                + jnp.einsum(
                    "hqk,qhd->khd", d_logits, query_blk, preferred_element_type=jnp.float32
                )
                * scale
            )
            d_value = carry[1] + jnp.einsum(
                "hqk,qhd->khd",
                probs.astype(jnp.bfloat16),
                d_blk,
                preferred_element_type=jnp.float32,
            )
            return ((d_key, d_value), d_query)

        blocks_in = (
            query.reshape(block_count, block_rows, head_count, head_size),
            log_row.reshape(head_count, block_count, block_rows).transpose(1, 0, 2),
            d_seq.reshape(block_count, block_rows, head_count, head_size),
        )
        zero_grad = jnp.zeros((full_len, head_count, head_size), jnp.float32)
        (d_key, d_value), d_query = lax.scan(one_block, (zero_grad, zero_grad), blocks_in)
        group_width = head_count * head_size
        return jnp.stack(
            [
                d_query.reshape(full_len, group_width),
                d_key.reshape(full_len, group_width),
                d_value.reshape(full_len, group_width),
            ],
            axis=1,
        ).astype(jnp.bfloat16)

    return lax.map(
        one_sequence,
        (heads_in[:, :, 0], heads_in[:, :, 1], heads_in[:, :, 2], log_totals, d_heads, live_keys),
    )


def on_device(
    tokens,
    cotangent,
    lengths,
    patch_mask,
    owners,
    master,
    moment_one,
    moment_two,
    left_stats,
    right_stats,
    left_basis,
    right_basis,
    vec_params,
    vec_one,
    vec_two,
):
    groups = lax.axis_size("seq")
    owner_count = lax.axis_size("dp")
    slot_count = master.shape[0]
    block_size = master.shape[-1]
    places, sources = block_layout(owners, owner_count, slot_count)
    master_low = master.astype(jnp.bfloat16)
    fetched = lax.all_gather(master_low, "dp", axis=0, tiled=True)
    w_qkv, w_out, w_up, w_down = assemble(jnp.take(fetched, places, axis=0))
    seq_count, part_len, model_width = tokens.shape
    full_len = part_len * groups
    group_width = model_width // groups
    head_count = group_width // HD
    flat_in = tokens.reshape(-1, model_width).astype(jnp.float32)
    normed_one, norm_one_pull = jax.vjp(layer_norm, flat_in, vec_params[0], vec_params[1])
    normed_one = normed_one.astype(jnp.bfloat16)
    bias_qkv = jnp.concatenate([vec_params[4], jnp.zeros_like(vec_params[4]), vec_params[5]])
    qkv_low = (jnp.dot(normed_one, w_qkv, preferred_element_type=jnp.float32) + bias_qkv).astype(
        jnp.bfloat16
    )
    heads_in = lax.all_to_all(
        qkv_low.reshape(seq_count, part_len, 3, groups, group_width),
        "seq",
        split_axis=3,
        concat_axis=1,
        tiled=True,
    )
    heads_in = heads_in.reshape(seq_count, full_len, 3, head_count, HD)
    live_keys = key_valid(lengths, patch_mask)
    heads_out, log_totals = attention_forward(heads_in, live_keys)
    attn_low = lax.all_to_all(
        heads_out.reshape(seq_count, full_len, 1, group_width),
        "seq",
        split_axis=1,
        concat_axis=2,
        tiled=True,
    )
    attn_low = attn_low.reshape(-1, model_width)
    middle = flat_in + jnp.dot(attn_low, w_out, preferred_element_type=jnp.float32) + vec_params[6]
    normed_two, norm_two_pull = jax.vjp(layer_norm, middle, vec_params[2], vec_params[3])
    normed_two = normed_two.astype(jnp.bfloat16)
    hidden = jnp.dot(normed_two, w_up, preferred_element_type=jnp.float32) + vec_params[8:].reshape(
        -1
    )
    activated, gelu_pull = jax.vjp(exact_gelu, hidden)
    act_low = activated.astype(jnp.bfloat16)
    result = middle + jnp.dot(act_low, w_down, preferred_element_type=jnp.float32) + vec_params[7]
    d_result = cotangent.reshape(-1, model_width)
    grad_down = jnp.dot(act_low.T, d_result, preferred_element_type=jnp.float32)
    d_hidden = gelu_pull(jnp.dot(d_result, w_down.T, preferred_element_type=jnp.float32))[0].astype(
        jnp.bfloat16
    )
    grad_up = jnp.dot(normed_two.T, d_hidden, preferred_element_type=jnp.float32)
    d_middle_norm, grad_gain_two, grad_shift_two = norm_two_pull(
        jnp.dot(d_hidden, w_up.T, preferred_element_type=jnp.float32)
    )
    d_middle = d_result.astype(jnp.float32) + d_middle_norm
    d_proj = d_middle.astype(jnp.bfloat16)
    grad_out = jnp.dot(attn_low.T, d_proj, preferred_element_type=jnp.float32)
    d_attn = jnp.dot(d_proj, w_out.T, preferred_element_type=jnp.float32).astype(jnp.bfloat16)
    d_heads = lax.all_to_all(
        d_attn.reshape(seq_count, part_len, groups, group_width),
        "seq",
        split_axis=2,
        concat_axis=1,
        tiled=True,
    )
    d_heads = d_heads.reshape(seq_count, full_len, head_count, HD)
    d_qkv_heads = attention_backward(heads_in, log_totals, d_heads, live_keys)
    d_qkv = lax.all_to_all(
        d_qkv_heads.reshape(seq_count, full_len, 3, 1, group_width),
        "seq",
        split_axis=1,
        concat_axis=3,
        tiled=True,
    )
    d_qkv = d_qkv.reshape(-1, 3 * model_width)
    grad_qkv = jnp.dot(normed_one.T, d_qkv, preferred_element_type=jnp.float32)
    d_in_norm, grad_gain_one, grad_shift_one = norm_one_pull(
        jnp.dot(d_qkv, w_qkv.T, preferred_element_type=jnp.float32)
    )
    d_tokens = (d_middle + d_in_norm).astype(jnp.bfloat16).reshape(tokens.shape)
    qkv_sums = column_sum(d_qkv)
    head_rows = jnp.stack(
        [
            grad_gain_one,
            grad_shift_one,
            grad_gain_two,
            grad_shift_two,
            qkv_sums[:model_width],
            qkv_sums[2 * model_width :],
            column_sum(d_proj),
            column_sum(d_result),
        ]
    )
    vec_grad = jnp.concatenate([head_rows, column_sum(d_hidden).reshape(-1, model_width)], axis=0)
    vec_total = lax.psum(vec_grad, ("dp", "seq"))
    grad_tiles = split_blocks((grad_qkv, grad_out, grad_up, grad_down))
    ordered = jnp.take(
        jnp.concatenate([grad_tiles, jnp.zeros((1, block_size, block_size), jnp.float32)], axis=0),
        sources,
        axis=0,
    )
    owned = lax.psum_scatter(ordered, "dp", scatter_dimension=0, tiled=True)
    owned = lax.psum(owned.astype(jnp.bfloat16), "seq").astype(jnp.float32)
    updates = lax.map(
        soap_update,
        (owned, master, moment_one, moment_two, left_stats, right_stats, left_basis, right_basis),
    )
    vec_first, vec_second, vec_next = adam_vectors(vec_total, vec_params, vec_one, vec_two)
    return (
        result.astype(jnp.bfloat16).reshape(tokens.shape),
        d_tokens,
        owned,
        updates[0],
        updates[1],
        updates[2],
        updates[3],
        updates[4],
        updates[5],
        updates[6],
        vec_first,
        vec_second,
        vec_next,
    )


def solution(mesh):
    return jax.shard_map(
        on_device,
        mesh=mesh,
        in_specs=(
            P("dp", "seq", None),
            P("dp", "seq", None),
            P("dp"),
            P("dp", None),
            P(),
            P("dp", None, None),
            P("dp", None, None),
            P("dp", None, None),
            P("dp", None, None),
            P("dp", None, None),
            P("dp", None, None),
            P("dp", None, None),
            P(),
            P(),
            P(),
        ),
        out_specs=(
            P("dp", "seq", None),
            P("dp", "seq", None),
            P("dp", None, None),
            P("dp", None, None),
            P("dp", None, None),
            P("dp", None, None),
            P("dp", None, None),
            P("dp", None, None),
            P("dp", None, None),
            P("dp", None, None),
            P(),
            P(),
            P(),
        ),
        check_vma=False,
    )
```

profile of v0, /device:TPU:0, one launch (start us, length us, event | category | flops | bytes accessed | tf_op | source)
XLA Modules:
  0.0 2917.2 jit_solution(13269214123807697151)
XLA Ops:
  15.6 193.7 %all-gather.2.cloned.1.call-done = bf16[48,384,384]{2,1,0:T(8,128)(2,1)} async-done(((bf16[6,384,384]{2,1,0:T(8,128)(2,1)}), bf16[48,384,384]{2,1,0:T(8,128)(2,1)}) %all-gather.2.cloned.1.call-update) | async-done | bytes 14155792 | tf_op jit(solution)/shard_map/all_gather | solution.py:270
  255.0 12.8 reshape.518
  267.9 17.3 copy.177
  291.6 53.1 %all-to-all-done = bf16[2,512,3,4,192]{1,0,4,2,3:T(2,128)(2,1)} async-done(((bf16[2,512,3,4,192]{1,0,4,2,3:T(2,128)(2,1)}), bf16[2,512,3,4,192]{1,0,4,2,3:T(2,128)(2,1)}, u32[]{:S(2)}, u32[]{:S(2)}) %all-to-all-start) | async-done | bytes 4718624 | tf_op jit(solution)/shard_map/all_to_all | solution.py:283
  366.1 85.4 %while.78 = (s32[]{:T(128)}, bf16[2,2048,192]{2,1,0:T(8,128)(2,1)}, f32[2,3,2048]{2,1,0:T(4,128)S(1)}, bf16[2,2048,3,64]{1,3,2,0:T(8,128)(2,1)S(1)}, bf16[2,2048...) while((s32[]{:T(128)}, bf16[2,2048,192]{2,1,0:T(8,128)(2,1)}, ...), condition=%wide.region_8.9_spmd, body=%wide.region_3.8_spmd.sunk | while | flops 843151872 | bytes 54657356 | solution.py:176
  369.4 36.9 %while.84 = (s32[]{:T(128)}, bf16[4,512,192]{1,2,0:T(8,128)(2,1)}, f32[4,3,512]{2,1,0:T(4,128)S(1)}, pred[2048]{0:T(1024)(128)(4,1)S(1)}, bf16[4,512,3,64]{1,3,2...) while((s32[]{:T(128)}, bf16[4,512,192]{1,2,0:T(8,128)(2,1)}, ...), condition=%wide.region_7.7_spmd, body=%wide.region_4.6_spmd.sunk | while | flops 843151872 | bytes 43315332 | solution.py:168
  412.1 36.9 %while.84 = (s32[]{:T(128)}, bf16[4,512,192]{1,2,0:T(8,128)(2,1)}, f32[4,3,512]{2,1,0:T(4,128)S(1)}, pred[2048]{0:T(1024)(128)(4,1)S(1)}, bf16[4,512,3,64]{1,3,2...) while((s32[]{:T(128)}, bf16[4,512,192]{1,2,0:T(8,128)(2,1)}, ...), condition=%wide.region_7.7_spmd, body=%wide.region_4.6_spmd.sunk | while | flops 843151872 | bytes 43315332 | solution.py:168
  518.1 34.6 %fusion.145 = (bf16[1024,3072]{1,0:T(8,128)(2,1)S(1)}, f32[1024,3072]{1,0:T(8,128)}, f32[3072,1024]{0,1:T(8,128)}) fusion(f32[1024,3072]{1,0:T(8,128)S(1)} %fusion.208, f32[3072]{0:T(1024)S(1)} %add.262, bf16[1024,768]{1,0:T(8,128)(2,1)S(1)} %bitcast.681, bf16[3072,768]{0,1:T(8,128)(2,1)S(1)} %bitcast.707), kind=kOutput, calls=%fused_computation.241 | convolution fusion | flops 5061476352 | bytes 50343936 | tf_op jit(solution)/shard_map/dot_general | solution.py:312
  571.8 33.0 %fusion.139 = (bf16[3072,1024]{0,1:T(8,128)(2,1)}, f32[3072,1024]{0,1:T(8,128)}) fusion(f32[3072,1024]{0,1:T(8,128)} %get-tuple-element.788, f32[1024,3072]{1,0:T(8,128)} %copy-done.3, f32[3072]{0:T(1024)S(1)} %add.262), kind=kLoop, calls=%fused_computation.233 | loop fusion | flops 229638144 | bytes 44052480 | tf_op jit(solution)/shard_map/convert_element_type | solution.py:312
  608.4 244.8 %while.80 = (s32[]{:T(128)}, bf16[2,2048,3,192]{1,3,2,0:T(8,128)(2,1)}, bf16[2,2048,3,64]{1,3,2,0:T(8,128)(2,1)}, f32[2,3,2048]{2,1,0:T(4,128)}, bf16[2,2048,3,6...) while((s32[]{:T(128)}, ...), condition=%wide.region_17.18_spmd, body=%wide.region_13.17_spmd.sunk | while | flops 2070379008 | bytes 220713648 | solution.py:241
  620.1 106.2 %while.85 = (s32[]{:T(128)}, f32[2048,3,64]{0,2,1:T(8,128)S(1)}, f32[2048,3,64]{0,2,1:T(8,128)}, bf16[4,512,3,64]{1,3,2,0:T(8,128)(2,1)}, bf16[4,512,3,64]{1,3,2...) while((s32[]{:T(128)}, f32[2048,3,64]{0,2,1:T(8,128)S(1)}, ...), condition=%wide.region_16.16_spmd.clone, body=%wide.region_14.15_spmd.clone.sunk | while | flops 2062514688 | bytes 192332144 | solution.py:230
  742.4 106.2 %while.85 = (s32[]{:T(128)}, f32[2048,3,64]{0,2,1:T(8,128)S(1)}, f32[2048,3,64]{0,2,1:T(8,128)}, bf16[4,512,3,64]{1,3,2,0:T(8,128)(2,1)}, bf16[4,512,3,64]{1,3,2...) while((s32[]{:T(128)}, f32[2048,3,64]{0,2,1:T(8,128)S(1)}, ...), condition=%wide.region_16.16_spmd.clone, body=%wide.region_14.15_spmd.clone.sunk | while | flops 2062514688 | bytes 192332144 | solution.py:230
  853.2 16.3 copy.187
  945.8 21.2 copy.188
  1008.6 21.2 gather_fusion.1
  1029.8 20.7 broadcast_select_fusion
  1057.1 13.2 add_convert_fusion.2
  1074.1 422.6 %reduce-scatter.2.cloned.1.call-done = f32[6,384,384]{2,1,0:T(8,128)} async-done(((f32[48,384,384]{2,1,0:T(8,128)}), f32[6,384,384]{2,1,0:T(8,128)}) %reduce-scatter.2.cloned.1.call-update) | async-done | bytes 3538960 | tf_op jit(solution)/shard_map/reduce_scatter | solution.py:366
  1500.2 40.4 %psum.15 = f32[12,768]{1,0:T(8,128)S(1)} all-reduce(f32[12,768]{1,0:T(8,128)S(1)} %concatenate.26), channel_id=1, replica_groups=mesh['dp'=8,'seq'=4] {'dp','seq'}, use_global_device_ids=true, to_apply=%region_36.39 | all-reduce | flops 9216 | bytes 73728 | tf_op jit(solution)/shard_map/psum | solution.py:359
  1549.9 1360.5 %while.83 = (s32[]{:T(128)}, f32[6,384,384]{2,1,0:T(8,128)}, f32[6,384,384]{2,1,0:T(8,128)}, f32[6,384,384]{2,1,0:T(8,128)}, f32[6,384,384]{2,1,0:T(8,128)}, /*i...) while((s32[]{:T(128)}, f32[6,384,384]{2,1,0:T(8,128)}, ...), condition=%wide.region_31.34_spmd, body=%wide.region_24.33_spmd.sunk | while | flops 8060469248 | bytes 49230440 | solution.py:368
  1640.3 29.5 %custom-call.65 = f32[3,128,128]{1,2,0:T(8,128)S(1)} custom-call(f32[3,128,128]{2,1,0:T(8,128)S(1)} %get-tuple-element.1235), custom_call_target="InvertDiagBlocksLowerTriangular" | custom-call | tf_op jit(solution)/shard_map/while/body/eval_jaxpr/triangular_solve/custom-call.2 | solution.py:91
  1742.9 29.9 %custom-call.68 = f32[3,128,128]{1,2,0:T(8,128)S(1)} custom-call(f32[3,128,128]{2,1,0:T(8,128)S(1)} %get-tuple-element.1246), custom_call_target="InvertDiagBlocksLowerTriangular" | custom-call | tf_op jit(solution)/shard_map/while/body/eval_jaxpr/triangular_solve/custom-call.2 | solution.py:91
  1866.9 29.5 %custom-call.65 = f32[3,128,128]{1,2,0:T(8,128)S(1)} custom-call(f32[3,128,128]{2,1,0:T(8,128)S(1)} %get-tuple-element.1235), custom_call_target="InvertDiagBlocksLowerTriangular" | custom-call | tf_op jit(solution)/shard_map/while/body/eval_jaxpr/triangular_solve/custom-call.2 | solution.py:91
  1969.4 29.9 %custom-call.68 = f32[3,128,128]{1,2,0:T(8,128)S(1)} custom-call(f32[3,128,128]{2,1,0:T(8,128)S(1)} %get-tuple-element.1246), custom_call_target="InvertDiagBlocksLowerTriangular" | custom-call | tf_op jit(solution)/shard_map/while/body/eval_jaxpr/triangular_solve/custom-call.2 | solution.py:91
  2093.4 29.5 %custom-call.65 = f32[3,128,128]{1,2,0:T(8,128)S(1)} custom-call(f32[3,128,128]{2,1,0:T(8,128)S(1)} %get-tuple-element.1235), custom_call_target="InvertDiagBlocksLowerTriangular" | custom-call | tf_op jit(solution)/shard_map/while/body/eval_jaxpr/triangular_solve/custom-call.2 | solution.py:91
  2195.9 29.9 %custom-call.68 = f32[3,128,128]{1,2,0:T(8,128)S(1)} custom-call(f32[3,128,128]{2,1,0:T(8,128)S(1)} %get-tuple-element.1246), custom_call_target="InvertDiagBlocksLowerTriangular" | custom-call | tf_op jit(solution)/shard_map/while/body/eval_jaxpr/triangular_solve/custom-call.2 | solution.py:91
  2320.0 29.5 %custom-call.65 = f32[3,128,128]{1,2,0:T(8,128)S(1)} custom-call(f32[3,128,128]{2,1,0:T(8,128)S(1)} %get-tuple-element.1235), custom_call_target="InvertDiagBlocksLowerTriangular" | custom-call | tf_op jit(solution)/shard_map/while/body/eval_jaxpr/triangular_solve/custom-call.2 | solution.py:91
  2422.5 29.9 %custom-call.68 = f32[3,128,128]{1,2,0:T(8,128)S(1)} custom-call(f32[3,128,128]{2,1,0:T(8,128)S(1)} %get-tuple-element.1246), custom_call_target="InvertDiagBlocksLowerTriangular" | custom-call | tf_op jit(solution)/shard_map/while/body/eval_jaxpr/triangular_solve/custom-call.2 | solution.py:91
  2546.5 29.5 %custom-call.65 = f32[3,128,128]{1,2,0:T(8,128)S(1)} custom-call(f32[3,128,128]{2,1,0:T(8,128)S(1)} %get-tuple-element.1235), custom_call_target="InvertDiagBlocksLowerTriangular" | custom-call | tf_op jit(solution)/shard_map/while/body/eval_jaxpr/triangular_solve/custom-call.2 | solution.py:91
  2649.0 29.9 %custom-call.68 = f32[3,128,128]{1,2,0:T(8,128)S(1)} custom-call(f32[3,128,128]{2,1,0:T(8,128)S(1)} %get-tuple-element.1246), custom_call_target="InvertDiagBlocksLowerTriangular" | custom-call | tf_op jit(solution)/shard_map/while/body/eval_jaxpr/triangular_solve/custom-call.2 | solution.py:91
  2773.0 29.5 %custom-call.65 = f32[3,128,128]{1,2,0:T(8,128)S(1)} custom-call(f32[3,128,128]{2,1,0:T(8,128)S(1)} %get-tuple-element.1235), custom_call_target="InvertDiagBlocksLowerTriangular" | custom-call | tf_op jit(solution)/shard_map/while/body/eval_jaxpr/triangular_solve/custom-call.2 | solution.py:91
  2875.6 29.9 %custom-call.68 = f32[3,128,128]{1,2,0:T(8,128)S(1)} custom-call(f32[3,128,128]{2,1,0:T(8,128)S(1)} %get-tuple-element.1246), custom_call_target="InvertDiagBlocksLowerTriangular" | custom-call | tf_op jit(solution)/shard_map/while/body/eval_jaxpr/triangular_solve/custom-call.2 | solution.py:91
  (1132 shorter events, 1687.5 us)
Async XLA Ops:
  7.2 202.1 %all-gather.2.cloned.1.call-start = ((), (), s32[]{:S(2)}) async-start(), calls=%async_computation.5 | async-start | bytes 15925248 | tf_op jit(solution)/shard_map/all_gather | solution.py:270
  11.0 279.8 %copy-start.75 = (s32[48]{0:T(128)}, s32[48]{0:T(128)S(1)}, u32[]{:S(2)}) copy-start(s32[48]{0:T(128)S(1)} %get-tuple-element.730) | copy-start | bytes 580
  285.2 59.5 %all-to-all-start = ((bf16[2,512,3,4,192]{1,0,4,2,3:T(2,128)(2,1)}), bf16[2,512,3,4,192]{1,0,4,2,3:T(2,128)(2,1)}, u32[]{:S(2)}, u32[]{:S(2)}) async-start(bf16[2,512,3,4,192]{1,0,4,2,3:T(2,128)(2,1)} %copy.177), calls=%async_computation | async-start | bytes 9437184 | tf_op jit(solution)/shard_map/all_to_all | solution.py:283
  451.5 15.1 copy-start.2
  451.5 15.1 copy-start.35
  451.5 15.1 copy-start.38
  451.6 11.1 copy-start.76
  451.6 11.2 slice-start.15
  451.6 11.3 copy-start.65
  451.6 11.8 copy-start.66
  457.9 40.3 %all-to-all-start.1 = ((bf16[2,2048,1,192]{3,0,2,1:T(2,128)(2,1)}), bf16[2,2048,1,192]{3,0,2,1:T(2,128)(2,1)}, u32[]{:S(2)}, u32[]{:S(2)}) async-start(bf16[2,2048,1,192]{3,0,2,1:T(2,128)(2,1)} %bitcast.698), calls=%async_computation.1 | async-start | bytes 4194304 | tf_op jit(solution)/shard_map/all_to_all | solution.py:293
  462.8 109.0 %copy-start.47 = (f32[3072]{0:T(1024)}, f32[3072]{0:T(1024)S(1)}, u32[]{:S(2)}) copy-start(f32[3072]{0:T(1024)S(1)} %add.262) | copy-start | bytes 36868
  479.2 12.9 slice-start.9
  518.0 34.8 %copy-start.3 = (f32[1024,3072]{1,0:T(8,128)}, f32[1024,3072]{1,0:T(8,128)S(1)}, u32[]{:S(2)}) copy-start(f32[1024,3072]{1,0:T(8,128)S(1)} %fusion.208) | copy-start | bytes 37748740
  518.0 34.7 %copy-start.10 = (f32[1024,768]{1,0:T(8,128)S(1)}, f32[1024,768]{1,0:T(8,128)}, u32[]{:S(2)}) copy-start(f32[1024,768]{1,0:T(8,128)} %copy-done.9) | copy-start | bytes 9437188
  518.1 34.7 %copy-start.26 = (bf16[96,8,8,384]{3,1,2,0:T(8,128)(2,1)S(1)}, bf16[96,8,8,384]{3,1,2,0:T(8,128)(2,1)}, u32[]{:S(2)}) copy-start(bf16[96,8,8,384]{3,1,2,0:T(8,128)(2,1)} %copy.232) | copy-start | bytes 14155780
  518.1 34.7 %copy-start.40 = (f32[1024]{0:T(1024)S(1)}, f32[1024]{0:T(1024)}, u32[]{:S(2)}) copy-start(f32[1024]{0:T(1024)} %copy-done.39) | copy-start | bytes 12292
  518.1 34.7 %copy-start.43 = (f32[1024]{0:T(1024)S(1)}, f32[1024]{0:T(1024)}, u32[]{:S(2)}) copy-start(f32[1024]{0:T(1024)} %copy-done.42) | copy-start | bytes 12292
  518.1 34.7 %copy-start.50 = (f32[768]{0:T(1024)S(1)}, f32[768]{0:T(1024)}, u32[]{:S(2)}) copy-start(f32[768]{0:T(1024)} %get-tuple-element.602) | copy-start | bytes 9220
  568.2 36.5 %all-to-all-start.2 = ((bf16[2,512,4,192]{1,0,3,2:T(2,128)(2,1)}), bf16[2,512,4,192]{1,0,3,2:T(2,128)(2,1)S(1)}, u32[]{:S(2)}, u32[]{:S(2)}) async-start(bf16[2,512,4,192]{1,0,3,2:T(2,128)(2,1)} %reshape.441), calls=%async_computation.2 | async-start | bytes 3145728 | tf_op jit(solution)/shard_map/all_to_all | solution.py:323
  755.2 10.8 slice-start
  869.5 76.3 %all-to-all-start.3 = ((bf16[2,2048,3,1,192]{4,0,3,2,1:T(2,128)(2,1)}), bf16[2,2048,3,1,192]{4,0,3,2,1:T(2,128)(2,1)}, u32[]{:S(2)}, u32[]{:S(2)}) async-start(bf16[2,2048,3,1,192]{4,0,3,2,1:T(2,128)(2,1)} %bitcast.683), calls=%async_computation.3 | async-start | bytes 12582912 | tf_op jit(solution)/shard_map/all_to_all | solution.py:332
  875.0 621.7 %reduce-scatter.2.cloned.1.call-start = ((), (), s32[]{:S(2)}) async-start(), calls=%async_computation.6 | async-start | bytes 31850496 | tf_op jit(solution)/shard_map/reduce_scatter | solution.py:366
  888.4 18.9 slice-start.3
  888.4 18.9 slice-start.4
  916.8 13.2 copy-start.30
  1008.6 21.2 copy-start.77
  1050.5 495.9 %all-reduce.3.cloned.1.call-start = ((), (), s32[]{:S(2)}) async-start(), calls=%async_computation.7 | async-start | bytes 3538944 | tf_op jit(solution)/shard_map/psum | solution.py:367
  1074.0 466.6 %copy-start.46 = (f32[12,768]{1,0:T(8,128)S(1)}, f32[12,768]{1,0:T(8,128)}, u32[]{:S(2)}) copy-start(f32[12,768]{1,0:T(8,128)} %param.40) | copy-start | bytes 110596
  1074.0 466.6 %copy-start.56 = (f32[12,768]{1,0:T(8,128)S(1)}, f32[12,768]{1,0:T(8,128)}, u32[]{:S(2)}) copy-start(f32[12,768]{1,0:T(8,128)} %param.42) | copy-start | bytes 110596
  1074.0 466.6 %copy-start.57 = (f32[12,768]{1,0:T(8,128)S(1)}, f32[12,768]{1,0:T(8,128)}, u32[]{:S(2)}) copy-start(f32[12,768]{1,0:T(8,128)} %param.41) | copy-start | bytes 110596
  1074.0 467.2 %copy-start.64 = (f32[1024]{0:T(1024)S(1)}, f32[1024]{0:T(1024)}, u32[]{:S(2)}) copy-start(f32[1024]{0:T(1024)} %copy-done.63) | copy-start | bytes 12292
  (128 other events, 615.7 us)
Sparse Core Ops, SparseCore 0:
  10.9 198.3 all-gather.1
  1050.6 446.0 reduce-scatter.1
  1500.2 46.0 all-reduce.2
where the time goes:
time: 2930 us; the launch traced here: 2920 us
  other arithmetic  1210 us (41%)
  waiting for transfers between devices  676 us (23%)
  matrix products  528 us (18%)
  local copies, waits for them, and re-layouts  397 us (14%)
  blocking collectives  40.4 us (1%)
    another operation x132, other arithmetic, orthonormal(): factor = jnp.linalg.cholesky(gram_matrix)  687 us
    reduce_scatter x1, waiting for transfers between devices, on_device(): owned = lax.psum_scatter(ordered, 'dp', scatter_dimension=0, tiled=True)  423 us
    another operation x30, other arithmetic, orthonormal(): lax.linalg.triangular_solve(factor, matrix, left_side=False, lower=True,...  357 us
    all_gather x1, waiting for transfers between devices, on_device(): fetched = lax.all_gather(master_low, 'dp', axis=0, tiled=True)  194 us
    another operation x126, local copies, waits for them, and re-layouts, orthonormal(): lax.linalg.triangular_solve(factor, matrix, left_side=False, lower=True,...  70.7 us
    unnamed x179, local copies, waits for them, and re-layouts  59.7 us
  transfers between devices with their start and end apart: 7, of which 5 were waited for; matrix products, arithmetic and copies ran while one was open for 6% of the time, Pallas kernels for 0%

commit v1 on v0

v1 whole, which is shorter than its diff:
```python
import functools

import jax
import jax.numpy as jnp
from jax import lax
from jax.experimental import pallas as pl
from jax.experimental.pallas import tpu as pltpu
from jax.sharding import PartitionSpec as P

D = 768
FF = 3072
BLK = 384
STEP = 10

HIGHEST = lax.Precision.HIGHEST
NORM_EPS = 1e-06
NEG_FILL = -1000000000.0
BETA_ONE = 0.9
BETA_TWO = 0.999
BETA_STAT = 0.95
RATE_MATRIX = 0.1
RATE_VECTOR = 0.3
DECAY_RATE = 0.01
ADAM_EPS = 1e-08

LOW = jnp.bfloat16
F32 = jnp.float32
AXES = ("dp", "seq")
MIB = 2**20

TAIL_P = 0.24
TAIL_C = (
    0.09575380798443668,
    0.09552183543465394,
    0.09284136585084933,
    0.06338567653857548,
    0.11841694922211018,
    -0.06574016740998187,
    0.15281935057715396,
    -0.052998628523732765,
)


def dot(a, b, ca, cb, precision=None):
    return lax.dot_general(
        a, b, (((ca,), (cb,)), ((), ())), precision=precision, preferred_element_type=F32
    )


def lanes(shape):
    return lax.broadcasted_iota(jnp.int32, shape, len(shape) - 1)


def gelu_pair(x):
    u = jnp.abs(x)
    t = 1.0 / (1.0 + TAIL_P * u)
    poly = TAIL_C[-1]
    for coeff in TAIL_C[-2::-1]:
        poly = poly * t + coeff
    expo = jnp.exp(-0.5 * u * u)
    tail = poly * t * expo
    cdf = jnp.where(x < 0, tail, 1.0 - tail)
    return x * cdf, cdf + x * (expo * 0.3989422804014327)


def norm_parts(rows):
    center = rows - jnp.mean(rows, axis=-1, keepdims=True)
    rstd = lax.rsqrt(jnp.mean(center * center, axis=-1, keepdims=True) + NORM_EPS)
    return center * rstd, rstd


def norm_back(grad, hat, rstd):
    return rstd * (
        grad
        - jnp.mean(grad, axis=-1, keepdims=True)
        - hat * jnp.mean(grad * hat, axis=-1, keepdims=True)
    )


def params(limit):
    return pltpu.CompilerParams(vmem_limit_bytes=limit * MIB)


def tile_spec(block_of):
    return pl.BlockSpec(
        (1, 4, 1, BLK // 4, BLK),
        lambda i, own, slot: (own[block_of(i)], 0, slot[block_of(i)], 0, 0),
    )


def tile(ref):
    return ref[...].reshape(BLK, BLK)


def full_spec(shape):
    return pl.BlockSpec(shape, lambda i, own, slot: (0,) * len(shape))


def put_tile(ref, i, value):
    rows = BLK // 4
    low = value.astype(LOW)
    for quarter in range(4):
        ref[quarter % 2, quarter // 2, i, 0] = low[quarter * rows : quarter * rows + rows]


def qkv_kernel(own, slot, x_ref, vec_ref, bias_ref, t0, t1, qkv_ref, a_ref):
    @pl.when(pl.program_id(0) == 0)
    def _():
        hat, _ = norm_parts(x_ref[...].astype(F32))
        a_ref[...] = (hat * vec_ref[0:1, :] + vec_ref[1:2, :]).astype(LOW)

    total = dot(a_ref[:, :BLK], tile(t0), 1, 0) + dot(a_ref[:, BLK:], tile(t1), 1, 0)
    qkv_ref[...] = (total + bias_ref[...]).astype(LOW)


def qkv_forward(own, slot, x, vec, bias, gathered):
    rows = x.shape[0]
    return pl.pallas_call(
        qkv_kernel,
        grid_spec=pltpu.PrefetchScalarGridSpec(
            num_scalar_prefetch=2,
            grid=(6,),
            in_specs=[
                full_spec((rows, D)),
                full_spec(vec.shape),
                pl.BlockSpec((1, BLK), lambda i, own, slot: (0, i)),
                tile_spec(lambda i: i),
                tile_spec(lambda i: 6 + i),
            ],
            out_specs=[
                pl.BlockSpec((rows, BLK), lambda i, own, slot: (0, i)),
                full_spec((rows, D)),
            ],
        ),
        out_shape=[
            jax.ShapeDtypeStruct((rows, 3 * D), LOW),
            jax.ShapeDtypeStruct((rows, D), LOW),
        ],
        compiler_params=params(48),
        name="qkv",
    )(own, slot, x, vec, bias, gathered, gathered)


def attn_fwd_kernel(q_ref, k1, v1, k2, v2, bias_ref, o_ref, lse_ref, ka, kb, va, vb):
    rows = k1.shape[0]

    @pl.when(pl.program_id(1) == 0)
    def _():
        ln = lanes((rows, 128))
        for i, (k, v) in enumerate(((k1, v1), (k2, v2))):
            r = slice(i * rows, i * rows + rows)
            keys, values, bias = k[...], v[...], bias_ref[r, :]
            one = jnp.ones_like(values)
            ka[r, :] = jnp.where(ln == 64, bias, keys)
            kb[r, :] = jnp.where(ln == 0, bias, keys)
            va[r, :] = jnp.where(ln < 64, values, one)
            vb[r, :] = jnp.where(ln < 64, one, values)

    q = q_ref[...] * jnp.asarray(0.125, LOW)
    ln = lanes(q.shape)
    one, zero = jnp.ones_like(q), jnp.zeros_like(q)
    qa = jnp.where(ln < 64, q, jnp.where(ln == 64, one, zero))
    qb = jnp.where(ln < 64, jnp.where(ln == 0, one, zero), q)
    outs, tops = [], []
    for query, keys, values in ((qa, ka, va), (qb, kb, vb)):
        logits = dot(query, keys[...], 1, 1)
        top = jnp.max(logits, axis=1, keepdims=True)
        expo = jnp.exp(logits - top).astype(LOW)
        outs.append(dot(expo, values[...], 1, 0))
        tops.append(top)
    total = jnp.where(ln < 64, outs[1], outs[0])
    attended = jnp.where(ln < 64, outs[0], outs[1])
    o_ref[...] = (attended / pltpu.roll(total, 64, 1)).astype(LOW)
    lse_ref[...] = jnp.where(ln < 64, tops[1], tops[0]) + jnp.log(total)


def attn_forward(qkv, other, bias, q_rows=256):
    rows, pairs = qkv.shape[0], D // 128
    keys = 2 * rows
    q_spec = pl.BlockSpec((q_rows, 128), lambda p, i: (i, p))
    return pl.pallas_call(
        attn_fwd_kernel,
        grid=(pairs, rows // q_rows),
        in_specs=[
            q_spec,
            pl.BlockSpec((rows, 128), lambda p, i: (0, pairs + p)),
            pl.BlockSpec((rows, 128), lambda p, i: (0, 2 * pairs + p)),
            pl.BlockSpec((rows, 128), lambda p, i: (0, p)),
            pl.BlockSpec((rows, 128), lambda p, i: (0, pairs + p)),
            pl.BlockSpec((keys, 128), lambda p, i: (0, 0)),
        ],
        out_specs=[q_spec, q_spec],
        out_shape=[
            jax.ShapeDtypeStruct((rows, D), LOW),
            jax.ShapeDtypeStruct((rows, D), F32),
        ],
        scratch_shapes=[pltpu.VMEM((keys, 128), LOW)] * 4,
        compiler_params=params(48),
        name="attn_fwd",
    )(qkv, qkv, qkv, other, other, bias)


def three_parts(x):
    high = x.astype(LOW).astype(F32)
    rest = x - high
    mid = rest.astype(LOW).astype(F32)
    return high, mid, rest - mid


def with_spare(x, spare, value, one, first):
    ln = lanes(x.shape)
    high, mid, low = three_parts(value)
    filled = jnp.where(ln == first + 3, one, 0.0)
    for i, part in enumerate((high, mid, low)):
        filled = jnp.where(ln == first + i, part, filled)
    return jnp.where(spare, filled, x).astype(LOW)


def attn_bwd_kernel(
    q_ref, k1, v1, k2, v2, bias_ref, o_ref, lse_ref, do_ref,
    dq_ref, dk1, dv1, dk2, dv2, ka, kb, va, vb, kt, dk, dv, *, chunk,
):
    rows = k1.shape[0]

    @pl.when(pl.program_id(1) == 0)
    def _():
        ln = lanes((rows, 128))
        for i, (k, v) in enumerate(((k1, v1), (k2, v2))):
            r = slice(i * rows, i * rows + rows)
            keys, values, bias = k[...], v[...], bias_ref[r, :]
            one, zero = jnp.ones_like(values), jnp.zeros_like(values)
            ka[r, :] = jnp.where(ln < 64, keys, jnp.where(ln < 67, one, jnp.where(ln == 67, bias, zero)))
            kb[r, :] = jnp.where(ln >= 64, keys, jnp.where(ln < 3, one, jnp.where(ln == 3, bias, zero)))
            va[r, :] = jnp.where(ln < 64, values, jnp.where(ln < 67, one, zero))
            vb[r, :] = jnp.where(ln >= 64, values, jnp.where(ln < 3, one, zero))
            kt[:, r] = keys.T
        dk[...] = jnp.zeros_like(dk)
        dv[...] = jnp.zeros_like(dv)

    q = q_ref[...].astype(F32) * 0.125
    left = lanes(q.shape) < 64
    grad = do_ref[...].astype(F32)
    prod = grad * o_ref[...].astype(F32)
    sum_a = jnp.sum(jnp.where(left, prod, 0.0), axis=1, keepdims=True)
    sum_b = jnp.sum(jnp.where(left, 0.0, prod), axis=1, keepdims=True)
    delta = jnp.where(left, sum_b, sum_a)
    lse = lse_ref[...]
    zero = jnp.zeros_like(q)
    heads = (
        (
            with_spare(q, ~left, -lse, 1.0, 64), with_spare(grad, ~left, -delta, 0.0, 64), ka, va,
            jnp.where(left, q, zero).astype(LOW), jnp.where(left, grad, zero).astype(LOW),
        ),
        (
            with_spare(q, left, -lse, 1.0, 0), with_spare(grad, left, -delta, 0.0, 0), kb, vb,
            jnp.where(left, zero, q).astype(LOW), jnp.where(left, zero, grad).astype(LOW),
        ),
    )
    d_query = [jnp.zeros((64, q.shape[0]), F32)] * 2
    for c in range(2 * rows // chunk):
        r = slice(c * chunk, c * chunk + chunk)
        dv_c, dk_c = dv[r, :], dk[r, :]
        for h, (q_aug, g_aug, keys, values, q_only, g_only) in enumerate(heads):
            probs = jnp.exp(dot(keys[r, :], q_aug, 1, 1))
            d_logits = (probs * dot(values[r, :], g_aug, 1, 1)).astype(LOW)
            dv_c = dv_c + dot(probs.astype(LOW), g_only, 1, 0)
            dk_c = dk_c + dot(d_logits, q_only, 1, 0)
            d_query[h] = d_query[h] + dot(kt[64 * h : 64 * h + 64, r], d_logits, 1, 0)
        dv[r, :] = dv_c
        dk[r, :] = dk_c
    dq_ref[...] = (jnp.concatenate(d_query, axis=0) * 0.125).T.astype(LOW)

    @pl.when(pl.program_id(1) == pl.num_programs(1) - 1)
    def _():
        dk1[...] = dk[:rows, :].astype(LOW)
        dk2[...] = dk[rows:, :].astype(LOW)
        dv1[...] = dv[:rows, :].astype(LOW)
        dv2[...] = dv[rows:, :].astype(LOW)


def attn_backward(qkv, other, bias, attn, lse, d_attn, q_rows=512, chunk=1024):
    rows, pairs = qkv.shape[0], D // 128
    keys = 2 * rows
    q_spec = pl.BlockSpec((q_rows, 128), lambda p, i: (i, p))
    k_spec = pl.BlockSpec((rows, 128), lambda p, i: (0, p))
    return pl.pallas_call(
        functools.partial(attn_bwd_kernel, chunk=chunk),
        grid=(pairs, rows // q_rows),
        in_specs=[
            q_spec,
            pl.BlockSpec((rows, 128), lambda p, i: (0, pairs + p)),
            pl.BlockSpec((rows, 128), lambda p, i: (0, 2 * pairs + p)),
            k_spec,
            pl.BlockSpec((rows, 128), lambda p, i: (0, pairs + p)),
            pl.BlockSpec((keys, 128), lambda p, i: (0, 0)),
            q_spec,
            q_spec,
            q_spec,
        ],
        out_specs=[q_spec, k_spec, k_spec, k_spec, k_spec],
        out_shape=[jax.ShapeDtypeStruct((rows, D), LOW)] * 5,
        scratch_shapes=[pltpu.VMEM((keys, 128), LOW)] * 4
        + [pltpu.VMEM((128, keys), LOW)]
        + [pltpu.VMEM((keys, 128), F32)] * 2,
        compiler_params=params(56),
        name="attn_bwd",
    )(qkv, qkv, qkv, other, other, bias, attn, lse, d_attn)


def mid_kernel(
    own, slot, x_ref, attn_ref, dy_ref, vec_ref, b1_ref, o00, o01, o10, o11, u0, u1, w0, w1,
    res_ref, dmid_ref, dattn_ref, g_up, g_down, g_out, sums_ref, gb1_ref,
    mid, a2, acc, da2, *, chunk,
):
    step = pl.program_id(0)
    last = pl.num_programs(0) - 1

    @pl.when(step == 0)
    def _():
        left, right = attn_ref[:, :BLK], attn_ref[:, BLK:]
        for j, (top, bottom) in enumerate(((o00, o10), (o01, o11))):
            c = slice(j * BLK, j * BLK + BLK)
            mid[:, c] = (
                x_ref[:, c].astype(F32)
                + (dot(left, tile(top), 1, 0) + dot(right, tile(bottom), 1, 0))
                + vec_ref[6:7, c]
            )
        hat, _ = norm_parts(mid[...])
        a2[...] = (hat * vec_ref[2:3, :] + vec_ref[3:4, :]).astype(LOW)
        acc[...] = jnp.zeros_like(acc)
        da2[...] = jnp.zeros_like(da2)

    @pl.when((step > 0) & (step < last))
    def _():
        rows = a2.shape[0]
        up0, up1, down0, down1 = tile(u0), tile(u1), tile(w0), tile(w1)
        bias_grad = jnp.zeros((1, BLK), F32)
        acts, d_hids = [], []
        for c in range(rows // chunk):
            r = slice(c * chunk, c * chunk + chunk)
            hidden = dot(a2[r, :BLK], up0, 1, 0) + dot(a2[r, BLK:], up1, 1, 0) + b1_ref[...]
            act, slope = gelu_pair(hidden)
            act = act.astype(LOW)
            back = dot(dy_ref[r, :BLK], down0, 1, 1) + dot(dy_ref[r, BLK:], down1, 1, 1)
            d_hid = (back * slope).astype(LOW)
            acc[r, :BLK] += dot(act, down0, 1, 0)
            acc[r, BLK:] += dot(act, down1, 1, 0)
            da2[r, :BLK] += dot(d_hid, up0, 1, 1)
            da2[r, BLK:] += dot(d_hid, up1, 1, 1)
            bias_grad = bias_grad + jnp.sum(d_hid.astype(F32), axis=0, keepdims=True)
            acts.append(act)
            d_hids.append(d_hid)
        gb1_ref[...] = bias_grad
        act = jnp.concatenate(acts, axis=0)
        d_hid = jnp.concatenate(d_hids, axis=0)
        for j in range(2):
            c = slice(j * BLK, j * BLK + BLK)
            put_tile(g_up, j, dot(a2[:, c], d_hid, 0, 0))
            rows_q = BLK // 4
            low = dot(act, dy_ref[:, c], 0, 0).astype(LOW)
            for quarter in range(4):
                g_down[quarter % 2, quarter // 2, 0, j] = low[quarter * rows_q : quarter * rows_q + rows_q]

    @pl.when(step == last)
    def _():
        res_ref[...] = (mid[...] + acc[...] + vec_ref[7:8, :]).astype(LOW)
        hat, rstd = norm_parts(mid[...])
        grad = da2[...]
        dy = dy_ref[...].astype(F32)
        sums_ref[0:1, :] = jnp.sum(hat * grad, axis=0, keepdims=True)
        sums_ref[1:2, :] = jnp.sum(grad, axis=0, keepdims=True)
        d_mid = dy + norm_back(grad * vec_ref[2:3, :], hat, rstd)
        dmid_ref[...] = d_mid
        d_proj = d_mid.astype(LOW)
        sums_ref[2:3, :] = jnp.sum(d_proj.astype(F32), axis=0, keepdims=True)
        sums_ref[3:4, :] = jnp.sum(dy, axis=0, keepdims=True)
        sums_ref[4:8, :] = jnp.zeros((4, D), F32)
        for i, (first, second) in enumerate(((o00, o01), (o10, o11))):
            c = slice(i * BLK, i * BLK + BLK)
            dattn_ref[:, c] = (
                dot(d_proj[:, :BLK], tile(first), 1, 1) + dot(d_proj[:, BLK:], tile(second), 1, 1)
            ).astype(LOW)
            for j in range(2):
                rows_q = BLK // 4
                low = dot(attn_ref[:, c], d_proj[:, j * BLK : j * BLK + BLK], 0, 0).astype(LOW)
                for quarter in range(4):
                    g_out[quarter % 2, quarter // 2, i, j] = low[quarter * rows_q : quarter * rows_q + rows_q]


def mid_layer(own, slot, x, attn, dy, vec, b1, gathered, chunk=256):
    rows = x.shape[0]
    wide = FF // BLK
    quarter = BLK // 4

    def part(i):
        return jnp.clip(i - 1, 0, wide - 1)

    row_spec = full_spec((rows, D))
    return pl.pallas_call(
        functools.partial(mid_kernel, chunk=chunk),
        grid_spec=pltpu.PrefetchScalarGridSpec(
            num_scalar_prefetch=2,
            grid=(wide + 2,),
            in_specs=[
                row_spec,
                row_spec,
                row_spec,
                full_spec(vec.shape),
                pl.BlockSpec((1, BLK), lambda i, own, slot: (0, part(i))),
                tile_spec(lambda i: 12),
                tile_spec(lambda i: 13),
                tile_spec(lambda i: 14),
                tile_spec(lambda i: 15),
                tile_spec(lambda i: 16 + part(i)),
                tile_spec(lambda i: 24 + part(i)),
                tile_spec(lambda i: 32 + 2 * part(i)),
                tile_spec(lambda i: 33 + 2 * part(i)),
            ],
            out_specs=[
                row_spec,
                row_spec,
                row_spec,
                pl.BlockSpec((2, 2, 2, 1, quarter, BLK), lambda i, own, slot: (0, 0, 0, part(i), 0, 0)),
                pl.BlockSpec((2, 2, 1, 2, quarter, BLK), lambda i, own, slot: (0, 0, part(i), 0, 0, 0)),
                full_spec((2, 2, 2, 2, quarter, BLK)),
                full_spec((8, D)),
                pl.BlockSpec((1, BLK), lambda i, own, slot: (0, part(i))),
            ],
            scratch_shapes=[
                pltpu.VMEM((rows, D), F32),
                pltpu.VMEM((rows, D), LOW),
                pltpu.VMEM((rows, D), F32),
                pltpu.VMEM((rows, D), F32),
            ],
        ),
        out_shape=[
            jax.ShapeDtypeStruct((rows, D), LOW),
            jax.ShapeDtypeStruct((rows, D), F32),
            jax.ShapeDtypeStruct((rows, D), LOW),
            jax.ShapeDtypeStruct((2, 2, 2, wide, quarter, BLK), LOW),
            jax.ShapeDtypeStruct((2, 2, wide, 2, quarter, BLK), LOW),
            jax.ShapeDtypeStruct((2, 2, 2, 2, quarter, BLK), LOW),
            jax.ShapeDtypeStruct((8, D), F32),
            jax.ShapeDtypeStruct((1, FF), F32),
        ],
        compiler_params=params(58),
        name="mid",
    )(own, slot, x, attn, dy, vec, b1, *([gathered] * 8))


def qkv_bwd_kernel(
    own, slot, x_ref, a_ref, dmid_ref, vec_ref, dq, dk, rk, dv, rv, t0, t1,
    dx_ref, g_qkv, sums_ref, cols_ref, acc,
):
    step = pl.program_id(0)

    @pl.when(step == 0)
    def _():
        acc[...] = jnp.zeros_like(acc)

    def work(d_cols):
        acc[:, :BLK] += dot(d_cols, tile(t0), 1, 1)
        acc[:, BLK:] += dot(d_cols, tile(t1), 1, 1)
        put_tile(g_qkv, 0, dot(a_ref[:, :BLK], d_cols, 0, 0))
        put_tile(g_qkv, 1, dot(a_ref[:, BLK:], d_cols, 0, 0))
        cols_ref[...] = jnp.sum(d_cols.astype(F32), axis=0, keepdims=True)

    @pl.when(step < 2)
    def _():
        work(dq[...])

    @pl.when((step >= 2) & (step < 4))
    def _():
        work((dk[...].astype(F32) + rk[...].astype(F32)).astype(LOW))

    @pl.when(step >= 4)
    def _():
        work((dv[...].astype(F32) + rv[...].astype(F32)).astype(LOW))

    @pl.when(step == 5)
    def _():
        hat, rstd = norm_parts(x_ref[...].astype(F32))
        grad = acc[...]
        sums_ref[0:1, :] = jnp.sum(hat * grad, axis=0, keepdims=True)
        sums_ref[1:2, :] = jnp.sum(grad, axis=0, keepdims=True)
        sums_ref[2:8, :] = jnp.zeros((6, D), F32)
        dx_ref[...] = (dmid_ref[...] + norm_back(grad * vec_ref[0:1, :], hat, rstd)).astype(LOW)


def qkv_backward(own, slot, x, normed, d_mid, vec, dq, dk, rk, dv, rv, gathered):
    rows = x.shape[0]
    quarter = BLK // 4
    row_spec = full_spec((rows, D))

    def cols(first):
        return pl.BlockSpec((rows, BLK), lambda i, own, slot: (0, jnp.clip(i - first, 0, 1)))

    return pl.pallas_call(
        qkv_bwd_kernel,
        grid_spec=pltpu.PrefetchScalarGridSpec(
            num_scalar_prefetch=2,
            grid=(6,),
            in_specs=[
                row_spec, row_spec, row_spec, full_spec(vec.shape),
                cols(0), cols(2), cols(2), cols(4), cols(4),
                tile_spec(lambda i: i), tile_spec(lambda i: 6 + i),
            ],
            out_specs=[
                row_spec,
                pl.BlockSpec((2, 2, 2, 1, quarter, BLK), lambda i, own, slot: (0, 0, 0, i, 0, 0)),
                full_spec((8, D)),
                pl.BlockSpec((1, BLK), lambda i, own, slot: (0, i)),
            ],
            scratch_shapes=[pltpu.VMEM((rows, D), F32)],
        ),
        out_shape=[
            jax.ShapeDtypeStruct((rows, D), LOW),
            jax.ShapeDtypeStruct((2, 2, 2, 6, quarter, BLK), LOW),
            jax.ShapeDtypeStruct((8, D), F32),
            jax.ShapeDtypeStruct((1, 3 * D), F32),
        ],
        compiler_params=params(58),
        name="qkv_bwd",
    )(own, slot, x, normed, d_mid, vec, dq, dk, rk, dv, rv, gathered, gathered)


def eliminate(y_ref):
    count, size = y_ref.shape[0], y_ref.shape[1]
    lane = lanes((1, 8, size))
    sub = lax.broadcasted_iota(jnp.int32, (1, 8, size), 1)
    wide_lane = lanes((size, size))
    shape = (count, 8, size)

    def group(g, carry):
        base = pl.multiple_of(8 * g, 8)
        slab = y_ref[:, pl.ds(base, 8), :]
        rolled = jnp.stack([pltpu.roll(slab[b], size - base, 1) for b in range(count)], axis=0)
        columns = [jnp.broadcast_to(rolled[:, :, k : k + 1], shape) for k in range(8)]
        inside = (lane >= base) & (lane < base + 8)
        rows = jnp.where(inside, jnp.where(lane - base == sub, 1.0, 0.0), slab)
        scale = jnp.zeros(shape, F32)
        for j in range(8):
            inv_root = lax.rsqrt(jnp.broadcast_to(columns[j][:, j : j + 1, :], shape))
            scale = jnp.where(sub == j, inv_root, scale)
            factor = jnp.where(sub > j, columns[j] * (inv_root * inv_root), 0.0)
            rows = rows - factor * jnp.broadcast_to(rows[:, j : j + 1, :], shape)
            for k in range(j + 1, 8):
                columns[k] = columns[k] - factor * jnp.broadcast_to(columns[k][:, j : j + 1, :], shape)
        rows = rows * scale
        below = jnp.where(lane >= base + 8, rows, 0.0)
        passed = (wide_lane >= base) & (wide_lane < base + 8)
        for b in range(count):
            high, mid, low = three_parts(rows[b])
            b_high, b_mid, b_low = three_parts(below[b])
            first = jnp.concatenate([b_high, b_high, b_mid, b_high, b_low, b_mid], axis=0)
            second = jnp.concatenate([high, mid, high, low, high, mid], axis=0)
            update = dot(first.astype(LOW), second.astype(LOW), 0, 0)
            y_ref[b] = jnp.where(passed, 0.0, y_ref[b]) - update
            y_ref[b, pl.ds(base, 8), :] = rows[b]
        return carry

    lax.fori_loop(0, size // 8, group, 0)


def soap_kernel(
    seq_ref, g0, g1, g2, g3, w_ref, one_ref, two_ref, ls_ref, rs_ref, lb_ref, rb_ref,
    grad_ref, w_out, one_out, two_out, ls_out, rs_out, lb_out, rb_out,
    grad_s, gram, work, inv,
):
    step = pl.program_id(0)
    slots = pl.num_programs(0)
    count = lb_out.shape[0]
    quarter = BLK // 4
    for piece, flip in ((g0, 0), (g1, 2), (g2, 1), (g3, 3)):
        start = pl.multiple_of((seq_ref[0] ^ flip) * quarter, quarter)
        grad_s[pl.ds(start, quarter), :] = piece[0].astype(F32)
    grad_ref[0] = grad_s[...]
    grad = grad_s[...].astype(LOW)
    left, right = lb_ref[0], rb_ref[0]
    left_low, right_low = left.astype(LOW), right.astype(LOW)
    rotated = dot(dot(left_low, grad, 0, 0).astype(LOW), right_low, 1, 0)
    one = BETA_ONE * one_ref[0] + (1.0 - BETA_ONE) * rotated
    two = BETA_TWO * two_ref[0] + (1.0 - BETA_TWO) * rotated * rotated
    one_out[0] = one
    two_out[0] = two
    scaled = (one / (1.0 - BETA_ONE**STEP)) / (jnp.sqrt(two / (1.0 - BETA_TWO**STEP)) + ADAM_EPS)
    back = dot(dot(left_low, scaled.astype(LOW), 1, 0).astype(LOW), right_low, 1, 1)
    w_out[0] = w_ref[0] - RATE_MATRIX * (back + DECAY_RATE * w_ref[0])
    left_new = BETA_STAT * ls_ref[0] + (1.0 - BETA_STAT) * dot(grad, grad, 1, 1)
    right_new = BETA_STAT * rs_ref[0] + (1.0 - BETA_STAT) * dot(grad, grad, 0, 0)
    ls_out[0] = left_new
    rs_out[0] = right_new
    for side, (stats, basis) in enumerate(((left_new, left), (right_new, right))):
        product = dot(stats, basis, 1, 0, HIGHEST)
        at = side * count + step
        work[at] = product
        gram[at] = dot(product, product, 0, 0, HIGHEST)

    @pl.when(step == slots - 1)
    def _():
        for p in range(BLK // 128):
            c = slice(128 * p, 128 * p + 128)
            rest = slice(128 * p + 128, BLK)
            inv[...] = gram[:, c, c]
            eliminate(inv)

            def solve(b, carry, out):
                at = b + (count if out is rb_out else 0)
                factor = inv[at]
                solved = dot(work[at, :, c], factor, 1, 1, HIGHEST)
                out[b, :, c] = solved
                if p < BLK // 128 - 1:
                    upper = dot(factor, gram[at, c, rest], 1, 0, HIGHEST)
                    work[at, :, rest] = work[at, :, rest] - dot(solved, upper, 1, 0, HIGHEST)
                    gram[at, rest, rest] = gram[at, rest, rest] - dot(upper, upper, 0, 0, HIGHEST)
                return carry

            lax.fori_loop(0, count, functools.partial(solve, out=lb_out), 0)
            lax.fori_loop(0, count, functools.partial(solve, out=rb_out), 0)


def soap_update(seq_id, pieces, master, one, two, left_stats, right_stats, left_basis, right_basis):
    count = master.shape[0]
    piece_spec = pl.BlockSpec((1, BLK // 4, BLK), lambda i, s: (i, 0, 0))
    block_spec = pl.BlockSpec((1, BLK, BLK), lambda i, s: (i, 0, 0))
    whole_spec = pl.BlockSpec((count, BLK, BLK), lambda i, s: (0, 0, 0))
    shape = jax.ShapeDtypeStruct((count, BLK, BLK), F32)
    return pl.pallas_call(
        soap_kernel,
        grid_spec=pltpu.PrefetchScalarGridSpec(
            num_scalar_prefetch=1,
            grid=(count,),
            in_specs=[piece_spec] * 4 + [block_spec] * 7,
            out_specs=[block_spec] * 6 + [whole_spec] * 2,
            scratch_shapes=[
                pltpu.VMEM((BLK, BLK), F32),
                pltpu.VMEM((2 * count, BLK, BLK), F32),
                pltpu.VMEM((2 * count, BLK, BLK), F32),
                pltpu.VMEM((2 * count, 128, 128), F32),
            ],
        ),
        out_shape=[shape] * 8,
        compiler_params=params(60),
        name="soap",
    )(seq_id, *pieces, master, one, two, left_stats, right_stats, left_basis, right_basis)


def swap(x, axis, bit):
    size = lax.axis_size(axis)
    return lax.ppermute(x, axis, [(i, i ^ bit) for i in range(size)])


def add_low(a, b):
    return (a.astype(F32) + b.astype(F32)).astype(LOW)


def halve(x, dim, axis, bit, mine):
    kept = lax.dynamic_index_in_dim(x, mine, dim, keepdims=False)
    sent = lax.dynamic_index_in_dim(x, 1 - mine, dim, keepdims=False)
    return add_low(kept, swap(sent, axis, bit))


def block_places(owners, owner_count, slot_count):
    block_count = owners.shape[0]
    ids = jnp.arange(block_count, dtype=jnp.int32)
    earlier = (owners[:, None] == owners[None, :]) & (ids[None, :] < ids[:, None])
    slots = jnp.sum(earlier.astype(jnp.int32), axis=1)
    places = owners * slot_count + slots
    matched = places[None, :] == jnp.arange(owner_count * slot_count, dtype=jnp.int32)[:, None]
    missing = 1 - jnp.any(matched, axis=1).astype(jnp.int32)
    sources = jnp.sum(jnp.where(matched, ids[None, :], 0), axis=1) + block_count * missing
    return slots, sources


def adam_vectors(gradient, vec, first_mom, second_mom):
    first_mom = BETA_ONE * first_mom + (1.0 - BETA_ONE) * gradient
    second_mom = BETA_TWO * second_mom + (1.0 - BETA_TWO) * gradient * gradient
    step_size = (first_mom / (1.0 - BETA_ONE**STEP)) / (
        jnp.sqrt(second_mom / (1.0 - BETA_TWO**STEP)) + ADAM_EPS
    )
    return first_mom, second_mom, vec - RATE_VECTOR * step_size


def on_device(
    tokens, cotangent, lengths, patch_mask, owners, master, moment_one, moment_two,
    left_stats, right_stats, left_basis, right_basis, vec, vec_one, vec_two,
):
    owner_count = lax.axis_size("dp")
    slot_count = master.shape[0]
    quarter = BLK // 4
    seq_id = lax.axis_index("seq").astype(jnp.int32)
    dp_id = lax.axis_index("dp").astype(jnp.int32)
    core, chip = seq_id % 2, seq_id // 2
    part_len = tokens.shape[1]
    slots, sources = block_places(owners, owner_count, slot_count)

    mine = lax.dynamic_index_in_dim(
        master.reshape(slot_count, 4, quarter, BLK), seq_id, 1, keepdims=False
    ).astype(LOW)
    gathered = lax.all_gather(mine, AXES, axis=0, tiled=False).reshape(
        owner_count, 4, slot_count, quarter, BLK
    )

    def to_sequence(pair):
        kept = lax.dynamic_index_in_dim(pair, chip, 0, keepdims=False)
        sent = lax.dynamic_index_in_dim(pair, 1 - chip, 0, keepdims=False)
        return jnp.concatenate([kept, swap(sent, "seq", 2)], axis=0)

    def to_positions(rows):
        other = swap(rows[part_len:], "seq", 2)
        mine = rows[:part_len]
        return jnp.where(chip == 0, jnp.stack([mine, other]), jnp.stack([other, mine]))

    x = to_sequence(tokens)
    dy = to_sequence(cotangent)

    positions = jnp.arange(patch_mask.shape[-1], dtype=jnp.int32)
    live = (positions[None, :] < lengths[:, None]) & ((patch_mask == 1) | (positions[None, :] == 0))
    live = lax.dynamic_index_in_dim(live, chip, 0, keepdims=False).reshape(4, part_len)
    order = seq_id ^ jnp.array([0, 2, 1, 3], jnp.int32)
    fill = jnp.where(jnp.take(live, order, axis=0).reshape(-1), 0.0, NEG_FILL).astype(LOW)
    fill = jnp.broadcast_to(fill[:, None], (fill.shape[0], 128))

    bias = jnp.concatenate([vec[4], jnp.zeros_like(vec[4]), vec[5]])[None, :]
    qkv, normed = qkv_forward(owners, slots, x, vec, bias, gathered)
    other = swap(qkv[:, D:], "seq", 1)
    attn, lse = attn_forward(qkv, other, fill)
    b1 = vec[8:].reshape(1, FF)
    result, d_mid, d_attn, g_up, g_down, g_out, sums_two, bias_grad = mid_layer(
        owners, slots, x, attn, dy, vec, b1, gathered
    )
    output = to_positions(result)
    early = jnp.concatenate(
        [g.reshape(2, 2, -1, quarter, BLK) for g in (g_out, g_up, g_down)], axis=2
    )
    early = halve(early, 0, "seq", 1, core)
    early = halve(early, 0, "seq", 2, chip)
    dq, dk, dv, sent_k, sent_v = attn_backward_order(qkv, other, fill, attn, lse, d_attn)
    got_k, got_v = swap(sent_k, "seq", 1), swap(sent_v, "seq", 1)
    d_x, g_qkv, sums_one, cols = qkv_backward(
        owners, slots, x, normed, d_mid, vec, dq, dk, got_k, dv, got_v, gathered
    )
    d_tokens = to_positions(d_x)
    late = g_qkv.reshape(2, 2, -1, quarter, BLK)
    late = halve(late, 0, "seq", 1, core)
    late = halve(late, 0, "seq", 2, chip)

    tiles = jnp.concatenate([late, early, jnp.zeros((1, quarter, BLK), LOW)], axis=0)
    owned = jnp.take(tiles, sources, axis=0).reshape(owner_count, slot_count, quarter, BLK)
    bit = 1
    while bit < owner_count:
        rest = owned.shape[0] // 2
        owned = halve(owned.reshape((rest, 2) + owned.shape[1:]), 1, "dp", bit, (dp_id // bit) % 2)
        bit *= 2
    owned = owned[0]

    across = swap(owned, "seq", 2)
    beside = swap(jnp.stack([owned, across]), "seq", 1)
    updates = soap_update(
        seq_id.reshape(1), (owned, across, beside[0], beside[1]), master, moment_one, moment_two,
        left_stats, right_stats, left_basis, right_basis,
    )

    vec_grad = jnp.concatenate(
        [
            sums_one[0:2],
            sums_two[0:2],
            cols[:, :D],
            cols[:, 2 * D :],
            sums_two[2:4],
            bias_grad.reshape(-1, D),
        ],
        axis=0,
    )
    vec_total = lax.psum(vec_grad, AXES)
    vec_first, vec_second, vec_next = adam_vectors(vec_total, vec, vec_one, vec_two)
    grad_blocks, w_new, one_new, two_new, ls_new, rs_new, lb_new, rb_new = updates
    return (
        output, d_tokens, grad_blocks, w_new, one_new, two_new, ls_new, rs_new, lb_new, rb_new,
        vec_first, vec_second, vec_next,
    )


def attn_backward_order(qkv, other, fill, attn, lse, d_attn):
    dq, dk1, dv1, dk2, dv2 = attn_backward(qkv, other, fill, attn, lse, d_attn)
    return dq, dk1, dv1, dk2, dv2


def solution(mesh):
    rows, blocks, whole = P("dp", "seq", None), P("dp", None, None), P()
    return jax.shard_map(
        on_device,
        mesh=mesh,
        in_specs=(rows, rows, P("dp"), P("dp", None), whole) + (blocks,) * 7 + (whole,) * 3,
        out_specs=(rows, rows) + (blocks,) * 8 + (whole,) * 3,
        check_vma=False,
    )
```

time: 2930 us -> 790 us (0.27)
  other arithmetic: 1210 us -> 32.1 us
  matrix products: 528 us -> 0 us
  waiting for transfers between devices: 676 us -> 296 us
  local copies, waits for them, and re-layouts: 397 us -> 36.7 us
  Pallas kernels: 0 us -> 343 us
    another operation x179 -> x1, other arithmetic: 1050 us -> 1.05 us  [on_device(): beside = swap(jnp.stack([owned, across]), 'seq', 1)]
    dot_general x132 -> x0, matrix products: 486 us -> none  [the longest x8 51.1 us: one_block(): jnp.einsum('hqk,qhd->khd', probs.astype(jnp.bfloat16), d_blk, preferred_e...]
    reduce_scatter x1 -> x0, waiting for transfers between devices: 423 us -> none  [on_device(): owned = lax.psum_scatter(ordered, 'dp', scatter_dimension=0, tiled=True)]
    pallas_call x0 -> x6, Pallas kernels: none -> 343 us  [the longest x1 115 us: soap_update(): pl.pallas_call(soap_kernel, grid_spec=pltpu.PrefetchScalarGridSpec(num_sc...]
    ppermute x0 -> x16, waiting for transfers between devices: none -> 211 us  [swap(): return lax.ppermute(x, axis, [(i, i ^ bit) for i in range(size)])]
    all_gather x1, waiting for transfers between devices: 194 us -> 85.3 us  [on_device(): lax.all_gather(mine, AXES, axis=0, tiled=False)]
    convert_element_type x16 -> x7, other arithmetic: 99.6 us -> 11.7 us  [add_low(): return (a.astype(F32) + b.astype(F32)).astype(LOW)]
    reshape x20 -> x2, local copies, waits for them, and re-layouts: 82.7 us -> 0.02 us  [the longest x1 0.01 us: on_device(): lax.dynamic_index_in_dim(live, chip, 0, keepdims=False).reshape(4, part_len)]
  transfers between devices with their start and end apart: 7 -> 17, of which waited for: 5 -> 11; matrix products, arithmetic and copies ran while one was open for 6% -> 4% of each run, Pallas kernels for 0% -> 12%
where the time goes in v1:
time: 790 us; the launch traced here: 784 us
  Pallas kernels  343 us (43%)
  waiting for transfers between devices  296 us (37%)
  blocking collectives  44.6 us (6%)
  local copies, waits for them, and re-layouts  36.7 us (5%)
  other arithmetic  32.1 us (4%)
  starting transfers between devices  16.1 us (2%)
  between operations  14.8 us (2%)
    ppermute x16, waiting for transfers between devices, swap(): return lax.ppermute(x, axis, [(i, i ^ bit) for i in range(size)])  211 us
    pallas_call x1, Pallas kernels, soap_update(): pl.pallas_call(soap_kernel, grid_spec=pltpu.PrefetchScalarGridSpec(num_sc...  115 us
    all_gather x1, waiting for transfers between devices, on_device(): lax.all_gather(mine, AXES, axis=0, tiled=False)  85.3 us
    pallas_call x1, Pallas kernels, mid_layer(): pl.pallas_call(functools.partial(mid_kernel, chunk=chunk), grid_spec=pltp...  74.9 us
    pallas_call x1, Pallas kernels, attn_backward(): pl.pallas_call(functools.partial(attn_bwd_kernel, chunk=chunk), grid=(pai...  73.5 us
    pallas_call x1, Pallas kernels, attn_forward(): pl.pallas_call(attn_fwd_kernel, grid=(pairs, rows // q_rows), in_specs=[q...  46.8 us
    psum x1, blocking collectives, on_device(): vec_total = lax.psum(vec_grad, AXES)  44.6 us
    pallas_call x1, Pallas kernels, qkv_backward(): pl.pallas_call(qkv_bwd_kernel, grid_spec=pltpu.PrefetchScalarGridSpec(num...  21.8 us
  transfers between devices with their start and end apart: 17, of which 11 were waited for; matrix products, arithmetic and copies ran while one was open for 4% of the time, Pallas kernels for 12%

profile of v1, /device:TPU:0, one launch (start us, length us, event | category | flops | bytes accessed | tf_op | source)
XLA Modules:
  0.0 783.7 jit_solution(5391320302751132347)
XLA Ops:
  10.8 3.0 collective-permute-start
  14.0 20.4 %collective-permute-done = bf16[512,768]{1,0:T(8,128)(2,1)S(1)} collective-permute-done((bf16[512,768]{1,0:T(8,128)(2,1)S(1)}, bf16[512,768]{1,0:T(8,128)(2,1)S(1)}, u32[]{:S(2)}, u32[]{:S(2)}) %collective-permute-start) | collective-permute-done | bytes 786464 | tf_op jit(solution)/shard_map/ppermute | solution.py:650
  34.6 85.3 %all-gather.3.cloned.1.call-done = bf16[192,1,96,384]{3,2,1,0:T(8,128)(2,1)} async-done(((bf16[6,1,96,384]{3,2,1,0:T(8,128)(2,1)}), bf16[192,1,96,384]{3,2,1,0:T(8,128)(2,1)}) %all-gather.3.cloned.1.call-update) | async-done | bytes 14155792 | tf_op jit(solution)/shard_map/all_gather | solution.py:700
  119.9 10.9 %qkv.1 = (bf16[1024,2304]{1,0:T(8,128)(2,1)}, bf16[1024,768]{1,0:T(8,128)(2,1)S(1)}) custom-call(s32[48]{0:T(128)S(1)} %copy-done.7, s32[48]{0:T(128)S(1)} %convert_reduce_fusion.slot, bf16[1024,768]{1,0:T(8,128)(2,1)S(1)} %pad_maximum_fusion.1.x_ref, f32[12,768]{1,0:T(8,128)S(1)} %copy-done.5, f32[1,2304]{1,0:T(1,128)S(1)} %broadcast_in_dim.66.bias_ref, ...), custom_call_target="tpu_custom_call" | custom-call | tf_op jit(solution)/shard_map/qkv/pallas_call | solution.py:118
  130.9 2.7 slice.47
  139.2 16.0 %collective-permute-done.2 = bf16[512,768]{1,0:T(8,128)(2,1)} collective-permute-done((bf16[512,768]{1,0:T(8,128)(2,1)}, bf16[512,768]{1,0:T(8,128)(2,1)}, u32[]{:S(2)}, u32[]{:S(2)}) %collective-permute-start.2) | collective-permute-done | bytes 786464 | tf_op jit(solution)/shard_map/ppermute | solution.py:650
  155.2 2.6 pad_maximum_fusion.2.dy_ref
  158.1 46.8 %attn_fwd.1 = (bf16[1024,768]{1,0:T(8,128)(2,1)S(1)}, f32[1024,768]{1,0:T(8,128)S(1)}) custom-call(bf16[1024,2304]{1,0:T(8,128)(2,1)} %get-tuple-element.42.q_ref.k1.v1, bf16[1024,2304]{1,0:T(8,128)(2,1)} %get-tuple-element.42.q_ref.k1.v1, bf16[1024,2304]{1,0:T(8,128)(2,1)} %get-tuple-element.42.q_ref.k1.v1, ...), custom_call_target="tpu_custom_call" | custom-call | tf_op jit(solution)/shard_map/attn_fwd/pallas_call | solution.py:181
  207.8 74.9 %mid.1 = (bf16[1024,768]{1,0:T(8,128)(2,1)}, f32[1024,768]{1,0:T(8,128)}, bf16[1024,768]{1,0:T(8,128)(2,1)}, bf16[2,2,2,8,96,384]{5,4,3,2,1,0:T(8,128)(2,1)}, bf...) custom-call(s32[48]{0:T(128)} %own.5, ...), custom_call_target="tpu_custom_call" | custom-call | tf_op jit(solution)/shard_map/mid/pallas_call | solution.py:399
  282.7 5.7 pad_maximum_fusion
  288.4 3.1 dynamic-slice_bitcast_fusion
  291.6 2.3 copy-done.11
  293.9 73.5 %attn_bwd.1 = (bf16[1024,768]{1,0:T(8,128)(2,1)}, bf16[1024,768]{1,0:T(8,128)(2,1)}, bf16[1024,768]{1,0:T(8,128)(2,1)}, bf16[1024,768]{1,0:T(8,128)(2,1)}, bf16[1024,768]{1,0:T(8,128)(2,1)}) custom-call(bf16[1024,2304]{1,0:T(8,128)(2,1)} %get-tuple-element.42.q_ref.k1.v1, bf16[1024,2304]{1,0:T(8,128)(2,1)} %get-tuple-element.42.q_ref.k1.v1, ...), custom_call_target="tpu_custom_call" | custom-call | tf_op jit(solution)/shard_map/attn_bwd/pallas_call | solution.py:286
  368.0 3.2 collective-permute-done.4.rk
  371.2 2.2 collective-permute-done.5.rv
  374.6 21.8 %qkv_bwd.1 = (bf16[1024,768]{1,0:T(8,128)(2,1)}, bf16[2,2,2,6,96,384]{5,4,3,2,1,0:T(8,128)(2,1)}, f32[8,768]{1,0:T(8,128)}, f32[1,2304]{1,0:T(1,128)}) custom-call(s32[48]{0:T(128)} %own.5, s32[48]{0:T(128)} %copy-done.9, bf16[1024,768]{1,0:T(8,128)(2,1)} %copy-done, bf16[1024,768]{1,0:T(8,128)(2,1)} %copy-done.4, f32[1024,768]{1,0:T(8,128)} %get-tuple-element.46.dmid_ref, ...), custom_call_target="tpu_custom_call" | custom-call | tf_op jit(solution)/shard_map/qkv_bwd/pallas_call | solution.py:498
  398.5 5.5 fusion
  411.1 73.5 %collective-permute-done.8 = bf16[12,96,384]{2,1,0:T(8,128)(2,1)S(1)} collective-permute-done((bf16[12,96,384]{2,1,0:T(8,128)(2,1)S(1)}, bf16[12,96,384]{2,1,0:T(8,128)(2,1)S(1)}, u32[]{:S(2)}, u32[]{:S(2)}) %collective-permute-start.8) | collective-permute-done | bytes 884768 | tf_op jit(solution)/shard_map/ppermute | solution.py:650
  484.8 3.2 fusion.1
  488.1 2.3 maximum_maximum_fusion
  490.4 3.4 gather_fusion.1
  497.8 38.3 %collective-permute-done.11 = bf16[4,6,96,384]{3,2,1,0:T(8,128)(2,1)S(1)} collective-permute-done((bf16[4,6,96,384]{3,2,1,0:T(8,128)(2,1)S(1)}, bf16[4,6,96,384]{3,2,1,0:T(8,128)(2,1)S(1)}, u32[]{:S(2)}, u32[]{:S(2)}) %collective-permute-start.11) | collective-permute-done | bytes 1769504 | tf_op jit(solution)/shard_map/ppermute | solution.py:650
  538.8 19.3 %collective-permute-done.12 = bf16[2,6,96,384]{3,2,1,0:T(8,128)(2,1)S(1)} collective-permute-done((bf16[2,6,96,384]{3,2,1,0:T(8,128)(2,1)S(1)}, bf16[2,6,96,384]{3,2,1,0:T(8,128)(2,1)S(1)}, u32[]{:S(2)}, u32[]{:S(2)}) %collective-permute-start.12) | collective-permute-done | bytes 884768 | tf_op jit(solution)/shard_map/ppermute | solution.py:650
  560.0 18.5 %collective-permute-done.13 = bf16[1,6,96,384]{3,2,1,0:T(8,128)(2,1)S(1)} collective-permute-done((bf16[1,6,96,384]{3,2,1,0:T(8,128)(2,1)S(1)}, bf16[1,6,96,384]{3,2,1,0:T(8,128)(2,1)S(1)}, u32[]{:S(2)}, u32[]{:S(2)}) %collective-permute-start.13) | collective-permute-done | bytes 442400 | tf_op jit(solution)/shard_map/ppermute | solution.py:650
  580.0 2.4 slice_bitcast_fusion.1
  583.0 2.4 slice_bitcast_fusion
  586.9 4.8 collective-permute-done.14.g1
  593.9 14.7 %collective-permute-done.3 = bf16[512,768]{1,0:T(8,128)(2,1)} collective-permute-done((bf16[512,768]{1,0:T(8,128)(2,1)}, bf16[512,768]{1,0:T(8,128)(2,1)}, u32[]{:S(2)}, u32[]{:S(2)}) %collective-permute-start.3) | collective-permute-done | bytes 786464 | tf_op jit(solution)/shard_map/ppermute | solution.py:650
  608.6 2.8 maximum_select_fusion
  612.3 44.6 %psum.7 = f32[12,768]{1,0:T(8,128)S(1)} all-reduce(f32[12,768]{1,0:T(8,128)S(1)} %concatenate.23), channel_id=1, replica_groups=mesh['dp'=8,'seq'=4] {'dp','seq'}, use_global_device_ids=true, to_apply=%region_3.4 | all-reduce | flops 9216 | bytes 73728 | tf_op jit(solution)/shard_map/psum | solution.py:775
  657.6 2.8 maximum_select_fusion.1
  661.4 115.3 %soap.1 = (f32[6,384,384]{2,1,0:T(8,128)}, f32[6,384,384]{2,1,0:T(8,128)}, f32[6,384,384]{2,1,0:T(8,128)}, f32[6,384,384]{2,1,0:T(8,128)}, f32[6,384,384]{2,1,0:...) custom-call(s32[1]{0:T(128)} %bitcast.10.seq_ref, bf16[6,96,384]{2,1,0:T(8,128)(2,1)} %bitcast.92, ...), custom_call_target="tpu_custom_call" | custom-call | tf_op jit(solution)/shard_map/soap/pallas_call | solution.py:628
  (129 shorter events, 40.7 us)
Async XLA Ops:
  7.2 6.6 copy-start.5
  7.2 6.7 copy-start.7
  7.2 112.7 %all-gather.3.cloned.1.call-start = ((), (), s32[]{:S(2)}) async-start(), calls=%async_computation | async-start | bytes 14598144 | tf_op jit(solution)/shard_map/all_gather | solution.py:700
  10.8 23.7 %collective-permute-start = (bf16[512,768]{1,0:T(8,128)(2,1)S(1)}, bf16[512,768]{1,0:T(8,128)(2,1)S(1)}, u32[]{:S(2)}, u32[]{:S(2)}) collective-permute-start(bf16[512,768]{1,0:T(8,128)(2,1)S(1)} %get-tuple-element.87), channel_id=1, source_target_pairs={{0,2},{1,3},{2,0},{3,1},{4,6},{5,7},{6,4},{7,5},{8,10},{9,11},{10,... | collective-permute-start | bytes 2359304 | tf_op jit(solution)/shard_map/ppermute | solution.py:650
  14.0 116.8 %copy-start.9 = (s32[48]{0:T(128)}, s32[48]{0:T(128)S(1)}, u32[]{:S(2)}) copy-start(s32[48]{0:T(128)S(1)} %convert_reduce_fusion.slot) | copy-start | bytes 580
  34.6 96.3 %copy-start = (bf16[1024,768]{1,0:T(8,128)(2,1)}, bf16[1024,768]{1,0:T(8,128)(2,1)S(1)}, u32[]{:S(2)}) copy-start(bf16[1024,768]{1,0:T(8,128)(2,1)S(1)} %pad_maximum_fusion.1.x_ref) | copy-start | bytes 4718596
  133.6 24.2 %collective-permute-start.1 = (bf16[1024,1536]{1,0:T(8,128)(2,1)S(1)}, bf16[1024,1536]{1,0:T(8,128)(2,1)}, u32[]{:S(2)}, u32[]{:S(2)}) collective-permute-start(bf16[1024,1536]{1,0:T(8,128)(2,1)S(1)} %slice.47), channel_id=1, source_target_pairs={{0,1},{1,0},{2,3},{3,2},{4,5},{5,4},{6,7},{7,6},{8,9},{9,8},{10,11... | collective-permute-start | bytes 9437192 | tf_op jit(solution)/shard_map/ppermute | solution.py:650
  135.2 20.0 %collective-permute-start.2 = (bf16[512,768]{1,0:T(8,128)(2,1)}, bf16[512,768]{1,0:T(8,128)(2,1)}, u32[]{:S(2)}, u32[]{:S(2)}) collective-permute-start(bf16[512,768]{1,0:T(8,128)(2,1)} %get-tuple-element.85), channel_id=1, source_target_pairs={{0,2},{1,3},{2,0},{3,1},{4,6},{5,7},{6,4},{7,5},{8,10},{9,11},{10,... | collective-permute-start | bytes 2359304 | tf_op jit(solution)/shard_map/ppermute | solution.py:650
  158.1 46.8 %copy-start.2 = (bf16[2048,128]{1,0:T(8,128)(2,1)}, bf16[2048,128]{1,0:T(8,128)(2,1)S(1)}, u32[]{:S(2)}) copy-start(bf16[2048,128]{1,0:T(8,128)(2,1)S(1)} %broadcast_in_dim.72.bias_ref) | copy-start | bytes 1572868
  288.4 5.5 copy-start.11
  293.9 104.6 %collective-permute-start.9 = (bf16[2,36,96,384]{3,2,1,0:T(8,128)(2,1)}, bf16[2,36,96,384]{3,2,1,0:T(8,128)(2,1)}, u32[]{:S(2)}, u32[]{:S(2)}) collective-permute-start(bf16[2,36,96,384]{3,2,1,0:T(8,128)(2,1)} %dynamic-slice_bitcast_fusion), channel_id=1, source_target_pairs={{0,1},{1,0},{2,3},{3,2},{4,5},{5,4},{6,7},{7,6},{8,9},{9,8},{10,11... | collective-permute-start | bytes 15925256 | tf_op jit(solution)/shard_map/ppermute | solution.py:650
  367.4 3.8 collective-permute-start.4
  368.0 5.5 collective-permute-start.5
  398.1 9.2 %collective-permute-start.7 = (bf16[2,12,96,384]{3,2,1,0:T(8,128)(2,1)S(1)}, bf16[2,12,96,384]{3,2,1,0:T(8,128)(2,1)S(1)}, u32[]{:S(2)}, u32[]{:S(2)}) collective-permute-start(bf16[2,12,96,384]{3,2,1,0:T(8,128)(2,1)S(1)} %dynamic-slice_bitcast_fusion.3), channel_id=1, source_target_pairs={{0,1},{1,0},{2,3},{3,2},{4,5},{5,4},{6,7},{7,6},{8,9},{9,8},{10,11... | collective-permute-start | bytes 5308424 | tf_op jit(solution)/shard_map/ppermute | solution.py:650
  404.0 5.1 copy-start.12
  405.8 79.0 %collective-permute-start.10 = (bf16[36,96,384]{2,1,0:T(8,128)(2,1)}, bf16[36,96,384]{2,1,0:T(8,128)(2,1)}, u32[]{:S(2)}, u32[]{:S(2)}) collective-permute-start(bf16[36,96,384]{2,1,0:T(8,128)(2,1)} %dynamic-slice_bitcast_fusion.1), channel_id=1, source_target_pairs={{0,2},{1,3},{2,0},{3,1},{4,6},{5,7},{6,4},{7,5},{8,10},{9,11},{10,... | collective-permute-start | bytes 7962632 | tf_op jit(solution)/shard_map/ppermute | solution.py:650
  409.2 75.4 %collective-permute-start.8 = (bf16[12,96,384]{2,1,0:T(8,128)(2,1)S(1)}, bf16[12,96,384]{2,1,0:T(8,128)(2,1)S(1)}, u32[]{:S(2)}, u32[]{:S(2)}) collective-permute-start(bf16[12,96,384]{2,1,0:T(8,128)(2,1)S(1)} %dynamic-slice_bitcast_fusion.5), channel_id=1, source_target_pairs={{0,2},{1,3},{2,0},{3,1},{4,6},{5,7},{6,4},{7,5},{8,10},{9,11},{10,... | collective-permute-start | bytes 2654216 | tf_op jit(solution)/shard_map/ppermute | solution.py:650
  496.2 39.9 %collective-permute-start.11 = (bf16[4,6,96,384]{3,2,1,0:T(8,128)(2,1)S(1)}, bf16[4,6,96,384]{3,2,1,0:T(8,128)(2,1)S(1)}, u32[]{:S(2)}, u32[]{:S(2)}) collective-permute-start(bf16[4,6,96,384]{3,2,1,0:T(8,128)(2,1)S(1)} %dynamic-slice_bitcast_fusion.2), channel_id=1, source_target_pairs={{0,4},{4,0},{8,12},{12,8},{16,20},{20,16},{24,28},{28,24},{1,5},{5... | collective-permute-start | bytes 5308424 | tf_op jit(solution)/shard_map/ppermute | solution.py:650
  538.2 20.0 %collective-permute-start.12 = (bf16[2,6,96,384]{3,2,1,0:T(8,128)(2,1)S(1)}, bf16[2,6,96,384]{3,2,1,0:T(8,128)(2,1)S(1)}, u32[]{:S(2)}, u32[]{:S(2)}) collective-permute-start(bf16[2,6,96,384]{3,2,1,0:T(8,128)(2,1)S(1)} %dynamic-slice_bitcast_fusion.4), channel_id=1, source_target_pairs={{0,8},{4,12},{8,0},{12,4},{16,24},{20,28},{24,16},{28,20},{1,9},{5... | collective-permute-start | bytes 2654216 | tf_op jit(solution)/shard_map/ppermute | solution.py:650
  558.4 20.0 %collective-permute-start.13 = (bf16[1,6,96,384]{3,2,1,0:T(8,128)(2,1)S(1)}, bf16[1,6,96,384]{3,2,1,0:T(8,128)(2,1)S(1)}, u32[]{:S(2)}, u32[]{:S(2)}) collective-permute-start(bf16[1,6,96,384]{3,2,1,0:T(8,128)(2,1)S(1)} %constant_dynamic-slice_fusion), channel_id=1, source_target_pairs={{0,16},{4,20},{8,24},{12,28},{16,0},{20,4},{24,8},{28,12},{1,17},{... | collective-permute-start | bytes 1327112 | tf_op jit(solution)/shard_map/ppermute | solution.py:650
  578.5 13.1 %copy-start.14 = (bf16[1,6,96,384]{3,2,1,0:T(8,128)(2,1)}, bf16[1,6,96,384]{3,2,1,0:T(8,128)(2,1)S(1)}, u32[]{:S(2)}) copy-start(bf16[1,6,96,384]{3,2,1,0:T(8,128)(2,1)S(1)} %add_convert_fusion) | copy-start | bytes 1327108
  578.6 13.1 %collective-permute-start.14 = (bf16[6,96,384]{2,1,0:T(8,128)(2,1)S(1)}, bf16[6,96,384]{2,1,0:T(8,128)(2,1)S(1)}, u32[]{:S(2)}, u32[]{:S(2)}) collective-permute-start(bf16[6,96,384]{2,1,0:T(8,128)(2,1)S(1)} %bitcast.91), channel_id=1, source_target_pairs={{0,2},{1,3},{2,0},{3,1},{4,6},{5,7},{6,4},{7,5},{8,10},{9,11},{10,... | collective-permute-start | bytes 1327112 | tf_op jit(solution)/shard_map/ppermute | solution.py:650
  582.4 10.3 %copy-start.23 = (f32[8,768]{1,0:T(8,128)S(1)}, f32[8,768]{1,0:T(8,128)}, u32[]{:S(2)}) copy-start(f32[8,768]{1,0:T(8,128)} %get-tuple-element.68) | copy-start | bytes 73732
  582.4 10.8 %copy-start.22 = (f32[1,3072]{1,0:T(1,128)S(1)}, f32[1,3072]{1,0:T(1,128)}, u32[]{:S(2)}) copy-start(f32[1,3072]{1,0:T(1,128)} %get-tuple-element.70) | copy-start | bytes 36868
  582.4 26.2 %collective-permute-start.3 = (bf16[512,768]{1,0:T(8,128)(2,1)}, bf16[512,768]{1,0:T(8,128)(2,1)}, u32[]{:S(2)}, u32[]{:S(2)}) collective-permute-start(bf16[512,768]{1,0:T(8,128)(2,1)} %get-tuple-element.83), channel_id=1, source_target_pairs={{0,2},{1,3},{2,0},{3,1},{4,6},{5,7},{6,4},{7,5},{8,10},{9,11},{10,... | collective-permute-start | bytes 2359304 | tf_op jit(solution)/shard_map/ppermute | solution.py:650
  585.3 26.9 %copy-start.24 = (f32[1,2304]{1,0:T(1,128)S(1)}, f32[1,2304]{1,0:T(1,128)}, u32[]{:S(2)}) copy-start(f32[1,2304]{1,0:T(1,128)} %get-tuple-element.69) | copy-start | bytes 27652
  585.4 71.6 %copy-start.6 = (f32[12,768]{1,0:T(8,128)S(1)}, f32[12,768]{1,0:T(8,128)}, u32[]{:S(2)}) copy-start(f32[12,768]{1,0:T(8,128)} %vec_ref.5) | copy-start | bytes 110596
  585.4 71.6 %copy-start.20 = (f32[12,768]{1,0:T(8,128)S(1)}, f32[12,768]{1,0:T(8,128)}, u32[]{:S(2)}) copy-start(f32[12,768]{1,0:T(8,128)} %param.30) | copy-start | bytes 110596
  585.4 71.6 %copy-start.21 = (f32[12,768]{1,0:T(8,128)S(1)}, f32[12,768]{1,0:T(8,128)}, u32[]{:S(2)}) copy-start(f32[12,768]{1,0:T(8,128)} %param.29) | copy-start | bytes 110596
  585.4 72.2 %collective-permute-start.6 = (bf16[512,768]{1,0:T(8,128)(2,1)}, bf16[512,768]{1,0:T(8,128)(2,1)}, u32[]{:S(2)}, u32[]{:S(2)}) collective-permute-start(bf16[512,768]{1,0:T(8,128)(2,1)} %get-tuple-element.81), channel_id=1, source_target_pairs={{0,2},{1,3},{2,0},{3,1},{4,6},{5,7},{6,4},{7,5},{8,10},{9,11},{10,... | collective-permute-start | bytes 2359304 | tf_op jit(solution)/shard_map/ppermute | solution.py:650
  591.7 68.7 %copy-start.16 = (bf16[6,96,384]{2,1,0:T(8,128)(2,1)}, bf16[6,96,384]{2,1,0:T(8,128)(2,1)S(1)}, u32[]{:S(2)}) copy-start(bf16[6,96,384]{2,1,0:T(8,128)(2,1)S(1)} %collective-permute-done.14.g1) | copy-start | bytes 1327108
  592.7 67.7 %collective-permute-start.15 = (bf16[2,6,96,384]{3,2,1,0:T(8,128)(2,1)}, bf16[2,6,96,384]{3,2,1,0:T(8,128)(2,1)S(1)}, u32[]{:S(2)}, u32[]{:S(2)}) collective-permute-start(bf16[2,6,96,384]{3,2,1,0:T(8,128)(2,1)} %pad_maximum_fusion.3), channel_id=1, source_target_pairs={{0,1},{1,0},{2,3},{3,2},{4,5},{5,4},{6,7},{7,6},{8,9},{9,8},{10,11... | collective-permute-start | bytes 2654216 | tf_op jit(solution)/shard_map/ppermute | solution.py:650
  (13 other events, 39.1 us)
Sparse Core Ops, SparseCore 0:
  11.5 108.3 all-gather.2

commit v2 on v1

--- a/solution.py
+++ b/solution.py
@@ -278,33 +278,42 @@
         dv2[...] = dv[rows:, :].astype(LOW)
 
 
-def attn_backward(qkv, other, bias, attn, lse, d_attn, q_rows=512, chunk=1024):
+def attn_backward(qkv, other, bias, attn, lse, d_attn, first, place, total, before, after, q_rows=512, chunk=1024):
     rows, pairs = qkv.shape[0], D // 128
     keys = 2 * rows
-    q_spec = pl.BlockSpec((q_rows, 128), lambda p, i: (i, p))
-    k_spec = pl.BlockSpec((rows, 128), lambda p, i: (0, p))
+    out_spec = pl.BlockSpec((q_rows, 128), lambda p, i: (i, place))
+    k_out = pl.BlockSpec((rows, 128), lambda p, i: (0, place))
+    anywhere = pl.BlockSpec(memory_space=pl.ANY)
+    q_spec = pl.BlockSpec((q_rows, 128), lambda p, i: (i, first))
+    extra = list(before) + list(after)
+
+    def kernel(*refs):
+        attn_bwd_kernel(*refs[:9], *refs[9 + len(extra) :], chunk=chunk)
+
     return pl.pallas_call(
-        functools.partial(attn_bwd_kernel, chunk=chunk),
-        grid=(pairs, rows // q_rows),
+        kernel,
+        grid=(1, rows // q_rows),
         in_specs=[
             q_spec,
-            pl.BlockSpec((rows, 128), lambda p, i: (0, pairs + p)),
-            pl.BlockSpec((rows, 128), lambda p, i: (0, 2 * pairs + p)),
-            k_spec,
-            pl.BlockSpec((rows, 128), lambda p, i: (0, pairs + p)),
+            pl.BlockSpec((rows, 128), lambda p, i: (0, pairs + first)),
+            pl.BlockSpec((rows, 128), lambda p, i: (0, 2 * pairs + first)),
+            pl.BlockSpec((rows, 128), lambda p, i: (0, first)),
+            pl.BlockSpec((rows, 128), lambda p, i: (0, pairs + first)),
             pl.BlockSpec((keys, 128), lambda p, i: (0, 0)),
             q_spec,
             q_spec,
             q_spec,
-        ],
-        out_specs=[q_spec, k_spec, k_spec, k_spec, k_spec],
-        out_shape=[jax.ShapeDtypeStruct((rows, D), LOW)] * 5,
+        ]
+        + [anywhere] * len(extra),
+        out_specs=[out_spec, k_out, k_out, k_out, k_out],
+        out_shape=[jax.ShapeDtypeStruct((rows, total * 128), LOW)] * 5,
         scratch_shapes=[pltpu.VMEM((keys, 128), LOW)] * 4
         + [pltpu.VMEM((128, keys), LOW)]
         + [pltpu.VMEM((keys, 128), F32)] * 2,
+        input_output_aliases={9 + i: i for i in range(len(before))},
         compiler_params=params(56),
         name="attn_bwd",
-    )(qkv, qkv, qkv, other, other, bias, attn, lse, d_attn)
+    )(qkv, qkv, qkv, other, other, bias, attn, lse, d_attn, *extra)
 
 
 def mid_kernel(
@@ -448,10 +457,8 @@
     )(own, slot, x, attn, dy, vec, b1, *([gathered] * 8))
 
 
-def qkv_bwd_kernel(
-    own, slot, x_ref, a_ref, dmid_ref, vec_ref, dq, dk, rk, dv, rv, t0, t1,
-    dx_ref, g_qkv, sums_ref, cols_ref, acc,
-):
+def qkv_bwd_kernel(own, slot, x_ref, a_ref, dmid_ref, vec_ref, *refs):
+    grads, (t0, t1, dx_ref, g_qkv, sums_ref, cols_ref, acc) = refs[:10], refs[10:]
     step = pl.program_id(0)
 
     @pl.when(step == 0)
@@ -465,17 +472,20 @@
         put_tile(g_qkv, 1, dot(a_ref[:, BLK:], d_cols, 0, 0))
         cols_ref[...] = jnp.sum(d_cols.astype(F32), axis=0, keepdims=True)
 
-    @pl.when(step < 2)
-    def _():
-        work(dq[...])
-
-    @pl.when((step >= 2) & (step < 4))
-    def _():
-        work((dk[...].astype(F32) + rk[...].astype(F32)).astype(LOW))
-
-    @pl.when(step >= 4)
-    def _():
-        work((dv[...].astype(F32) + rv[...].astype(F32)).astype(LOW))
+    for half in range(2):
+        dq, dk, rk, dv, rv = grads[5 * half : 5 * half + 5]
+
+        @pl.when(step == half)
+        def _():
+            work(dq[...])
+
+        @pl.when(step == 2 + half)
+        def _():
+            work((dk[...].astype(F32) + rk[...].astype(F32)).astype(LOW))
+
+        @pl.when(step == 4 + half)
+        def _():
+            work((dv[...].astype(F32) + rv[...].astype(F32)).astype(LOW))
 
     @pl.when(step == 5)
     def _():
@@ -487,24 +497,18 @@
         dx_ref[...] = (dmid_ref[...] + norm_back(grad * vec_ref[0:1, :], hat, rstd)).astype(LOW)
 
 
-def qkv_backward(own, slot, x, normed, d_mid, vec, dq, dk, rk, dv, rv, gathered):
+def qkv_backward(own, slot, x, normed, d_mid, vec, halves, gathered):
     rows = x.shape[0]
     quarter = BLK // 4
     row_spec = full_spec((rows, D))
-
-    def cols(first):
-        return pl.BlockSpec((rows, BLK), lambda i, own, slot: (0, jnp.clip(i - first, 0, 1)))
-
     return pl.pallas_call(
         qkv_bwd_kernel,
         grid_spec=pltpu.PrefetchScalarGridSpec(
             num_scalar_prefetch=2,
             grid=(6,),
-            in_specs=[
-                row_spec, row_spec, row_spec, full_spec(vec.shape),
-                cols(0), cols(2), cols(2), cols(4), cols(4),
-                tile_spec(lambda i: i), tile_spec(lambda i: 6 + i),
-            ],
+            in_specs=[row_spec, row_spec, row_spec, full_spec(vec.shape)]
+            + [full_spec((rows, BLK))] * 10
+            + [tile_spec(lambda i: i), tile_spec(lambda i: 6 + i)],
             out_specs=[
                 row_spec,
                 pl.BlockSpec((2, 2, 2, 1, quarter, BLK), lambda i, own, slot: (0, 0, 0, i, 0, 0)),
@@ -519,9 +523,9 @@
             jax.ShapeDtypeStruct((8, D), F32),
             jax.ShapeDtypeStruct((1, 3 * D), F32),
         ],
-        compiler_params=params(58),
+        compiler_params=params(60),
         name="qkv_bwd",
-    )(own, slot, x, normed, d_mid, vec, dq, dk, rk, dv, rv, gathered, gathered)
+    )(own, slot, x, normed, d_mid, vec, *halves[0], *halves[1], gathered, gathered)
 
 
 def eliminate(y_ref):
@@ -564,9 +568,12 @@
 
 def soap_kernel(
     seq_ref, g0, g1, g2, g3, w_ref, one_ref, two_ref, ls_ref, rs_ref, lb_ref, rb_ref,
-    grad_ref, w_out, one_out, two_out, ls_out, rs_out, lb_out, rb_out,
-    grad_s, gram, work, inv,
+    *refs,
 ):
+    (
+        grad_ref, w_out, one_out, two_out, ls_out, rs_out, lb_out, rb_out,
+        grad_s, gram, work, inv,
+    ) = refs[-12:]
     step = pl.program_id(0)
     slots = pl.num_programs(0)
     count = lb_out.shape[0]
@@ -619,18 +626,20 @@
             lax.fori_loop(0, count, functools.partial(solve, out=rb_out), 0)
 
 
-def soap_update(seq_id, pieces, master, one, two, left_stats, right_stats, left_basis, right_basis):
-    count = master.shape[0]
+def soap_update(seq_id, pieces, state, first, count, before):
+    slots = state[0].shape[0]
     piece_spec = pl.BlockSpec((1, BLK // 4, BLK), lambda i, s: (i, 0, 0))
-    block_spec = pl.BlockSpec((1, BLK, BLK), lambda i, s: (i, 0, 0))
-    whole_spec = pl.BlockSpec((count, BLK, BLK), lambda i, s: (0, 0, 0))
-    shape = jax.ShapeDtypeStruct((count, BLK, BLK), F32)
+    block_spec = pl.BlockSpec((1, BLK, BLK), lambda i, s: (first + i, 0, 0))
+    whole_spec = pl.BlockSpec((count, BLK, BLK), lambda i, s: (first // count, 0, 0))
+    shape = jax.ShapeDtypeStruct((slots, BLK, BLK), F32)
     return pl.pallas_call(
         soap_kernel,
         grid_spec=pltpu.PrefetchScalarGridSpec(
             num_scalar_prefetch=1,
             grid=(count,),
-            in_specs=[piece_spec] * 4 + [block_spec] * 7,
+            in_specs=[piece_spec] * 4
+            + [block_spec] * 7
+            + [pl.BlockSpec(memory_space=pl.ANY)] * len(before),
             out_specs=[block_spec] * 6 + [whole_spec] * 2,
             scratch_shapes=[
                 pltpu.VMEM((BLK, BLK), F32),
@@ -640,9 +649,10 @@
             ],
         ),
         out_shape=[shape] * 8,
+        input_output_aliases={12 + i: i for i in range(len(before))},
         compiler_params=params(60),
         name="soap",
-    )(seq_id, *pieces, master, one, two, left_stats, right_stats, left_basis, right_basis)
+    )(seq_id, *pieces, *state, *before)
 
 
 def swap(x, axis, bit):
@@ -658,6 +668,12 @@
     kept = lax.dynamic_index_in_dim(x, mine, dim, keepdims=False)
     sent = lax.dynamic_index_in_dim(x, 1 - mine, dim, keepdims=False)
     return add_low(kept, swap(sent, axis, bit))
+
+
+def quarters(piece):
+    across = swap(piece, "seq", 2)
+    beside = swap(jnp.stack([piece, across]), "seq", 1)
+    return piece, across, beside[0], beside[1]
 
 
 def block_places(owners, owner_count, slot_count):
@@ -693,6 +709,7 @@
     core, chip = seq_id % 2, seq_id // 2
     part_len = tokens.shape[1]
     slots, sources = block_places(owners, owner_count, slot_count)
+    first_blocks = 3 * (D // BLK) ** 2
 
     mine = lax.dynamic_index_in_dim(
         master.reshape(slot_count, 4, quarter, BLK), seq_id, 1, keepdims=False
@@ -734,32 +751,86 @@
         [g.reshape(2, 2, -1, quarter, BLK) for g in (g_out, g_up, g_down)], axis=2
     )
     early = halve(early, 0, "seq", 1, core)
-    early = halve(early, 0, "seq", 2, chip)
-    dq, dk, dv, sent_k, sent_v = attn_backward_order(qkv, other, fill, attn, lse, d_attn)
-    got_k, got_v = swap(sent_k, "seq", 1), swap(sent_v, "seq", 1)
-    d_x, g_qkv, sums_one, cols = qkv_backward(
-        owners, slots, x, normed, d_mid, vec, dq, dk, got_k, dv, got_v, gathered
-    )
+
+    bits = owner_count.bit_length() - 1
+    dims = ["x"] + list(range(bits))[::-1]
+    if slot_count % 3 == 0 and bits == 3:
+        plans = [["x", 0, 1, 2], [0, 1, "x", 2], [1, "x", 0, 2]]
+    else:
+        plans = [["x"] + list(range(bits))]
+    per = slot_count // len(plans)
+    early = jnp.concatenate([early, jnp.zeros((2, 1, quarter, BLK), LOW)], axis=1)
+    early_at = jnp.where(sources >= first_blocks, sources - first_blocks, sources.shape[0])
+    early_at = jnp.minimum(early_at, early.shape[1] - 1).reshape(owner_count, slot_count)
+    groups = [
+        jnp.take(early, early_at[:, per * g : per * g + per].reshape(-1), axis=1).reshape(
+            (2,) * len(dims) + (per, quarter, BLK)
+        )
+        for g in range(len(plans))
+    ]
+    left = [list(dims) for _ in plans]
+
+    def advance(step):
+        for g, plan in enumerate(plans):
+            name = plan[step]
+            at = left[g].index(name)
+            left[g].pop(at)
+            if name == "x":
+                groups[g] = halve(groups[g], at, "seq", 2, chip)
+            else:
+                groups[g] = halve(groups[g], at, "dp", 2**name, (dp_id // 2**name) % 2)
+
+    halves = []
+    pairs = D // 128 // 2
+    call = taken = 0
+    for half in range(2):
+        before = []
+        for place in range(pairs):
+            after = list(groups) if call else []
+            if call > 1 and taken < len(dims) - 1:
+                advance(taken)
+                taken += 1
+                after = list(groups)
+            before = attn_backward(
+                qkv, other, fill, attn, lse, d_attn, pairs * half + place, place, pairs, before, after
+            )
+            call += 1
+        dq, dk, dv, sent_k, sent_v = before
+        halves.append((dq, dk, swap(sent_k, "seq", 1), dv, swap(sent_v, "seq", 1)))
+    for step in range(taken, len(dims)):
+        advance(step)
+    early = jnp.concatenate(groups, axis=0)
+    early_pieces = quarters(early)
+
+    d_x, g_qkv, sums_one, cols = qkv_backward(owners, slots, x, normed, d_mid, vec, halves, gathered)
     d_tokens = to_positions(d_x)
     late = g_qkv.reshape(2, 2, -1, quarter, BLK)
     late = halve(late, 0, "seq", 1, core)
     late = halve(late, 0, "seq", 2, chip)
-
-    tiles = jnp.concatenate([late, early, jnp.zeros((1, quarter, BLK), LOW)], axis=0)
-    owned = jnp.take(tiles, sources, axis=0).reshape(owner_count, slot_count, quarter, BLK)
-    bit = 1
-    while bit < owner_count:
-        rest = owned.shape[0] // 2
-        owned = halve(owned.reshape((rest, 2) + owned.shape[1:]), 1, "dp", bit, (dp_id // bit) % 2)
-        bit *= 2
-    owned = owned[0]
-
-    across = swap(owned, "seq", 2)
-    beside = swap(jnp.stack([owned, across]), "seq", 1)
-    updates = soap_update(
-        seq_id.reshape(1), (owned, across, beside[0], beside[1]), master, moment_one, moment_two,
-        left_stats, right_stats, left_basis, right_basis,
-    )
+    late = jnp.concatenate([late, jnp.zeros((1, quarter, BLK), LOW)], axis=0)
+    late_at = jnp.minimum(sources, first_blocks).reshape(owner_count, slot_count)
+    state = (master, moment_one, moment_two, left_stats, right_stats, left_basis, right_basis)
+
+    def finish(count, late, early_pieces, state):
+        sent = jnp.take(late, late_at[:, :count].reshape(-1), axis=0)
+        got = lax.all_to_all(
+            sent.reshape(owner_count, count, quarter, BLK), "dp", split_axis=0, concat_axis=0, tiled=True
+        )
+        total = jnp.sum(got.astype(F32), axis=0) + early_pieces[0][:count].astype(F32)
+        pieces = quarters(total.astype(LOW))
+        done = []
+        if count < slot_count:
+            rest = [piece[count:] for piece in early_pieces]
+            done = soap_update(seq_id.reshape(1), rest, state, count, slot_count - count, done)
+        return soap_update(seq_id.reshape(1), pieces, state, 0, count, done)
+
+    counts = [3, 4, 6] if slot_count == 6 else [slot_count]
+    most = jnp.max(jnp.sum((owners[:first_blocks, None] == jnp.arange(owner_count)[None, :]).astype(jnp.int32), axis=0))
+    if len(counts) == 1:
+        updates = finish(counts[0], late, early_pieces, state)
+    else:
+        which = sum((most > count).astype(jnp.int32) for count in counts[:-1])
+        updates = lax.switch(which, [functools.partial(finish, count) for count in counts], late, early_pieces, state)
 
     vec_grad = jnp.concatenate(
         [
@@ -772,18 +843,13 @@
         ],
         axis=0,
     )
-    vec_total = lax.psum(vec_grad, AXES)
+    vec_total = jnp.sum(lax.all_gather(vec_grad, AXES, axis=0, tiled=False), axis=0)
     vec_first, vec_second, vec_next = adam_vectors(vec_total, vec, vec_one, vec_two)
     grad_blocks, w_new, one_new, two_new, ls_new, rs_new, lb_new, rb_new = updates
     return (
         output, d_tokens, grad_blocks, w_new, one_new, two_new, ls_new, rs_new, lb_new, rb_new,
         vec_first, vec_second, vec_next,
     )
-
-
-def attn_backward_order(qkv, other, fill, attn, lse, d_attn):
-    dq, dk1, dv1, dk2, dv2 = attn_backward(qkv, other, fill, attn, lse, d_attn)
-    return dq, dk1, dv1, dk2, dv2
 
 
 def solution(mesh):

time: 790 us -> 808 us (1.023); the launches traced: 784 us -> 810 us
  waiting for transfers between devices: 296 us -> 190 us
  Pallas kernels: 343 us -> 386 us
  local copies, waits for them, and re-layouts: 36.7 us -> 77.3 us
  other arithmetic: 32.1 us -> 48.7 us
  blocking collectives: 44.6 us -> 57.4 us
  loops' own time: 0 us -> 10.6 us
    ppermute x16 -> x28, waiting for transfers between devices: 211 us -> 103 us  [swap(): return lax.ppermute(x, axis, [(i, i ^ bit) for i in range(size)])]
    all_to_all x0 -> x1, blocking collectives: none -> 57.4 us  [finish(): lax.all_to_all(sent.reshape(owner_count, count, quarter, BLK), 'dp', spli...]
    psum x1 -> x0, blocking collectives: 44.6 us -> none  [on_device(): vec_total = lax.psum(vec_grad, AXES)]
    pallas_call x1 -> x2, Pallas kernels: 115 us -> 135 us  [soap_update(): pl.pallas_call(soap_kernel, grid_spec=pltpu.PrefetchScalarGridSpec(num_sc...]
    pallas_call x1 -> x6, Pallas kernels: 73.5 us -> 87.6 us  [attn_backward(): pl.pallas_call(kernel, grid=(1, rows // q_rows), in_specs=[q_spec, pl.Blo...]
    gather x1 -> x4, local copies, waits for them, and re-layouts: 3.42 us -> 14.3 us  [the longest x3 10.8 us: on_device(): jnp.take(early, early_at[:, per * g:per * g + per].reshape(-1), axis=1)]
    another operation x0 -> x1, loops' own time: none -> 10.6 us  [on_device(): lax.switch(which, [functools.partial(finish, count) for count in counts],...]
    pallas_call x1, Pallas kernels: 74.9 us -> 84.1 us  [mid_layer(): pl.pallas_call(functools.partial(mid_kernel, chunk=chunk), grid_spec=pltp...]
  transfers between devices with their start and end apart: 17 -> 30, of which waited for: 11 -> 12; matrix products, arithmetic and copies ran while one was open for 4% -> 7% of each run, Pallas kernels for 12% -> 20%
where the time goes in v2:
time: 808 us; the launch traced here: 810 us
  Pallas kernels  386 us (48%)
  waiting for transfers between devices  190 us (24%)
  local copies, waits for them, and re-layouts  77.3 us (10%)
  blocking collectives  57.4 us (7%)
  other arithmetic  48.7 us (6%)
  starting transfers between devices  23.8 us (3%)
  between operations  16.6 us (2%)
  loops' own time  10.6 us (1%)
    pallas_call x2, Pallas kernels, soap_update(): pl.pallas_call(soap_kernel, grid_spec=pltpu.PrefetchScalarGridSpec(num_sc...  135 us
    ppermute x28, waiting for transfers between devices, swap(): return lax.ppermute(x, axis, [(i, i ^ bit) for i in range(size)])  103 us
    pallas_call x6, Pallas kernels, attn_backward(): pl.pallas_call(kernel, grid=(1, rows // q_rows), in_specs=[q_spec, pl.Blo...  87.6 us
    all_gather x1, waiting for transfers between devices, on_device(): lax.all_gather(mine, AXES, axis=0, tiled=False)  85.3 us
    pallas_call x1, Pallas kernels, mid_layer(): pl.pallas_call(functools.partial(mid_kernel, chunk=chunk), grid_spec=pltp...  84.1 us
    all_to_all x1, blocking collectives, finish(): lax.all_to_all(sent.reshape(owner_count, count, quarter, BLK), 'dp', spli...  57.4 us
    pallas_call x1, Pallas kernels, attn_forward(): pl.pallas_call(attn_fwd_kernel, grid=(pairs, rows // q_rows), in_specs=[q...  46.8 us
    ppermute x28, starting transfers between devices, swap(): return lax.ppermute(x, axis, [(i, i ^ bit) for i in range(size)])  23.7 us
  transfers between devices with their start and end apart: 30, of which 12 were waited for; matrix products, arithmetic and copies ran while one was open for 7% of the time, Pallas kernels for 20%

profile of v2, /device:TPU:0, one launch (start us, length us, event | category | flops | bytes accessed | tf_op | source)
XLA Modules:
  0.0 810.3 jit_solution(5123577410330851716)
XLA Ops:
  10.8 3.0 collective-permute-start.6
  14.1 20.4 %collective-permute-done.6 = bf16[512,768]{1,0:T(8,128)(2,1)S(1)} collective-permute-done((bf16[512,768]{1,0:T(8,128)(2,1)S(1)}, bf16[512,768]{1,0:T(8,128)(2,1)S(1)}, u32[]{:S(2)}, u32[]{:S(2)}) %collective-permute-start.6) | collective-permute-done | bytes 786464 | tf_op jit(solution)/shard_map/ppermute | solution.py:660
  34.6 85.3 %all-gather.6.cloned.1.call-done = bf16[192,1,96,384]{3,2,1,0:T(8,128)(2,1)} async-done(((bf16[6,1,96,384]{3,2,1,0:T(8,128)(2,1)}), bf16[192,1,96,384]{3,2,1,0:T(8,128)(2,1)}) %all-gather.6.cloned.1.call-update) | async-done | bytes 14155792 | tf_op jit(solution)/shard_map/all_gather | solution.py:717
  119.9 11.0 %qkv.1 = (bf16[1024,2304]{1,0:T(8,128)(2,1)}, bf16[1024,768]{1,0:T(8,128)(2,1)S(1)}) custom-call(s32[48]{0:T(128)S(1)} %copy-done.7, s32[48]{0:T(128)S(1)} %convert_reduce_fusion.3.slot, bf16[1024,768]{1,0:T(8,128)(2,1)S(1)} %pad_maximum_fusion.4.x_ref, f32[12,768]{1,0:T(8,128)S(1)} %copy-done.5, f32[1,2304]{1,0:T(1,128)S(1)} %broadcast_in_dim.102.bias_ref, ...), custom_call_target="tpu_custom_call" | custom-call | tf_op jit(solution)/shard_map/qkv/pallas_call | solution.py:118
  139.3 16.0 %collective-permute-done.8 = bf16[512,768]{1,0:T(8,128)(2,1)} collective-permute-done((bf16[512,768]{1,0:T(8,128)(2,1)}, bf16[512,768]{1,0:T(8,128)(2,1)}, u32[]{:S(2)}, u32[]{:S(2)}) %collective-permute-start.8) | collective-permute-done | bytes 786464 | tf_op jit(solution)/shard_map/ppermute | solution.py:660
  158.2 46.8 %attn_fwd.1 = (bf16[1024,768]{1,0:T(8,128)(2,1)S(1)}, f32[1024,768]{1,0:T(8,128)S(1)}) custom-call(bf16[1024,2304]{1,0:T(8,128)(2,1)} %get-tuple-element.217.q_ref.k1.v1.refs_0_.refs_1_.refs_2_, bf16[1024,2304]{1,0:T(8,128)(2,1)} %get-tuple-element.217.q_ref.k1.v1.refs_0_.refs_1_.refs_2_, ...), custom_call_target="tpu_custom_call" | custom-call | tf_op jit(solution)/shard_map/attn_fwd/pallas_call | solution.py:181
  207.8 84.1 %mid.1 = (bf16[1024,768]{1,0:T(8,128)(2,1)}, f32[1024,768]{1,0:T(8,128)}, bf16[1024,768]{1,0:T(8,128)(2,1)}, bf16[2,2,2,8,96,384]{5,4,3,2,1,0:T(8,128)(2,1)}, bf...) custom-call(s32[48]{0:T(128)} %own.5, ...), custom_call_target="tpu_custom_call" | custom-call | tf_op jit(solution)/shard_map/mid/pallas_call | solution.py:408
  291.9 5.7 pad_maximum_fusion.3
  297.7 3.2 dynamic-slice_bitcast_fusion
  304.7 14.5 %attn_bwd.6 = (bf16[1024,384]{1,0:T(8,128)(2,1)}, bf16[1024,384]{1,0:T(8,128)(2,1)}, bf16[1024,384]{1,0:T(8,128)(2,1)}, bf16[1024,384]{1,0:T(8,128)(2,1)}, bf16[1024,384]{1,0:T(8,128)(2,1)}) custom-call(bf16[1024,2304]{1,0:T(8,128)(2,1)} %get-tuple-element.217.q_ref.k1.v1.refs_0_.refs_1_.refs_2_, ...), custom_call_target="tpu_custom_call" | custom-call | tf_op jit(solution)/shard_map/attn_bwd/pallas_call | solution.py:293
  319.2 5.5 fusion.2
  327.6 3.6 gather_fusion.4
  334.2 3.6 gather_fusion.5
  340.9 3.6 gather_fusion.6
  357.8 14.6 %attn_bwd.7 = (bf16[1024,384]{1,0:T(8,128)(2,1)}, bf16[1024,384]{1,0:T(8,128)(2,1)}, bf16[1024,384]{1,0:T(8,128)(2,1)}, bf16[1024,384]{1,0:T(8,128)(2,1)}, bf16[1024,384]{1,0:T(8,128)(2,1)}) custom-call(bf16[1024,2304]{1,0:T(8,128)(2,1)} %get-tuple-element.217.q_ref.k1.v1.refs_0_.refs_, ...), custom_call_target="tpu_custom_call", output_to_operand_aliasing={{0}: (9, {}), {1}: (10, {}), {2}: (11, {}), {3}: (12, {}), ... | custom-call | tf_op jit(solution)/shard_map/attn_bwd/pallas_call | solution.py:293
  388.8 14.9 %attn_bwd.8 = (bf16[1024,384]{1,0:T(8,128)(2,1)}, bf16[1024,384]{1,0:T(8,128)(2,1)}, bf16[1024,384]{1,0:T(8,128)(2,1)}, bf16[1024,384]{1,0:T(8,128)(2,1)}, bf16[1024,384]{1,0:T(8,128)(2,1)}) custom-call(bf16[1024,2304]{1,0:T(8,128)(2,1)} %get-tuple-element.217.q_ref.k1.v1.refs_0_.refs_, ...), custom_call_target="tpu_custom_call", output_to_operand_aliasing={{0}: (9, {}), {1}: (10, {}), {2}: (11, {}), {3}: (12, {}), ... | custom-call | tf_op jit(solution)/shard_map/attn_bwd/pallas_call | solution.py:293
  408.8 11.7 %collective-permute-done.18 = bf16[2,2,2,96,384]{4,3,2,0,1:T(8,128)(2,1)S(1)} collective-permute-done((bf16[2,2,2,96,384]{4,3,2,0,1:T(8,128)(2,1)S(1)}, bf16[2,2,2,96,384]{4,3,2,0,1:T(8,128)(2,1)S(1)}, u32[]{:S(2)}, u32[]{:S(2)}) %collective-permute-start.18) | collective-permute-done | bytes 589856 | tf_op jit(solution)/shard_map/ppermute | solution.py:660
  423.1 14.6 %attn_bwd.9 = (bf16[1024,384]{1,0:T(8,128)(2,1)}, bf16[1024,384]{1,0:T(8,128)(2,1)}, bf16[1024,384]{1,0:T(8,128)(2,1)}, bf16[1024,384]{1,0:T(8,128)(2,1)}, bf16[1024,384]{1,0:T(8,128)(2,1)}) custom-call(bf16[1024,2304]{1,0:T(8,128)(2,1)} %get-tuple-element.217.q_ref.k1.v1.refs_0_.refs_1_.refs_2_, ...), custom_call_target="tpu_custom_call" | custom-call | tf_op jit(solution)/shard_map/attn_bwd/pallas_call | solution.py:293
  440.1 14.4 %attn_bwd.10 = (bf16[1024,384]{1,0:T(8,128)(2,1)}, bf16[1024,384]{1,0:T(8,128)(2,1)}, bf16[1024,384]{1,0:T(8,128)(2,1)}, bf16[1024,384]{1,0:T(8,128)(2,1)}, bf16[1024,384]{1,0:T(8,128)(2,1)}) custom-call(bf16[1024,2304]{1,0:T(8,128)(2,1)} %get-tuple-element.217.q_ref.k1.v1.refs_0_.refs, ...), custom_call_target="tpu_custom_call", output_to_operand_aliasing={{0}: (9, {}), {1}: (10, {}), {2}: (11, {}), {3}: (12, {}), ... | custom-call | tf_op jit(solution)/shard_map/attn_bwd/pallas_call | solution.py:293
  454.5 14.6 %attn_bwd.11 = (bf16[1024,384]{1,0:T(8,128)(2,1)}, bf16[1024,384]{1,0:T(8,128)(2,1)}, bf16[1024,384]{1,0:T(8,128)(2,1)}, bf16[1024,384]{1,0:T(8,128)(2,1)}, bf16[1024,384]{1,0:T(8,128)(2,1)}) custom-call(bf16[1024,2304]{1,0:T(8,128)(2,1)} %get-tuple-element.217.q_ref.k1.v1.refs_0_.refs, ...), custom_call_target="tpu_custom_call", output_to_operand_aliasing={{0}: (9, {}), {1}: (10, {}), {2}: (11, {}), {3}: (12, {}), ... | custom-call | tf_op jit(solution)/shard_map/attn_bwd/pallas_call | solution.py:293
  477.1 21.2 %qkv_bwd.1 = (bf16[1024,768]{1,0:T(8,128)(2,1)}, bf16[2,2,2,6,96,384]{5,4,3,2,1,0:T(8,128)(2,1)}, f32[8,768]{1,0:T(8,128)}, f32[1,2304]{1,0:T(1,128)}) custom-call(s32[48]{0:T(128)} %own.5, s32[48]{0:T(128)} %copy-done.10, bf16[1024,768]{1,0:T(8,128)(2,1)} %copy-done.3, bf16[1024,768]{1,0:T(8,128)(2,1)} %copy-done.4, ...), custom_call_target="tpu_custom_call" | custom-call | tf_op jit(solution)/shard_map/qkv_bwd/pallas_call | solution.py:504
  498.4 3.0 dynamic-slice_bitcast_fusion.1
  507.8 10.4 %collective-permute-done.30 = bf16[6,96,384]{2,1,0:T(8,128)(2,1)} collective-permute-done((bf16[6,96,384]{2,1,0:T(8,128)(2,1)S(1)}, bf16[6,96,384]{2,1,0:T(8,128)(2,1)}, u32[]{:S(2)}, u32[]{:S(2)}) %collective-permute-start.30) | collective-permute-done | bytes 442400 | tf_op jit(solution)/shard_map/ppermute | solution.py:660
  530.2 6.3 collective-permute-done.9
  540.2 15.8 %collective-permute-done.24 = bf16[512,768]{1,0:T(8,128)(2,1)} collective-permute-done((bf16[512,768]{1,0:T(8,128)(2,1)}, bf16[512,768]{1,0:T(8,128)(2,1)}, u32[]{:S(2)}, u32[]{:S(2)}) %collective-permute-start.24) | collective-permute-done | bytes 786464 | tf_op jit(solution)/shard_map/ppermute | solution.py:660
  563.4 11.3 %collective-permute-done.26 = bf16[12,96,384]{2,1,0:T(8,128)(2,1)} collective-permute-done((bf16[12,96,384]{2,1,0:T(8,128)(2,1)}, bf16[12,96,384]{2,1,0:T(8,128)(2,1)}, u32[]{:S(2)}, u32[]{:S(2)}) %collective-permute-start.26) | collective-permute-done | bytes 884768 | tf_op jit(solution)/shard_map/ppermute | solution.py:660
  577.4 225.8 %conditional.1 = ((f32[6,384,384]{2,1,0:T(8,128)}, f32[6,384,384]{2,1,0:T(8,128)}, f32[6,384,384]{2,1,0:T(8,128)}, f32[6,384,384]{2,1,0:T(8,128)}, f32[6,384,384...) conditional(s32[]{:T(128)} %clamp.3, (s32[]{:T(128)}, ...), branch_computations={%region_5.8_spmd, %region_7.10_spmd, %region_9.12_spmd} | conditional | flops 6194656 | bytes 41588012 | solution.py:833
  586.7 3.5 gather_fusion.1
  592.2 57.4 %all_to_all.13 = bf16[8,4,96,384]{3,2,1,0:T(8,128)(2,1)S(1)} all-to-all(bf16[8,4,96,384]{3,2,1,0:T(8,128)(2,1)S(1)} %broadcast_select_fusion.1), channel_id=1, replica_groups=mesh['dp'=8,'seq'=4] {'dp'}, dimensions={0} | all-to-all | bytes 4718592 | tf_op jit(solution)/shard_map/cond/branch_1_fun/all_to_all | solution.py:816
  651.3 7.0 collective-permute-done.2.g1
  664.7 52.3 %soap.7 = (f32[6,384,384]{2,1,0:T(8,128)}, f32[6,384,384]{2,1,0:T(8,128)}, f32[6,384,384]{2,1,0:T(8,128)}, f32[6,384,384]{2,1,0:T(8,128)}, f32[6,384,384]{2,1,0:...) custom-call(s32[1]{0:T(128)} %bitcast.7.seq_ref, ...), custom_call_target="tpu_custom_call" | custom-call | tf_op jit(solution)/shard_map/cond/branch_1_fun/soap/pallas_call | solution.py:635
  719.0 83.0 %soap.8 = (f32[6,384,384]{2,1,0:T(8,128)}, f32[6,384,384]{2,1,0:T(8,128)}, f32[6,384,384]{2,1,0:T(8,128)}, f32[6,384,384]{2,1,0:T(8,128)}, f32[6,384,384]{2,1,0:...) custom-call(s32[1]{0:T(128)} %bitcast.7.seq_ref, ...), custom_call_target="tpu_custom_call", output_to_operand_aliasing={{0}: (12, {}), {1}: (13, {}), {2}: (14, {}), {3}: (15, {}),... | custom-call | tf_op jit(solution)/shard_map/cond/branch_1_fun/soap/pallas_call | solution.py:635
  (280 shorter events, 120.8 us)
Async XLA Ops:
  7.2 112.7 %all-gather.6.cloned.1.call-start = ((), (), s32[]{:S(2)}) async-start(), calls=%async_computation.3 | async-start | bytes 14598144 | tf_op jit(solution)/shard_map/all_gather | solution.py:717
  9.3 551.9 %all-gather.8.cloned.1.call-start = ((), (), s32[]{:S(2)}) async-start(), calls=%async_computation.4 | async-start | bytes 1622016 | tf_op jit(solution)/shard_map/all_gather | solution.py:846
  10.8 23.7 %collective-permute-start.6 = (bf16[512,768]{1,0:T(8,128)(2,1)S(1)}, bf16[512,768]{1,0:T(8,128)(2,1)S(1)}, u32[]{:S(2)}, u32[]{:S(2)}) collective-permute-start(bf16[512,768]{1,0:T(8,128)(2,1)S(1)} %get-tuple-element.293), channel_id=1, source_target_pairs={{0,2},{1,3},{2,0},{3,1},{4,6},{5,7},{6,4},{7,5},{8,10},{9,11},{10,... | collective-permute-start | bytes 2359304 | tf_op jit(solution)/shard_map/ppermute | solution.py:660
  14.1 116.8 %copy-start.10 = (s32[48]{0:T(128)}, s32[48]{0:T(128)S(1)}, u32[]{:S(2)}) copy-start(s32[48]{0:T(128)S(1)} %convert_reduce_fusion.3.slot) | copy-start | bytes 580
  34.6 96.3 %copy-start.3 = (bf16[1024,768]{1,0:T(8,128)(2,1)}, bf16[1024,768]{1,0:T(8,128)(2,1)S(1)}, u32[]{:S(2)}) copy-start(bf16[1024,768]{1,0:T(8,128)(2,1)S(1)} %pad_maximum_fusion.4.x_ref) | copy-start | bytes 4718596
  133.7 24.2 %collective-permute-start.7 = (bf16[1024,1536]{1,0:T(8,128)(2,1)S(1)}, bf16[1024,1536]{1,0:T(8,128)(2,1)}, u32[]{:S(2)}, u32[]{:S(2)}) collective-permute-start(bf16[1024,1536]{1,0:T(8,128)(2,1)S(1)} %slice.110), channel_id=1, source_target_pairs={{0,1},{1,0},{2,3},{3,2},{4,5},{5,4},{6,7},{7,6},{8,9},{9,8},{10,11... | collective-permute-start | bytes 9437192 | tf_op jit(solution)/shard_map/ppermute | solution.py:660
  135.2 20.0 %collective-permute-start.8 = (bf16[512,768]{1,0:T(8,128)(2,1)}, bf16[512,768]{1,0:T(8,128)(2,1)}, u32[]{:S(2)}, u32[]{:S(2)}) collective-permute-start(bf16[512,768]{1,0:T(8,128)(2,1)} %get-tuple-element.291), channel_id=1, source_target_pairs={{0,2},{1,3},{2,0},{3,1},{4,6},{5,7},{6,4},{7,5},{8,10},{9,11},{10,... | collective-permute-start | bytes 2359304 | tf_op jit(solution)/shard_map/ppermute | solution.py:660
  303.3 15.8 %collective-permute-start.10 = (bf16[2,36,96,384]{3,2,1,0:T(8,128)(2,1)}, bf16[2,36,96,384]{3,2,1,0:T(8,128)(2,1)}, u32[]{:S(2)}, u32[]{:S(2)}) collective-permute-start(bf16[2,36,96,384]{3,2,1,0:T(8,128)(2,1)} %dynamic-slice_bitcast_fusion), channel_id=1, source_target_pairs={{0,1},{1,0},{2,3},{3,2},{4,5},{5,4},{6,7},{7,6},{8,9},{9,8},{10,11... | collective-permute-start | bytes 15925256 | tf_op jit(solution)/shard_map/ppermute | solution.py:660
  346.9 28.7 %collective-permute-start.11 = (bf16[2,2,2,2,96,384]{5,4,3,0,1,2:T(8,128)(2,1)}, bf16[2,2,2,2,96,384]{5,4,3,0,1,2:T(8,128)(2,1)}, u32[]{:S(2)}, u32[]{:S(2)}) collective-permute-start(bf16[2,2,2,2,96,384]{5,4,3,0,1,2:T(8,128)(2,1)} %copy_bitcast_fusion.5), channel_id=1, source_target_pairs={{0,2},{1,3},{2,0},{3,1},{4,6},{5,7},{6,4},{7,5},{8,10},{9,11},{10,... | collective-permute-start | bytes 3538952 | tf_op jit(solution)/shard_map/ppermute | solution.py:660
  350.5 29.3 %collective-permute-start.12 = (bf16[2,2,2,2,96,384]{5,4,3,1,0,2:T(8,128)(2,1)S(1)}, bf16[2,2,2,2,96,384]{5,4,3,1,0,2:T(8,128)(2,1)}, u32[]{:S(2)}, u32[]{:S(2)}) collective-permute-start(bf16[2,2,2,2,96,384]{5,4,3,1,0,2:T(8,128)(2,1)S(1)} %copy_bitcast_fusion.4), channel_id=1, source_target_pairs={{0,4},{4,0},{8,12},{12,8},{16,20},{20,16},{24,28},{28,24},{1,5},{5... | collective-permute-start | bytes 3538952 | tf_op jit(solution)/shard_map/ppermute | solution.py:660
  354.6 28.2 %collective-permute-start.13 = (bf16[2,2,2,2,96,384]{5,4,3,1,2,0:T(8,128)(2,1)S(1)}, bf16[2,2,2,2,96,384]{5,4,3,1,2,0:T(8,128)(2,1)S(1)}, u32[]{:S(2)}, u32[]{:S(2)}) collective-permute-start(bf16[2,2,2,2,96,384]{5,4,3,1,2,0:T(8,128)(2,1)S(1)} %copy_bitcast_fusion.3), channel_id=1, source_target_pairs={{0,8},{4,12},{8,0},{12,4},{16,24},{20,28},{24,16},{28,20},{1,9},{5... | collective-permute-start | bytes 3538952 | tf_op jit(solution)/shard_map/ppermute | solution.py:660
  378.3 26.7 %collective-permute-start.16 = (bf16[2,2,2,96,384]{4,3,2,0,1:T(8,128)(2,1)}, bf16[2,2,2,96,384]{4,3,2,0,1:T(8,128)(2,1)}, u32[]{:S(2)}, u32[]{:S(2)}) collective-permute-start(bf16[2,2,2,96,384]{4,3,2,0,1:T(8,128)(2,1)} %dynamic-slice_bitcast_fusion.9), channel_id=1, source_target_pairs={{0,4},{4,0},{8,12},{12,8},{16,20},{20,16},{24,28},{28,24},{1,5},{5... | collective-permute-start | bytes 1769480 | tf_op jit(solution)/shard_map/ppermute | solution.py:660
  381.4 25.6 %collective-permute-start.17 = (bf16[2,2,2,96,384]{4,3,2,1,0:T(8,128)(2,1)S(1)}, bf16[2,2,2,96,384]{4,3,2,1,0:T(8,128)(2,1)S(1)}, u32[]{:S(2)}, u32[]{:S(2)}) collective-permute-start(bf16[2,2,2,96,384]{4,3,2,1,0:T(8,128)(2,1)S(1)} %dynamic-slice_bitcast_fusion.8), channel_id=1, source_target_pairs={{0,8},{4,12},{8,0},{12,4},{16,24},{20,28},{24,16},{28,20},{1,9},{5... | collective-permute-start | bytes 1769480 | tf_op jit(solution)/shard_map/ppermute | solution.py:660
  403.6 69.5 %collective-permute-start.14 = (bf16[1024,384]{1,0:T(8,128)(2,1)}, bf16[1024,384]{1,0:T(8,128)(2,1)S(1)}, u32[]{:S(2)}, u32[]{:S(2)}) collective-permute-start(bf16[1024,384]{1,0:T(8,128)(2,1)} %get-tuple-element.239), channel_id=1, source_target_pairs={{0,1},{1,0},{2,3},{3,2},{4,5},{5,4},{6,7},{7,6},{8,9},{9,8},{10,11... | collective-permute-start | bytes 2359304 | tf_op jit(solution)/shard_map/ppermute | solution.py:660
  403.7 71.0 %collective-permute-start.15 = (bf16[1024,384]{1,0:T(8,128)(2,1)}, bf16[1024,384]{1,0:T(8,128)(2,1)S(1)}, u32[]{:S(2)}, u32[]{:S(2)}) collective-permute-start(bf16[1024,384]{1,0:T(8,128)(2,1)} %get-tuple-element.241), channel_id=1, source_target_pairs={{0,1},{1,0},{2,3},{3,2},{4,5},{5,4},{6,7},{7,6},{8,9},{9,8},{10,11... | collective-permute-start | bytes 2359304 | tf_op jit(solution)/shard_map/ppermute | solution.py:660
  404.3 16.2 %collective-permute-start.18 = (bf16[2,2,2,96,384]{4,3,2,0,1:T(8,128)(2,1)S(1)}, bf16[2,2,2,96,384]{4,3,2,0,1:T(8,128)(2,1)S(1)}, u32[]{:S(2)}, u32[]{:S(2)}) collective-permute-start(bf16[2,2,2,96,384]{4,3,2,0,1:T(8,128)(2,1)S(1)} %dynamic-slice_bitcast_fusion.7), channel_id=1, source_target_pairs={{0,2},{1,3},{2,0},{3,1},{4,6},{5,7},{6,4},{7,5},{8,10},{9,11},{10,... | collective-permute-start | bytes 1769480 | tf_op jit(solution)/shard_map/ppermute | solution.py:660
  406.2 31.5 %collective-permute-start.19 = (bf16[2,2,96,384]{3,2,1,0:T(8,128)(2,1)S(1)}, bf16[2,2,96,384]{3,2,1,0:T(8,128)(2,1)S(1)}, u32[]{:S(2)}, u32[]{:S(2)}) collective-permute-start(bf16[2,2,96,384]{3,2,1,0:T(8,128)(2,1)S(1)} %dynamic-slice_bitcast_fusion.12), channel_id=1, source_target_pairs={{0,8},{4,12},{8,0},{12,4},{16,24},{20,28},{24,16},{28,20},{1,9},{5... | collective-permute-start | bytes 884744 | tf_op jit(solution)/shard_map/ppermute | solution.py:660
  407.2 31.2 %collective-permute-start.20 = (bf16[2,2,96,384]{3,2,1,0:T(8,128)(2,1)S(1)}, bf16[2,2,96,384]{3,2,1,0:T(8,128)(2,1)S(1)}, u32[]{:S(2)}, u32[]{:S(2)}) collective-permute-start(bf16[2,2,96,384]{3,2,1,0:T(8,128)(2,1)S(1)} %dynamic-slice_bitcast_fusion.11), channel_id=1, source_target_pairs={{0,2},{1,3},{2,0},{3,1},{4,6},{5,7},{6,4},{7,5},{8,10},{9,11},{10,... | collective-permute-start | bytes 884744 | tf_op jit(solution)/shard_map/ppermute | solution.py:660
  422.5 16.8 %collective-permute-start.21 = (bf16[2,2,96,384]{3,2,1,0:T(8,128)(2,1)S(1)}, bf16[2,2,96,384]{3,2,1,0:T(8,128)(2,1)S(1)}, u32[]{:S(2)}, u32[]{:S(2)}) collective-permute-start(bf16[2,2,96,384]{3,2,1,0:T(8,128)(2,1)S(1)} %dynamic-slice_bitcast_fusion.10), channel_id=1, source_target_pairs={{0,4},{4,0},{8,12},{12,8},{16,20},{20,16},{24,28},{28,24},{1,5},{5... | collective-permute-start | bytes 884744 | tf_op jit(solution)/shard_map/ppermute | solution.py:660
  469.2 7.0 collective-permute-start.22
  469.3 7.0 collective-permute-start.23
  471.6 29.8 %collective-permute-start.29 = (bf16[2,96,384]{2,1,0:T(8,128)(2,1)S(1)}, bf16[2,96,384]{2,1,0:T(8,128)(2,1)S(1)}, u32[]{:S(2)}, u32[]{:S(2)}) collective-permute-start(bf16[2,96,384]{2,1,0:T(8,128)(2,1)S(1)} %dynamic-slice_bitcast_fusion.13), channel_id=1, source_target_pairs={{0,16},{4,20},{8,24},{12,28},{16,0},{20,4},{24,8},{28,12},{1,17},{... | collective-permute-start | bytes 442376 | tf_op jit(solution)/shard_map/ppermute | solution.py:660
  473.2 28.2 %collective-permute-start.28 = (bf16[2,96,384]{2,1,0:T(8,128)(2,1)S(1)}, bf16[2,96,384]{2,1,0:T(8,128)(2,1)}, u32[]{:S(2)}, u32[]{:S(2)}) collective-permute-start(bf16[2,96,384]{2,1,0:T(8,128)(2,1)S(1)} %dynamic-slice_bitcast_fusion.14), channel_id=1, source_target_pairs={{0,16},{4,20},{8,24},{12,28},{16,0},{20,4},{24,8},{28,12},{1,17},{... | collective-permute-start | bytes 442376 | tf_op jit(solution)/shard_map/ppermute | solution.py:660
  474.8 29.8 %collective-permute-start.27 = (bf16[2,96,384]{2,1,0:T(8,128)(2,1)S(1)}, bf16[2,96,384]{2,1,0:T(8,128)(2,1)S(1)}, u32[]{:S(2)}, u32[]{:S(2)}) collective-permute-start(bf16[2,96,384]{2,1,0:T(8,128)(2,1)S(1)} %dynamic-slice_bitcast_fusion.15), channel_id=1, source_target_pairs={{0,16},{4,20},{8,24},{12,28},{16,0},{20,4},{24,8},{28,12},{1,17},{... | collective-permute-start | bytes 442376 | tf_op jit(solution)/shard_map/ppermute | solution.py:660
  501.4 21.4 %collective-permute-start.25 = (bf16[2,12,96,384]{3,2,1,0:T(8,128)(2,1)}, bf16[2,12,96,384]{3,2,1,0:T(8,128)(2,1)}, u32[]{:S(2)}, u32[]{:S(2)}) collective-permute-start(bf16[2,12,96,384]{3,2,1,0:T(8,128)(2,1)} %dynamic-slice_bitcast_fusion.1), channel_id=1, source_target_pairs={{0,1},{1,0},{2,3},{3,2},{4,5},{5,4},{6,7},{7,6},{8,9},{9,8},{10,11... | collective-permute-start | bytes 5308424 | tf_op jit(solution)/shard_map/ppermute | solution.py:660
  504.7 13.5 %collective-permute-start.30 = (bf16[6,96,384]{2,1,0:T(8,128)(2,1)S(1)}, bf16[6,96,384]{2,1,0:T(8,128)(2,1)}, u32[]{:S(2)}, u32[]{:S(2)}) collective-permute-start(bf16[6,96,384]{2,1,0:T(8,128)(2,1)S(1)} %get-tuple-element.297), channel_id=1, source_target_pairs={{0,2},{1,3},{2,0},{3,1},{4,6},{5,7},{6,4},{7,5},{8,10},{9,11},{10,... | collective-permute-start | bytes 1327112 | tf_op jit(solution)/shard_map/ppermute | solution.py:660
  507.2 29.2 %collective-permute-start.9 = (bf16[512,768]{1,0:T(8,128)(2,1)}, bf16[512,768]{1,0:T(8,128)(2,1)}, u32[]{:S(2)}, u32[]{:S(2)}) collective-permute-start(bf16[512,768]{1,0:T(8,128)(2,1)} %get-tuple-element.289), channel_id=1, source_target_pairs={{0,2},{1,3},{2,0},{3,1},{4,6},{5,7},{6,4},{7,5},{8,10},{9,11},{10,... | collective-permute-start | bytes 2359304 | tf_op jit(solution)/shard_map/ppermute | solution.py:660
  520.4 18.9 %collective-permute-start.31 = (bf16[2,6,96,384]{3,2,1,0:T(8,128)(2,1)}, bf16[2,6,96,384]{3,2,1,0:T(8,128)(2,1)S(1)}, u32[]{:S(2)}, u32[]{:S(2)}) collective-permute-start(bf16[2,6,96,384]{3,2,1,0:T(8,128)(2,1)} %pad_maximum_fusion.6), channel_id=1, source_target_pairs={{0,1},{1,0},{2,3},{3,2},{4,5},{5,4},{6,7},{7,6},{8,9},{9,8},{10,11... | collective-permute-start | bytes 2654216 | tf_op jit(solution)/shard_map/ppermute | solution.py:660
  521.3 34.7 %collective-permute-start.24 = (bf16[512,768]{1,0:T(8,128)(2,1)}, bf16[512,768]{1,0:T(8,128)(2,1)}, u32[]{:S(2)}, u32[]{:S(2)}) collective-permute-start(bf16[512,768]{1,0:T(8,128)(2,1)} %get-tuple-element.287), channel_id=1, source_target_pairs={{0,2},{1,3},{2,0},{3,1},{4,6},{5,7},{6,4},{7,5},{8,10},{9,11},{10,... | collective-permute-start | bytes 2359304 | tf_op jit(solution)/shard_map/ppermute | solution.py:660
  527.0 47.7 %collective-permute-start.26 = (bf16[12,96,384]{2,1,0:T(8,128)(2,1)}, bf16[12,96,384]{2,1,0:T(8,128)(2,1)}, u32[]{:S(2)}, u32[]{:S(2)}) collective-permute-start(bf16[12,96,384]{2,1,0:T(8,128)(2,1)} %dynamic-slice_bitcast_fusion.2), channel_id=1, source_target_pairs={{0,2},{1,3},{2,0},{3,1},{4,6},{5,7},{6,4},{7,5},{8,10},{9,11},{10,... | collective-permute-start | bytes 2654216 | tf_op jit(solution)/shard_map/ppermute | solution.py:660
  650.7 7.7 collective-permute-start.2
  659.9 57.1 %collective-permute-start.3 = (bf16[2,4,96,384]{3,2,1,0:T(8,128)(2,1)}, bf16[2,4,96,384]{3,2,1,0:T(8,128)(2,1)}, u32[]{:S(2)}, u32[]{:S(2)}) collective-permute-start(bf16[2,4,96,384]{3,2,1,0:T(8,128)(2,1)} %pad_maximum_fusion.1), channel_id=1, source_target_pairs={{0,1},{1,0},{2,3},{3,2},{4,5},{5,4},{6,7},{7,6},{8,9},{9,8},{10,11... | collective-permute-start | bytes 1769480 | tf_op jit(solution)/shard_map/cond/branch_1_fun/ppermute | solution.py:660
  (55 other events, 464.9 us)
Sparse Core Ops, SparseCore 0:
  11.5 108.3 all-gather.5
  504.6 56.4 all-gather.7

commit v3 on v2

--- a/solution.py
+++ b/solution.py
@@ -96,21 +96,26 @@
     return pl.BlockSpec(shape, lambda i, own, slot: (0,) * len(shape))
 
 
-def put_tile(ref, i, value):
-    rows = BLK // 4
-    low = value.astype(LOW)
-    for quarter in range(4):
-        ref[quarter % 2, quarter // 2, i, 0] = low[quarter * rows : quarter * rows + rows]
-
-
-def qkv_kernel(own, slot, x_ref, vec_ref, bias_ref, t0, t1, qkv_ref, a_ref):
+def quarter_at(seq, rel_core, rel_x):
+    return seq ^ (2 * rel_x + rel_core)
+
+
+def qkv_kernel(own, slot, x_ref, vec_ref, bias_ref, t0, t1, q_ref, kv_ref, a_ref):
     @pl.when(pl.program_id(0) == 0)
     def _():
         hat, _ = norm_parts(x_ref[...].astype(F32))
         a_ref[...] = (hat * vec_ref[0:1, :] + vec_ref[1:2, :]).astype(LOW)
 
     total = dot(a_ref[:, :BLK], tile(t0), 1, 0) + dot(a_ref[:, BLK:], tile(t1), 1, 0)
-    qkv_ref[...] = (total + bias_ref[...]).astype(LOW)
+    low = (total + bias_ref[...]).astype(LOW)
+
+    @pl.when(pl.program_id(0) < 2)
+    def _():
+        q_ref[...] = low
+
+    @pl.when(pl.program_id(0) >= 2)
+    def _():
+        kv_ref[...] = low
 
 
 def qkv_forward(own, slot, x, vec, bias, gathered):
@@ -128,12 +133,14 @@
                 tile_spec(lambda i: 6 + i),
             ],
             out_specs=[
-                pl.BlockSpec((rows, BLK), lambda i, own, slot: (0, i)),
+                pl.BlockSpec((rows, BLK), lambda i, own, slot: (0, jnp.minimum(i, 1))),
+                pl.BlockSpec((rows, BLK), lambda i, own, slot: (0, jnp.maximum(i - 2, 0))),
                 full_spec((rows, D)),
             ],
         ),
         out_shape=[
-            jax.ShapeDtypeStruct((rows, 3 * D), LOW),
+            jax.ShapeDtypeStruct((rows, D), LOW),
+            jax.ShapeDtypeStruct((rows, 2 * D), LOW),
             jax.ShapeDtypeStruct((rows, D), LOW),
         ],
         compiler_params=params(48),
@@ -174,8 +181,8 @@
     lse_ref[...] = jnp.where(ln < 64, tops[1], tops[0]) + jnp.log(total)
 
 
-def attn_forward(qkv, other, bias, q_rows=256):
-    rows, pairs = qkv.shape[0], D // 128
+def attn_forward(q, kv, other, bias, q_rows=256):
+    rows, pairs = q.shape[0], D // 128
     keys = 2 * rows
     q_spec = pl.BlockSpec((q_rows, 128), lambda p, i: (i, p))
     return pl.pallas_call(
@@ -183,8 +190,8 @@
         grid=(pairs, rows // q_rows),
         in_specs=[
             q_spec,
+            pl.BlockSpec((rows, 128), lambda p, i: (0, p)),
             pl.BlockSpec((rows, 128), lambda p, i: (0, pairs + p)),
-            pl.BlockSpec((rows, 128), lambda p, i: (0, 2 * pairs + p)),
             pl.BlockSpec((rows, 128), lambda p, i: (0, p)),
             pl.BlockSpec((rows, 128), lambda p, i: (0, pairs + p)),
             pl.BlockSpec((keys, 128), lambda p, i: (0, 0)),
@@ -197,7 +204,7 @@
         scratch_shapes=[pltpu.VMEM((keys, 128), LOW)] * 4,
         compiler_params=params(48),
         name="attn_fwd",
-    )(qkv, qkv, qkv, other, other, bias)
+    )(q, kv, kv, other, other, bias)
 
 
 def three_parts(x):
@@ -278,33 +285,26 @@
         dv2[...] = dv[rows:, :].astype(LOW)
 
 
-def attn_backward(qkv, other, bias, attn, lse, d_attn, first, place, total, before, after, q_rows=512, chunk=1024):
-    rows, pairs = qkv.shape[0], D // 128
+def attn_backward(q, kv, other, bias, attn, lse, d_attn, first, count, place, total, before, q_rows=512, chunk=1024):
+    rows, pairs = q.shape[0], D // 128
     keys = 2 * rows
-    out_spec = pl.BlockSpec((q_rows, 128), lambda p, i: (i, place))
-    k_out = pl.BlockSpec((rows, 128), lambda p, i: (0, place))
-    anywhere = pl.BlockSpec(memory_space=pl.ANY)
-    q_spec = pl.BlockSpec((q_rows, 128), lambda p, i: (i, first))
-    extra = list(before) + list(after)
+    out_spec = pl.BlockSpec((q_rows, 128), lambda p, i: (i, place + p))
+    k_out = pl.BlockSpec((rows, 128), lambda p, i: (0, place + p))
+    q_spec = pl.BlockSpec((q_rows, 128), lambda p, i: (i, first + p))
+    k_spec = pl.BlockSpec((rows, 128), lambda p, i: (0, first + p))
+    v_spec = pl.BlockSpec((rows, 128), lambda p, i: (0, pairs + first + p))
 
     def kernel(*refs):
-        attn_bwd_kernel(*refs[:9], *refs[9 + len(extra) :], chunk=chunk)
+        attn_bwd_kernel(*refs[:9], *refs[9 + len(before) :], chunk=chunk)
 
     return pl.pallas_call(
         kernel,
-        grid=(1, rows // q_rows),
+        grid=(count, rows // q_rows),
         in_specs=[
-            q_spec,
-            pl.BlockSpec((rows, 128), lambda p, i: (0, pairs + first)),
-            pl.BlockSpec((rows, 128), lambda p, i: (0, 2 * pairs + first)),
-            pl.BlockSpec((rows, 128), lambda p, i: (0, first)),
-            pl.BlockSpec((rows, 128), lambda p, i: (0, pairs + first)),
-            pl.BlockSpec((keys, 128), lambda p, i: (0, 0)),
-            q_spec,
-            q_spec,
-            q_spec,
+            q_spec, k_spec, v_spec, k_spec, v_spec, pl.BlockSpec((keys, 128), lambda p, i: (0, 0)),
+            q_spec, q_spec, q_spec,
         ]
-        + [anywhere] * len(extra),
+        + [pl.BlockSpec(memory_space=pl.ANY)] * len(before),
         out_specs=[out_spec, k_out, k_out, k_out, k_out],
         out_shape=[jax.ShapeDtypeStruct((rows, total * 128), LOW)] * 5,
         scratch_shapes=[pltpu.VMEM((keys, 128), LOW)] * 4
@@ -313,16 +313,42 @@
         input_output_aliases={9 + i: i for i in range(len(before))},
         compiler_params=params(56),
         name="attn_bwd",
-    )(qkv, qkv, qkv, other, other, bias, attn, lse, d_attn, *extra)
+    )(q, kv, kv, other, other, bias, attn, lse, d_attn, *before)
 
 
 def mid_kernel(
-    own, slot, x_ref, attn_ref, dy_ref, vec_ref, b1_ref, o00, o01, o10, o11, u0, u1, w0, w1,
-    res_ref, dmid_ref, dattn_ref, g_up, g_down, g_out, sums_ref, gb1_ref,
-    mid, a2, acc, da2, *, chunk,
+    own, slot, rel, seq, x_ref, attn_ref, dy_ref, vec_ref, b1_ref, o00, o01, o10, o11, u0, u1, w0, w1,
+    res_ref, dmid_ref, dattn_ref, keep, send, sums_ref, gb1_ref,
+    mid, a2, acc, da2, stage, sems, *, chunk,
 ):
     step = pl.program_id(0)
     last = pl.num_programs(0) - 1
+    quarter = BLK // 4
+
+    def copies(buf, i, block):
+        found = []
+        for rel_core, out in enumerate((keep, send)):
+            for rel_x in range(2):
+                found.append(
+                    pltpu.make_async_copy(
+                        stage.at[buf, i, quarter_at(seq[0], rel_core, rel_x)],
+                        out.at[rel_x, rel[block], slot[block]],
+                        sems.at[buf, i, 2 * rel_core + rel_x],
+                    )
+                )
+        return found
+
+    def put(buf, i, block, value):
+        low = value.astype(LOW)
+        for part in range(4):
+            stage[buf, i, part] = low[part * quarter : part * quarter + quarter]
+        for copy in copies(buf, i, block):
+            copy.start()
+
+    def settle(buf):
+        for i in range(4):
+            for copy in copies(buf, i, 0):
+                copy.wait()
 
     @pl.when(step == 0)
     def _():
@@ -362,13 +388,16 @@
         gb1_ref[...] = bias_grad
         act = jnp.concatenate(acts, axis=0)
         d_hid = jnp.concatenate(d_hids, axis=0)
+        buf = step % 2
+
+        @pl.when(step > 2)
+        def _():
+            settle(buf)
+
         for j in range(2):
             c = slice(j * BLK, j * BLK + BLK)
-            put_tile(g_up, j, dot(a2[:, c], d_hid, 0, 0))
-            rows_q = BLK // 4
-            low = dot(act, dy_ref[:, c], 0, 0).astype(LOW)
-            for quarter in range(4):
-                g_down[quarter % 2, quarter // 2, 0, j] = low[quarter * rows_q : quarter * rows_q + rows_q]
+            put(buf, j, 16 + 8 * j + step - 1, dot(a2[:, c], d_hid, 0, 0))
+            put(buf, 2 + j, 32 + 2 * (step - 1) + j, dot(act, dy_ref[:, c], 0, 0))
 
     @pl.when(step == last)
     def _():
@@ -389,76 +418,130 @@
             dattn_ref[:, c] = (
                 dot(d_proj[:, :BLK], tile(first), 1, 1) + dot(d_proj[:, BLK:], tile(second), 1, 1)
             ).astype(LOW)
+        settle(0)
+        for i in range(2):
             for j in range(2):
-                rows_q = BLK // 4
-                low = dot(attn_ref[:, c], d_proj[:, j * BLK : j * BLK + BLK], 0, 0).astype(LOW)
-                for quarter in range(4):
-                    g_out[quarter % 2, quarter // 2, i, j] = low[quarter * rows_q : quarter * rows_q + rows_q]
-
-
-def mid_layer(own, slot, x, attn, dy, vec, b1, gathered, chunk=256):
+                c, k = slice(i * BLK, i * BLK + BLK), slice(j * BLK, j * BLK + BLK)
+                put(0, 2 * i + j, 12 + 2 * i + j, dot(attn_ref[:, c], d_proj[:, k], 0, 0))
+        settle(1)
+        settle(0)
+
+
+def mid_layer(own, slot, rel, seq, x, attn, dy, vec, b1, gathered, chunk=256):
     rows = x.shape[0]
     wide = FF // BLK
     quarter = BLK // 4
+    owners, slots = gathered.shape[0], gathered.shape[2]
 
     def part(i):
         return jnp.clip(i - 1, 0, wide - 1)
 
-    row_spec = full_spec((rows, D))
+    def full(shape):
+        return pl.BlockSpec(shape, lambda i, own, slot, rel, seq: (0,) * len(shape))
+
+    def tile_at(block_of):
+        return pl.BlockSpec(
+            (1, 4, 1, quarter, BLK),
+            lambda i, own, slot, rel, seq: (own[block_of(i)], 0, slot[block_of(i)], 0, 0),
+        )
+
+    row_spec = full((rows, D))
+    strip = pl.BlockSpec((1, BLK), lambda i, own, slot, rel, seq: (0, part(i)))
+    anywhere = pl.BlockSpec(memory_space=pl.ANY)
+    place_shape = jax.ShapeDtypeStruct((2, owners, slots, quarter, BLK), LOW)
     return pl.pallas_call(
         functools.partial(mid_kernel, chunk=chunk),
         grid_spec=pltpu.PrefetchScalarGridSpec(
-            num_scalar_prefetch=2,
+            num_scalar_prefetch=4,
             grid=(wide + 2,),
-            in_specs=[
-                row_spec,
-                row_spec,
-                row_spec,
-                full_spec(vec.shape),
-                pl.BlockSpec((1, BLK), lambda i, own, slot: (0, part(i))),
-                tile_spec(lambda i: 12),
-                tile_spec(lambda i: 13),
-                tile_spec(lambda i: 14),
-                tile_spec(lambda i: 15),
-                tile_spec(lambda i: 16 + part(i)),
-                tile_spec(lambda i: 24 + part(i)),
-                tile_spec(lambda i: 32 + 2 * part(i)),
-                tile_spec(lambda i: 33 + 2 * part(i)),
+            in_specs=[row_spec, row_spec, row_spec, full(vec.shape), strip]
+            + [tile_at(lambda i, b=b: b) for b in (12, 13, 14, 15)]
+            + [
+                tile_at(lambda i: 16 + part(i)),
+                tile_at(lambda i: 24 + part(i)),
+                tile_at(lambda i: 32 + 2 * part(i)),
+                tile_at(lambda i: 33 + 2 * part(i)),
             ],
-            out_specs=[
-                row_spec,
-                row_spec,
-                row_spec,
-                pl.BlockSpec((2, 2, 2, 1, quarter, BLK), lambda i, own, slot: (0, 0, 0, part(i), 0, 0)),
-                pl.BlockSpec((2, 2, 1, 2, quarter, BLK), lambda i, own, slot: (0, 0, part(i), 0, 0, 0)),
-                full_spec((2, 2, 2, 2, quarter, BLK)),
-                full_spec((8, D)),
-                pl.BlockSpec((1, BLK), lambda i, own, slot: (0, part(i))),
-            ],
+            out_specs=[row_spec, row_spec, row_spec, anywhere, anywhere, full((8, D)), strip],
             scratch_shapes=[
                 pltpu.VMEM((rows, D), F32),
                 pltpu.VMEM((rows, D), LOW),
                 pltpu.VMEM((rows, D), F32),
                 pltpu.VMEM((rows, D), F32),
+                pltpu.VMEM((2, 4, 4, quarter, BLK), LOW),
+                pltpu.SemaphoreType.DMA((2, 4, 4)),
             ],
         ),
         out_shape=[
             jax.ShapeDtypeStruct((rows, D), LOW),
             jax.ShapeDtypeStruct((rows, D), F32),
             jax.ShapeDtypeStruct((rows, D), LOW),
-            jax.ShapeDtypeStruct((2, 2, 2, wide, quarter, BLK), LOW),
-            jax.ShapeDtypeStruct((2, 2, wide, 2, quarter, BLK), LOW),
-            jax.ShapeDtypeStruct((2, 2, 2, 2, quarter, BLK), LOW),
+            place_shape,
+            place_shape,
             jax.ShapeDtypeStruct((8, D), F32),
             jax.ShapeDtypeStruct((1, FF), F32),
         ],
-        compiler_params=params(58),
+        compiler_params=params(60),
         name="mid",
-    )(own, slot, x, attn, dy, vec, b1, *([gathered] * 8))
-
-
-def qkv_bwd_kernel(own, slot, x_ref, a_ref, dmid_ref, vec_ref, *refs):
-    grads, (t0, t1, dx_ref, g_qkv, sums_ref, cols_ref, acc) = refs[:10], refs[10:]
+    )(own, slot, rel, seq, x, attn, dy, vec, b1, *([gathered] * 8))
+
+
+def d_columns(step, grads, work):
+    for half in range(2):
+        dq, dk, rk, dv, rv = grads[5 * half : 5 * half + 5]
+
+        @pl.when(step == half)
+        def _():
+            work(dq[...])
+
+        @pl.when(step == 2 + half)
+        def _():
+            work((dk[...].astype(F32) + rk[...].astype(F32)).astype(LOW))
+
+        @pl.when(step == 4 + half)
+        def _():
+            work((dv[...].astype(F32) + rv[...].astype(F32)).astype(LOW))
+
+
+def qkv_grad_kernel(seq, a_ref, *refs):
+    grads, (keep, send, cols_ref, stage) = refs[:10], refs[10:]
+    quarter = BLK // 4
+
+    def work(d_cols):
+        cols_ref[...] = jnp.sum(d_cols.astype(F32), axis=0, keepdims=True)
+        for i in range(2):
+            stage[...] = dot(a_ref[:, i * BLK : i * BLK + BLK], d_cols, 0, 0).astype(LOW)
+            for rel_core, out in enumerate((keep, send)):
+                for rel_x in range(2):
+                    start = pl.multiple_of(quarter_at(seq[0], rel_core, rel_x) * quarter, quarter)
+                    out[rel_x, i, 0] = stage[pl.ds(start, quarter), :]
+
+    d_columns(pl.program_id(0), grads, work)
+
+
+def qkv_grad(seq, normed, halves):
+    rows = normed.shape[0]
+    quarter = BLK // 4
+    tile_out = pl.BlockSpec((2, 2, 1, quarter, BLK), lambda i, seq: (0, 0, i, 0, 0))
+    shape = jax.ShapeDtypeStruct((2, 2, 6, quarter, BLK), LOW)
+    return pl.pallas_call(
+        qkv_grad_kernel,
+        grid_spec=pltpu.PrefetchScalarGridSpec(
+            num_scalar_prefetch=1,
+            grid=(6,),
+            in_specs=[pl.BlockSpec((rows, D), lambda i, seq: (0, 0))]
+            + [pl.BlockSpec((rows, BLK), lambda i, seq: (0, 0))] * 10,
+            out_specs=[tile_out, tile_out, pl.BlockSpec((1, BLK), lambda i, seq: (0, i))],
+            scratch_shapes=[pltpu.VMEM((BLK, BLK), LOW)],
+        ),
+        out_shape=[shape, shape, jax.ShapeDtypeStruct((1, 3 * D), F32)],
+        compiler_params=params(48),
+        name="qkv_grad",
+    )(seq, normed, *halves[0], *halves[1])
+
+
+def qkv_bwd_kernel(own, slot, x_ref, dmid_ref, vec_ref, *refs):
+    grads, (t0, t1, dx_ref, sums_ref, acc) = refs[:10], refs[10:]
     step = pl.program_id(0)
 
     @pl.when(step == 0)
@@ -468,24 +551,8 @@
     def work(d_cols):
         acc[:, :BLK] += dot(d_cols, tile(t0), 1, 1)
         acc[:, BLK:] += dot(d_cols, tile(t1), 1, 1)
-        put_tile(g_qkv, 0, dot(a_ref[:, :BLK], d_cols, 0, 0))
-        put_tile(g_qkv, 1, dot(a_ref[:, BLK:], d_cols, 0, 0))
-        cols_ref[...] = jnp.sum(d_cols.astype(F32), axis=0, keepdims=True)
-
-    for half in range(2):
-        dq, dk, rk, dv, rv = grads[5 * half : 5 * half + 5]
-
-        @pl.when(step == half)
-        def _():
-            work(dq[...])
-
-        @pl.when(step == 2 + half)
-        def _():
-            work((dk[...].astype(F32) + rk[...].astype(F32)).astype(LOW))
-
-        @pl.when(step == 4 + half)
-        def _():
-            work((dv[...].astype(F32) + rv[...].astype(F32)).astype(LOW))
+
+    d_columns(step, grads, work)
 
     @pl.when(step == 5)
     def _():
@@ -497,35 +564,24 @@
         dx_ref[...] = (dmid_ref[...] + norm_back(grad * vec_ref[0:1, :], hat, rstd)).astype(LOW)
 
 
-def qkv_backward(own, slot, x, normed, d_mid, vec, halves, gathered):
+def qkv_backward(own, slot, x, d_mid, vec, halves, gathered):
     rows = x.shape[0]
-    quarter = BLK // 4
     row_spec = full_spec((rows, D))
     return pl.pallas_call(
         qkv_bwd_kernel,
         grid_spec=pltpu.PrefetchScalarGridSpec(
             num_scalar_prefetch=2,
             grid=(6,),
-            in_specs=[row_spec, row_spec, row_spec, full_spec(vec.shape)]
+            in_specs=[row_spec, row_spec, full_spec(vec.shape)]
             + [full_spec((rows, BLK))] * 10
             + [tile_spec(lambda i: i), tile_spec(lambda i: 6 + i)],
-            out_specs=[
-                row_spec,
-                pl.BlockSpec((2, 2, 2, 1, quarter, BLK), lambda i, own, slot: (0, 0, 0, i, 0, 0)),
-                full_spec((8, D)),
-                pl.BlockSpec((1, BLK), lambda i, own, slot: (0, i)),
-            ],
+            out_specs=[row_spec, full_spec((8, D))],
             scratch_shapes=[pltpu.VMEM((rows, D), F32)],
         ),
-        out_shape=[
-            jax.ShapeDtypeStruct((rows, D), LOW),
-            jax.ShapeDtypeStruct((2, 2, 2, 6, quarter, BLK), LOW),
-            jax.ShapeDtypeStruct((8, D), F32),
-            jax.ShapeDtypeStruct((1, 3 * D), F32),
-        ],
+        out_shape=[jax.ShapeDtypeStruct((rows, D), LOW), jax.ShapeDtypeStruct((8, D), F32)],
         compiler_params=params(60),
         name="qkv_bwd",
-    )(own, slot, x, normed, d_mid, vec, *halves[0], *halves[1], gathered, gathered)
+    )(own, slot, x, d_mid, vec, *halves[0], *halves[1], gathered, gathered)
 
 
 def eliminate(y_ref):
@@ -626,20 +682,18 @@
             lax.fori_loop(0, count, functools.partial(solve, out=rb_out), 0)
 
 
-def soap_update(seq_id, pieces, state, first, count, before):
-    slots = state[0].shape[0]
+def soap_update(seq, pieces, state):
+    count = state[0].shape[0]
     piece_spec = pl.BlockSpec((1, BLK // 4, BLK), lambda i, s: (i, 0, 0))
-    block_spec = pl.BlockSpec((1, BLK, BLK), lambda i, s: (first + i, 0, 0))
-    whole_spec = pl.BlockSpec((count, BLK, BLK), lambda i, s: (first // count, 0, 0))
-    shape = jax.ShapeDtypeStruct((slots, BLK, BLK), F32)
+    block_spec = pl.BlockSpec((1, BLK, BLK), lambda i, s: (i, 0, 0))
+    whole_spec = pl.BlockSpec((count, BLK, BLK), lambda i, s: (0, 0, 0))
+    shape = jax.ShapeDtypeStruct((count, BLK, BLK), F32)
     return pl.pallas_call(
         soap_kernel,
         grid_spec=pltpu.PrefetchScalarGridSpec(
             num_scalar_prefetch=1,
             grid=(count,),
-            in_specs=[piece_spec] * 4
-            + [block_spec] * 7
-            + [pl.BlockSpec(memory_space=pl.ANY)] * len(before),
+            in_specs=[piece_spec] * 4 + [block_spec] * 7,
             out_specs=[block_spec] * 6 + [whole_spec] * 2,
             scratch_shapes=[
                 pltpu.VMEM((BLK, BLK), F32),
@@ -649,10 +703,74 @@
             ],
         ),
         out_shape=[shape] * 8,
-        input_output_aliases={12 + i: i for i in range(len(before))},
         compiler_params=params(60),
         name="soap",
-    )(seq_id, *pieces, *state, *before)
+    )(seq, *pieces, *state)
+
+
+def split_kernel(dp, a_ref, b_ref, *outs):
+    for k, out in enumerate(outs):
+        out[...] = (a_ref[dp[0] ^ k].astype(F32) + b_ref[dp[0] ^ k].astype(F32)).astype(LOW)
+
+
+def split_sum(dp, a, b):
+    parts = a.shape[0]
+    shape = a.shape[1:]
+    return pl.pallas_call(
+        split_kernel,
+        grid_spec=pltpu.PrefetchScalarGridSpec(
+            num_scalar_prefetch=1,
+            grid=(1,),
+            in_specs=[pl.BlockSpec(a.shape, lambda i, dp: (0,) * a.ndim)] * 2,
+            out_specs=[pl.BlockSpec(shape, lambda i, dp: (0,) * len(shape))] * parts,
+        ),
+        out_shape=[jax.ShapeDtypeStruct(shape, LOW)] * parts,
+        compiler_params=params(32),
+        name="split_sum",
+    )(dp, a, b)
+
+
+def choose_kernel(dp, source, *refs):
+    parts, early, out, held = refs[:-3], refs[-3], refs[-2], refs[-1]
+    per, half = held.shape[1], held.shape[2]
+    for k, part in enumerate(parts):
+        held[k] = part[...]
+    slots = out.shape[0]
+    units = len(parts) * per
+
+    def one(i, carry):
+        block = source[i]
+
+        @pl.when(2 * block >= units)
+        def _():
+            out[i] = early[i]
+
+        @pl.when(2 * block < units)
+        def _():
+            for h in range(2):
+                unit = 2 * block + h
+                out[i, h * half : h * half + half] = held[lax.div(unit, per) ^ dp[0], lax.rem(unit, per)]
+
+        return carry
+
+    lax.fori_loop(0, slots, one, 0)
+
+
+def choose(dp, source, parts, early):
+    return pl.pallas_call(
+        choose_kernel,
+        grid_spec=pltpu.PrefetchScalarGridSpec(
+            num_scalar_prefetch=2,
+            grid=(1,),
+            in_specs=[pl.BlockSpec(parts[0].shape, lambda i, dp, src: (0, 0, 0))] * len(parts)
+            + [pl.BlockSpec(early.shape, lambda i, dp, src: (0, 0, 0))],
+            out_specs=pl.BlockSpec(early.shape, lambda i, dp, src: (0, 0, 0)),
+            scratch_shapes=[pltpu.VMEM((len(parts),) + parts[0].shape, LOW)],
+        ),
+        out_shape=jax.ShapeDtypeStruct(early.shape, LOW),
+        compiler_params=params(32),
+        name="choose",
+    )(dp, source, *parts, early)
 
 
 def swap(x, axis, bit):
@@ -664,10 +782,27 @@
     return (a.astype(F32) + b.astype(F32)).astype(LOW)
 
 
-def halve(x, dim, axis, bit, mine):
-    kept = lax.dynamic_index_in_dim(x, mine, dim, keepdims=False)
-    sent = lax.dynamic_index_in_dim(x, 1 - mine, dim, keepdims=False)
-    return add_low(kept, swap(sent, axis, bit))
+class Halving:
+    def __init__(self, kept, got, names):
+        self.kept, self.got, self.names = kept, got, list(names)
+
+    def take(self, name, index):
+        at = (slice(None),) * self.names.index(name) + (index,)
+        return add_low(self.kept[at], self.got[at])
+
+    def send(self, name):
+        sent, kept = self.take(name, 1), self.take(name, 0)
+        self.names.remove(name)
+        self.kept = kept
+        self.sent, self.name = sent, name
+        return sent
+
+    def receive(self, sent):
+        axis, bit = ("seq", 2) if self.name == "x" else ("dp", 2**self.name)
+        self.got = swap(sent, axis, bit)
+
+    def total(self):
+        return add_low(self.kept, self.got)
 
 
 def quarters(piece):
@@ -718,18 +853,16 @@
         owner_count, 4, slot_count, quarter, BLK
     )
 
-    def to_sequence(pair):
-        kept = lax.dynamic_index_in_dim(pair, chip, 0, keepdims=False)
-        sent = lax.dynamic_index_in_dim(pair, 1 - chip, 0, keepdims=False)
-        return jnp.concatenate([kept, swap(sent, "seq", 2)], axis=0)
+    pair = jnp.stack([tokens, cotangent])
+    kept = lax.dynamic_index_in_dim(pair, chip, 1, keepdims=False)
+    got = swap(lax.dynamic_index_in_dim(pair, 1 - chip, 1, keepdims=False), "seq", 2)
+    x = jnp.concatenate([kept[0], got[0]], axis=0)
+    dy = jnp.concatenate([kept[1], got[1]], axis=0)
 
     def to_positions(rows):
         other = swap(rows[part_len:], "seq", 2)
         mine = rows[:part_len]
         return jnp.where(chip == 0, jnp.stack([mine, other]), jnp.stack([other, mine]))
-
-    x = to_sequence(tokens)
-    dy = to_sequence(cotangent)
 
     positions = jnp.arange(patch_mask.shape[-1], dtype=jnp.int32)
     live = (positions[None, :] < lengths[:, None]) & ((patch_mask == 1) | (positions[None, :] == 0))
@@ -739,98 +872,89 @@
     fill = jnp.broadcast_to(fill[:, None], (fill.shape[0], 128))
 
     bias = jnp.concatenate([vec[4], jnp.zeros_like(vec[4]), vec[5]])[None, :]
-    qkv, normed = qkv_forward(owners, slots, x, vec, bias, gathered)
-    other = swap(qkv[:, D:], "seq", 1)
-    attn, lse = attn_forward(qkv, other, fill)
+    q, kv, normed = qkv_forward(owners, slots, x, vec, bias, gathered)
+    other = swap(kv, "seq", 1)
+    attn, lse = attn_forward(q, kv, other, fill)
     b1 = vec[8:].reshape(1, FF)
-    result, d_mid, d_attn, g_up, g_down, g_out, sums_two, bias_grad = mid_layer(
-        owners, slots, x, attn, dy, vec, b1, gathered
+    seq_of, dp_of = seq_id.reshape(1), dp_id.reshape(1)
+    result, d_mid, d_attn, keep, send, sums_two, bias_grad = mid_layer(
+        owners, slots, owners ^ dp_id, seq_of, x, attn, dy, vec, b1, gathered
     )
     output = to_positions(result)
-    early = jnp.concatenate(
-        [g.reshape(2, 2, -1, quarter, BLK) for g in (g_out, g_up, g_down)], axis=2
-    )
-    early = halve(early, 0, "seq", 1, core)
 
     bits = owner_count.bit_length() - 1
-    dims = ["x"] + list(range(bits))[::-1]
     if slot_count % 3 == 0 and bits == 3:
         plans = [["x", 0, 1, 2], [0, 1, "x", 2], [1, "x", 0, 2]]
     else:
         plans = [["x"] + list(range(bits))]
     per = slot_count // len(plans)
-    early = jnp.concatenate([early, jnp.zeros((2, 1, quarter, BLK), LOW)], axis=1)
-    early_at = jnp.where(sources >= first_blocks, sources - first_blocks, sources.shape[0])
-    early_at = jnp.minimum(early_at, early.shape[1] - 1).reshape(owner_count, slot_count)
+    names = ["x"] + list(range(bits))[::-1]
+    shape = (2,) * (1 + bits) + keep.shape[2:]
+    keep, got = keep.reshape(shape), swap(send, "seq", 1).reshape(shape)
     groups = [
-        jnp.take(early, early_at[:, per * g : per * g + per].reshape(-1), axis=1).reshape(
-            (2,) * len(dims) + (per, quarter, BLK)
-        )
-        for g in range(len(plans))
+        Halving(keep[..., per * g : per * g + per, :, :], got, names) for g in range(len(plans))
     ]
-    left = [list(dims) for _ in plans]
-
-    def advance(step):
-        for g, plan in enumerate(plans):
-            name = plan[step]
-            at = left[g].index(name)
-            left[g].pop(at)
-            if name == "x":
-                groups[g] = halve(groups[g], at, "seq", 2, chip)
-            else:
-                groups[g] = halve(groups[g], at, "dp", 2**name, (dp_id // 2**name) % 2)
+    guard = fill
+
+    def advance(step, guard):
+        if step == 0:
+            for g, group in enumerate(groups):
+                group.got = group.got[..., per * g : per * g + per, :, :]
+        sent = [group.send(plan[step]) for group, plan in zip(groups, plans, strict=True)]
+        *sent, guard = lax.optimization_barrier((*sent, guard))
+        for group, array in zip(groups, sent, strict=True):
+            group.receive(array)
+        return guard
 
     halves = []
-    pairs = D // 128 // 2
-    call = taken = 0
+    half_pairs = D // 128 // 2
+    taken = 0
     for half in range(2):
-        before = []
-        for place in range(pairs):
-            after = list(groups) if call else []
-            if call > 1 and taken < len(dims) - 1:
-                advance(taken)
+        before, first = [], half * half_pairs
+        for place, count in ((0, 2), (2, 1)):
+            if (half or place) and (half, place) != (1, 0):
+                guard = advance(taken, guard)
                 taken += 1
-                after = list(groups)
             before = attn_backward(
-                qkv, other, fill, attn, lse, d_attn, pairs * half + place, place, pairs, before, after
+                q, kv, other, guard, attn, lse, d_attn, first + place, count, place, half_pairs, before
             )
-            call += 1
+            got, before = lax.optimization_barrier(([group.got for group in groups], before))
+            for group, array in zip(groups, got, strict=True):
+                group.got = array
         dq, dk, dv, sent_k, sent_v = before
         halves.append((dq, dk, swap(sent_k, "seq", 1), dv, swap(sent_v, "seq", 1)))
-    for step in range(taken, len(dims)):
-        advance(step)
-    early = jnp.concatenate(groups, axis=0)
-    early_pieces = quarters(early)
-
-    d_x, g_qkv, sums_one, cols = qkv_backward(owners, slots, x, normed, d_mid, vec, halves, gathered)
+    late_keep, late_send, cols = qkv_grad(seq_of, normed, halves)
+    late_shape = (2, -1, quarter, BLK)
+    late_got = swap(late_send.reshape(late_shape), "seq", 1)
+    d_x, sums_one = qkv_backward(owners, slots, x, d_mid, vec, halves, gathered)
     d_tokens = to_positions(d_x)
-    late = g_qkv.reshape(2, 2, -1, quarter, BLK)
-    late = halve(late, 0, "seq", 1, core)
-    late = halve(late, 0, "seq", 2, chip)
-    late = jnp.concatenate([late, jnp.zeros((1, quarter, BLK), LOW)], axis=0)
-    late_at = jnp.minimum(sources, first_blocks).reshape(owner_count, slot_count)
+    while taken < len(names):
+        advance(taken, guard)
+        taken += 1
+    early = jnp.concatenate([group.total() for group in groups], axis=0)
+
+    late = Halving(late_keep.reshape(late_shape), late_got, ["x"])
+    late.receive(late.send("x"))
+    mine_from = lax.dynamic_slice_in_dim(sources, dp_id * slot_count, slot_count)
+    if 2 * first_blocks % owner_count == 0:
+        unit = (owner_count, 2 * first_blocks // owner_count, quarter // 2, BLK)
+        parts = split_sum(dp_of, late.kept.reshape(unit), late.got.reshape(unit))
+        parts = [parts[0]] + [swap(part, "dp", k) for k, part in enumerate(parts) if k]
+        total = sum(part.astype(F32) for part in parts).astype(LOW)
+        parts = [total] + [swap(total, "dp", k) for k in range(1, owner_count)]
+        piece = choose(dp_of, mine_from, parts, early)
+    else:
+        tiles = jnp.concatenate([late.total(), jnp.zeros((1, quarter, BLK), LOW)], axis=0)
+        at = sources.reshape(owner_count, slot_count)[dp_id ^ jnp.arange(owner_count)]
+        tiles = jnp.take(tiles, jnp.minimum(at, first_blocks).reshape(-1), axis=0)
+        tiles = tiles.reshape((2,) * bits + (slot_count, quarter, BLK))
+        owned = Halving(tiles, jnp.zeros_like(tiles), names[1:])
+        for bit in range(bits):
+            owned.receive(owned.send(bit))
+        piece = jnp.where((mine_from < first_blocks)[:, None, None], owned.total(), early)
     state = (master, moment_one, moment_two, left_stats, right_stats, left_basis, right_basis)
-
-    def finish(count, late, early_pieces, state):
-        sent = jnp.take(late, late_at[:, :count].reshape(-1), axis=0)
-        got = lax.all_to_all(
-            sent.reshape(owner_count, count, quarter, BLK), "dp", split_axis=0, concat_axis=0, tiled=True
-        )
-        total = jnp.sum(got.astype(F32), axis=0) + early_pieces[0][:count].astype(F32)
-        pieces = quarters(total.astype(LOW))
-        done = []
-        if count < slot_count:
-            rest = [piece[count:] for piece in early_pieces]
-            done = soap_update(seq_id.reshape(1), rest, state, count, slot_count - count, done)
-        return soap_update(seq_id.reshape(1), pieces, state, 0, count, done)
-
-    counts = [3, 4, 6] if slot_count == 6 else [slot_count]
-    most = jnp.max(jnp.sum((owners[:first_blocks, None] == jnp.arange(owner_count)[None, :]).astype(jnp.int32), axis=0))
-    if len(counts) == 1:
-        updates = finish(counts[0], late, early_pieces, state)
-    else:
-        which = sum((most > count).astype(jnp.int32) for count in counts[:-1])
-        updates = lax.switch(which, [functools.partial(finish, count) for count in counts], late, early_pieces, state)
+    piece = jnp.where((mine_from < owners.shape[0])[:, None, None], piece, jnp.zeros_like(piece))
+    updates = soap_update(seq_of, quarters(piece), state)
 
     vec_grad = jnp.concatenate(
         [

time: 808 us -> 681 us (0.84)
  blocking collectives: 57.4 us -> 0 us
  local copies, waits for them, and re-layouts: 77.3 us -> 21.8 us
  starting transfers between devices: 23.8 us -> 47.9 us
  Pallas kernels: 386 us -> 370 us
  loops' own time: 10.6 us -> 0 us
    all_to_all x1 -> x0, blocking collectives: 57.4 us -> none  [finish(): lax.all_to_all(sent.reshape(owner_count, count, quarter, BLK), 'dp', spli...]
    ppermute x28 -> x39, starting transfers between devices: 23.7 us -> 47.9 us  [swap(): return lax.ppermute(x, axis, [(i, i ^ bit) for i in range(size)])]
    pallas_call x2 -> x1, Pallas kernels: 135 us -> 115 us  [soap_update(): pl.pallas_call(soap_kernel, grid_spec=pltpu.PrefetchScalarGridSpec(num_sc...]
    all_gather x1, waiting for transfers between devices: 85.3 us -> 66.8 us  [on_device(): lax.all_gather(mine, AXES, axis=0, tiled=False)]
    ppermute x28 -> x39, waiting for transfers between devices: 103 us -> 117 us  [swap(): return lax.ppermute(x, axis, [(i, i ^ bit) for i in range(size)])]
    gather x4 -> x0, local copies, waits for them, and re-layouts: 14.3 us -> none  [the longest x3 10.8 us: on_device(): jnp.take(early, early_at[:, per * g:per * g + per].reshape(-1), axis=1)]
    squeeze x17 -> x2, local copies, waits for them, and re-layouts: 13.8 us -> 1.96 us  [on_device(): dy = jnp.concatenate([kept[1], got[1]], axis=0)]
    another operation x1 -> x0, loops' own time: 10.6 us -> none  [on_device(): lax.switch(which, [functools.partial(finish, count) for count in counts],...]
  transfers between devices with their start and end apart: 30 -> 41, of which waited for: 12 -> 13; matrix products, arithmetic and copies ran while one was open for 7% -> 6% of each run, Pallas kernels for 20% -> 14%
where the time goes in v3:
time: 681 us; the launch traced here: 682 us
  Pallas kernels  370 us (54%)
  waiting for transfers between devices  184 us (27%)
  starting transfers between devices  47.9 us (7%)
  other arithmetic  43.3 us (6%)
  local copies, waits for them, and re-layouts  21.8 us (3%)
  between operations  14.8 us (2%)
    ppermute x39, waiting for transfers between devices, swap(): return lax.ppermute(x, axis, [(i, i ^ bit) for i in range(size)])  117 us
    pallas_call x1, Pallas kernels, soap_update(): pl.pallas_call(soap_kernel, grid_spec=pltpu.PrefetchScalarGridSpec(num_sc...  115 us
    pallas_call x1, Pallas kernels, mid_layer(): pl.pallas_call(functools.partial(mid_kernel, chunk=chunk), grid_spec=pltp...  87.1 us
    pallas_call x4, Pallas kernels, attn_backward(): pl.pallas_call(kernel, grid=(count, rows // q_rows), in_specs=[q_spec, k_...  81.7 us
    all_gather x1, waiting for transfers between devices, on_device(): lax.all_gather(mine, AXES, axis=0, tiled=False)  66.8 us
    ppermute x39, starting transfers between devices, swap(): return lax.ppermute(x, axis, [(i, i ^ bit) for i in range(size)])  47.9 us
    pallas_call x1, Pallas kernels, attn_forward(): pl.pallas_call(attn_fwd_kernel, grid=(pairs, rows // q_rows), in_specs=[q...  47.2 us
    convert_element_type x17, other arithmetic, add_low(): return (a.astype(F32) + b.astype(F32)).astype(LOW)  26.8 us
  transfers between devices with their start and end apart: 41, of which 13 were waited for; matrix products, arithmetic and copies ran while one was open for 6% of the time, Pallas kernels for 14%

profile of v3, /device:TPU:0, one launch (start us, length us, event | category | flops | bytes accessed | tf_op | source)
XLA Modules:
  0.0 681.8 jit_solution(80631375308606428)
XLA Ops:
  11.5 3.0 collective-permute-start
  15.7 42.9 %collective-permute-done = bf16[2,512,768]{2,1,0:T(8,128)(2,1)S(1)} collective-permute-done((bf16[2,512,768]{2,1,0:T(8,128)(2,1)S(1)}, bf16[2,512,768]{2,1,0:T(8,128)(2,1)S(1)}, u32[]{:S(2)}, u32[]{:S(2)}) %collective-permute-start) | collective-permute-done | bytes 1572896 | tf_op jit(solution)/shard_map/ppermute | solution.py:778
  59.8 66.8 %all-gather.6.cloned.1.call-done = bf16[192,1,96,384]{3,2,1,0:T(8,128)(2,1)} async-done(((bf16[6,1,96,384]{3,2,1,0:T(8,128)(2,1)}), bf16[192,1,96,384]{3,2,1,0:T(8,128)(2,1)}) %all-gather.6.cloned.1.call-update) | async-done | bytes 14155792 | tf_op jit(solution)/shard_map/all_gather | solution.py:852
  126.5 11.3 %qkv.1 = (bf16[1024,768]{1,0:T(8,128)(2,1)S(1)}, bf16[1024,1536]{1,0:T(8,128)(2,1)}, bf16[1024,768]{1,0:T(8,128)(2,1)S(1)}) custom-call(s32[48]{0:T(128)S(1)} %copy-done.13, s32[48]{0:T(128)S(1)} %convert_reduce_fusion.slot, bf16[1024,768]{1,0:T(8,128)(2,1)S(1)} %pad_maximum_fusion.x_ref, f32[12,768]{1,0:T(8,128)S(1)} %copy-done.11, ...), custom_call_target="tpu_custom_call" | custom-call | tf_op jit(solution)/shard_map/qkv/pallas_call | solution.py:123
  142.6 2.6 pad_maximum_fusion.1.dy_ref
  145.5 47.2 %attn_fwd.1 = (bf16[1024,768]{1,0:T(8,128)(2,1)S(1)}, f32[1024,768]{1,0:T(8,128)}) custom-call(bf16[1024,768]{1,0:T(8,128)(2,1)S(1)} %get-tuple-element.112.q_ref.refs_0_, bf16[1024,1536]{1,0:T(8,128)(2,1)} %get-tuple-element.113.k1.v1.refs_1_.refs_2_, bf16[1024,1536]{1,0:T(8,128)(2,1)} %get-tuple-element.113.k1.v1.refs_1_.refs_2_, ...), custom_call_target="tpu_custom_call" | custom-call | tf_op jit(solution)/shard_map/attn_fwd/pallas_call | solution.py:188
  193.9 87.1 %mid.1 = (bf16[1024,768]{1,0:T(8,128)(2,1)}, f32[1024,768]{1,0:T(8,128)}, bf16[1024,768]{1,0:T(8,128)(2,1)}, bf16[2,8,6,96,384]{4,3,2,1,0:T(8,128)(2,1)}, bf16[2...) custom-call(s32[48]{0:T(128)} %own.5, s32[48]{0:T(128)} %copy-done.14, ...), custom_call_target="tpu_custom_call" | custom-call | tf_op jit(solution)/shard_map/mid/pallas_call | solution.py:452
  281.3 26.3 %attn_bwd.4 = (bf16[1024,384]{1,0:T(8,128)(2,1)}, bf16[1024,384]{1,0:T(8,128)(2,1)}, bf16[1024,384]{1,0:T(8,128)(2,1)}, bf16[1024,384]{1,0:T(8,128)(2,1)}, bf16[1024,384]{1,0:T(8,128)(2,1)}) custom-call(bf16[1024,768]{1,0:T(8,128)(2,1)} %copy-done.1, bf16[1024,1536]{1,0:T(8,128)(2,1)} %get-tuple-element.113.k1.v1.refs_1_.refs_2_, ...), custom_call_target="tpu_custom_call" | custom-call | tf_op jit(solution)/shard_map/attn_bwd/pallas_call | solution.py:300
  311.5 2.6 fusion.7
  320.7 26.3 %attn_bwd.6 = (bf16[1024,384]{1,0:T(8,128)(2,1)}, bf16[1024,384]{1,0:T(8,128)(2,1)}, bf16[1024,384]{1,0:T(8,128)(2,1)}, bf16[1024,384]{1,0:T(8,128)(2,1)}, bf16[1024,384]{1,0:T(8,128)(2,1)}) custom-call(bf16[1024,768]{1,0:T(8,128)(2,1)} %copy-done.1, bf16[1024,1536]{1,0:T(8,128)(2,1)} %get-tuple-element.113.k1.v1.refs_1_.refs_2_, ...), custom_call_target="tpu_custom_call" | custom-call | tf_op jit(solution)/shard_map/attn_bwd/pallas_call | solution.py:300
  347.1 14.7 %attn_bwd.5 = (bf16[1024,384]{1,0:T(8,128)(2,1)}, bf16[1024,384]{1,0:T(8,128)(2,1)}, bf16[1024,384]{1,0:T(8,128)(2,1)}, bf16[1024,384]{1,0:T(8,128)(2,1)}, bf16[1024,384]{1,0:T(8,128)(2,1)}) custom-call(bf16[1024,768]{1,0:T(8,128)(2,1)} %copy-done.1, ...), custom_call_target="tpu_custom_call", output_to_operand_aliasing={{0}: (9, {}), {1}: (10, {}), {2}: (11, {}), {3}: (12, {}), ... | custom-call | tf_op jit(solution)/shard_map/attn_bwd/pallas_call | solution.py:300
  365.7 2.5 add_convert_fusion.6
  374.6 14.4 %attn_bwd.7 = (bf16[1024,384]{1,0:T(8,128)(2,1)}, bf16[1024,384]{1,0:T(8,128)(2,1)}, bf16[1024,384]{1,0:T(8,128)(2,1)}, bf16[1024,384]{1,0:T(8,128)(2,1)}, bf16[1024,384]{1,0:T(8,128)(2,1)}) custom-call(bf16[1024,768]{1,0:T(8,128)(2,1)} %copy-done.1, ...), custom_call_target="tpu_custom_call", output_to_operand_aliasing={{0}: (9, {}), {1}: (10, {}), {2}: (11, {}), {3}: (12, {}), ... | custom-call | tf_op jit(solution)/shard_map/attn_bwd/pallas_call | solution.py:300
  395.2 10.2 %qkv_grad.1 = (bf16[2,2,6,96,384]{4,3,2,1,0:T(8,128)(2,1)}, bf16[2,2,6,96,384]{4,3,2,1,0:T(8,128)(2,1)}, f32[1,2304]{1,0:T(1,128)S(1)}) custom-call(s32[1]{0:T(128)} %bitcast.seq.seq_ref, bf16[1024,768]{1,0:T(8,128)(2,1)} %copy-done.10, bf16[1024,384]{1,0:T(8,128)(2,1)S(1)} %copy-done.6, bf16[1024,384]{1,0:T(8,128)(2,1)S(1)} %copy-done.7, ...), custom_call_target="tpu_custom_call" | custom-call | tf_op jit(solution)/shard_map/qkv_grad/pallas_call | solution.py:527
  407.7 2.5 add_convert_fusion.10
  415.1 4.5 collective-permute-done.33
  429.1 9.3 %collective-permute-done.34 = bf16[2,96,384]{2,1,0:T(8,128)(2,1)S(1)} collective-permute-done((bf16[2,96,384]{2,1,0:T(8,128)(2,1)S(1)}, bf16[2,96,384]{2,1,0:T(8,128)(2,1)S(1)}, u32[]{:S(2)}, u32[]{:S(2)}) %collective-permute-start.34) | collective-permute-done | bytes 147488 | tf_op jit(solution)/shard_map/ppermute | solution.py:778
  439.9 5.6 collective-permute-done.16
  447.9 16.0 %qkv_bwd.1 = (bf16[1024,768]{1,0:T(8,128)(2,1)}, f32[8,768]{1,0:T(8,128)}) custom-call(s32[48]{0:T(128)} %own.5, s32[48]{0:T(128)} %copy-done.14, bf16[1024,768]{1,0:T(8,128)(2,1)} %copy-done.2, f32[1024,768]{1,0:T(8,128)} %get-tuple-element.116.dmid_ref, f32[12,768]{1,0:T(8,128)} %vec_ref.5, bf16[1024,384]{1,0:T(8,128)(2,1)} %get-tuple-element.143.refs_0_, ...), custom_call_target="tpu_custom_call" | custom-call | tf_op jit(solution)/shard_map/qkv_bwd/pallas_call | solution.py:570
  468.8 2.4 collective-permute-start.21
  472.7 2.4 collective-permute-start.23
  476.1 9.6 %collective-permute-done.20 = bf16[3,48,384]{2,1,0:T(8,128)(2,1)S(1)} collective-permute-done((bf16[3,48,384]{2,1,0:T(8,128)(2,1)S(1)}, bf16[3,48,384]{2,1,0:T(8,128)(2,1)S(1)}, u32[]{:S(2)}, u32[]{:S(2)}) %collective-permute-start.20) | collective-permute-done | bytes 110624 | tf_op jit(solution)/shard_map/ppermute | solution.py:778
  485.7 3.0 collective-permute-done.21
  489.9 5.6 collective-permute-start.25
  502.0 2.5 collective-permute-start.30
  506.1 8.1 %collective-permute-done.27.refs_4_ = bf16[3,48,384]{2,1,0:T(8,128)(2,1)S(1)} collective-permute-done((bf16[3,48,384]{2,1,0:T(8,128)(2,1)S(1)}, bf16[3,48,384]{2,1,0:T(8,128)(2,1)S(1)}, u32[]{:S(2)}, u32[]{:S(2)}) %collective-permute-start.27) | collective-permute-done | bytes 110624 | tf_op jit(solution)/shard_map/ppermute | solution.py:778
  514.3 2.7 collective-permute-done.28.refs_5_
  521.1 16.5 %collective-permute-done.37.g1 = bf16[6,96,384]{2,1,0:T(8,128)(2,1)S(1)} collective-permute-done((bf16[6,96,384]{2,1,0:T(8,128)(2,1)S(1)}, bf16[6,96,384]{2,1,0:T(8,128)(2,1)S(1)}, u32[]{:S(2)}, u32[]{:S(2)}) %collective-permute-start.37) | collective-permute-done | bytes 442400 | tf_op jit(solution)/shard_map/ppermute | solution.py:778
  538.7 2.8 maximum_select_fusion
  541.4 11.9 %collective-permute-done.14 = bf16[512,768]{1,0:T(8,128)(2,1)} collective-permute-done((bf16[512,768]{1,0:T(8,128)(2,1)}, bf16[512,768]{1,0:T(8,128)(2,1)}, u32[]{:S(2)}, u32[]{:S(2)}) %collective-permute-start.14) | collective-permute-done | bytes 786464 | tf_op jit(solution)/shard_map/ppermute | solution.py:778
  553.4 2.8 maximum_select_fusion.1
  559.4 115.3 %soap.1 = (f32[6,384,384]{2,1,0:T(8,128)}, f32[6,384,384]{2,1,0:T(8,128)}, f32[6,384,384]{2,1,0:T(8,128)}, f32[6,384,384]{2,1,0:T(8,128)}, f32[6,384,384]{2,1,0:...) custom-call(s32[1]{0:T(128)} %bitcast.seq.seq_ref, ...), custom_call_target="tpu_custom_call" | custom-call | tf_op jit(solution)/shard_map/soap/pallas_call | solution.py:691
  (196 shorter events, 85.4 us)
Async XLA Ops:
  7.2 119.4 %all-gather.6.cloned.1.call-start = ((), (), s32[]{:S(2)}) async-start(), calls=%async_computation | async-start | bytes 14598144 | tf_op jit(solution)/shard_map/all_gather | solution.py:852
  9.2 546.9 %all-gather.8.cloned.1.call-start = ((), (), s32[]{:S(2)}) async-start(), calls=%async_computation.1 | async-start | bytes 1622016 | tf_op jit(solution)/shard_map/all_gather | solution.py:970
  11.5 47.2 %collective-permute-start = (bf16[2,512,768]{2,1,0:T(8,128)(2,1)S(1)}, bf16[2,512,768]{2,1,0:T(8,128)(2,1)S(1)}, u32[]{:S(2)}, u32[]{:S(2)}) collective-permute-start(bf16[2,512,768]{2,1,0:T(8,128)(2,1)S(1)} %get-tuple-element.229), channel_id=1, source_target_pairs={{0,2},{1,3},{2,0},{3,1},{4,6},{5,7},{6,4},{7,5},{8,10},{9,11},{10,... | collective-permute-start | bytes 4718600 | tf_op jit(solution)/shard_map/ppermute | solution.py:778
  281.0 30.5 %collective-permute-start.3 = (bf16[2,8,6,96,384]{4,3,2,1,0:T(8,128)(2,1)}, bf16[2,8,6,96,384]{4,3,2,1,0:T(8,128)(2,1)S(1)}, u32[]{:S(2)}, u32[]{:S(2)}) collective-permute-start(bf16[2,8,6,96,384]{4,3,2,1,0:T(8,128)(2,1)} %get-tuple-element.118), channel_id=1, source_target_pairs={{0,1},{1,0},{2,3},{3,2},{4,5},{5,4},{6,7},{7,6},{8,9},{9,8},{10,11... | collective-permute-start | bytes 21233672 | tf_op jit(solution)/shard_map/ppermute | solution.py:778
  318.1 45.2 %collective-permute-start.4 = (bf16[2,2,2,2,96,384]{5,4,3,1,0,2:T(8,128)(2,1)}, bf16[2,2,2,2,96,384]{5,4,3,1,0,2:T(8,128)(2,1)}, u32[]{:S(2)}, u32[]{:S(2)}) collective-permute-start(bf16[2,2,2,2,96,384]{5,4,3,1,0,2:T(8,128)(2,1)} %get-tuple-element.129), channel_id=1, source_target_pairs={{0,2},{1,3},{2,0},{3,1},{4,6},{5,7},{6,4},{7,5},{8,10},{9,11},{10,... | collective-permute-start | bytes 3538952 | tf_op jit(solution)/shard_map/ppermute | solution.py:778
  319.5 43.8 %collective-permute-start.5 = (bf16[2,2,2,2,96,384]{5,4,3,1,2,0:T(8,128)(2,1)}, bf16[2,2,2,2,96,384]{5,4,3,1,2,0:T(8,128)(2,1)}, u32[]{:S(2)}, u32[]{:S(2)}) collective-permute-start(bf16[2,2,2,2,96,384]{5,4,3,1,2,0:T(8,128)(2,1)} %get-tuple-element.130), channel_id=1, source_target_pairs={{0,4},{4,0},{8,12},{12,8},{16,20},{20,16},{24,28},{28,24},{1,5},{5... | collective-permute-start | bytes 3538952 | tf_op jit(solution)/shard_map/ppermute | solution.py:778
  320.1 43.2 %collective-permute-start.6 = (bf16[2,2,2,2,96,384]{5,4,3,2,1,0:T(8,128)(2,1)}, bf16[2,2,2,2,96,384]{5,4,3,2,1,0:T(8,128)(2,1)}, u32[]{:S(2)}, u32[]{:S(2)}) collective-permute-start(bf16[2,2,2,2,96,384]{5,4,3,2,1,0:T(8,128)(2,1)} %fusion.7), channel_id=1, source_target_pairs={{0,8},{4,12},{8,0},{12,4},{16,24},{20,28},{24,16},{28,20},{1,9},{5... | collective-permute-start | bytes 3538952 | tf_op jit(solution)/shard_map/ppermute | solution.py:778
  370.6 18.4 %collective-permute-start.10 = (bf16[2,2,2,96,384]{4,3,2,1,0:T(8,128)(2,1)S(1)}, bf16[2,2,2,96,384]{4,3,2,1,0:T(8,128)(2,1)}, u32[]{:S(2)}, u32[]{:S(2)}) collective-permute-start(bf16[2,2,2,96,384]{4,3,2,1,0:T(8,128)(2,1)S(1)} %get-tuple-element.160), channel_id=1, source_target_pairs={{0,8},{4,12},{8,0},{12,4},{16,24},{20,28},{24,16},{28,20},{1,9},{5... | collective-permute-start | bytes 1769480 | tf_op jit(solution)/shard_map/ppermute | solution.py:778
  372.1 17.0 %collective-permute-start.11 = (bf16[2,2,2,96,384]{4,3,2,1,0:T(8,128)(2,1)S(1)}, bf16[2,2,2,96,384]{4,3,2,1,0:T(8,128)(2,1)}, u32[]{:S(2)}, u32[]{:S(2)}) collective-permute-start(bf16[2,2,2,96,384]{4,3,2,1,0:T(8,128)(2,1)S(1)} %get-tuple-element.161), channel_id=1, source_target_pairs={{0,2},{1,3},{2,0},{3,1},{4,6},{5,7},{6,4},{7,5},{8,10},{9,11},{10,... | collective-permute-start | bytes 1769480 | tf_op jit(solution)/shard_map/ppermute | solution.py:778
  373.5 15.6 %collective-permute-start.9 = (bf16[2,2,2,96,384]{4,3,2,1,0:T(8,128)(2,1)S(1)}, bf16[2,2,2,96,384]{4,3,2,1,0:T(8,128)(2,1)}, u32[]{:S(2)}, u32[]{:S(2)}) collective-permute-start(bf16[2,2,2,96,384]{4,3,2,1,0:T(8,128)(2,1)S(1)} %get-tuple-element.159), channel_id=1, source_target_pairs={{0,4},{4,0},{8,12},{12,8},{16,20},{20,16},{24,28},{28,24},{1,5},{5... | collective-permute-start | bytes 1769480 | tf_op jit(solution)/shard_map/ppermute | solution.py:778
  374.1 15.8 %collective-permute-start.7 = (bf16[1024,384]{1,0:T(8,128)(2,1)}, bf16[1024,384]{1,0:T(8,128)(2,1)S(1)}, u32[]{:S(2)}, u32[]{:S(2)}) collective-permute-start(bf16[1024,384]{1,0:T(8,128)(2,1)} %get-tuple-element.145), channel_id=1, source_target_pairs={{0,1},{1,0},{2,3},{3,2},{4,5},{5,4},{6,7},{7,6},{8,9},{9,8},{10,11... | collective-permute-start | bytes 2359304 | tf_op jit(solution)/shard_map/ppermute | solution.py:778
  374.1 15.8 %collective-permute-start.8 = (bf16[1024,384]{1,0:T(8,128)(2,1)}, bf16[1024,384]{1,0:T(8,128)(2,1)}, u32[]{:S(2)}, u32[]{:S(2)}) collective-permute-start(bf16[1024,384]{1,0:T(8,128)(2,1)} %get-tuple-element.147), channel_id=1, source_target_pairs={{0,1},{1,0},{2,3},{3,2},{4,5},{5,4},{6,7},{7,6},{8,9},{9,8},{10,11... | collective-permute-start | bytes 2359304 | tf_op jit(solution)/shard_map/ppermute | solution.py:778
  405.5 17.6 %collective-permute-start.15 = (bf16[2,12,96,384]{3,2,1,0:T(8,128)(2,1)}, bf16[2,12,96,384]{3,2,1,0:T(8,128)(2,1)}, u32[]{:S(2)}, u32[]{:S(2)}) collective-permute-start(bf16[2,12,96,384]{3,2,1,0:T(8,128)(2,1)} %bitcast.188), channel_id=1, source_target_pairs={{0,1},{1,0},{2,3},{3,2},{4,5},{5,4},{6,7},{7,6},{8,9},{9,8},{10,11... | collective-permute-start | bytes 5308424 | tf_op jit(solution)/shard_map/ppermute | solution.py:778
  424.5 21.1 %collective-permute-start.16 = (bf16[12,96,384]{2,1,0:T(8,128)(2,1)S(1)}, bf16[12,96,384]{2,1,0:T(8,128)(2,1)S(1)}, u32[]{:S(2)}, u32[]{:S(2)}) collective-permute-start(bf16[12,96,384]{2,1,0:T(8,128)(2,1)S(1)} %fusion), channel_id=1, source_target_pairs={{0,2},{1,3},{2,0},{3,1},{4,6},{5,7},{6,4},{7,5},{8,10},{9,11},{10,... | collective-permute-start | bytes 2654216 | tf_op jit(solution)/shard_map/ppermute | solution.py:778
  426.0 12.3 %collective-permute-start.34 = (bf16[2,96,384]{2,1,0:T(8,128)(2,1)S(1)}, bf16[2,96,384]{2,1,0:T(8,128)(2,1)S(1)}, u32[]{:S(2)}, u32[]{:S(2)}) collective-permute-start(bf16[2,96,384]{2,1,0:T(8,128)(2,1)S(1)} %fusion.32), channel_id=1, source_target_pairs={{0,16},{4,20},{8,24},{12,28},{16,0},{20,4},{24,8},{28,12},{1,17},{... | collective-permute-start | bytes 442376 | tf_op jit(solution)/shard_map/ppermute | solution.py:778
  427.6 41.2 %collective-permute-start.35 = (bf16[2,96,384]{2,1,0:T(8,128)(2,1)}, bf16[2,96,384]{2,1,0:T(8,128)(2,1)S(1)}, u32[]{:S(2)}, u32[]{:S(2)}) collective-permute-start(bf16[2,96,384]{2,1,0:T(8,128)(2,1)} %fusion.33), channel_id=1, source_target_pairs={{0,16},{4,20},{8,24},{12,28},{16,0},{20,4},{24,8},{28,12},{1,17},{... | collective-permute-start | bytes 442376 | tf_op jit(solution)/shard_map/ppermute | solution.py:778
  445.8 25.4 %collective-permute-start.17 = (bf16[3,48,384]{2,1,0:T(8,128)(2,1)S(1)}, bf16[3,48,384]{2,1,0:T(8,128)(2,1)S(1)}, u32[]{:S(2)}, u32[]{:S(2)}) collective-permute-start(bf16[3,48,384]{2,1,0:T(8,128)(2,1)S(1)} %get-tuple-element.183), channel_id=1, source_target_pairs={{0,4},{4,0},{8,12},{12,8},{16,20},{20,16},{24,28},{28,24},{1,5},{5... | collective-permute-start | bytes 331784 | tf_op jit(solution)/shard_map/ppermute | solution.py:778
  447.3 25.4 %collective-permute-start.18 = (bf16[3,48,384]{2,1,0:T(8,128)(2,1)S(1)}, bf16[3,48,384]{2,1,0:T(8,128)(2,1)S(1)}, u32[]{:S(2)}, u32[]{:S(2)}) collective-permute-start(bf16[3,48,384]{2,1,0:T(8,128)(2,1)S(1)} %get-tuple-element.184), channel_id=1, source_target_pairs={{0,8},{4,12},{8,0},{12,4},{16,24},{20,28},{24,16},{28,20},{1,9},{5... | collective-permute-start | bytes 331784 | tf_op jit(solution)/shard_map/ppermute | solution.py:778
  467.4 18.3 %collective-permute-start.20 = (bf16[3,48,384]{2,1,0:T(8,128)(2,1)S(1)}, bf16[3,48,384]{2,1,0:T(8,128)(2,1)S(1)}, u32[]{:S(2)}, u32[]{:S(2)}) collective-permute-start(bf16[3,48,384]{2,1,0:T(8,128)(2,1)S(1)} %get-tuple-element.186), channel_id=1, source_target_pairs={{0,16},{4,20},{8,24},{12,28},{16,0},{20,4},{24,8},{28,12},{1,17},{... | collective-permute-start | bytes 331784 | tf_op jit(solution)/shard_map/ppermute | solution.py:778
  468.8 19.8 %collective-permute-start.21 = (bf16[3,48,384]{2,1,0:T(8,128)(2,1)S(1)}, bf16[3,48,384]{2,1,0:T(8,128)(2,1)S(1)}, u32[]{:S(2)}, u32[]{:S(2)}) collective-permute-start(bf16[3,48,384]{2,1,0:T(8,128)(2,1)S(1)} %get-tuple-element.187), channel_id=1, source_target_pairs={{0,20},{4,16},{8,28},{12,24},{16,4},{20,0},{24,12},{28,8},{1,21},{... | collective-permute-start | bytes 331784 | tf_op jit(solution)/shard_map/ppermute | solution.py:778
  471.2 17.4 %collective-permute-start.22 = (bf16[3,48,384]{2,1,0:T(8,128)(2,1)S(1)}, bf16[3,48,384]{2,1,0:T(8,128)(2,1)S(1)}, u32[]{:S(2)}, u32[]{:S(2)}) collective-permute-start(bf16[3,48,384]{2,1,0:T(8,128)(2,1)S(1)} %get-tuple-element.188), channel_id=1, source_target_pairs={{0,24},{4,28},{8,16},{12,20},{16,8},{20,12},{24,0},{28,4},{1,25},{... | collective-permute-start | bytes 331784 | tf_op jit(solution)/shard_map/ppermute | solution.py:778
  472.7 16.0 %collective-permute-start.23 = (bf16[3,48,384]{2,1,0:T(8,128)(2,1)S(1)}, bf16[3,48,384]{2,1,0:T(8,128)(2,1)S(1)}, u32[]{:S(2)}, u32[]{:S(2)}) collective-permute-start(bf16[3,48,384]{2,1,0:T(8,128)(2,1)S(1)} %get-tuple-element.189), channel_id=1, source_target_pairs={{0,28},{4,24},{8,20},{12,16},{16,12},{20,8},{24,4},{28,0},{1,29},{... | collective-permute-start | bytes 331784 | tf_op jit(solution)/shard_map/ppermute | solution.py:778
  476.0 19.5 %collective-permute-start.36 = (bf16[2,96,384]{2,1,0:T(8,128)(2,1)S(1)}, bf16[2,96,384]{2,1,0:T(8,128)(2,1)S(1)}, u32[]{:S(2)}, u32[]{:S(2)}) collective-permute-start(bf16[2,96,384]{2,1,0:T(8,128)(2,1)S(1)} %copy-done.24), channel_id=1, source_target_pairs={{0,16},{4,20},{8,24},{12,28},{16,0},{20,4},{24,8},{28,12},{1,17},{... | collective-permute-start | bytes 442376 | tf_op jit(solution)/shard_map/ppermute | solution.py:778
  489.9 12.1 %collective-permute-start.25 = (bf16[3,48,384]{2,1,0:T(8,128)(2,1)S(1)}, bf16[3,48,384]{2,1,0:T(8,128)(2,1)S(1)}, u32[]{:S(2)}, u32[]{:S(2)}) collective-permute-start(bf16[3,48,384]{2,1,0:T(8,128)(2,1)S(1)} %add_convert_fusion.14.refs_0_), channel_id=1, source_target_pairs={{0,8},{4,12},{8,0},{12,4},{16,24},{20,28},{24,16},{28,20},{1,9},{5... | collective-permute-start | bytes 331784 | tf_op jit(solution)/shard_map/ppermute | solution.py:778
  496.9 17.4 %collective-permute-start.27 = (bf16[3,48,384]{2,1,0:T(8,128)(2,1)S(1)}, bf16[3,48,384]{2,1,0:T(8,128)(2,1)S(1)}, u32[]{:S(2)}, u32[]{:S(2)}) collective-permute-start(bf16[3,48,384]{2,1,0:T(8,128)(2,1)S(1)} %add_convert_fusion.14.refs_0_), channel_id=1, source_target_pairs={{0,16},{4,20},{8,24},{12,28},{16,0},{20,4},{24,8},{28,12},{1,17},{... | collective-permute-start | bytes 331784 | tf_op jit(solution)/shard_map/ppermute | solution.py:778
  499.2 17.8 %collective-permute-start.28 = (bf16[3,48,384]{2,1,0:T(8,128)(2,1)S(1)}, bf16[3,48,384]{2,1,0:T(8,128)(2,1)S(1)}, u32[]{:S(2)}, u32[]{:S(2)}) collective-permute-start(bf16[3,48,384]{2,1,0:T(8,128)(2,1)S(1)} %add_convert_fusion.14.refs_0_), channel_id=1, source_target_pairs={{0,20},{4,16},{8,28},{12,24},{16,4},{20,0},{24,12},{28,8},{1,21},{... | collective-permute-start | bytes 331784 | tf_op jit(solution)/shard_map/ppermute | solution.py:778
  500.4 16.6 %collective-permute-start.29 = (bf16[3,48,384]{2,1,0:T(8,128)(2,1)S(1)}, bf16[3,48,384]{2,1,0:T(8,128)(2,1)S(1)}, u32[]{:S(2)}, u32[]{:S(2)}) collective-permute-start(bf16[3,48,384]{2,1,0:T(8,128)(2,1)S(1)} %add_convert_fusion.14.refs_0_), channel_id=1, source_target_pairs={{0,24},{4,28},{8,16},{12,20},{16,8},{20,12},{24,0},{28,4},{1,25},{... | collective-permute-start | bytes 331784 | tf_op jit(solution)/shard_map/ppermute | solution.py:778
  502.0 15.0 %collective-permute-start.30 = (bf16[3,48,384]{2,1,0:T(8,128)(2,1)S(1)}, bf16[3,48,384]{2,1,0:T(8,128)(2,1)S(1)}, u32[]{:S(2)}, u32[]{:S(2)}) collective-permute-start(bf16[3,48,384]{2,1,0:T(8,128)(2,1)S(1)} %add_convert_fusion.14.refs_0_), channel_id=1, source_target_pairs={{0,28},{4,24},{8,20},{12,16},{16,12},{20,8},{24,4},{28,0},{1,29},{... | collective-permute-start | bytes 331784 | tf_op jit(solution)/shard_map/ppermute | solution.py:778
  504.6 34.1 %collective-permute-start.2 = (bf16[512,768]{1,0:T(8,128)(2,1)}, bf16[512,768]{1,0:T(8,128)(2,1)}, u32[]{:S(2)}, u32[]{:S(2)}) collective-permute-start(bf16[512,768]{1,0:T(8,128)(2,1)} %get-tuple-element.241), channel_id=1, source_target_pairs={{0,2},{1,3},{2,0},{3,1},{4,6},{5,7},{6,4},{7,5},{8,10},{9,11},{10,... | collective-permute-start | bytes 2359304 | tf_op jit(solution)/shard_map/ppermute | solution.py:778
  517.9 19.7 %collective-permute-start.37 = (bf16[6,96,384]{2,1,0:T(8,128)(2,1)S(1)}, bf16[6,96,384]{2,1,0:T(8,128)(2,1)S(1)}, u32[]{:S(2)}, u32[]{:S(2)}) collective-permute-start(bf16[6,96,384]{2,1,0:T(8,128)(2,1)S(1)} %broadcast_select_fusion.g0), channel_id=1, source_target_pairs={{0,2},{1,3},{2,0},{3,1},{4,6},{5,7},{6,4},{7,5},{8,10},{9,11},{10,... | collective-permute-start | bytes 1327112 | tf_op jit(solution)/shard_map/ppermute | solution.py:778
  520.3 33.0 %collective-permute-start.14 = (bf16[512,768]{1,0:T(8,128)(2,1)}, bf16[512,768]{1,0:T(8,128)(2,1)}, u32[]{:S(2)}, u32[]{:S(2)}) collective-permute-start(bf16[512,768]{1,0:T(8,128)(2,1)} %get-tuple-element.239), channel_id=1, source_target_pairs={{0,2},{1,3},{2,0},{3,1},{4,6},{5,7},{6,4},{7,5},{8,10},{9,11},{10,... | collective-permute-start | bytes 2359304 | tf_op jit(solution)/shard_map/ppermute | solution.py:778
  538.7 19.7 %collective-permute-start.38 = (bf16[2,6,96,384]{3,2,1,0:T(8,128)(2,1)}, bf16[2,6,96,384]{3,2,1,0:T(8,128)(2,1)S(1)}, u32[]{:S(2)}, u32[]{:S(2)}) collective-permute-start(bf16[2,6,96,384]{3,2,1,0:T(8,128)(2,1)} %pad_maximum_fusion.2), channel_id=1, source_target_pairs={{0,1},{1,0},{2,3},{3,2},{4,5},{5,4},{6,7},{7,6},{8,9},{9,8},{10,11... | collective-permute-start | bytes 2654216 | tf_op jit(solution)/shard_map/ppermute | solution.py:778
  (41 other events, 570.7 us)
Sparse Core Ops, SparseCore 0:
  11.5 114.9 all-gather.5
  466.0 70.6 all-gather.7

commit v4 on v3

--- a/solution.py
+++ b/solution.py
@@ -12,7 +12,6 @@
 BLK = 384
 STEP = 10
 
-HIGHEST = lax.Precision.HIGHEST
 NORM_EPS = 1e-06
 NEG_FILL = -1000000000.0
 BETA_ONE = 0.9
@@ -41,10 +40,8 @@
 )
 
 
-def dot(a, b, ca, cb, precision=None):
-    return lax.dot_general(
-        a, b, (((ca,), (cb,)), ((), ())), precision=precision, preferred_element_type=F32
-    )
+def dot(a, b, ca, cb):
+    return lax.dot_general(a, b, (((ca,), (cb,)), ((), ())), preferred_element_type=F32)
 
 
 def lanes(shape):
@@ -100,22 +97,32 @@
     return seq ^ (2 * rel_x + rel_core)
 
 
-def qkv_kernel(own, slot, x_ref, vec_ref, bias_ref, t0, t1, q_ref, kv_ref, a_ref):
+def square(tiles, held):
+    for i in range(2):
+        for j in range(2):
+            held[i * BLK : i * BLK + BLK, j * BLK : j * BLK + BLK] = tile(tiles[2 * i + j])
+    return held[...]
+
+
+def qkv_kernel(own, slot, x_ref, vec_ref, bias_ref, t00, t01, t10, t11, q_ref, kv_ref, a_ref, held):
     @pl.when(pl.program_id(0) == 0)
     def _():
         hat, _ = norm_parts(x_ref[...].astype(F32))
         a_ref[...] = (hat * vec_ref[0:1, :] + vec_ref[1:2, :]).astype(LOW)
 
-    total = dot(a_ref[:, :BLK], tile(t0), 1, 0) + dot(a_ref[:, BLK:], tile(t1), 1, 0)
-    low = (total + bias_ref[...]).astype(LOW)
-
-    @pl.when(pl.program_id(0) < 2)
+    low = (dot(a_ref[...], square((t00, t01, t10, t11), held), 1, 0) + bias_ref[...]).astype(LOW)
+
+    @pl.when(pl.program_id(0) == 0)
     def _():
         q_ref[...] = low
 
-    @pl.when(pl.program_id(0) >= 2)
+    @pl.when(pl.program_id(0) > 0)
     def _():
         kv_ref[...] = low
+
+
+def qkv_tiles():
+    return [tile_spec(lambda i, n=n: 6 * (n // 2) + 2 * i + n % 2) for n in range(4)]
 
 
 def qkv_forward(own, slot, x, vec, bias, gathered):
@@ -124,19 +131,19 @@
         qkv_kernel,
         grid_spec=pltpu.PrefetchScalarGridSpec(
             num_scalar_prefetch=2,
-            grid=(6,),
+            grid=(3,),
             in_specs=[
                 full_spec((rows, D)),
                 full_spec(vec.shape),
-                pl.BlockSpec((1, BLK), lambda i, own, slot: (0, i)),
-                tile_spec(lambda i: i),
-                tile_spec(lambda i: 6 + i),
-            ],
+                pl.BlockSpec((1, D), lambda i, own, slot: (0, i)),
+            ]
+            + qkv_tiles(),
             out_specs=[
-                pl.BlockSpec((rows, BLK), lambda i, own, slot: (0, jnp.minimum(i, 1))),
-                pl.BlockSpec((rows, BLK), lambda i, own, slot: (0, jnp.maximum(i - 2, 0))),
+                full_spec((rows, D)),
+                pl.BlockSpec((rows, D), lambda i, own, slot: (0, jnp.maximum(i - 1, 0))),
                 full_spec((rows, D)),
             ],
+            scratch_shapes=[pltpu.VMEM((D, D), LOW)],
         ),
         out_shape=[
             jax.ShapeDtypeStruct((rows, D), LOW),
@@ -145,7 +152,7 @@
         ],
         compiler_params=params(48),
         name="qkv",
-    )(own, slot, x, vec, bias, gathered, gathered)
+    )(own, slot, x, vec, bias, *([gathered] * 4))
 
 
 def attn_fwd_kernel(q_ref, k1, v1, k2, v2, bias_ref, o_ref, lse_ref, ka, kb, va, vb):
@@ -212,6 +219,22 @@
     rest = x - high
     mid = rest.astype(LOW).astype(F32)
     return high, mid, rest - mid
+
+
+def low_parts(x, count):
+    found = []
+    for _ in range(count):
+        part = x.astype(LOW)
+        found.append(part)
+        x = x - part.astype(F32)
+    return found
+
+
+def dot_parts(a, b, ca, cb, order):
+    pairs = [(i, j) for i in range(len(a)) for j in range(len(b)) if i + j < order]
+    a = jnp.concatenate([a[i] for i, _ in pairs], axis=ca)
+    b = jnp.concatenate([b[j] for _, j in pairs], axis=cb)
+    return dot(a, b, ca, cb)
 
 
 def with_spare(x, spare, value, one, first):
@@ -317,10 +340,12 @@
 
 
 def mid_kernel(
-    own, slot, rel, seq, x_ref, attn_ref, dy_ref, vec_ref, b1_ref, o00, o01, o10, o11, u0, u1, w0, w1,
-    res_ref, dmid_ref, dattn_ref, keep, send, sums_ref, gb1_ref,
-    mid, a2, acc, da2, stage, sems, *, chunk,
-):
+    own, slot, rel, seq, x_ref, attn_ref, dy_ref, vec_ref, b1_ref, o00, o01, o10, o11, *refs, chunk):
+    ups, downs = refs[:4], refs[4:8]
+    (
+        res_ref, dmid_ref, dattn_ref, keep, send, sums_ref, gb1_ref,
+        mid, a2, acc, da2, up_s, down_s, stage, sems,
+    ) = refs[8:]
     step = pl.program_id(0)
     last = pl.num_programs(0) - 1
     quarter = BLK // 4
@@ -345,21 +370,18 @@
         for copy in copies(buf, i, block):
             copy.start()
 
-    def settle(buf):
-        for i in range(4):
+    def settle(buf, count=8):
+        for i in range(count):
             for copy in copies(buf, i, 0):
                 copy.wait()
 
     @pl.when(step == 0)
     def _():
-        left, right = attn_ref[:, :BLK], attn_ref[:, BLK:]
-        for j, (top, bottom) in enumerate(((o00, o10), (o01, o11))):
-            c = slice(j * BLK, j * BLK + BLK)
-            mid[:, c] = (
-                x_ref[:, c].astype(F32)
-                + (dot(left, tile(top), 1, 0) + dot(right, tile(bottom), 1, 0))
-                + vec_ref[6:7, c]
-            )
+        mid[...] = (
+            x_ref[...].astype(F32)
+            + dot(attn_ref[...], square((o00, o01, o10, o11), up_s), 1, 0)
+            + vec_ref[6:7, :]
+        )
         hat, _ = norm_parts(mid[...])
         a2[...] = (hat * vec_ref[2:3, :] + vec_ref[3:4, :]).astype(LOW)
         acc[...] = jnp.zeros_like(acc)
@@ -368,20 +390,16 @@
     @pl.when((step > 0) & (step < last))
     def _():
         rows = a2.shape[0]
-        up0, up1, down0, down1 = tile(u0), tile(u1), tile(w0), tile(w1)
-        bias_grad = jnp.zeros((1, BLK), F32)
+        up, down = square(ups, up_s), square(downs, down_s)
+        bias_grad = jnp.zeros((1, D), F32)
         acts, d_hids = [], []
         for c in range(rows // chunk):
             r = slice(c * chunk, c * chunk + chunk)
-            hidden = dot(a2[r, :BLK], up0, 1, 0) + dot(a2[r, BLK:], up1, 1, 0) + b1_ref[...]
-            act, slope = gelu_pair(hidden)
+            act, slope = gelu_pair(dot(a2[r, :], up, 1, 0) + b1_ref[...])
             act = act.astype(LOW)
-            back = dot(dy_ref[r, :BLK], down0, 1, 1) + dot(dy_ref[r, BLK:], down1, 1, 1)
-            d_hid = (back * slope).astype(LOW)
-            acc[r, :BLK] += dot(act, down0, 1, 0)
-            acc[r, BLK:] += dot(act, down1, 1, 0)
-            da2[r, :BLK] += dot(d_hid, up0, 1, 1)
-            da2[r, BLK:] += dot(d_hid, up1, 1, 1)
+            d_hid = (dot(dy_ref[r, :], down, 1, 1) * slope).astype(LOW)
+            acc[r, :] += dot(act, down, 1, 0)
+            da2[r, :] += dot(d_hid, up, 1, 1)
             bias_grad = bias_grad + jnp.sum(d_hid.astype(F32), axis=0, keepdims=True)
             acts.append(act)
             d_hids.append(d_hid)
@@ -394,10 +412,14 @@
         def _():
             settle(buf)
 
-        for j in range(2):
-            c = slice(j * BLK, j * BLK + BLK)
-            put(buf, j, 16 + 8 * j + step - 1, dot(a2[:, c], d_hid, 0, 0))
-            put(buf, 2 + j, 32 + 2 * (step - 1) + j, dot(act, dy_ref[:, c], 0, 0))
+        for i in range(2):
+            c = slice(i * BLK, i * BLK + BLK)
+            up_grad = dot(a2[:, c], d_hid, 0, 0)
+            down_grad = dot(act[:, c], dy_ref[...], 0, 0)
+            for j in range(2):
+                k = slice(j * BLK, j * BLK + BLK)
+                put(buf, 2 * i + j, 16 + 8 * i + 2 * (step - 1) + j, up_grad[:, k])
+                put(buf, 4 + 2 * i + j, 32 + 4 * (step - 1) + 2 * i + j, down_grad[:, k])
 
     @pl.when(step == last)
     def _():
@@ -413,23 +435,19 @@
         sums_ref[2:3, :] = jnp.sum(d_proj.astype(F32), axis=0, keepdims=True)
         sums_ref[3:4, :] = jnp.sum(dy, axis=0, keepdims=True)
         sums_ref[4:8, :] = jnp.zeros((4, D), F32)
-        for i, (first, second) in enumerate(((o00, o01), (o10, o11))):
-            c = slice(i * BLK, i * BLK + BLK)
-            dattn_ref[:, c] = (
-                dot(d_proj[:, :BLK], tile(first), 1, 1) + dot(d_proj[:, BLK:], tile(second), 1, 1)
-            ).astype(LOW)
+        dattn_ref[...] = dot(d_proj, square((o00, o01, o10, o11), up_s), 1, 1).astype(LOW)
         settle(0)
         for i in range(2):
+            out_grad = dot(attn_ref[:, i * BLK : i * BLK + BLK], d_proj, 0, 0)
             for j in range(2):
-                c, k = slice(i * BLK, i * BLK + BLK), slice(j * BLK, j * BLK + BLK)
-                put(0, 2 * i + j, 12 + 2 * i + j, dot(attn_ref[:, c], d_proj[:, k], 0, 0))
+                put(0, 2 * i + j, 12 + 2 * i + j, out_grad[:, j * BLK : j * BLK + BLK])
         settle(1)
-        settle(0)
-
-
-def mid_layer(own, slot, rel, seq, x, attn, dy, vec, b1, gathered, chunk=256):
+        settle(0, 4)
+
+
+def mid_layer(own, slot, rel, seq, x, attn, dy, vec, b1, gathered, chunk=512):
     rows = x.shape[0]
-    wide = FF // BLK
+    wide = FF // D
     quarter = BLK // 4
     owners, slots = gathered.shape[0], gathered.shape[2]
 
@@ -446,7 +464,7 @@
         )
 
     row_spec = full((rows, D))
-    strip = pl.BlockSpec((1, BLK), lambda i, own, slot, rel, seq: (0, part(i)))
+    strip = pl.BlockSpec((1, D), lambda i, own, slot, rel, seq: (0, part(i)))
     anywhere = pl.BlockSpec(memory_space=pl.ANY)
     place_shape = jax.ShapeDtypeStruct((2, owners, slots, quarter, BLK), LOW)
     return pl.pallas_call(
@@ -456,20 +474,18 @@
             grid=(wide + 2,),
             in_specs=[row_spec, row_spec, row_spec, full(vec.shape), strip]
             + [tile_at(lambda i, b=b: b) for b in (12, 13, 14, 15)]
-            + [
-                tile_at(lambda i: 16 + part(i)),
-                tile_at(lambda i: 24 + part(i)),
-                tile_at(lambda i: 32 + 2 * part(i)),
-                tile_at(lambda i: 33 + 2 * part(i)),
-            ],
+            + [tile_at(lambda i, n=n: 16 + 8 * (n // 2) + 2 * part(i) + n % 2) for n in range(4)]
+            + [tile_at(lambda i, n=n: 32 + 4 * part(i) + n) for n in range(4)],
             out_specs=[row_spec, row_spec, row_spec, anywhere, anywhere, full((8, D)), strip],
             scratch_shapes=[
                 pltpu.VMEM((rows, D), F32),
                 pltpu.VMEM((rows, D), LOW),
                 pltpu.VMEM((rows, D), F32),
                 pltpu.VMEM((rows, D), F32),
-                pltpu.VMEM((2, 4, 4, quarter, BLK), LOW),
-                pltpu.SemaphoreType.DMA((2, 4, 4)),
+                pltpu.VMEM((D, D), LOW),
+                pltpu.VMEM((D, D), LOW),
+                pltpu.VMEM((2, 8, 4, quarter, BLK), LOW),
+                pltpu.SemaphoreType.DMA((2, 8, 4)),
             ],
         ),
         out_shape=[
@@ -483,24 +499,22 @@
         ],
         compiler_params=params(60),
         name="mid",
-    )(own, slot, rel, seq, x, attn, dy, vec, b1, *([gathered] * 8))
+    )(own, slot, rel, seq, x, attn, dy, vec, b1, *([gathered] * 12))
 
 
 def d_columns(step, grads, work):
-    for half in range(2):
-        dq, dk, rk, dv, rv = grads[5 * half : 5 * half + 5]
-
-        @pl.when(step == half)
+    def both(n):
+        return jnp.concatenate([grads[n][...], grads[5 + n][...]], axis=1)
+
+    @pl.when(step == 0)
+    def _():
+        work(both(0))
+
+    for n in (1, 3):
+
+        @pl.when(step == (n + 1) // 2)
         def _():
-            work(dq[...])
-
-        @pl.when(step == 2 + half)
-        def _():
-            work((dk[...].astype(F32) + rk[...].astype(F32)).astype(LOW))
-
-        @pl.when(step == 4 + half)
-        def _():
-            work((dv[...].astype(F32) + rv[...].astype(F32)).astype(LOW))
+            work((both(n).astype(F32) + both(n + 1).astype(F32)).astype(LOW))
 
 
 def qkv_grad_kernel(seq, a_ref, *refs):
@@ -514,7 +528,8 @@
             for rel_core, out in enumerate((keep, send)):
                 for rel_x in range(2):
                     start = pl.multiple_of(quarter_at(seq[0], rel_core, rel_x) * quarter, quarter)
-                    out[rel_x, i, 0] = stage[pl.ds(start, quarter), :]
+                    for j in range(2):
+                        out[rel_x, i, j] = stage[pl.ds(start, quarter), j * BLK : j * BLK + BLK]
 
     d_columns(pl.program_id(0), grads, work)
 
@@ -522,17 +537,17 @@
 def qkv_grad(seq, normed, halves):
     rows = normed.shape[0]
     quarter = BLK // 4
-    tile_out = pl.BlockSpec((2, 2, 1, quarter, BLK), lambda i, seq: (0, 0, i, 0, 0))
+    tile_out = pl.BlockSpec((2, 2, 2, quarter, BLK), lambda i, seq: (0, 0, i, 0, 0))
     shape = jax.ShapeDtypeStruct((2, 2, 6, quarter, BLK), LOW)
     return pl.pallas_call(
         qkv_grad_kernel,
         grid_spec=pltpu.PrefetchScalarGridSpec(
             num_scalar_prefetch=1,
-            grid=(6,),
+            grid=(3,),
             in_specs=[pl.BlockSpec((rows, D), lambda i, seq: (0, 0))]
             + [pl.BlockSpec((rows, BLK), lambda i, seq: (0, 0))] * 10,
-            out_specs=[tile_out, tile_out, pl.BlockSpec((1, BLK), lambda i, seq: (0, i))],
-            scratch_shapes=[pltpu.VMEM((BLK, BLK), LOW)],
+            out_specs=[tile_out, tile_out, pl.BlockSpec((1, D), lambda i, seq: (0, i))],
+            scratch_shapes=[pltpu.VMEM((BLK, D), LOW)],
         ),
         out_shape=[shape, shape, jax.ShapeDtypeStruct((1, 3 * D), F32)],
         compiler_params=params(48),
@@ -541,7 +556,7 @@
 
 
 def qkv_bwd_kernel(own, slot, x_ref, dmid_ref, vec_ref, *refs):
-    grads, (t0, t1, dx_ref, sums_ref, acc) = refs[:10], refs[10:]
+    grads, tiles, (dx_ref, sums_ref, acc, held) = refs[:10], refs[10:14], refs[14:]
     step = pl.program_id(0)
 
     @pl.when(step == 0)
@@ -549,12 +564,11 @@
         acc[...] = jnp.zeros_like(acc)
 
     def work(d_cols):
-        acc[:, :BLK] += dot(d_cols, tile(t0), 1, 1)
-        acc[:, BLK:] += dot(d_cols, tile(t1), 1, 1)
+        acc[...] += dot(d_cols, square(tiles, held), 1, 1)
 
     d_columns(step, grads, work)
 
-    @pl.when(step == 5)
+    @pl.when(step == 2)
     def _():
         hat, rstd = norm_parts(x_ref[...].astype(F32))
         grad = acc[...]
@@ -571,118 +585,142 @@
         qkv_bwd_kernel,
         grid_spec=pltpu.PrefetchScalarGridSpec(
             num_scalar_prefetch=2,
-            grid=(6,),
+            grid=(3,),
             in_specs=[row_spec, row_spec, full_spec(vec.shape)]
             + [full_spec((rows, BLK))] * 10
-            + [tile_spec(lambda i: i), tile_spec(lambda i: 6 + i)],
+            + qkv_tiles(),
             out_specs=[row_spec, full_spec((8, D))],
-            scratch_shapes=[pltpu.VMEM((rows, D), F32)],
+            scratch_shapes=[pltpu.VMEM((rows, D), F32), pltpu.VMEM((D, D), LOW)],
         ),
         out_shape=[jax.ShapeDtypeStruct((rows, D), LOW), jax.ShapeDtypeStruct((8, D), F32)],
         compiler_params=params(60),
         name="qkv_bwd",
-    )(own, slot, x, d_mid, vec, *halves[0], *halves[1], gathered, gathered)
-
-
-def eliminate(y_ref):
-    count, size = y_ref.shape[0], y_ref.shape[1]
+    )(own, slot, x, d_mid, vec, *halves[0], *halves[1], *([gathered] * 4))
+
+
+def eliminate(blocks):
+    count, size = len(blocks), blocks[0].shape[0]
+    batch = min(count, 6)
     lane = lanes((1, 8, size))
     sub = lax.broadcasted_iota(jnp.int32, (1, 8, size), 1)
     wide_lane = lanes((size, size))
-    shape = (count, 8, size)
+    shape = (batch, 8, size)
 
     def group(g, carry):
         base = pl.multiple_of(8 * g, 8)
-        slab = y_ref[:, pl.ds(base, 8), :]
-        rolled = jnp.stack([pltpu.roll(slab[b], size - base, 1) for b in range(count)], axis=0)
-        columns = [jnp.broadcast_to(rolled[:, :, k : k + 1], shape) for k in range(8)]
-        inside = (lane >= base) & (lane < base + 8)
-        rows = jnp.where(inside, jnp.where(lane - base == sub, 1.0, 0.0), slab)
-        scale = jnp.zeros(shape, F32)
-        for j in range(8):
-            inv_root = lax.rsqrt(jnp.broadcast_to(columns[j][:, j : j + 1, :], shape))
-            scale = jnp.where(sub == j, inv_root, scale)
-            factor = jnp.where(sub > j, columns[j] * (inv_root * inv_root), 0.0)
-            rows = rows - factor * jnp.broadcast_to(rows[:, j : j + 1, :], shape)
-            for k in range(j + 1, 8):
-                columns[k] = columns[k] - factor * jnp.broadcast_to(columns[k][:, j : j + 1, :], shape)
-        rows = rows * scale
-        below = jnp.where(lane >= base + 8, rows, 0.0)
-        passed = (wide_lane >= base) & (wide_lane < base + 8)
-        for b in range(count):
-            high, mid, low = three_parts(rows[b])
-            b_high, b_mid, b_low = three_parts(below[b])
-            first = jnp.concatenate([b_high, b_high, b_mid, b_high, b_low, b_mid], axis=0)
-            second = jnp.concatenate([high, mid, high, low, high, mid], axis=0)
-            update = dot(first.astype(LOW), second.astype(LOW), 0, 0)
-            y_ref[b] = jnp.where(passed, 0.0, y_ref[b]) - update
-            y_ref[b, pl.ds(base, 8), :] = rows[b]
+        for at in range(0, count, batch):
+            some = blocks[at : at + batch]
+            slab = jnp.stack([y[pl.ds(base, 8), :] for y in some], axis=0)
+            rolled = jnp.stack([pltpu.roll(slab[b], size - base, 1) for b in range(batch)], axis=0)
+            columns = [jnp.broadcast_to(rolled[:, :, k : k + 1], shape) for k in range(8)]
+            inside = (lane >= base) & (lane < base + 8)
+            rows = jnp.where(inside, jnp.where(lane - base == sub, 1.0, 0.0), slab)
+            scale = jnp.zeros(shape, F32)
+            for j in range(8):
+                inv_root = lax.rsqrt(jnp.broadcast_to(columns[j][:, j : j + 1, :], shape))
+                scale = jnp.where(sub == j, inv_root, scale)
+                factor = jnp.where(sub > j, columns[j] * (inv_root * inv_root), 0.0)
+                rows = rows - factor * jnp.broadcast_to(rows[:, j : j + 1, :], shape)
+                for k in range(j + 1, 8):
+                    columns[k] = columns[k] - factor * jnp.broadcast_to(columns[k][:, j : j + 1, :], shape)
+            rows = rows * scale
+            passed = (wide_lane >= base) & (wide_lane < base + 8)
+            for b, y in enumerate(some):
+                high, mid, low = three_parts(rows[b])
+                first = jnp.concatenate([high, high, mid, high, low, mid], axis=0)
+                first = jnp.where(jnp.broadcast_to(lane[0, :1] >= base + 8, first.shape), first, 0.0)
+                second = jnp.concatenate([high, mid, high, low, high, mid], axis=0)
+                update = dot(first.astype(LOW), second.astype(LOW), 0, 0)
+                y[...] = jnp.where(passed, 0.0, y[...]) - update
+                y[pl.ds(base, 8), :] = rows[b]
         return carry
 
     lax.fori_loop(0, size // 8, group, 0)
 
 
+def stats_kernel(ls_ref, rs_ref, lb_ref, rb_ref, left, right):
+    for stats, basis, out in ((ls_ref, lb_ref, left), (rs_ref, rb_ref, right)):
+        out[0] = BETA_STAT * dot_parts(low_parts(stats[0], 3), low_parts(basis[0], 3), 1, 0, 3)
+
+
+def stats_product(left_stats, right_stats, left_basis, right_basis):
+    count = left_stats.shape[0]
+    block_spec = pl.BlockSpec((1, BLK, BLK), lambda i: (i, 0, 0))
+    return pl.pallas_call(
+        stats_kernel,
+        grid=(count,),
+        in_specs=[block_spec] * 4,
+        out_specs=[block_spec] * 2,
+        out_shape=[jax.ShapeDtypeStruct((count, BLK, BLK), F32)] * 2,
+        compiler_params=params(32),
+        name="stats",
+    )(left_stats, right_stats, left_basis, right_basis)
+
+
 def soap_kernel(
-    seq_ref, g0, g1, g2, g3, w_ref, one_ref, two_ref, ls_ref, rs_ref, lb_ref, rb_ref,
-    *refs,
+    seq_ref, g0, g1, g2, g3, w_ref, one_ref, two_ref, ls_ref, rs_ref, lb_ref, rb_ref, lp_ref, rp_ref,
+    grad_ref, w_out, one_out, two_out, ls_out, rs_out, lb_out, rb_out,
+    grad_s, gram, work, *inv,
 ):
-    (
-        grad_ref, w_out, one_out, two_out, ls_out, rs_out, lb_out, rb_out,
-        grad_s, gram, work, inv,
-    ) = refs[-12:]
     step = pl.program_id(0)
     slots = pl.num_programs(0)
     count = lb_out.shape[0]
     quarter = BLK // 4
     for piece, flip in ((g0, 0), (g1, 2), (g2, 1), (g3, 3)):
         start = pl.multiple_of((seq_ref[0] ^ flip) * quarter, quarter)
-        grad_s[pl.ds(start, quarter), :] = piece[0].astype(F32)
-    grad_ref[0] = grad_s[...]
-    grad = grad_s[...].astype(LOW)
-    left, right = lb_ref[0], rb_ref[0]
-    left_low, right_low = left.astype(LOW), right.astype(LOW)
-    rotated = dot(dot(left_low, grad, 0, 0).astype(LOW), right_low, 1, 0)
+        grad_s[pl.ds(start, quarter), :] = piece[0]
+    grad = grad_s[...]
+    grad_ref[0] = grad.astype(F32)
+    left, right = low_parts(lb_ref[0], 2), low_parts(rb_ref[0], 2)
+    left_grad = dot_parts(left, [grad], 0, 0, 2)
+    grad_right = dot_parts([grad], right, 1, 0, 2)
+    rotated = dot(left_grad.astype(LOW), right[0], 1, 0)
     one = BETA_ONE * one_ref[0] + (1.0 - BETA_ONE) * rotated
     two = BETA_TWO * two_ref[0] + (1.0 - BETA_TWO) * rotated * rotated
     one_out[0] = one
     two_out[0] = two
     scaled = (one / (1.0 - BETA_ONE**STEP)) / (jnp.sqrt(two / (1.0 - BETA_TWO**STEP)) + ADAM_EPS)
-    back = dot(dot(left_low, scaled.astype(LOW), 1, 0).astype(LOW), right_low, 1, 1)
+    back = dot(dot(left[0], scaled.astype(LOW), 1, 0).astype(LOW), right[0], 1, 1)
     w_out[0] = w_ref[0] - RATE_MATRIX * (back + DECAY_RATE * w_ref[0])
-    left_new = BETA_STAT * ls_ref[0] + (1.0 - BETA_STAT) * dot(grad, grad, 1, 1)
-    right_new = BETA_STAT * rs_ref[0] + (1.0 - BETA_STAT) * dot(grad, grad, 0, 0)
-    ls_out[0] = left_new
-    rs_out[0] = right_new
-    for side, (stats, basis) in enumerate(((left_new, left), (right_new, right))):
-        product = dot(stats, basis, 1, 0, HIGHEST)
+    ls_out[0] = BETA_STAT * ls_ref[0] + (1.0 - BETA_STAT) * dot(grad, grad, 1, 1)
+    rs_out[0] = BETA_STAT * rs_ref[0] + (1.0 - BETA_STAT) * dot(grad, grad, 0, 0)
+    left_new = lp_ref[0] + (1.0 - BETA_STAT) * dot_parts([grad], low_parts(left_grad, 2), 1, 1, 2)
+    right_new = rp_ref[0] + (1.0 - BETA_STAT) * dot_parts([grad], low_parts(grad_right, 2), 0, 0, 2)
+    for side, product in enumerate((left_new, right_new)):
         at = side * count + step
         work[at] = product
-        gram[at] = dot(product, product, 0, 0, HIGHEST)
+        parts = low_parts(product, 3)
+        for p in range(BLK // 128):
+            c, on = slice(128 * p, 128 * p + 128), slice(128 * p, BLK)
+            gram[at, c, on] = dot_parts([part[:, c] for part in parts], [part[:, on] for part in parts], 0, 0, 3)
 
     @pl.when(step == slots - 1)
     def _():
         for p in range(BLK // 128):
             c = slice(128 * p, 128 * p + 128)
             rest = slice(128 * p + 128, BLK)
-            inv[...] = gram[:, c, c]
+            for b, block in enumerate(inv):
+                block[...] = gram[b, c, c]
             eliminate(inv)
+            for b, block in enumerate(inv):
+                gram[b, c, c] = block[...]
 
             def solve(b, carry, out):
                 at = b + (count if out is rb_out else 0)
-                factor = inv[at]
-                solved = dot(work[at, :, c], factor, 1, 1, HIGHEST)
+                factor = low_parts(gram[at, c, c], 3)
+                solved = dot_parts(low_parts(work[at, :, c], 2), factor, 1, 1, 2)
                 out[b, :, c] = solved
                 if p < BLK // 128 - 1:
-                    upper = dot(factor, gram[at, c, rest], 1, 0, HIGHEST)
-                    work[at, :, rest] = work[at, :, rest] - dot(solved, upper, 1, 0, HIGHEST)
-                    gram[at, rest, rest] = gram[at, rest, rest] - dot(upper, upper, 0, 0, HIGHEST)
+                    upper = low_parts(dot_parts(factor, low_parts(gram[at, c, rest], 3), 1, 0, 3), 3)
+                    work[at, :, rest] = work[at, :, rest] - dot_parts(low_parts(solved, 2), upper, 1, 0, 2)
+                    gram[at, rest, rest] = gram[at, rest, rest] - dot_parts(upper, upper, 0, 0, 3)
                 return carry
 
             lax.fori_loop(0, count, functools.partial(solve, out=lb_out), 0)
             lax.fori_loop(0, count, functools.partial(solve, out=rb_out), 0)
 
 
-def soap_update(seq, pieces, state):
+def soap_update(seq, pieces, state, products):
     count = state[0].shape[0]
     piece_spec = pl.BlockSpec((1, BLK // 4, BLK), lambda i, s: (i, 0, 0))
     block_spec = pl.BlockSpec((1, BLK, BLK), lambda i, s: (i, 0, 0))
@@ -693,19 +731,19 @@
         grid_spec=pltpu.PrefetchScalarGridSpec(
             num_scalar_prefetch=1,
             grid=(count,),
-            in_specs=[piece_spec] * 4 + [block_spec] * 7,
+            in_specs=[piece_spec] * 4 + [block_spec] * 9,
             out_specs=[block_spec] * 6 + [whole_spec] * 2,
             scratch_shapes=[
-                pltpu.VMEM((BLK, BLK), F32),
+                pltpu.VMEM((BLK, BLK), LOW),
                 pltpu.VMEM((2 * count, BLK, BLK), F32),
                 pltpu.VMEM((2 * count, BLK, BLK), F32),
-                pltpu.VMEM((2 * count, 128, 128), F32),
-            ],
+            ]
+            + [pltpu.VMEM((128, 128), F32)] * (2 * count),
         ),
         out_shape=[shape] * 8,
         compiler_params=params(60),
         name="soap",
-    )(seq, *pieces, *state)
+    )(seq, *pieces, *state, *products)
 
 
 def split_kernel(dp, a_ref, b_ref, *outs):
@@ -853,15 +891,15 @@
         owner_count, 4, slot_count, quarter, BLK
     )
 
+    products = stats_product(left_stats, right_stats, left_basis, right_basis)
+
     pair = jnp.stack([tokens, cotangent])
     kept = lax.dynamic_index_in_dim(pair, chip, 1, keepdims=False)
     got = swap(lax.dynamic_index_in_dim(pair, 1 - chip, 1, keepdims=False), "seq", 2)
     x = jnp.concatenate([kept[0], got[0]], axis=0)
     dy = jnp.concatenate([kept[1], got[1]], axis=0)
 
-    def to_positions(rows):
-        other = swap(rows[part_len:], "seq", 2)
-        mine = rows[:part_len]
+    def to_positions(mine, other):
         return jnp.where(chip == 0, jnp.stack([mine, other]), jnp.stack([other, mine]))
 
     positions = jnp.arange(patch_mask.shape[-1], dtype=jnp.int32)
@@ -872,6 +910,7 @@
     fill = jnp.broadcast_to(fill[:, None], (fill.shape[0], 128))
 
     bias = jnp.concatenate([vec[4], jnp.zeros_like(vec[4]), vec[5]])[None, :]
+    gathered, products = lax.optimization_barrier((gathered, products))
     q, kv, normed = qkv_forward(owners, slots, x, vec, bias, gathered)
     other = swap(kv, "seq", 1)
     attn, lse = attn_forward(q, kv, other, fill)
@@ -880,7 +919,7 @@
     result, d_mid, d_attn, keep, send, sums_two, bias_grad = mid_layer(
         owners, slots, owners ^ dp_id, seq_of, x, attn, dy, vec, b1, gathered
     )
-    output = to_positions(result)
+    result_other = swap(result[part_len:], "seq", 2)
 
     bits = owner_count.bit_length() - 1
     if slot_count % 3 == 0 and bits == 3:
@@ -918,23 +957,29 @@
             before = attn_backward(
                 q, kv, other, guard, attn, lse, d_attn, first + place, count, place, half_pairs, before
             )
-            got, before = lax.optimization_barrier(([group.got for group in groups], before))
+            got, before, result_other = lax.optimization_barrier(
+                ([group.got for group in groups], before, result_other)
+            )
             for group, array in zip(groups, got, strict=True):
                 group.got = array
         dq, dk, dv, sent_k, sent_v = before
         halves.append((dq, dk, swap(sent_k, "seq", 1), dv, swap(sent_v, "seq", 1)))
+    normed = advance(taken, normed)
+    taken += 1
     late_keep, late_send, cols = qkv_grad(seq_of, normed, halves)
     late_shape = (2, -1, quarter, BLK)
-    late_got = swap(late_send.reshape(late_shape), "seq", 1)
+    late = Halving(late_keep.reshape(late_shape), swap(late_send.reshape(late_shape), "seq", 1), ["x"])
+    late.receive(late.send("x"))
     d_x, sums_one = qkv_backward(owners, slots, x, d_mid, vec, halves, gathered)
-    d_tokens = to_positions(d_x)
+    got, late.got, d_x = lax.optimization_barrier(([group.got for group in groups], late.got, d_x))
+    for group, array in zip(groups, got, strict=True):
+        group.got = array
+    d_x_other = swap(d_x[part_len:], "seq", 2)
     while taken < len(names):
-        advance(taken, guard)
+        advance(taken, fill)
         taken += 1
     early = jnp.concatenate([group.total() for group in groups], axis=0)
 
-    late = Halving(late_keep.reshape(late_shape), late_got, ["x"])
-    late.receive(late.send("x"))
     mine_from = lax.dynamic_slice_in_dim(sources, dp_id * slot_count, slot_count)
     if 2 * first_blocks % owner_count == 0:
         unit = (owner_count, 2 * first_blocks // owner_count, quarter // 2, BLK)
@@ -954,7 +999,7 @@
         piece = jnp.where((mine_from < first_blocks)[:, None, None], owned.total(), early)
     state = (master, moment_one, moment_two, left_stats, right_stats, left_basis, right_basis)
     piece = jnp.where((mine_from < owners.shape[0])[:, None, None], piece, jnp.zeros_like(piece))
-    updates = soap_update(seq_of, quarters(piece), state)
+    updates = soap_update(seq_of, quarters(piece), state, products)
 
     vec_grad = jnp.concatenate(
         [
@@ -967,7 +1012,13 @@
         ],
         axis=0,
     )
-    vec_total = jnp.sum(lax.all_gather(vec_grad, AXES, axis=0, tiled=False), axis=0)
+    vec_parts = lax.all_gather(vec_grad, AXES, axis=0, tiled=False)
+    updates, vec_parts, d_x, d_x_other, result, result_other = lax.optimization_barrier(
+        (updates, vec_parts, d_x, d_x_other, result, result_other)
+    )
+    output = to_positions(result[:part_len], result_other)
+    d_tokens = to_positions(d_x[:part_len], d_x_other)
+    vec_total = jnp.sum(vec_parts, axis=0)
     vec_first, vec_second, vec_next = adam_vectors(vec_total, vec, vec_one, vec_two)
     grad_blocks, w_new, one_new, two_new, ls_new, rs_new, lb_new, rb_new = updates
     return (

time: 681 us -> 600 us (0.88); the launches traced: 682 us -> 588 us
  Pallas kernels: 370 us -> 318 us
  waiting for transfers between devices: 184 us -> 132 us
  local copies, waits for them, and re-layouts: 21.8 us -> 37.6 us
    ppermute x39, waiting for transfers between devices: 117 us -> 65.9 us  [swap(): return lax.ppermute(x, axis, [(i, i ^ bit) for i in range(size)])]
    pallas_call x1, Pallas kernels: 87.1 us -> 58 us  [mid_layer(): pl.pallas_call(functools.partial(mid_kernel, chunk=chunk), grid_spec=pltp...]
    pallas_call x1, Pallas kernels: 115 us -> 87.3 us  [soap_update(): pl.pallas_call(soap_kernel, grid_spec=pltpu.PrefetchScalarGridSpec(num_sc...]
    pallas_call x0 -> x1, Pallas kernels: none -> 12.1 us  [stats_product(): pl.pallas_call(stats_kernel, grid=(count,), in_specs=[block_spec] * 4, ou...]
    unnamed x67 -> x93, local copies, waits for them, and re-layouts: 5.29 us -> 15 us
  transfers between devices with their start and end apart: 41 -> 41, of which waited for: 13 -> 12; matrix products, arithmetic and copies ran while one was open for 6% -> 7% of each run, Pallas kernels for 14% -> 33%
where the time goes in v4:
time: 600 us; the launch traced here: 588 us
  Pallas kernels  318 us (53%)
  waiting for transfers between devices  132 us (22%)
  starting transfers between devices  43.3 us (7%)
  other arithmetic  41.5 us (7%)
  local copies, waits for them, and re-layouts  37.6 us (6%)
  between operations  15.3 us (3%)
    pallas_call x1, Pallas kernels, soap_update(): pl.pallas_call(soap_kernel, grid_spec=pltpu.PrefetchScalarGridSpec(num_sc...  87.3 us
    pallas_call x4, Pallas kernels, attn_backward(): pl.pallas_call(kernel, grid=(count, rows // q_rows), in_specs=[q_spec, k_...  82.1 us
    all_gather x1, waiting for transfers between devices, on_device(): lax.all_gather(mine, AXES, axis=0, tiled=False)  66.5 us
    ppermute x39, waiting for transfers between devices, swap(): return lax.ppermute(x, axis, [(i, i ^ bit) for i in range(size)])  65.9 us
    pallas_call x1, Pallas kernels, mid_layer(): pl.pallas_call(functools.partial(mid_kernel, chunk=chunk), grid_spec=pltp...  58 us
    pallas_call x1, Pallas kernels, attn_forward(): pl.pallas_call(attn_fwd_kernel, grid=(pairs, rows // q_rows), in_specs=[q...  47.2 us
    ppermute x39, starting transfers between devices, swap(): return lax.ppermute(x, axis, [(i, i ^ bit) for i in range(size)])  43.2 us
    convert_element_type x17, other arithmetic, add_low(): return (a.astype(F32) + b.astype(F32)).astype(LOW)  24.3 us
  transfers between devices with their start and end apart: 41, of which 12 were waited for; matrix products, arithmetic and copies ran while one was open for 7% of the time, Pallas kernels for 33%

profile of v4, /device:TPU:0, one launch (start us, length us, event | category | flops | bytes accessed | tf_op | source)
XLA Modules:
  0.0 588.4 jit_solution(5328065796942851908)
XLA Ops:
  11.8 3.0 collective-permute-start
  19.7 12.1 %stats.1 = (f32[6,384,384]{2,1,0:T(8,128)S(1)}, f32[6,384,384]{2,1,0:T(8,128)S(1)}) custom-call(f32[6,384,384]{2,1,0:T(8,128)S(1)} %copy-done.4, f32[6,384,384]{2,1,0:T(8,128)S(1)} %copy-done.5, f32[6,384,384]{2,1,0:T(8,128)S(1)} %copy-done.6, f32[6,384,384]{2,1,0:T(8,128)S(1)} %copy-done.7), custom_call_target="tpu_custom_call" | custom-call | tf_op jit(solution)/shard_map/stats/pallas_call | solution.py:649
  36.4 22.8 %collective-permute-done = bf16[2,512,768]{2,1,0:T(8,128)(2,1)S(1)} collective-permute-done((bf16[2,512,768]{2,1,0:T(8,128)(2,1)S(1)}, bf16[2,512,768]{2,1,0:T(8,128)(2,1)S(1)}, u32[]{:S(2)}, u32[]{:S(2)}) %collective-permute-start) | collective-permute-done | bytes 1572896 | tf_op jit(solution)/shard_map/ppermute | solution.py:816
  60.3 66.5 %all-gather.6.cloned.1.call-done = bf16[192,1,96,384]{3,2,1,0:T(8,128)(2,1)} async-done(((bf16[6,1,96,384]{3,2,1,0:T(8,128)(2,1)}), bf16[192,1,96,384]{3,2,1,0:T(8,128)(2,1)}) %all-gather.6.cloned.1.call-update) | async-done | bytes 14155792 | tf_op jit(solution)/shard_map/all_gather | solution.py:890
  126.8 9.1 %qkv.1 = (bf16[1024,768]{1,0:T(8,128)(2,1)S(1)}, bf16[1024,1536]{1,0:T(8,128)(2,1)}, bf16[1024,768]{1,0:T(8,128)(2,1)S(1)}) custom-call(s32[48]{0:T(128)S(1)} %copy-done.20, s32[48]{0:T(128)S(1)} %convert_reduce_fusion.slot, bf16[1024,768]{1,0:T(8,128)(2,1)S(1)} %pad_maximum_fusion.x_ref, f32[12,768]{1,0:T(8,128)S(1)} %copy-done.18, ...), custom_call_target="tpu_custom_call" | custom-call | tf_op jit(solution)/shard_map/qkv/pallas_call | solution.py:130
  140.7 2.6 pad_maximum_fusion.1.dy_ref
  143.6 47.2 %attn_fwd.1 = (bf16[1024,768]{1,0:T(8,128)(2,1)S(1)}, f32[1024,768]{1,0:T(8,128)}) custom-call(bf16[1024,768]{1,0:T(8,128)(2,1)S(1)} %get-tuple-element.143.q_ref.refs_0_, bf16[1024,1536]{1,0:T(8,128)(2,1)} %get-tuple-element.144.k1.v1.refs_1_.refs_2_, bf16[1024,1536]{1,0:T(8,128)(2,1)} %get-tuple-element.144.k1.v1.refs_1_.refs_2_, ...), custom_call_target="tpu_custom_call" | custom-call | tf_op jit(solution)/shard_map/attn_fwd/pallas_call | solution.py:195
  192.0 58.0 %mid.1 = (bf16[1024,768]{1,0:T(8,128)(2,1)}, f32[1024,768]{1,0:T(8,128)}, bf16[1024,768]{1,0:T(8,128)(2,1)}, bf16[2,8,6,96,384]{4,3,2,1,0:T(8,128)(2,1)}, bf16[2...) custom-call(s32[48]{0:T(128)} %own.5, s32[48]{0:T(128)} %copy-done.21, ...), custom_call_target="tpu_custom_call" | custom-call | tf_op jit(solution)/shard_map/mid/pallas_call | solution.py:470
  253.0 26.3 %attn_bwd.4 = (bf16[1024,384]{1,0:T(8,128)(2,1)}, bf16[1024,384]{1,0:T(8,128)(2,1)}, bf16[1024,384]{1,0:T(8,128)(2,1)}, bf16[1024,384]{1,0:T(8,128)(2,1)}, bf16[1024,384]{1,0:T(8,128)(2,1)}) custom-call(bf16[1024,768]{1,0:T(8,128)(2,1)} %copy-done.1, bf16[1024,1536]{1,0:T(8,128)(2,1)} %get-tuple-element.144.k1.v1.refs_1_.refs_2_, ...), custom_call_target="tpu_custom_call" | custom-call | tf_op jit(solution)/shard_map/attn_bwd/pallas_call | solution.py:323
  283.2 2.6 fusion.8
  292.3 26.7 %attn_bwd.6 = (bf16[1024,384]{1,0:T(8,128)(2,1)}, bf16[1024,384]{1,0:T(8,128)(2,1)}, bf16[1024,384]{1,0:T(8,128)(2,1)}, bf16[1024,384]{1,0:T(8,128)(2,1)}, bf16[1024,384]{1,0:T(8,128)(2,1)}) custom-call(bf16[1024,768]{1,0:T(8,128)(2,1)} %copy-done.1, bf16[1024,1536]{1,0:T(8,128)(2,1)} %get-tuple-element.144.k1.v1.refs_1_.refs_2_, ...), custom_call_target="tpu_custom_call" | custom-call | tf_op jit(solution)/shard_map/attn_bwd/pallas_call | solution.py:323
  319.0 14.6 %attn_bwd.5 = (bf16[1024,384]{1,0:T(8,128)(2,1)}, bf16[1024,384]{1,0:T(8,128)(2,1)}, bf16[1024,384]{1,0:T(8,128)(2,1)}, bf16[1024,384]{1,0:T(8,128)(2,1)}, bf16[1024,384]{1,0:T(8,128)(2,1)}) custom-call(bf16[1024,768]{1,0:T(8,128)(2,1)} %copy-done.1, ...), custom_call_target="tpu_custom_call", output_to_operand_aliasing={{0}: (9, {}), {1}: (10, {}), {2}: (11, {}), {3}: (12, {}), ... | custom-call | tf_op jit(solution)/shard_map/attn_bwd/pallas_call | solution.py:323
  336.9 2.5 fusion.13
  344.9 14.5 %attn_bwd.7 = (bf16[1024,384]{1,0:T(8,128)(2,1)}, bf16[1024,384]{1,0:T(8,128)(2,1)}, bf16[1024,384]{1,0:T(8,128)(2,1)}, bf16[1024,384]{1,0:T(8,128)(2,1)}, bf16[1024,384]{1,0:T(8,128)(2,1)}) custom-call(bf16[1024,768]{1,0:T(8,128)(2,1)} %copy-done.1, ...), custom_call_target="tpu_custom_call", output_to_operand_aliasing={{0}: (9, {}), {1}: (10, {}), {2}: (11, {}), {3}: (12, {}), ... | custom-call | tf_op jit(solution)/shard_map/attn_bwd/pallas_call | solution.py:323
  361.0 2.4 add_convert_fusion.10
  365.3 8.0 %qkv_grad.1 = (bf16[2,2,6,96,384]{4,3,2,1,0:T(8,128)(2,1)}, bf16[2,2,6,96,384]{4,3,2,1,0:T(8,128)(2,1)}, f32[1,2304]{1,0:T(1,128)S(1)}) custom-call(s32[1]{0:T(128)} %bitcast.seq.seq_ref, bf16[1024,768]{1,0:T(8,128)(2,1)} %copy-done.17, bf16[1024,384]{1,0:T(8,128)(2,1)S(1)} %copy-done.10, bf16[1024,384]{1,0:T(8,128)(2,1)S(1)} %copy-done.11, ...), custom_call_target="tpu_custom_call" | custom-call | tf_op jit(solution)/shard_map/qkv_grad/pallas_call | solution.py:542
  389.4 13.4 %qkv_bwd.1 = (bf16[1024,768]{1,0:T(8,128)(2,1)}, f32[8,768]{1,0:T(8,128)}) custom-call(s32[48]{0:T(128)} %own.5, s32[48]{0:T(128)} %copy-done.21, bf16[1024,768]{1,0:T(8,128)(2,1)} %copy-done.2, f32[1024,768]{1,0:T(8,128)} %get-tuple-element.221.dmid_ref, f32[12,768]{1,0:T(8,128)} %vec_ref.5, bf16[1024,384]{1,0:T(8,128)(2,1)} %get-tuple-element.206.refs_0_, ...), custom_call_target="tpu_custom_call" | custom-call | tf_op jit(solution)/shard_map/qkv_bwd/pallas_call | solution.py:584
  407.1 3.0 collective-permute-start.25
  411.6 3.3 collective-permute-start.22
  417.3 7.7 %collective-permute-start.20 = (bf16[3,48,384]{2,1,0:T(8,128)(2,1)S(1)}, bf16[3,48,384]{2,1,0:T(8,128)(2,1)S(1)}, u32[]{:S(2)}, u32[]{:S(2)}) collective-permute-start(bf16[3,48,384]{2,1,0:T(8,128)(2,1)S(1)} %get-tuple-element.226), channel_id=1, source_target_pairs={{0,8},{4,12},{8,0},{12,4},{16,24},{20,28},{24,16},{28,20},{1,9},{5... | collective-permute-start | bytes 331784 | tf_op jit(solution)/shard_map/ppermute | solution.py:816
  429.6 9.8 %collective-permute-done.22 = bf16[3,48,384]{2,1,0:T(8,128)(2,1)S(1)} collective-permute-done((bf16[3,48,384]{2,1,0:T(8,128)(2,1)S(1)}, bf16[3,48,384]{2,1,0:T(8,128)(2,1)S(1)}, u32[]{:S(2)}, u32[]{:S(2)}) %collective-permute-start.22) | collective-permute-done | bytes 110624 | tf_op jit(solution)/shard_map/ppermute | solution.py:816
  439.4 2.9 collective-permute-start.33
  442.6 3.3 collective-permute-done.35
  447.0 3.4 collective-permute-done.34
  451.4 4.5 collective-permute-done.33
  457.0 4.2 collective-permute-start.32
  461.3 5.1 collective-permute-done.29.refs_4_
  466.3 3.8 collective-permute-done.30.refs_5_
  472.1 8.6 %collective-permute-done.36.g1 = bf16[6,96,384]{2,1,0:T(8,128)(2,1)S(1)} collective-permute-done((bf16[6,96,384]{2,1,0:T(8,128)(2,1)S(1)}, bf16[6,96,384]{2,1,0:T(8,128)(2,1)S(1)}, u32[]{:S(2)}, u32[]{:S(2)}) %collective-permute-start.36) | collective-permute-done | bytes 442400 | tf_op jit(solution)/shard_map/ppermute | solution.py:816
  484.6 87.3 %soap.1 = (f32[6,384,384]{2,1,0:T(8,128)}, f32[6,384,384]{2,1,0:T(8,128)}, f32[6,384,384]{2,1,0:T(8,128)}, f32[6,384,384]{2,1,0:T(8,128)}, f32[6,384,384]{2,1,0:...) custom-call(s32[1]{0:T(128)} %bitcast.seq.seq_ref, ...), custom_call_target="tpu_custom_call" | custom-call | tf_op jit(solution)/shard_map/soap/pallas_call | solution.py:729
  574.9 2.8 maximum_select_fusion
  577.7 2.8 maximum_select_fusion.1
  (225 shorter events, 88.5 us)
Async XLA Ops:
  7.2 119.6 %all-gather.6.cloned.1.call-start = ((), (), s32[]{:S(2)}) async-start(), calls=%async_computation | async-start | bytes 14598144 | tf_op jit(solution)/shard_map/all_gather | solution.py:890
  9.4 562.5 %all-gather.8.cloned.1.call-start = ((), (), s32[]{:S(2)}) async-start(), calls=%async_computation.1 | async-start | bytes 1622016 | tf_op jit(solution)/shard_map/all_gather | solution.py:1015
  11.8 47.5 %collective-permute-start = (bf16[2,512,768]{2,1,0:T(8,128)(2,1)S(1)}, bf16[2,512,768]{2,1,0:T(8,128)(2,1)S(1)}, u32[]{:S(2)}, u32[]{:S(2)}) collective-permute-start(bf16[2,512,768]{2,1,0:T(8,128)(2,1)S(1)} %get-tuple-element.285), channel_id=1, source_target_pairs={{0,2},{1,3},{2,0},{3,1},{4,6},{5,7},{6,4},{7,5},{8,10},{9,11},{10,... | collective-permute-start | bytes 4718600 | tf_op jit(solution)/shard_map/ppermute | solution.py:816
  250.0 33.2 %collective-permute-start.2 = (bf16[2,8,6,96,384]{4,3,2,1,0:T(8,128)(2,1)}, bf16[2,8,6,96,384]{4,3,2,1,0:T(8,128)(2,1)S(1)}, u32[]{:S(2)}, u32[]{:S(2)}) collective-permute-start(bf16[2,8,6,96,384]{4,3,2,1,0:T(8,128)(2,1)} %get-tuple-element.147), channel_id=1, source_target_pairs={{0,1},{1,0},{2,3},{3,2},{4,5},{5,4},{6,7},{7,6},{8,9},{9,8},{10,11... | collective-permute-start | bytes 21233672 | tf_op jit(solution)/shard_map/ppermute | solution.py:816
  251.5 31.7 %collective-permute-start.3 = (bf16[512,768]{1,0:T(8,128)(2,1)S(1)}, bf16[512,768]{1,0:T(8,128)(2,1)}, u32[]{:S(2)}, u32[]{:S(2)}) collective-permute-start(bf16[512,768]{1,0:T(8,128)(2,1)S(1)} %slice.250), channel_id=1, source_target_pairs={{0,2},{1,3},{2,0},{3,1},{4,6},{5,7},{6,4},{7,5},{8,10},{9,11},{10,... | collective-permute-start | bytes 2359304 | tf_op jit(solution)/shard_map/ppermute | solution.py:816
  289.7 45.6 %collective-permute-start.4 = (bf16[2,2,2,2,96,384]{5,4,3,1,0,2:T(8,128)(2,1)}, bf16[2,2,2,2,96,384]{5,4,3,1,0,2:T(8,128)(2,1)}, u32[]{:S(2)}, u32[]{:S(2)}) collective-permute-start(bf16[2,2,2,2,96,384]{5,4,3,1,0,2:T(8,128)(2,1)} %get-tuple-element.159), channel_id=1, source_target_pairs={{0,2},{1,3},{2,0},{3,1},{4,6},{5,7},{6,4},{7,5},{8,10},{9,11},{10,... | collective-permute-start | bytes 3538952 | tf_op jit(solution)/shard_map/ppermute | solution.py:816
  290.3 45.0 %collective-permute-start.5 = (bf16[2,2,2,2,96,384]{5,4,3,1,2,0:T(8,128)(2,1)}, bf16[2,2,2,2,96,384]{5,4,3,1,2,0:T(8,128)(2,1)}, u32[]{:S(2)}, u32[]{:S(2)}) collective-permute-start(bf16[2,2,2,2,96,384]{5,4,3,1,2,0:T(8,128)(2,1)} %get-tuple-element.160), channel_id=1, source_target_pairs={{0,4},{4,0},{8,12},{12,8},{16,20},{20,16},{24,28},{28,24},{1,5},{5... | collective-permute-start | bytes 3538952 | tf_op jit(solution)/shard_map/ppermute | solution.py:816
  291.8 43.5 %collective-permute-start.6 = (bf16[2,2,2,2,96,384]{5,4,3,2,1,0:T(8,128)(2,1)}, bf16[2,2,2,2,96,384]{5,4,3,2,1,0:T(8,128)(2,1)}, u32[]{:S(2)}, u32[]{:S(2)}) collective-permute-start(bf16[2,2,2,2,96,384]{5,4,3,2,1,0:T(8,128)(2,1)} %fusion.8), channel_id=1, source_target_pairs={{0,8},{4,12},{8,0},{12,4},{16,24},{20,28},{24,16},{28,20},{1,9},{5... | collective-permute-start | bytes 3538952 | tf_op jit(solution)/shard_map/ppermute | solution.py:816
  341.0 18.5 %collective-permute-start.7 = (bf16[2,2,2,96,384]{4,3,2,1,0:T(8,128)(2,1)S(1)}, bf16[2,2,2,96,384]{4,3,2,1,0:T(8,128)(2,1)S(1)}, u32[]{:S(2)}, u32[]{:S(2)}) collective-permute-start(bf16[2,2,2,96,384]{4,3,2,1,0:T(8,128)(2,1)S(1)} %get-tuple-element.186), channel_id=1, source_target_pairs={{0,4},{4,0},{8,12},{12,8},{16,20},{20,16},{24,28},{28,24},{1,5},{5... | collective-permute-start | bytes 1769480 | tf_op jit(solution)/shard_map/ppermute | solution.py:816
  341.6 17.9 %collective-permute-start.8 = (bf16[2,2,2,96,384]{4,3,2,1,0:T(8,128)(2,1)S(1)}, bf16[2,2,2,96,384]{4,3,2,1,0:T(8,128)(2,1)S(1)}, u32[]{:S(2)}, u32[]{:S(2)}) collective-permute-start(bf16[2,2,2,96,384]{4,3,2,1,0:T(8,128)(2,1)S(1)} %get-tuple-element.187), channel_id=1, source_target_pairs={{0,8},{4,12},{8,0},{12,4},{16,24},{20,28},{24,16},{28,20},{1,9},{5... | collective-permute-start | bytes 1769480 | tf_op jit(solution)/shard_map/ppermute | solution.py:816
  343.0 16.4 %collective-permute-start.9 = (bf16[2,2,2,96,384]{4,3,2,1,0:T(8,128)(2,1)S(1)}, bf16[2,2,2,96,384]{4,3,2,1,0:T(8,128)(2,1)S(1)}, u32[]{:S(2)}, u32[]{:S(2)}) collective-permute-start(bf16[2,2,2,96,384]{4,3,2,1,0:T(8,128)(2,1)S(1)} %get-tuple-element.188), channel_id=1, source_target_pairs={{0,2},{1,3},{2,0},{3,1},{4,6},{5,7},{6,4},{7,5},{8,10},{9,11},{10,... | collective-permute-start | bytes 1769480 | tf_op jit(solution)/shard_map/ppermute | solution.py:816
  344.4 19.0 %collective-permute-start.10 = (bf16[1024,384]{1,0:T(8,128)(2,1)S(1)}, bf16[1024,384]{1,0:T(8,128)(2,1)S(1)}, u32[]{:S(2)}, u32[]{:S(2)}) collective-permute-start(bf16[1024,384]{1,0:T(8,128)(2,1)S(1)} %copy-done.35), channel_id=1, source_target_pairs={{0,1},{1,0},{2,3},{3,2},{4,5},{5,4},{6,7},{7,6},{8,9},{9,8},{10,11... | collective-permute-start | bytes 2359304 | tf_op jit(solution)/shard_map/ppermute | solution.py:816
  344.4 19.0 %collective-permute-start.11 = (bf16[1024,384]{1,0:T(8,128)(2,1)}, bf16[1024,384]{1,0:T(8,128)(2,1)S(1)}, u32[]{:S(2)}, u32[]{:S(2)}) collective-permute-start(bf16[1024,384]{1,0:T(8,128)(2,1)} %get-tuple-element.210), channel_id=1, source_target_pairs={{0,1},{1,0},{2,3},{3,2},{4,5},{5,4},{6,7},{7,6},{8,9},{9,8},{10,11... | collective-permute-start | bytes 2359304 | tf_op jit(solution)/shard_map/ppermute | solution.py:816
  378.5 28.3 %collective-permute-start.18 = (bf16[12,96,384]{2,1,0:T(8,128)(2,1)}, bf16[12,96,384]{2,1,0:T(8,128)(2,1)S(1)}, u32[]{:S(2)}, u32[]{:S(2)}) collective-permute-start(bf16[12,96,384]{2,1,0:T(8,128)(2,1)} %fusion), channel_id=1, source_target_pairs={{0,2},{1,3},{2,0},{3,1},{4,6},{5,7},{6,4},{7,5},{8,10},{9,11},{10,... | collective-permute-start | bytes 2654216 | tf_op jit(solution)/shard_map/ppermute | solution.py:816
  386.1 20.4 %collective-permute-start.15 = (bf16[2,2,96,384]{3,2,1,0:T(8,128)(2,1)}, bf16[2,2,96,384]{3,2,1,0:T(8,128)(2,1)}, u32[]{:S(2)}, u32[]{:S(2)}) collective-permute-start(bf16[2,2,96,384]{3,2,1,0:T(8,128)(2,1)} %get-tuple-element.218), channel_id=1, source_target_pairs={{0,8},{4,12},{8,0},{12,4},{16,24},{20,28},{24,16},{28,20},{1,9},{5... | collective-permute-start | bytes 884744 | tf_op jit(solution)/shard_map/ppermute | solution.py:816
  386.7 20.1 %collective-permute-start.16 = (bf16[2,2,96,384]{3,2,1,0:T(8,128)(2,1)}, bf16[2,2,96,384]{3,2,1,0:T(8,128)(2,1)}, u32[]{:S(2)}, u32[]{:S(2)}) collective-permute-start(bf16[2,2,96,384]{3,2,1,0:T(8,128)(2,1)} %get-tuple-element.219), channel_id=1, source_target_pairs={{0,2},{1,3},{2,0},{3,1},{4,6},{5,7},{6,4},{7,5},{8,10},{9,11},{10,... | collective-permute-start | bytes 884744 | tf_op jit(solution)/shard_map/ppermute | solution.py:816
  388.1 18.7 %collective-permute-start.17 = (bf16[2,2,96,384]{3,2,1,0:T(8,128)(2,1)}, bf16[2,2,96,384]{3,2,1,0:T(8,128)(2,1)}, u32[]{:S(2)}, u32[]{:S(2)}) collective-permute-start(bf16[2,2,96,384]{3,2,1,0:T(8,128)(2,1)} %get-tuple-element.220), channel_id=1, source_target_pairs={{0,4},{4,0},{8,12},{12,8},{16,20},{20,16},{24,28},{28,24},{1,5},{5... | collective-permute-start | bytes 884744 | tf_op jit(solution)/shard_map/ppermute | solution.py:816
  410.1 14.9 %collective-permute-start.24 = (bf16[3,48,384]{2,1,0:T(8,128)(2,1)S(1)}, bf16[3,48,384]{2,1,0:T(8,128)(2,1)S(1)}, u32[]{:S(2)}, u32[]{:S(2)}) collective-permute-start(bf16[3,48,384]{2,1,0:T(8,128)(2,1)S(1)} %get-tuple-element.230), channel_id=1, source_target_pairs={{0,24},{4,28},{8,16},{12,20},{16,8},{20,12},{24,0},{28,4},{1,25},{... | collective-permute-start | bytes 331784 | tf_op jit(solution)/shard_map/ppermute | solution.py:816
  411.6 17.7 %collective-permute-start.23 = (bf16[3,48,384]{2,1,0:T(8,128)(2,1)S(1)}, bf16[3,48,384]{2,1,0:T(8,128)(2,1)S(1)}, u32[]{:S(2)}, u32[]{:S(2)}) collective-permute-start(bf16[3,48,384]{2,1,0:T(8,128)(2,1)S(1)} %get-tuple-element.229), channel_id=1, source_target_pairs={{0,20},{4,16},{8,28},{12,24},{16,4},{20,0},{24,12},{28,8},{1,21},{... | collective-permute-start | bytes 331784 | tf_op jit(solution)/shard_map/ppermute | solution.py:816
  411.6 27.8 %collective-permute-start.22 = (bf16[3,48,384]{2,1,0:T(8,128)(2,1)S(1)}, bf16[3,48,384]{2,1,0:T(8,128)(2,1)S(1)}, u32[]{:S(2)}, u32[]{:S(2)}) collective-permute-start(bf16[3,48,384]{2,1,0:T(8,128)(2,1)S(1)} %get-tuple-element.228), channel_id=1, source_target_pairs={{0,16},{4,20},{8,24},{12,28},{16,0},{20,4},{24,8},{28,12},{1,17},{... | collective-permute-start | bytes 331784 | tf_op jit(solution)/shard_map/ppermute | solution.py:816
  414.8 24.5 %collective-permute-start.21 = (bf16[3,48,384]{2,1,0:T(8,128)(2,1)S(1)}, bf16[3,48,384]{2,1,0:T(8,128)(2,1)S(1)}, u32[]{:S(2)}, u32[]{:S(2)}) collective-permute-start(bf16[3,48,384]{2,1,0:T(8,128)(2,1)S(1)} %get-tuple-element.227), channel_id=1, source_target_pairs={{0,12},{4,8},{8,4},{12,0},{16,28},{20,24},{24,20},{28,16},{1,13},{... | collective-permute-start | bytes 331784 | tf_op jit(solution)/shard_map/ppermute | solution.py:816
  417.3 25.0 %collective-permute-start.20 = (bf16[3,48,384]{2,1,0:T(8,128)(2,1)S(1)}, bf16[3,48,384]{2,1,0:T(8,128)(2,1)S(1)}, u32[]{:S(2)}, u32[]{:S(2)}) collective-permute-start(bf16[3,48,384]{2,1,0:T(8,128)(2,1)S(1)} %get-tuple-element.226), channel_id=1, source_target_pairs={{0,8},{4,12},{8,0},{12,4},{16,24},{20,28},{24,16},{28,20},{1,9},{5... | collective-permute-start | bytes 331784 | tf_op jit(solution)/shard_map/ppermute | solution.py:816
  425.0 17.3 %collective-permute-start.19 = (bf16[3,48,384]{2,1,0:T(8,128)(2,1)S(1)}, bf16[3,48,384]{2,1,0:T(8,128)(2,1)S(1)}, u32[]{:S(2)}, u32[]{:S(2)}) collective-permute-start(bf16[3,48,384]{2,1,0:T(8,128)(2,1)S(1)} %get-tuple-element.225), channel_id=1, source_target_pairs={{0,4},{4,0},{8,12},{12,8},{16,20},{20,16},{24,28},{28,24},{1,5},{5... | collective-permute-start | bytes 331784 | tf_op jit(solution)/shard_map/ppermute | solution.py:816
  429.3 16.6 %collective-permute-start.35 = (bf16[2,96,384]{2,1,0:T(8,128)(2,1)S(1)}, bf16[2,96,384]{2,1,0:T(8,128)(2,1)S(1)}, u32[]{:S(2)}, u32[]{:S(2)}) collective-permute-start(bf16[2,96,384]{2,1,0:T(8,128)(2,1)S(1)} %fusion.34), channel_id=1, source_target_pairs={{0,16},{4,20},{8,24},{12,28},{16,0},{20,4},{24,8},{28,12},{1,17},{... | collective-permute-start | bytes 442376 | tf_op jit(solution)/shard_map/ppermute | solution.py:816
  439.4 16.5 %collective-permute-start.33 = (bf16[2,96,384]{2,1,0:T(8,128)(2,1)S(1)}, bf16[2,96,384]{2,1,0:T(8,128)(2,1)S(1)}, u32[]{:S(2)}, u32[]{:S(2)}) collective-permute-start(bf16[2,96,384]{2,1,0:T(8,128)(2,1)S(1)} %fusion.32), channel_id=1, source_target_pairs={{0,16},{4,20},{8,24},{12,28},{16,0},{20,4},{24,8},{28,12},{1,17},{... | collective-permute-start | bytes 442376 | tf_op jit(solution)/shard_map/ppermute | solution.py:816
  442.4 14.4 %collective-permute-start.26 = (bf16[3,48,384]{2,1,0:T(8,128)(2,1)S(1)}, bf16[3,48,384]{2,1,0:T(8,128)(2,1)S(1)}, u32[]{:S(2)}, u32[]{:S(2)}) collective-permute-start(bf16[3,48,384]{2,1,0:T(8,128)(2,1)S(1)} %add_convert_fusion.14.refs_0_), channel_id=1, source_target_pairs={{0,4},{4,0},{8,12},{12,8},{16,20},{20,16},{24,28},{28,24},{1,5},{5... | collective-permute-start | bytes 331784 | tf_op jit(solution)/shard_map/ppermute | solution.py:816
  442.5 14.5 %collective-permute-start.27 = (bf16[3,48,384]{2,1,0:T(8,128)(2,1)S(1)}, bf16[3,48,384]{2,1,0:T(8,128)(2,1)S(1)}, u32[]{:S(2)}, u32[]{:S(2)}) collective-permute-start(bf16[3,48,384]{2,1,0:T(8,128)(2,1)S(1)} %add_convert_fusion.14.refs_0_), channel_id=1, source_target_pairs={{0,8},{4,12},{8,0},{12,4},{16,24},{20,28},{24,16},{28,20},{1,9},{5... | collective-permute-start | bytes 331784 | tf_op jit(solution)/shard_map/ppermute | solution.py:816
  445.9 15.4 %collective-permute-start.28 = (bf16[3,48,384]{2,1,0:T(8,128)(2,1)S(1)}, bf16[3,48,384]{2,1,0:T(8,128)(2,1)S(1)}, u32[]{:S(2)}, u32[]{:S(2)}) collective-permute-start(bf16[3,48,384]{2,1,0:T(8,128)(2,1)S(1)} %add_convert_fusion.14.refs_0_), channel_id=1, source_target_pairs={{0,12},{4,8},{8,4},{12,0},{16,28},{20,24},{24,20},{28,16},{1,13},{... | collective-permute-start | bytes 331784 | tf_op jit(solution)/shard_map/ppermute | solution.py:816
  450.4 16.0 %collective-permute-start.29 = (bf16[3,48,384]{2,1,0:T(8,128)(2,1)S(1)}, bf16[3,48,384]{2,1,0:T(8,128)(2,1)S(1)}, u32[]{:S(2)}, u32[]{:S(2)}) collective-permute-start(bf16[3,48,384]{2,1,0:T(8,128)(2,1)S(1)} %add_convert_fusion.14.refs_0_), channel_id=1, source_target_pairs={{0,16},{4,20},{8,24},{12,28},{16,0},{20,4},{24,8},{28,12},{1,17},{... | collective-permute-start | bytes 331784 | tf_op jit(solution)/shard_map/ppermute | solution.py:816
  455.9 14.3 %collective-permute-start.30 = (bf16[3,48,384]{2,1,0:T(8,128)(2,1)S(1)}, bf16[3,48,384]{2,1,0:T(8,128)(2,1)S(1)}, u32[]{:S(2)}, u32[]{:S(2)}) collective-permute-start(bf16[3,48,384]{2,1,0:T(8,128)(2,1)S(1)} %add_convert_fusion.14.refs_0_), channel_id=1, source_target_pairs={{0,20},{4,16},{8,28},{12,24},{16,4},{20,0},{24,12},{28,8},{1,21},{... | collective-permute-start | bytes 331784 | tf_op jit(solution)/shard_map/ppermute | solution.py:816
  456.9 13.3 %collective-permute-start.31 = (bf16[3,48,384]{2,1,0:T(8,128)(2,1)S(1)}, bf16[3,48,384]{2,1,0:T(8,128)(2,1)S(1)}, u32[]{:S(2)}, u32[]{:S(2)}) collective-permute-start(bf16[3,48,384]{2,1,0:T(8,128)(2,1)S(1)} %add_convert_fusion.14.refs_0_), channel_id=1, source_target_pairs={{0,24},{4,28},{8,16},{12,20},{16,8},{20,12},{24,0},{28,4},{1,25},{... | collective-permute-start | bytes 331784 | tf_op jit(solution)/shard_map/ppermute | solution.py:816
  481.8 90.1 %collective-permute-start.38 = (bf16[512,768]{1,0:T(8,128)(2,1)}, bf16[512,768]{1,0:T(8,128)(2,1)}, u32[]{:S(2)}, u32[]{:S(2)}) collective-permute-start(bf16[512,768]{1,0:T(8,128)(2,1)} %slice.309), channel_id=1, source_target_pairs={{0,2},{1,3},{2,0},{3,1},{4,6},{5,7},{6,4},{7,5},{8,10},{9,11},{10,... | collective-permute-start | bytes 2359304 | tf_op jit(solution)/shard_map/ppermute | solution.py:816
  (54 other events, 697.1 us)
Sparse Core Ops, SparseCore 0:
  11.5 115.2 all-gather.5
  406.3 67.8 all-gather.7

commit v5 on v4

--- a/solution.py
+++ b/solution.py
@@ -821,18 +821,25 @@
 
 
 class Halving:
-    def __init__(self, kept, got, names):
-        self.kept, self.got, self.names = kept, got, list(names)
+    def __init__(self, kept, got, names, slots=None):
+        self.kept, self.got, self.names, self.slots = kept, got, list(names), slots
 
     def take(self, name, index):
-        at = (slice(None),) * self.names.index(name) + (index,)
-        return add_low(self.kept[at], self.got[at])
+        axis = self.names.index(name)
+        found = []
+        for array in (self.kept, self.got):
+            starts, limits = [0] * array.ndim, list(array.shape)
+            starts[axis], limits[axis] = index, index + 1
+            if self.slots is not None:
+                starts[-3], limits[-3] = self.slots
+            part = lax.slice(array, starts, limits)
+            found.append(part.reshape(part.shape[:axis] + part.shape[axis + 1 :]))
+        return add_low(*found)
 
     def send(self, name):
         sent, kept = self.take(name, 1), self.take(name, 0)
         self.names.remove(name)
-        self.kept = kept
-        self.sent, self.name = sent, name
+        self.kept, self.slots, self.name = kept, None, name
         return sent
 
     def receive(self, sent):
@@ -893,11 +900,13 @@
 
     products = stats_product(left_stats, right_stats, left_basis, right_basis)
 
-    pair = jnp.stack([tokens, cotangent])
-    kept = lax.dynamic_index_in_dim(pair, chip, 1, keepdims=False)
-    got = swap(lax.dynamic_index_in_dim(pair, 1 - chip, 1, keepdims=False), "seq", 2)
-    x = jnp.concatenate([kept[0], got[0]], axis=0)
-    dy = jnp.concatenate([kept[1], got[1]], axis=0)
+    def halves_of(pair):
+        kept = lax.dynamic_index_in_dim(pair, chip, 0, keepdims=False)
+        return kept, lax.dynamic_index_in_dim(pair, 1 - chip, 0, keepdims=False)
+
+    kept, sent = halves_of(tokens)
+    x = jnp.concatenate([kept, swap(sent, "seq", 2)], axis=0)
+    dy_kept, dy_sent = halves_of(cotangent)
 
     def to_positions(mine, other):
         return jnp.where(chip == 0, jnp.stack([mine, other]), jnp.stack([other, mine]))
@@ -910,10 +919,13 @@
     fill = jnp.broadcast_to(fill[:, None], (fill.shape[0], 128))
 
     bias = jnp.concatenate([vec[4], jnp.zeros_like(vec[4]), vec[5]])[None, :]
-    gathered, products = lax.optimization_barrier((gathered, products))
+    gathered, products, dy_sent = lax.optimization_barrier((gathered, products, dy_sent))
+    dy_got = swap(dy_sent, "seq", 2)
     q, kv, normed = qkv_forward(owners, slots, x, vec, bias, gathered)
     other = swap(kv, "seq", 1)
     attn, lse = attn_forward(q, kv, other, fill)
+    attn, dy_got = lax.optimization_barrier((attn, dy_got))
+    dy = jnp.concatenate([dy_kept, dy_got], axis=0)
     b1 = vec[8:].reshape(1, FF)
     seq_of, dp_of = seq_id.reshape(1), dp_id.reshape(1)
     result, d_mid, d_attn, keep, send, sums_two, bias_grad = mid_layer(
@@ -931,14 +943,11 @@
     shape = (2,) * (1 + bits) + keep.shape[2:]
     keep, got = keep.reshape(shape), swap(send, "seq", 1).reshape(shape)
     groups = [
-        Halving(keep[..., per * g : per * g + per, :, :], got, names) for g in range(len(plans))
+        Halving(keep, got, names, (per * g, per * g + per)) for g in range(len(plans))
     ]
     guard = fill
 
     def advance(step, guard):
-        if step == 0:
-            for g, group in enumerate(groups):
-                group.got = group.got[..., per * g : per * g + per, :, :]
         sent = [group.send(plan[step]) for group, plan in zip(groups, plans, strict=True)]
         *sent, guard = lax.optimization_barrier((*sent, guard))
         for group, array in zip(groups, sent, strict=True):
@@ -969,16 +978,26 @@
     late_keep, late_send, cols = qkv_grad(seq_of, normed, halves)
     late_shape = (2, -1, quarter, BLK)
     late = Halving(late_keep.reshape(late_shape), swap(late_send.reshape(late_shape), "seq", 1), ["x"])
+
+    def after(value):
+        got, value = lax.optimization_barrier(([group.got for group in groups], value))
+        for group, array in zip(groups, got, strict=True):
+            group.got = array
+        return value
+
     late.receive(late.send("x"))
-    d_x, sums_one = qkv_backward(owners, slots, x, d_mid, vec, halves, gathered)
-    got, late.got, d_x = lax.optimization_barrier(([group.got for group in groups], late.got, d_x))
-    for group, array in zip(groups, got, strict=True):
-        group.got = array
-    d_x_other = swap(d_x[part_len:], "seq", 2)
+    cols = after(cols)
     while taken < len(names):
         advance(taken, fill)
         taken += 1
+    d_x, sums_one = qkv_backward(owners, slots, x, d_mid, vec, halves, gathered)
+    late.got, d_x = lax.optimization_barrier((late.got, d_x))
+    d_x = after(d_x)
+    d_x_other = swap(d_x[part_len:], "seq", 2)
     early = jnp.concatenate([group.total() for group in groups], axis=0)
+    output = to_positions(result[:part_len], result_other)
+    d_tokens = to_positions(d_x[:part_len], d_x_other)
+    early, output, d_tokens = lax.optimization_barrier((early, output, d_tokens))
 
     mine_from = lax.dynamic_slice_in_dim(sources, dp_id * slot_count, slot_count)
     if 2 * first_blocks % owner_count == 0:
@@ -999,6 +1018,9 @@
         piece = jnp.where((mine_from < first_blocks)[:, None, None], owned.total(), early)
     state = (master, moment_one, moment_two, left_stats, right_stats, left_basis, right_basis)
     piece = jnp.where((mine_from < owners.shape[0])[:, None, None], piece, jnp.zeros_like(piece))
+    piece, sums_one, sums_two, cols, bias_grad = lax.optimization_barrier(
+        (piece, sums_one, sums_two, cols, bias_grad)
+    )
     updates = soap_update(seq_of, quarters(piece), state, products)
 
     vec_grad = jnp.concatenate(
@@ -1013,11 +1035,7 @@
         axis=0,
     )
     vec_parts = lax.all_gather(vec_grad, AXES, axis=0, tiled=False)
-    updates, vec_parts, d_x, d_x_other, result, result_other = lax.optimization_barrier(
-        (updates, vec_parts, d_x, d_x_other, result, result_other)
-    )
-    output = to_positions(result[:part_len], result_other)
-    d_tokens = to_positions(d_x[:part_len], d_x_other)
+    updates, vec_parts = lax.optimization_barrier((updates, vec_parts))
     vec_total = jnp.sum(vec_parts, axis=0)
     vec_first, vec_second, vec_next = adam_vectors(vec_total, vec, vec_one, vec_two)
     grad_blocks, w_new, one_new, two_new, ls_new, rs_new, lb_new, rb_new = updates

time: 600 us -> 575 us (0.958)
  waiting for transfers between devices: 132 us -> 114 us
  starting transfers between devices: 43.3 us -> 53.2 us
  local copies, waits for them, and re-layouts: 37.6 us -> 30.2 us
  other arithmetic: 41.5 us -> 35.2 us
    ppermute x39 -> x40, waiting for transfers between devices: 65.9 us -> 32.2 us  [swap(): return lax.ppermute(x, axis, [(i, i ^ bit) for i in range(size)])]
    all_gather x1, waiting for transfers between devices: 66.5 us -> 81.9 us  [on_device(): lax.all_gather(mine, AXES, axis=0, tiled=False)]
    ppermute x39 -> x40, starting transfers between devices: 43.2 us -> 53.2 us  [swap(): return lax.ppermute(x, axis, [(i, i ^ bit) for i in range(size)])]
    unnamed x93 -> x103, local copies, waits for them, and re-layouts: 15 us -> 12.6 us
  transfers between devices with their start and end apart: 41 -> 42, of which waited for: 12 -> 17; matrix products, arithmetic and copies ran while one was open for 7% -> 5% of each run, Pallas kernels for 33% -> 43%
where the time goes in v5:
time: 575 us; the launch traced here: 566 us
  Pallas kernels  318 us (55%)
  waiting for transfers between devices  114 us (20%)
  starting transfers between devices  53.2 us (9%)
  other arithmetic  35.2 us (6%)
  local copies, waits for them, and re-layouts  30.2 us (5%)
  between operations  15.3 us (3%)
    pallas_call x1, Pallas kernels, soap_update(): pl.pallas_call(soap_kernel, grid_spec=pltpu.PrefetchScalarGridSpec(num_sc...  87.2 us
    pallas_call x4, Pallas kernels, attn_backward(): pl.pallas_call(kernel, grid=(count, rows // q_rows), in_specs=[q_spec, k_...  82.1 us
    all_gather x1, waiting for transfers between devices, on_device(): lax.all_gather(mine, AXES, axis=0, tiled=False)  81.9 us
    pallas_call x1, Pallas kernels, mid_layer(): pl.pallas_call(functools.partial(mid_kernel, chunk=chunk), grid_spec=pltp...  58 us
    ppermute x40, starting transfers between devices, swap(): return lax.ppermute(x, axis, [(i, i ^ bit) for i in range(size)])  53.2 us
    pallas_call x1, Pallas kernels, attn_forward(): pl.pallas_call(attn_fwd_kernel, grid=(pairs, rows // q_rows), in_specs=[q...  47.3 us
    ppermute x40, waiting for transfers between devices, swap(): return lax.ppermute(x, axis, [(i, i ^ bit) for i in range(size)])  32.2 us
    convert_element_type x17, other arithmetic, add_low(): return (a.astype(F32) + b.astype(F32)).astype(LOW)  24.4 us
  transfers between devices with their start and end apart: 42, of which 17 were waited for; matrix products, arithmetic and copies ran while one was open for 5% of the time, Pallas kernels for 43%

profile of v5, /device:TPU:0, one launch (start us, length us, event | category | flops | bytes accessed | tf_op | source)
XLA Modules:
  0.0 566.1 jit_solution(17441636725036701243)
XLA Ops:
  10.9 3.0 collective-permute-start
  16.8 2.0 copy-done.6
  20.9 12.1 %stats.1 = (f32[6,384,384]{2,1,0:T(8,128)S(1)}, f32[6,384,384]{2,1,0:T(8,128)S(1)}) custom-call(f32[6,384,384]{2,1,0:T(8,128)S(1)} %copy-done.4, f32[6,384,384]{2,1,0:T(8,128)S(1)} %copy-done.5, f32[6,384,384]{2,1,0:T(8,128)S(1)} %copy-done.6, f32[6,384,384]{2,1,0:T(8,128)S(1)} %copy-done.7), custom_call_target="tpu_custom_call" | custom-call | tf_op jit(solution)/shard_map/stats/pallas_call | solution.py:649
  38.0 81.9 %all-gather.6.cloned.1.call-done = bf16[192,1,96,384]{3,2,1,0:T(8,128)(2,1)} async-done(((bf16[6,1,96,384]{3,2,1,0:T(8,128)(2,1)}), bf16[192,1,96,384]{3,2,1,0:T(8,128)(2,1)}) %all-gather.6.cloned.1.call-update) | async-done | bytes 14155792 | tf_op jit(solution)/shard_map/all_gather | solution.py:897
  119.9 9.1 %qkv.1 = (bf16[1024,768]{1,0:T(8,128)(2,1)S(1)}, bf16[1024,1536]{1,0:T(8,128)(2,1)}, bf16[1024,768]{1,0:T(8,128)(2,1)S(1)}) custom-call(s32[48]{0:T(128)S(1)} %copy-done.20, s32[48]{0:T(128)S(1)} %convert_reduce_fusion.slot, bf16[1024,768]{1,0:T(8,128)(2,1)S(1)} %pad_maximum_fusion.x_ref, f32[12,768]{1,0:T(8,128)S(1)} %copy-done.18, ...), custom_call_target="tpu_custom_call" | custom-call | tf_op jit(solution)/shard_map/qkv/pallas_call | solution.py:130
  136.5 47.3 %attn_fwd.1 = (bf16[1024,768]{1,0:T(8,128)(2,1)S(1)}, f32[1024,768]{1,0:T(8,128)}) custom-call(bf16[1024,768]{1,0:T(8,128)(2,1)S(1)} %get-tuple-element.155.q_ref.refs_0_, bf16[1024,1536]{1,0:T(8,128)(2,1)} %get-tuple-element.156.k1.v1.refs_1_.refs_2_, bf16[1024,1536]{1,0:T(8,128)(2,1)} %get-tuple-element.156.k1.v1.refs_1_.refs_2_, ...), custom_call_target="tpu_custom_call" | custom-call | tf_op jit(solution)/shard_map/attn_fwd/pallas_call | solution.py:195
  185.5 58.0 %mid.1 = (bf16[1024,768]{1,0:T(8,128)(2,1)}, f32[1024,768]{1,0:T(8,128)}, bf16[1024,768]{1,0:T(8,128)(2,1)}, bf16[2,8,6,96,384]{4,3,2,1,0:T(8,128)(2,1)}, bf16[2...) custom-call(s32[48]{0:T(128)} %own.5, s32[48]{0:T(128)} %copy-done.21, ...), custom_call_target="tpu_custom_call" | custom-call | tf_op jit(solution)/shard_map/mid/pallas_call | solution.py:470
  243.8 2.4 slice_bitcast_fusion.4
  247.6 26.2 %attn_bwd.4 = (bf16[1024,384]{1,0:T(8,128)(2,1)}, bf16[1024,384]{1,0:T(8,128)(2,1)}, bf16[1024,384]{1,0:T(8,128)(2,1)}, bf16[1024,384]{1,0:T(8,128)(2,1)}, bf16[1024,384]{1,0:T(8,128)(2,1)}) custom-call(bf16[1024,768]{1,0:T(8,128)(2,1)} %copy-done.1, bf16[1024,1536]{1,0:T(8,128)(2,1)} %get-tuple-element.156.k1.v1.refs_1_.refs_2_, ...), custom_call_target="tpu_custom_call" | custom-call | tf_op jit(solution)/shard_map/attn_bwd/pallas_call | solution.py:323
  277.7 2.6 fusion.5
  282.1 2.2 fusion.6
  286.9 26.8 %attn_bwd.6 = (bf16[1024,384]{1,0:T(8,128)(2,1)}, bf16[1024,384]{1,0:T(8,128)(2,1)}, bf16[1024,384]{1,0:T(8,128)(2,1)}, bf16[1024,384]{1,0:T(8,128)(2,1)}, bf16[1024,384]{1,0:T(8,128)(2,1)}) custom-call(bf16[1024,768]{1,0:T(8,128)(2,1)} %copy-done.1, bf16[1024,1536]{1,0:T(8,128)(2,1)} %get-tuple-element.156.k1.v1.refs_1_.refs_2_, ...), custom_call_target="tpu_custom_call" | custom-call | tf_op jit(solution)/shard_map/attn_bwd/pallas_call | solution.py:323
  313.7 14.7 %attn_bwd.5 = (bf16[1024,384]{1,0:T(8,128)(2,1)}, bf16[1024,384]{1,0:T(8,128)(2,1)}, bf16[1024,384]{1,0:T(8,128)(2,1)}, bf16[1024,384]{1,0:T(8,128)(2,1)}, bf16[1024,384]{1,0:T(8,128)(2,1)}) custom-call(bf16[1024,768]{1,0:T(8,128)(2,1)} %copy-done.1, ...), custom_call_target="tpu_custom_call", output_to_operand_aliasing={{0}: (9, {}), {1}: (10, {}), {2}: (11, {}), {3}: (12, {}), ... | custom-call | tf_op jit(solution)/shard_map/attn_bwd/pallas_call | solution.py:323
  331.5 2.5 fusion.10
  339.6 14.4 %attn_bwd.7 = (bf16[1024,384]{1,0:T(8,128)(2,1)}, bf16[1024,384]{1,0:T(8,128)(2,1)}, bf16[1024,384]{1,0:T(8,128)(2,1)}, bf16[1024,384]{1,0:T(8,128)(2,1)}, bf16[1024,384]{1,0:T(8,128)(2,1)}) custom-call(bf16[1024,768]{1,0:T(8,128)(2,1)} %copy-done.1, ...), custom_call_target="tpu_custom_call", output_to_operand_aliasing={{0}: (9, {}), {1}: (10, {}), {2}: (11, {}), {3}: (12, {}), ... | custom-call | tf_op jit(solution)/shard_map/attn_bwd/pallas_call | solution.py:323
  358.6 8.0 %qkv_grad.1 = (bf16[2,2,6,96,384]{4,3,2,1,0:T(8,128)(2,1)}, bf16[2,2,6,96,384]{4,3,2,1,0:T(8,128)(2,1)}, f32[1,2304]{1,0:T(1,128)S(1)}) custom-call(s32[1]{0:T(128)} %bitcast.seq.seq_ref, bf16[1024,768]{1,0:T(8,128)(2,1)} %copy-done.17, bf16[1024,384]{1,0:T(8,128)(2,1)S(1)} %copy-done.10, bf16[1024,384]{1,0:T(8,128)(2,1)S(1)} %copy-done.11, ...), custom_call_target="tpu_custom_call" | custom-call | tf_op jit(solution)/shard_map/qkv_grad/pallas_call | solution.py:542
  370.0 2.9 maximum_select_fusion
  372.8 3.7 collective-permute-done.11
  388.7 13.3 %qkv_bwd.1 = (bf16[1024,768]{1,0:T(8,128)(2,1)}, f32[8,768]{1,0:T(8,128)}) custom-call(s32[48]{0:T(128)} %own.5, s32[48]{0:T(128)} %copy-done.21, bf16[1024,768]{1,0:T(8,128)(2,1)} %copy-done.2, f32[1024,768]{1,0:T(8,128)} %get-tuple-element.243.dmid_ref, f32[12,768]{1,0:T(8,128)} %vec_ref.5, bf16[1024,384]{1,0:T(8,128)(2,1)} %get-tuple-element.224.refs_0_, ...), custom_call_target="tpu_custom_call" | custom-call | tf_op jit(solution)/shard_map/qkv_bwd/pallas_call | solution.py:584
  403.5 2.3 collective-permute-done.20
  407.9 3.3 collective-permute-start.30
  413.7 3.0 collective-permute-start.27
  416.7 7.3 %collective-permute-start.26 = (bf16[3,48,384]{2,1,0:T(8,128)(2,1)S(1)}, bf16[3,48,384]{2,1,0:T(8,128)(2,1)S(1)}, u32[]{:S(2)}, u32[]{:S(2)}) collective-permute-start(bf16[3,48,384]{2,1,0:T(8,128)(2,1)S(1)} %get-tuple-element.257), channel_id=1, source_target_pairs={{0,12},{4,8},{8,4},{12,0},{16,28},{20,24},{24,20},{28,16},{1,13},{... | collective-permute-start | bytes 331784 | tf_op jit(solution)/shard_map/ppermute | solution.py:816
  424.0 2.1 collective-permute-start.25
  432.9 2.4 collective-permute-start.31
  438.0 3.3 collective-permute-start.35
  442.0 2.7 collective-permute-start.37
  446.0 4.6 collective-permute-done.34.refs_4_
  450.7 2.5 collective-permute-done.35.refs_5_
  458.7 7.0 %collective-permute-done.38.g1 = bf16[6,96,384]{2,1,0:T(8,128)(2,1)S(1)} collective-permute-done((bf16[6,96,384]{2,1,0:T(8,128)(2,1)S(1)}, bf16[6,96,384]{2,1,0:T(8,128)(2,1)S(1)}, u32[]{:S(2)}, u32[]{:S(2)}) %collective-permute-start.38) | collective-permute-done | bytes 442400 | tf_op jit(solution)/shard_map/ppermute | solution.py:816
  465.9 2.4 collective-permute-done.39
  469.4 87.2 %soap.1 = (f32[6,384,384]{2,1,0:T(8,128)}, f32[6,384,384]{2,1,0:T(8,128)}, f32[6,384,384]{2,1,0:T(8,128)}, f32[6,384,384]{2,1,0:T(8,128)}, f32[6,384,384]{2,1,0:...) custom-call(s32[1]{0:T(128)} %bitcast.seq.seq_ref, ...), custom_call_target="tpu_custom_call" | custom-call | tf_op jit(solution)/shard_map/soap/pallas_call | solution.py:729
  (233 shorter events, 87.9 us)
Async XLA Ops:
  7.2 112.7 %all-gather.6.cloned.1.call-start = ((), (), s32[]{:S(2)}) async-start(), calls=%async_computation | async-start | bytes 14598144 | tf_op jit(solution)/shard_map/all_gather | solution.py:897
  9.2 547.4 %all-gather.8.cloned.1.call-start = ((), (), s32[]{:S(2)}) async-start(), calls=%async_computation.1 | async-start | bytes 1622016 | tf_op jit(solution)/shard_map/all_gather | solution.py:1037
  10.9 27.0 %collective-permute-start = (bf16[512,768]{1,0:T(8,128)(2,1)S(1)}, bf16[512,768]{1,0:T(8,128)(2,1)S(1)}, u32[]{:S(2)}, u32[]{:S(2)}) collective-permute-start(bf16[512,768]{1,0:T(8,128)(2,1)S(1)} %get-tuple-element.323), channel_id=1, source_target_pairs={{0,2},{1,3},{2,0},{3,1},{4,6},{5,7},{6,4},{7,5},{8,10},{9,11},{10,... | collective-permute-start | bytes 2359304 | tf_op jit(solution)/shard_map/ppermute | solution.py:816
  131.2 52.6 %collective-permute-start.2 = (bf16[512,768]{1,0:T(8,128)(2,1)}, bf16[512,768]{1,0:T(8,128)(2,1)S(1)}, u32[]{:S(2)}, u32[]{:S(2)}) collective-permute-start(bf16[512,768]{1,0:T(8,128)(2,1)} %get-tuple-element.158), channel_id=1, source_target_pairs={{0,2},{1,3},{2,0},{3,1},{4,6},{5,7},{6,4},{7,5},{8,10},{9,11},{10,... | collective-permute-start | bytes 2359304 | tf_op jit(solution)/shard_map/ppermute | solution.py:816
  243.5 34.3 %collective-permute-start.3 = (bf16[2,8,6,96,384]{4,3,2,1,0:T(8,128)(2,1)}, bf16[2,8,6,96,384]{4,3,2,1,0:T(8,128)(2,1)S(1)}, u32[]{:S(2)}, u32[]{:S(2)}) collective-permute-start(bf16[2,8,6,96,384]{4,3,2,1,0:T(8,128)(2,1)} %get-tuple-element.162), channel_id=1, source_target_pairs={{0,1},{1,0},{2,3},{3,2},{4,5},{5,4},{6,7},{7,6},{8,9},{9,8},{10,11... | collective-permute-start | bytes 21233672 | tf_op jit(solution)/shard_map/ppermute | solution.py:816
  246.1 31.6 %collective-permute-start.4 = (bf16[512,768]{1,0:T(8,128)(2,1)S(1)}, bf16[512,768]{1,0:T(8,128)(2,1)}, u32[]{:S(2)}, u32[]{:S(2)}) collective-permute-start(bf16[512,768]{1,0:T(8,128)(2,1)S(1)} %get-tuple-element.319), channel_id=1, source_target_pairs={{0,2},{1,3},{2,0},{3,1},{4,6},{5,7},{6,4},{7,5},{8,10},{9,11},{10,... | collective-permute-start | bytes 2359304 | tf_op jit(solution)/shard_map/ppermute | solution.py:816
  284.2 45.7 %collective-permute-start.5 = (bf16[2,2,2,2,96,384]{5,4,3,1,0,2:T(8,128)(2,1)}, bf16[2,2,2,2,96,384]{5,4,3,1,0,2:T(8,128)(2,1)}, u32[]{:S(2)}, u32[]{:S(2)}) collective-permute-start(bf16[2,2,2,2,96,384]{5,4,3,1,0,2:T(8,128)(2,1)} %get-tuple-element.174), channel_id=1, source_target_pairs={{0,2},{1,3},{2,0},{3,1},{4,6},{5,7},{6,4},{7,5},{8,10},{9,11},{10,... | collective-permute-start | bytes 3538952 | tf_op jit(solution)/shard_map/ppermute | solution.py:816
  284.8 45.1 %collective-permute-start.6 = (bf16[2,2,2,2,96,384]{5,4,3,1,2,0:T(8,128)(2,1)}, bf16[2,2,2,2,96,384]{5,4,3,1,2,0:T(8,128)(2,1)}, u32[]{:S(2)}, u32[]{:S(2)}) collective-permute-start(bf16[2,2,2,2,96,384]{5,4,3,1,2,0:T(8,128)(2,1)} %get-tuple-element.175), channel_id=1, source_target_pairs={{0,4},{4,0},{8,12},{12,8},{16,20},{20,16},{24,28},{28,24},{1,5},{5... | collective-permute-start | bytes 3538952 | tf_op jit(solution)/shard_map/ppermute | solution.py:816
  286.3 43.6 %collective-permute-start.7 = (bf16[2,2,2,2,96,384]{5,4,3,2,1,0:T(8,128)(2,1)}, bf16[2,2,2,2,96,384]{5,4,3,2,1,0:T(8,128)(2,1)}, u32[]{:S(2)}, u32[]{:S(2)}) collective-permute-start(bf16[2,2,2,2,96,384]{5,4,3,2,1,0:T(8,128)(2,1)} %fusion.5), channel_id=1, source_target_pairs={{0,8},{4,12},{8,0},{12,4},{16,24},{20,28},{24,16},{28,20},{1,9},{5... | collective-permute-start | bytes 3538952 | tf_op jit(solution)/shard_map/ppermute | solution.py:816
  335.6 18.4 %collective-permute-start.8 = (bf16[2,2,2,96,384]{4,3,2,1,0:T(8,128)(2,1)}, bf16[2,2,2,96,384]{4,3,2,1,0:T(8,128)(2,1)S(1)}, u32[]{:S(2)}, u32[]{:S(2)}) collective-permute-start(bf16[2,2,2,96,384]{4,3,2,1,0:T(8,128)(2,1)} %get-tuple-element.201), channel_id=1, source_target_pairs={{0,4},{4,0},{8,12},{12,8},{16,20},{20,16},{24,28},{28,24},{1,5},{5... | collective-permute-start | bytes 1769480 | tf_op jit(solution)/shard_map/ppermute | solution.py:816
  336.2 17.8 %collective-permute-start.9 = (bf16[2,2,2,96,384]{4,3,2,1,0:T(8,128)(2,1)S(1)}, bf16[2,2,2,96,384]{4,3,2,1,0:T(8,128)(2,1)S(1)}, u32[]{:S(2)}, u32[]{:S(2)}) collective-permute-start(bf16[2,2,2,96,384]{4,3,2,1,0:T(8,128)(2,1)S(1)} %get-tuple-element.202), channel_id=1, source_target_pairs={{0,8},{4,12},{8,0},{12,4},{16,24},{20,28},{24,16},{28,20},{1,9},{5... | collective-permute-start | bytes 1769480 | tf_op jit(solution)/shard_map/ppermute | solution.py:816
  337.7 16.4 %collective-permute-start.10 = (bf16[2,2,2,96,384]{4,3,2,1,0:T(8,128)(2,1)S(1)}, bf16[2,2,2,96,384]{4,3,2,1,0:T(8,128)(2,1)S(1)}, u32[]{:S(2)}, u32[]{:S(2)}) collective-permute-start(bf16[2,2,2,96,384]{4,3,2,1,0:T(8,128)(2,1)S(1)} %get-tuple-element.203), channel_id=1, source_target_pairs={{0,2},{1,3},{2,0},{3,1},{4,6},{5,7},{6,4},{7,5},{8,10},{9,11},{10,... | collective-permute-start | bytes 1769480 | tf_op jit(solution)/shard_map/ppermute | solution.py:816
  339.1 17.6 %collective-permute-start.14 = (bf16[1024,384]{1,0:T(8,128)(2,1)S(1)}, bf16[1024,384]{1,0:T(8,128)(2,1)S(1)}, u32[]{:S(2)}, u32[]{:S(2)}) collective-permute-start(bf16[1024,384]{1,0:T(8,128)(2,1)S(1)} %copy-done.38), channel_id=1, source_target_pairs={{0,1},{1,0},{2,3},{3,2},{4,5},{5,4},{6,7},{7,6},{8,9},{9,8},{10,11... | collective-permute-start | bytes 2359304 | tf_op jit(solution)/shard_map/ppermute | solution.py:816
  339.1 17.6 %collective-permute-start.15 = (bf16[1024,384]{1,0:T(8,128)(2,1)}, bf16[1024,384]{1,0:T(8,128)(2,1)S(1)}, u32[]{:S(2)}, u32[]{:S(2)}) collective-permute-start(bf16[1024,384]{1,0:T(8,128)(2,1)} %get-tuple-element.228), channel_id=1, source_target_pairs={{0,1},{1,0},{2,3},{3,2},{4,5},{5,4},{6,7},{7,6},{8,9},{9,8},{10,11... | collective-permute-start | bytes 2359304 | tf_op jit(solution)/shard_map/ppermute | solution.py:816
  366.7 10.7 %collective-permute-start.21 = (bf16[2,12,96,384]{3,2,1,0:T(8,128)(2,1)}, bf16[2,12,96,384]{3,2,1,0:T(8,128)(2,1)S(1)}, u32[]{:S(2)}, u32[]{:S(2)}) collective-permute-start(bf16[2,12,96,384]{3,2,1,0:T(8,128)(2,1)} %bitcast.191), channel_id=1, source_target_pairs={{0,1},{1,0},{2,3},{3,2},{4,5},{5,4},{6,7},{7,6},{8,9},{9,8},{10,11... | collective-permute-start | bytes 5308424 | tf_op jit(solution)/shard_map/ppermute | solution.py:816
  367.1 9.5 %collective-permute-start.11 = (bf16[2,2,96,384]{3,2,1,0:T(8,128)(2,1)S(1)}, bf16[2,2,96,384]{3,2,1,0:T(8,128)(2,1)}, u32[]{:S(2)}, u32[]{:S(2)}) collective-permute-start(bf16[2,2,96,384]{3,2,1,0:T(8,128)(2,1)S(1)} %get-tuple-element.220), channel_id=1, source_target_pairs={{0,8},{4,12},{8,0},{12,4},{16,24},{20,28},{24,16},{28,20},{1,9},{5... | collective-permute-start | bytes 884744 | tf_op jit(solution)/shard_map/ppermute | solution.py:816
  367.8 9.1 %collective-permute-start.12 = (bf16[2,2,96,384]{3,2,1,0:T(8,128)(2,1)S(1)}, bf16[2,2,96,384]{3,2,1,0:T(8,128)(2,1)}, u32[]{:S(2)}, u32[]{:S(2)}) collective-permute-start(bf16[2,2,96,384]{3,2,1,0:T(8,128)(2,1)S(1)} %get-tuple-element.221), channel_id=1, source_target_pairs={{0,2},{1,3},{2,0},{3,1},{4,6},{5,7},{6,4},{7,5},{8,10},{9,11},{10,... | collective-permute-start | bytes 884744 | tf_op jit(solution)/shard_map/ppermute | solution.py:816
  368.4 8.8 %collective-permute-start.13 = (bf16[2,2,96,384]{3,2,1,0:T(8,128)(2,1)S(1)}, bf16[2,2,96,384]{3,2,1,0:T(8,128)(2,1)}, u32[]{:S(2)}, u32[]{:S(2)}) collective-permute-start(bf16[2,2,96,384]{3,2,1,0:T(8,128)(2,1)S(1)} %get-tuple-element.222), channel_id=1, source_target_pairs={{0,4},{4,0},{8,12},{12,8},{16,20},{20,16},{24,28},{28,24},{1,5},{5... | collective-permute-start | bytes 884744 | tf_op jit(solution)/shard_map/ppermute | solution.py:816
  378.7 23.7 %collective-permute-start.22 = (bf16[12,96,384]{2,1,0:T(8,128)(2,1)}, bf16[12,96,384]{2,1,0:T(8,128)(2,1)S(1)}, u32[]{:S(2)}, u32[]{:S(2)}) collective-permute-start(bf16[12,96,384]{2,1,0:T(8,128)(2,1)} %fusion.1), channel_id=1, source_target_pairs={{0,2},{1,3},{2,0},{3,1},{4,6},{5,7},{6,4},{7,5},{8,10},{9,11},{10,... | collective-permute-start | bytes 2654216 | tf_op jit(solution)/shard_map/ppermute | solution.py:816
  384.3 18.1 %collective-permute-start.18 = (bf16[2,96,384]{2,1,0:T(8,128)(2,1)}, bf16[2,96,384]{2,1,0:T(8,128)(2,1)S(1)}, u32[]{:S(2)}, u32[]{:S(2)}) collective-permute-start(bf16[2,96,384]{2,1,0:T(8,128)(2,1)} %fusion.29), channel_id=1, source_target_pairs={{0,16},{4,20},{8,24},{12,28},{16,0},{20,4},{24,8},{28,12},{1,17},{... | collective-permute-start | bytes 442376 | tf_op jit(solution)/shard_map/ppermute | solution.py:816
  385.8 17.8 %collective-permute-start.19 = (bf16[2,96,384]{2,1,0:T(8,128)(2,1)}, bf16[2,96,384]{2,1,0:T(8,128)(2,1)S(1)}, u32[]{:S(2)}, u32[]{:S(2)}) collective-permute-start(bf16[2,96,384]{2,1,0:T(8,128)(2,1)} %fusion.30), channel_id=1, source_target_pairs={{0,16},{4,20},{8,24},{12,28},{16,0},{20,4},{24,8},{28,12},{1,17},{... | collective-permute-start | bytes 442376 | tf_op jit(solution)/shard_map/ppermute | solution.py:816
  387.3 18.5 %collective-permute-start.20 = (bf16[2,96,384]{2,1,0:T(8,128)(2,1)S(1)}, bf16[2,96,384]{2,1,0:T(8,128)(2,1)}, u32[]{:S(2)}, u32[]{:S(2)}) collective-permute-start(bf16[2,96,384]{2,1,0:T(8,128)(2,1)S(1)} %fusion.31), channel_id=1, source_target_pairs={{0,16},{4,20},{8,24},{12,28},{16,0},{20,4},{24,8},{28,12},{1,17},{... | collective-permute-start | bytes 442376 | tf_op jit(solution)/shard_map/ppermute | solution.py:816
  407.0 34.9 %collective-permute-start.23 = (bf16[512,768]{1,0:T(8,128)(2,1)S(1)}, bf16[512,768]{1,0:T(8,128)(2,1)S(1)}, u32[]{:S(2)}, u32[]{:S(2)}) collective-permute-start(bf16[512,768]{1,0:T(8,128)(2,1)S(1)} %get-tuple-element.317), channel_id=1, source_target_pairs={{0,2},{1,3},{2,0},{3,1},{4,6},{5,7},{6,4},{7,5},{8,10},{9,11},{10,... | collective-permute-start | bytes 2359304 | tf_op jit(solution)/shard_map/ppermute | solution.py:816
  411.2 12.8 %collective-permute-start.29 = (bf16[3,48,384]{2,1,0:T(8,128)(2,1)S(1)}, bf16[3,48,384]{2,1,0:T(8,128)(2,1)S(1)}, u32[]{:S(2)}, u32[]{:S(2)}) collective-permute-start(bf16[3,48,384]{2,1,0:T(8,128)(2,1)S(1)} %get-tuple-element.260), channel_id=1, source_target_pairs={{0,24},{4,28},{8,16},{12,20},{16,8},{20,12},{24,0},{28,4},{1,25},{... | collective-permute-start | bytes 331784 | tf_op jit(solution)/shard_map/ppermute | solution.py:816
  412.7 15.3 %collective-permute-start.28 = (bf16[3,48,384]{2,1,0:T(8,128)(2,1)S(1)}, bf16[3,48,384]{2,1,0:T(8,128)(2,1)S(1)}, u32[]{:S(2)}, u32[]{:S(2)}) collective-permute-start(bf16[3,48,384]{2,1,0:T(8,128)(2,1)S(1)} %get-tuple-element.259), channel_id=1, source_target_pairs={{0,20},{4,16},{8,28},{12,24},{16,4},{20,0},{24,12},{28,8},{1,21},{... | collective-permute-start | bytes 331784 | tf_op jit(solution)/shard_map/ppermute | solution.py:816
  413.7 16.8 %collective-permute-start.27 = (bf16[3,48,384]{2,1,0:T(8,128)(2,1)S(1)}, bf16[3,48,384]{2,1,0:T(8,128)(2,1)S(1)}, u32[]{:S(2)}, u32[]{:S(2)}) collective-permute-start(bf16[3,48,384]{2,1,0:T(8,128)(2,1)S(1)} %get-tuple-element.258), channel_id=1, source_target_pairs={{0,16},{4,20},{8,24},{12,28},{16,0},{20,4},{24,8},{28,12},{1,17},{... | collective-permute-start | bytes 331784 | tf_op jit(solution)/shard_map/ppermute | solution.py:816
  416.7 13.8 %collective-permute-start.26 = (bf16[3,48,384]{2,1,0:T(8,128)(2,1)S(1)}, bf16[3,48,384]{2,1,0:T(8,128)(2,1)S(1)}, u32[]{:S(2)}, u32[]{:S(2)}) collective-permute-start(bf16[3,48,384]{2,1,0:T(8,128)(2,1)S(1)} %get-tuple-element.257), channel_id=1, source_target_pairs={{0,12},{4,8},{8,4},{12,0},{16,28},{20,24},{24,20},{28,16},{1,13},{... | collective-permute-start | bytes 331784 | tf_op jit(solution)/shard_map/ppermute | solution.py:816
  435.4 10.7 %collective-permute-start.33 = (bf16[3,48,384]{2,1,0:T(8,128)(2,1)S(1)}, bf16[3,48,384]{2,1,0:T(8,128)(2,1)S(1)}, u32[]{:S(2)}, u32[]{:S(2)}) collective-permute-start(bf16[3,48,384]{2,1,0:T(8,128)(2,1)S(1)} %add_convert_fusion.14.refs_0_), channel_id=1, source_target_pairs={{0,12},{4,8},{8,4},{12,0},{16,28},{20,24},{24,20},{28,16},{1,13},{... | collective-permute-start | bytes 331784 | tf_op jit(solution)/shard_map/ppermute | solution.py:816
  437.0 13.7 %collective-permute-start.34 = (bf16[3,48,384]{2,1,0:T(8,128)(2,1)S(1)}, bf16[3,48,384]{2,1,0:T(8,128)(2,1)S(1)}, u32[]{:S(2)}, u32[]{:S(2)}) collective-permute-start(bf16[3,48,384]{2,1,0:T(8,128)(2,1)S(1)} %add_convert_fusion.14.refs_0_), channel_id=1, source_target_pairs={{0,16},{4,20},{8,24},{12,28},{16,0},{20,4},{24,8},{28,12},{1,17},{... | collective-permute-start | bytes 331784 | tf_op jit(solution)/shard_map/ppermute | solution.py:816
  438.0 15.1 %collective-permute-start.35 = (bf16[3,48,384]{2,1,0:T(8,128)(2,1)S(1)}, bf16[3,48,384]{2,1,0:T(8,128)(2,1)S(1)}, u32[]{:S(2)}, u32[]{:S(2)}) collective-permute-start(bf16[3,48,384]{2,1,0:T(8,128)(2,1)S(1)} %add_convert_fusion.14.refs_0_), channel_id=1, source_target_pairs={{0,20},{4,16},{8,28},{12,24},{16,4},{20,0},{24,12},{28,8},{1,21},{... | collective-permute-start | bytes 331784 | tf_op jit(solution)/shard_map/ppermute | solution.py:816
  442.0 11.2 %collective-permute-start.36 = (bf16[3,48,384]{2,1,0:T(8,128)(2,1)S(1)}, bf16[3,48,384]{2,1,0:T(8,128)(2,1)S(1)}, u32[]{:S(2)}, u32[]{:S(2)}) collective-permute-start(bf16[3,48,384]{2,1,0:T(8,128)(2,1)S(1)} %add_convert_fusion.14.refs_0_), channel_id=1, source_target_pairs={{0,24},{4,28},{8,16},{12,20},{16,8},{20,12},{24,0},{28,4},{1,25},{... | collective-permute-start | bytes 331784 | tf_op jit(solution)/shard_map/ppermute | solution.py:816
  442.0 11.2 %collective-permute-start.37 = (bf16[3,48,384]{2,1,0:T(8,128)(2,1)S(1)}, bf16[3,48,384]{2,1,0:T(8,128)(2,1)S(1)}, u32[]{:S(2)}, u32[]{:S(2)}) collective-permute-start(bf16[3,48,384]{2,1,0:T(8,128)(2,1)S(1)} %add_convert_fusion.14.refs_0_), channel_id=1, source_target_pairs={{0,28},{4,24},{8,20},{12,16},{16,12},{20,8},{24,4},{28,0},{1,29},{... | collective-permute-start | bytes 331784 | tf_op jit(solution)/shard_map/ppermute | solution.py:816
  (60 other events, 753.2 us)
Sparse Core Ops, SparseCore 0:
  11.5 108.3 all-gather.5
  457.5 54.8 all-gather.7

commit v6 on v5

--- a/solution.py
+++ b/solution.py
@@ -308,35 +308,29 @@
         dv2[...] = dv[rows:, :].astype(LOW)
 
 
-def attn_backward(q, kv, other, bias, attn, lse, d_attn, first, count, place, total, before, q_rows=512, chunk=1024):
+def attn_backward(q, kv, other, bias, attn, lse, d_attn, first, count, q_rows=512, chunk=1024):
     rows, pairs = q.shape[0], D // 128
     keys = 2 * rows
-    out_spec = pl.BlockSpec((q_rows, 128), lambda p, i: (i, place + p))
-    k_out = pl.BlockSpec((rows, 128), lambda p, i: (0, place + p))
+    out_spec = pl.BlockSpec((q_rows, 128), lambda p, i: (i, p))
+    k_out = pl.BlockSpec((rows, 128), lambda p, i: (0, p))
     q_spec = pl.BlockSpec((q_rows, 128), lambda p, i: (i, first + p))
     k_spec = pl.BlockSpec((rows, 128), lambda p, i: (0, first + p))
     v_spec = pl.BlockSpec((rows, 128), lambda p, i: (0, pairs + first + p))
-
-    def kernel(*refs):
-        attn_bwd_kernel(*refs[:9], *refs[9 + len(before) :], chunk=chunk)
-
     return pl.pallas_call(
-        kernel,
+        functools.partial(attn_bwd_kernel, chunk=chunk),
         grid=(count, rows // q_rows),
         in_specs=[
             q_spec, k_spec, v_spec, k_spec, v_spec, pl.BlockSpec((keys, 128), lambda p, i: (0, 0)),
             q_spec, q_spec, q_spec,
-        ]
-        + [pl.BlockSpec(memory_space=pl.ANY)] * len(before),
+        ],
         out_specs=[out_spec, k_out, k_out, k_out, k_out],
-        out_shape=[jax.ShapeDtypeStruct((rows, total * 128), LOW)] * 5,
+        out_shape=[jax.ShapeDtypeStruct((rows, count * 128), LOW)] * 5,
         scratch_shapes=[pltpu.VMEM((keys, 128), LOW)] * 4
         + [pltpu.VMEM((128, keys), LOW)]
         + [pltpu.VMEM((keys, 128), F32)] * 2,
-        input_output_aliases={9 + i: i for i in range(len(before))},
         compiler_params=params(56),
         name="attn_bwd",
-    )(q, kv, kv, other, other, bias, attn, lse, d_attn, *before)
+    )(q, kv, kv, other, other, bias, attn, lse, d_attn)
 
 
 def mid_kernel(
@@ -504,7 +498,7 @@
 
 def d_columns(step, grads, work):
     def both(n):
-        return jnp.concatenate([grads[n][...], grads[5 + n][...]], axis=1)
+        return jnp.concatenate([ref[...] for ref in grads[n::5]], axis=1)
 
     @pl.when(step == 0)
     def _():
@@ -518,7 +512,7 @@
 
 
 def qkv_grad_kernel(seq, a_ref, *refs):
-    grads, (keep, send, cols_ref, stage) = refs[:10], refs[10:]
+    grads, (keep, send, cols_ref, stage) = refs[:-4], refs[-4:]
     quarter = BLK // 4
 
     def work(d_cols):
@@ -534,7 +528,7 @@
     d_columns(pl.program_id(0), grads, work)
 
 
-def qkv_grad(seq, normed, halves):
+def qkv_grad(seq, normed, grads):
     rows = normed.shape[0]
     quarter = BLK // 4
     tile_out = pl.BlockSpec((2, 2, 2, quarter, BLK), lambda i, seq: (0, 0, i, 0, 0))
@@ -545,18 +539,18 @@
             num_scalar_prefetch=1,
             grid=(3,),
             in_specs=[pl.BlockSpec((rows, D), lambda i, seq: (0, 0))]
-            + [pl.BlockSpec((rows, BLK), lambda i, seq: (0, 0))] * 10,
+            + [pl.BlockSpec(grad.shape, lambda i, seq: (0, 0)) for grad in grads],
             out_specs=[tile_out, tile_out, pl.BlockSpec((1, D), lambda i, seq: (0, i))],
             scratch_shapes=[pltpu.VMEM((BLK, D), LOW)],
         ),
         out_shape=[shape, shape, jax.ShapeDtypeStruct((1, 3 * D), F32)],
         compiler_params=params(48),
         name="qkv_grad",
-    )(seq, normed, *halves[0], *halves[1])
+    )(seq, normed, *grads)
 
 
 def qkv_bwd_kernel(own, slot, x_ref, dmid_ref, vec_ref, *refs):
-    grads, tiles, (dx_ref, sums_ref, acc, held) = refs[:10], refs[10:14], refs[14:]
+    grads, tiles, (dx_ref, sums_ref, acc, held) = refs[:-8], refs[-8:-4], refs[-4:]
     step = pl.program_id(0)
 
     @pl.when(step == 0)
@@ -578,7 +572,7 @@
         dx_ref[...] = (dmid_ref[...] + norm_back(grad * vec_ref[0:1, :], hat, rstd)).astype(LOW)
 
 
-def qkv_backward(own, slot, x, d_mid, vec, halves, gathered):
+def qkv_backward(own, slot, x, d_mid, vec, grads, gathered):
     rows = x.shape[0]
     row_spec = full_spec((rows, D))
     return pl.pallas_call(
@@ -587,7 +581,7 @@
             num_scalar_prefetch=2,
             grid=(3,),
             in_specs=[row_spec, row_spec, full_spec(vec.shape)]
-            + [full_spec((rows, BLK))] * 10
+            + [full_spec(grad.shape) for grad in grads]
             + qkv_tiles(),
             out_specs=[row_spec, full_spec((8, D))],
             scratch_shapes=[pltpu.VMEM((rows, D), F32), pltpu.VMEM((D, D), LOW)],
@@ -595,7 +589,7 @@
         out_shape=[jax.ShapeDtypeStruct((rows, D), LOW), jax.ShapeDtypeStruct((8, D), F32)],
         compiler_params=params(60),
         name="qkv_bwd",
-    )(own, slot, x, d_mid, vec, *halves[0], *halves[1], *([gathered] * 4))
+    )(own, slot, x, d_mid, vec, *grads, *([gathered] * 4))
 
 
 def eliminate(blocks):
@@ -705,19 +699,36 @@
             for b, block in enumerate(inv):
                 gram[b, c, c] = block[...]
 
-            def solve(b, carry, out):
-                at = b + (count if out is rb_out else 0)
-                factor = low_parts(gram[at, c, c], 3)
-                solved = dot_parts(low_parts(work[at, :, c], 2), factor, 1, 1, 2)
-                out[b, :, c] = solved
+            def solve(i, carry):
+                wide = 2 if count % 2 == 0 else 1
+                at = [side * count + wide * i + j for side in range(2) for j in range(wide)]
+                factors = [low_parts(gram[b, c, c], 3) for b in at]
+                solved = [
+                    dot_parts(low_parts(work[b, :, c], 2), factor, 1, 1, 2)
+                    for b, factor in zip(at, factors, strict=True)
+                ]
                 if p < BLK // 128 - 1:
-                    upper = low_parts(dot_parts(factor, low_parts(gram[at, c, rest], 3), 1, 0, 3), 3)
-                    work[at, :, rest] = work[at, :, rest] - dot_parts(low_parts(solved, 2), upper, 1, 0, 2)
-                    gram[at, rest, rest] = gram[at, rest, rest] - dot_parts(upper, upper, 0, 0, 3)
+                    uppers = [
+                        low_parts(dot_parts(factor, low_parts(gram[b, c, rest], 3), 1, 0, 3), 3)
+                        for b, factor in zip(at, factors, strict=True)
+                    ]
+                    works = [
+                        work[b, :, rest] - dot_parts(low_parts(part, 2), upper, 1, 0, 2)
+                        for b, part, upper in zip(at, solved, uppers, strict=True)
+                    ]
+                    grams = [
+                        gram[b, rest, rest] - dot_parts(upper, upper, 0, 0, 3)
+                        for b, upper in zip(at, uppers, strict=True)
+                    ]
+                    for b, new_work, new_gram in zip(at, works, grams, strict=True):
+                        work[b, :, rest] = new_work
+                        gram[b, rest, rest] = new_gram
+                for j in range(wide):
+                    lb_out[wide * i + j, :, c] = solved[j]
+                    rb_out[wide * i + j, :, c] = solved[wide + j]
                 return carry
 
-            lax.fori_loop(0, count, functools.partial(solve, out=lb_out), 0)
-            lax.fori_loop(0, count, functools.partial(solve, out=rb_out), 0)
+            lax.fori_loop(0, count // (2 if count % 2 == 0 else 1), solve, 0)
 
 
 def soap_update(seq, pieces, state, products):
@@ -768,6 +779,46 @@
     )(dp, a, b)
 
 
+def first_halves_kernel(keep, got, *outs, plans):
+    per = keep.shape[4] // len(plans)
+    names = ("x", 2, 1, 0)
+    for g, plan in enumerate(plans):
+        for out, side in zip(outs[2 * g : 2 * g + 2], (1, 0), strict=True):
+            for n in range(4):
+                where = {plan[0]: side, 2: 0}
+                free = [name for name in plan[1:] if name != 2]
+                where[free[0]], where[free[1]] = n // 2, n % 2
+                at = tuple(where[name] for name in names) + (slice(per * g, per * g + per),)
+                to = tuple(where[name] for name in plan[1:])
+                out[to] = (keep[at].astype(F32) + got[at].astype(F32)).astype(LOW)
+
+
+def first_halves(keep, got, plans):
+    slots, rows, cols = keep.shape[4:]
+    per, cut = slots // len(plans), rows // 3
+    whole = pl.BlockSpec((2, 1, 2, 2, slots, cut, cols), lambda i, j: (0, i, 0, 0, 0, j, 0))
+    outs = []
+    for plan in plans:
+        place = plan[1:].index(2)
+        block = tuple(1 if n == place else 2 for n in range(3)) + (per, cut, cols)
+        outs += [
+            pl.BlockSpec(
+                block,
+                lambda i, j, place=place: tuple(i if n == place else 0 for n in range(3)) + (0, j, 0),
+            )
+        ] * 2
+    shape = jax.ShapeDtypeStruct((2, 2, 2, per, rows, cols), LOW)
+    return pl.pallas_call(
+        functools.partial(first_halves_kernel, plans=plans),
+        grid=(2, 3),
+        in_specs=[whole, whole],
+        out_specs=outs,
+        out_shape=[shape] * len(outs),
+        compiler_params=params(60),
+        name="first_halves",
+    )(keep, got)
+
+
 def choose_kernel(dp, source, *refs):
     parts, early, out, held = refs[:-3], refs[-3], refs[-2], refs[-1]
     per, half = held.shape[1], held.shape[2]
@@ -836,8 +887,8 @@
             found.append(part.reshape(part.shape[:axis] + part.shape[axis + 1 :]))
         return add_low(*found)
 
-    def send(self, name):
-        sent, kept = self.take(name, 1), self.take(name, 0)
+    def send(self, name, ready=None):
+        sent, kept = ready or (self.take(name, 1), self.take(name, 0))
         self.names.remove(name)
         self.kept, self.slots, self.name = kept, None, name
         return sent
@@ -948,34 +999,35 @@
     guard = fill
 
     def advance(step, guard):
-        sent = [group.send(plan[step]) for group, plan in zip(groups, plans, strict=True)]
+        ready = [None] * len(plans)
+        if step == 0 and len(plans) == 3:
+            made = first_halves(keep, groups[0].got, plans)
+            ready = [tuple(made[2 * g : 2 * g + 2]) for g in range(3)]
+            for group, plan in zip(groups, plans, strict=True):
+                group.names = list(plan)
+        sent = [group.send(plan[step], own) for group, plan, own in zip(groups, plans, ready, strict=True)]
         *sent, guard = lax.optimization_barrier((*sent, guard))
         for group, array in zip(groups, sent, strict=True):
             group.receive(array)
         return guard
 
-    halves = []
-    half_pairs = D // 128 // 2
+    grads = []
     taken = 0
-    for half in range(2):
-        before, first = [], half * half_pairs
-        for place, count in ((0, 2), (2, 1)):
-            if (half or place) and (half, place) != (1, 0):
-                guard = advance(taken, guard)
-                taken += 1
-            before = attn_backward(
-                q, kv, other, guard, attn, lse, d_attn, first + place, count, place, half_pairs, before
-            )
-            got, before, result_other = lax.optimization_barrier(
-                ([group.got for group in groups], before, result_other)
-            )
-            for group, array in zip(groups, got, strict=True):
-                group.got = array
-        dq, dk, dv, sent_k, sent_v = before
-        halves.append((dq, dk, swap(sent_k, "seq", 1), dv, swap(sent_v, "seq", 1)))
+    for first, count in ((0, 2), (2, 3), (5, 1)):
+        if first:
+            guard = advance(taken, guard)
+            taken += 1
+        parts = attn_backward(q, kv, other, guard, attn, lse, d_attn, first, count)
+        got, parts, result_other = lax.optimization_barrier(
+            ([group.got for group in groups], parts, result_other)
+        )
+        for group, array in zip(groups, got, strict=True):
+            group.got = array
+        dq, dk, dv, sent_k, sent_v = parts
+        grads += [dq, dk, swap(sent_k, "seq", 1), dv, swap(sent_v, "seq", 1)]
     normed = advance(taken, normed)
     taken += 1
-    late_keep, late_send, cols = qkv_grad(seq_of, normed, halves)
+    late_keep, late_send, cols = qkv_grad(seq_of, normed, grads)
     late_shape = (2, -1, quarter, BLK)
     late = Halving(late_keep.reshape(late_shape), swap(late_send.reshape(late_shape), "seq", 1), ["x"])
 
@@ -985,12 +1037,13 @@
             group.got = array
         return value
 
-    late.receive(late.send("x"))
+    sent_x, d_mid = lax.optimization_barrier((late.send("x"), d_mid))
+    late.receive(sent_x)
     cols = after(cols)
     while taken < len(names):
         advance(taken, fill)
         taken += 1
-    d_x, sums_one = qkv_backward(owners, slots, x, d_mid, vec, halves, gathered)
+    d_x, sums_one = qkv_backward(owners, slots, x, d_mid, vec, grads, gathered)
     late.got, d_x = lax.optimization_barrier((late.got, d_x))
     d_x = after(d_x)
     d_x_other = swap(d_x[part_len:], "seq", 2)

time: 575 us -> 567 us (0.986)
  other arithmetic: 35.2 us -> 17.6 us
  waiting for transfers between devices: 114 us -> 124 us
    convert_element_type x17 -> x13, other arithmetic: 24.4 us -> 8.34 us  [add_low(): return (a.astype(F32) + b.astype(F32)).astype(LOW)]
    ppermute x40 -> x42, waiting for transfers between devices: 32.2 us -> 42 us  [swap(): return lax.ppermute(x, axis, [(i, i ^ bit) for i in range(size)])]
    pallas_call x1, Pallas kernels: 87.2 us -> 78.3 us  [soap_update(): pl.pallas_call(soap_kernel, grid_spec=pltpu.PrefetchScalarGridSpec(num_sc...]
    pallas_call x4, Pallas kernels: 82.1 us -> 88.4 us  [the longest x3 79 us: attn_backward(): pl.pallas_call(functools.partial(attn_bwd_kernel, chunk=chunk), grid=(cou...]
    unnamed x103 -> x127, local copies, waits for them, and re-layouts: 12.6 us -> 15.8 us
    ppermute x40 -> x42, starting transfers between devices: 53.2 us -> 54.7 us  [swap(): return lax.ppermute(x, axis, [(i, i ^ bit) for i in range(size)])]
  transfers between devices with their start and end apart: 42 -> 44, of which waited for: 17 -> 15; matrix products, arithmetic and copies ran while one was open for 5% -> 4% of each run, Pallas kernels for 43% -> 41%
where the time goes in v6:
time: 567 us; the launch traced here: 557 us
  Pallas kernels  316 us (56%)
  waiting for transfers between devices  124 us (22%)
  starting transfers between devices  54.8 us (10%)
  local copies, waits for them, and re-layouts  29.8 us (5%)
  other arithmetic  17.6 us (3%)
  between operations  15.1 us (3%)
    all_gather x1, waiting for transfers between devices, on_device(): lax.all_gather(mine, AXES, axis=0, tiled=False)  81.8 us
    pallas_call x3, Pallas kernels, attn_backward(): pl.pallas_call(functools.partial(attn_bwd_kernel, chunk=chunk), grid=(cou...  79 us
    pallas_call x1, Pallas kernels, soap_update(): pl.pallas_call(soap_kernel, grid_spec=pltpu.PrefetchScalarGridSpec(num_sc...  78.3 us
    pallas_call x1, Pallas kernels, mid_layer(): pl.pallas_call(functools.partial(mid_kernel, chunk=chunk), grid_spec=pltp...  58.3 us
    ppermute x42, starting transfers between devices, swap(): return lax.ppermute(x, axis, [(i, i ^ bit) for i in range(size)])  54.7 us
    pallas_call x1, Pallas kernels, attn_forward(): pl.pallas_call(attn_fwd_kernel, grid=(pairs, rows // q_rows), in_specs=[q...  47.3 us
    ppermute x42, waiting for transfers between devices, swap(): return lax.ppermute(x, axis, [(i, i ^ bit) for i in range(size)])  42 us
    unnamed x127, local copies, waits for them, and re-layouts  15.8 us
  transfers between devices with their start and end apart: 44, of which 15 were waited for; matrix products, arithmetic and copies ran while one was open for 4% of the time, Pallas kernels for 41%

profile of v6, /device:TPU:0, one launch (start us, length us, event | category | flops | bytes accessed | tf_op | source)
XLA Modules:
  0.0 557.2 jit_solution(1585781956875289180)
XLA Ops:
  10.9 3.0 collective-permute-start
  14.9 2.0 copy-done.4
  16.8 2.0 copy-done.5
  18.9 2.0 copy-done.6
  20.9 12.1 %stats.1 = (f32[6,384,384]{2,1,0:T(8,128)S(1)}, f32[6,384,384]{2,1,0:T(8,128)S(1)}) custom-call(f32[6,384,384]{2,1,0:T(8,128)S(1)} %copy-done.3, f32[6,384,384]{2,1,0:T(8,128)S(1)} %copy-done.4, f32[6,384,384]{2,1,0:T(8,128)S(1)} %copy-done.5, f32[6,384,384]{2,1,0:T(8,128)S(1)} %copy-done.6), custom_call_target="tpu_custom_call" | custom-call | tf_op jit(solution)/shard_map/stats/pallas_call | solution.py:643
  38.1 81.8 %all-gather.6.cloned.1.call-done = bf16[192,1,96,384]{3,2,1,0:T(8,128)(2,1)} async-done(((bf16[6,1,96,384]{3,2,1,0:T(8,128)(2,1)}), bf16[192,1,96,384]{3,2,1,0:T(8,128)(2,1)}) %all-gather.6.cloned.1.call-update) | async-done | bytes 14155792 | tf_op jit(solution)/shard_map/all_gather | solution.py:948
  120.0 9.1 %qkv.1 = (bf16[1024,768]{1,0:T(8,128)(2,1)S(1)}, bf16[1024,1536]{1,0:T(8,128)(2,1)}, bf16[1024,768]{1,0:T(8,128)(2,1)S(1)}) custom-call(s32[48]{0:T(128)S(1)} %copy-done.25, s32[48]{0:T(128)S(1)} %convert_reduce_fusion.slot, bf16[1024,768]{1,0:T(8,128)(2,1)S(1)} %pad_maximum_fusion.x_ref, f32[12,768]{1,0:T(8,128)S(1)} %copy-done.23, ...), custom_call_target="tpu_custom_call" | custom-call | tf_op jit(solution)/shard_map/qkv/pallas_call | solution.py:130
  136.6 47.3 %attn_fwd.1 = (bf16[1024,768]{1,0:T(8,128)(2,1)S(1)}, f32[1024,768]{1,0:T(8,128)}) custom-call(bf16[1024,768]{1,0:T(8,128)(2,1)S(1)} %get-tuple-element.147.q_ref, bf16[1024,1536]{1,0:T(8,128)(2,1)} %get-tuple-element.148.k1.v1, bf16[1024,1536]{1,0:T(8,128)(2,1)} %get-tuple-element.148.k1.v1, bf16[1024,1536]{1,0:T(8,128)(2,1)} %collective-permute-done.1.k2.v2, ...), custom_call_target="tpu_custom_call" | custom-call | tf_op jit(solution)/shard_map/attn_fwd/pallas_call | solution.py:195
  185.5 58.3 %mid.1 = (bf16[1024,768]{1,0:T(8,128)(2,1)}, f32[1024,768]{1,0:T(8,128)}, bf16[1024,768]{1,0:T(8,128)(2,1)}, bf16[2,8,6,96,384]{4,3,2,1,0:T(8,128)(2,1)}, bf16[2...) custom-call(s32[48]{0:T(128)} %own.5, s32[48]{0:T(128)} %copy-done.26, ...), custom_call_target="tpu_custom_call" | custom-call | tf_op jit(solution)/shard_map/mid/pallas_call | solution.py:464
  247.1 26.3 %attn_bwd.3 = (bf16[1024,256]{1,0:T(8,128)(2,1)}, bf16[1024,256]{1,0:T(8,128)(2,1)}, bf16[1024,256]{1,0:T(8,128)(2,1)}, bf16[1024,256]{1,0:T(8,128)(2,1)}, bf16[1024,256]{1,0:T(8,128)(2,1)}) custom-call(bf16[1024,768]{1,0:T(8,128)(2,1)} %copy-done.2, bf16[1024,1536]{1,0:T(8,128)(2,1)} %get-tuple-element.148.k1.v1, ...), custom_call_target="tpu_custom_call" | custom-call | tf_op jit(solution)/shard_map/attn_bwd/pallas_call | solution.py:319
  274.3 9.4 %first_halves.1 = (bf16[2,2,2,2,96,384]{5,4,3,2,1,0:T(8,128)(2,1)}, bf16[2,2,2,2,96,384]{5,4,3,2,1,0:T(8,128)(2,1)}, bf16[2,2,2,2,96,384]{5,4,3,2,1,0:T(8,128)(2...) custom-call(bf16[2,2,2,2,6,96,384]{6,5,4,3,2,1,0:T(8,128)(2,1)} %bit, ...), custom_call_target="tpu_custom_call" | custom-call | tf_op jit(solution)/shard_map/first_halves/pallas_call | solution.py:811
  286.4 38.1 %attn_bwd.4 = (bf16[1024,384]{1,0:T(8,128)(2,1)}, bf16[1024,384]{1,0:T(8,128)(2,1)}, bf16[1024,384]{1,0:T(8,128)(2,1)}, bf16[1024,384]{1,0:T(8,128)(2,1)}, bf16[1024,384]{1,0:T(8,128)(2,1)}) custom-call(bf16[1024,768]{1,0:T(8,128)(2,1)} %copy-done.2, bf16[1024,1536]{1,0:T(8,128)(2,1)} %get-tuple-element.148.k1.v1, ...), custom_call_target="tpu_custom_call" | custom-call | tf_op jit(solution)/shard_map/attn_bwd/pallas_call | solution.py:319
  331.8 10.5 %collective-permute-done.8 = bf16[2,2,2,96,384]{4,3,2,1,0:T(8,128)(2,1)S(1)} collective-permute-done((bf16[2,2,2,96,384]{4,3,2,1,0:T(8,128)(2,1)S(1)}, bf16[2,2,2,96,384]{4,3,2,1,0:T(8,128)(2,1)S(1)}, u32[]{:S(2)}, u32[]{:S(2)}) %collective-permute-start.8) | collective-permute-done | bytes 589856 | tf_op jit(solution)/shard_map/ppermute | solution.py:867
  342.3 14.6 %attn_bwd.5 = (bf16[1024,128]{1,0:T(8,128)(2,1)}, bf16[1024,128]{1,0:T(8,128)(2,1)}, bf16[1024,128]{1,0:T(8,128)(2,1)}, bf16[1024,128]{1,0:T(8,128)(2,1)}, bf16[1024,128]{1,0:T(8,128)(2,1)}) custom-call(bf16[1024,768]{1,0:T(8,128)(2,1)} %copy-done.2, bf16[1024,1536]{1,0:T(8,128)(2,1)} %get-tuple-element.148.k1.v1, ...), custom_call_target="tpu_custom_call" | custom-call | tf_op jit(solution)/shard_map/attn_bwd/pallas_call | solution.py:319
  362.3 8.3 %qkv_grad.1 = (bf16[2,2,6,96,384]{4,3,2,1,0:T(8,128)(2,1)}, bf16[2,2,6,96,384]{4,3,2,1,0:T(8,128)(2,1)}, f32[1,2304]{1,0:T(1,128)S(1)}) custom-call(s32[1]{0:T(128)} %bitcast.seq.seq_ref, bf16[1024,768]{1,0:T(8,128)(2,1)} %copy-done.17, bf16[1024,256]{1,0:T(8,128)(2,1)S(1)} %copy-done.12, bf16[1024,256]{1,0:T(8,128)(2,1)S(1)} %copy-done.13, ...), custom_call_target="tpu_custom_call" | custom-call | tf_op jit(solution)/shard_map/qkv_grad/pallas_call | solution.py:536
  376.8 3.9 collective-permute-done.11
  392.2 13.3 %qkv_bwd.1 = (bf16[1024,768]{1,0:T(8,128)(2,1)}, f32[8,768]{1,0:T(8,128)}) custom-call(s32[48]{0:T(128)} %own.5, s32[48]{0:T(128)} %copy-done.26, bf16[1024,768]{1,0:T(8,128)(2,1)} %copy-done.1, f32[1024,768]{1,0:T(8,128)} %get-tuple-element.227.dmid_ref, f32[12,768]{1,0:T(8,128)} %vec_ref.5, bf16[1024,256]{1,0:T(8,128)(2,1)} %get-tuple-element.201.refs_0_, ...), custom_call_target="tpu_custom_call" | custom-call | tf_op jit(solution)/shard_map/qkv_bwd/pallas_call | solution.py:578
  405.9 2.1 collective-permute-done.22
  409.2 2.3 collective-permute-start.32
  411.5 2.4 collective-permute-start.31
  413.9 3.1 collective-permute-start.29
  418.0 4.7 collective-permute-start.28
  422.7 3.7 collective-permute-start.27
  426.4 2.0 collective-permute-done.30
  430.9 2.3 collective-permute-done.26
  434.9 2.2 collective-permute-start.35
  440.8 3.2 collective-permute-start.38
  446.1 3.5 collective-permute-done.36.refs_4_
  449.6 3.8 collective-permute-done.37.refs_5_
  458.9 7.1 %collective-permute-done.40.g1 = bf16[6,96,384]{2,1,0:T(8,128)(2,1)S(1)} collective-permute-done((bf16[6,96,384]{2,1,0:T(8,128)(2,1)S(1)}, bf16[6,96,384]{2,1,0:T(8,128)(2,1)S(1)}, u32[]{:S(2)}, u32[]{:S(2)}) %collective-permute-start.40) | collective-permute-done | bytes 442400 | tf_op jit(solution)/shard_map/ppermute | solution.py:867
  466.1 2.4 collective-permute-done.41
  469.6 78.3 %soap.1 = (f32[6,384,384]{2,1,0:T(8,128)}, f32[6,384,384]{2,1,0:T(8,128)}, f32[6,384,384]{2,1,0:T(8,128)}, f32[6,384,384]{2,1,0:T(8,128)}, f32[6,384,384]{2,1,0:...) custom-call(s32[1]{0:T(128)} %bitcast.seq.seq_ref, ...), custom_call_target="tpu_custom_call" | custom-call | tf_op jit(solution)/shard_map/soap/pallas_call | solution.py:740
  (255 shorter events, 77.2 us)
Async XLA Ops:
  7.2 112.8 %all-gather.6.cloned.1.call-start = ((), (), s32[]{:S(2)}) async-start(), calls=%async_computation | async-start | bytes 14598144 | tf_op jit(solution)/shard_map/all_gather | solution.py:948
  9.2 538.7 %all-gather.8.cloned.1.call-start = ((), (), s32[]{:S(2)}) async-start(), calls=%async_computation.1 | async-start | bytes 1622016 | tf_op jit(solution)/shard_map/all_gather | solution.py:1090
  10.9 27.0 %collective-permute-start = (bf16[512,768]{1,0:T(8,128)(2,1)S(1)}, bf16[512,768]{1,0:T(8,128)(2,1)S(1)}, u32[]{:S(2)}, u32[]{:S(2)}) collective-permute-start(bf16[512,768]{1,0:T(8,128)(2,1)S(1)} %get-tuple-element.299), channel_id=1, source_target_pairs={{0,2},{1,3},{2,0},{3,1},{4,6},{5,7},{6,4},{7,5},{8,10},{9,11},{10,... | collective-permute-start | bytes 2359304 | tf_op jit(solution)/shard_map/ppermute | solution.py:867
  131.2 52.6 %collective-permute-start.2 = (bf16[512,768]{1,0:T(8,128)(2,1)}, bf16[512,768]{1,0:T(8,128)(2,1)S(1)}, u32[]{:S(2)}, u32[]{:S(2)}) collective-permute-start(bf16[512,768]{1,0:T(8,128)(2,1)} %get-tuple-element.150), channel_id=1, source_target_pairs={{0,2},{1,3},{2,0},{3,1},{4,6},{5,7},{6,4},{7,5},{8,10},{9,11},{10,... | collective-permute-start | bytes 2359304 | tf_op jit(solution)/shard_map/ppermute | solution.py:867
  243.8 30.5 %collective-permute-start.3 = (bf16[2,8,6,96,384]{4,3,2,1,0:T(8,128)(2,1)}, bf16[2,8,6,96,384]{4,3,2,1,0:T(8,128)(2,1)}, u32[]{:S(2)}, u32[]{:S(2)}) collective-permute-start(bf16[2,8,6,96,384]{4,3,2,1,0:T(8,128)(2,1)} %get-tuple-element.154), channel_id=1, source_target_pairs={{0,1},{1,0},{2,3},{3,2},{4,5},{5,4},{6,7},{7,6},{8,9},{9,8},{10,11... | collective-permute-start | bytes 21233672 | tf_op jit(solution)/shard_map/ppermute | solution.py:867
  245.6 27.8 %collective-permute-start.4 = (bf16[512,768]{1,0:T(8,128)(2,1)S(1)}, bf16[512,768]{1,0:T(8,128)(2,1)S(1)}, u32[]{:S(2)}, u32[]{:S(2)}) collective-permute-start(bf16[512,768]{1,0:T(8,128)(2,1)S(1)} %get-tuple-element.295), channel_id=1, source_target_pairs={{0,2},{1,3},{2,0},{3,1},{4,6},{5,7},{6,4},{7,5},{8,10},{9,11},{10,... | collective-permute-start | bytes 2359304 | tf_op jit(solution)/shard_map/ppermute | solution.py:867
  283.7 40.8 %collective-permute-start.5 = (bf16[2,2,2,2,96,384]{5,4,3,2,1,0:T(8,128)(2,1)}, bf16[2,2,2,2,96,384]{5,4,3,2,1,0:T(8,128)(2,1)S(1)}, u32[]{:S(2)}, u32[]{:S(2)}) collective-permute-start(bf16[2,2,2,2,96,384]{5,4,3,2,1,0:T(8,128)(2,1)} %get-tuple-element.168), channel_id=1, source_target_pairs={{0,2},{1,3},{2,0},{3,1},{4,6},{5,7},{6,4},{7,5},{8,10},{9,11},{10,... | collective-permute-start | bytes 3538952 | tf_op jit(solution)/shard_map/ppermute | solution.py:867
  284.4 40.2 %collective-permute-start.6 = (bf16[2,2,2,2,96,384]{5,4,3,2,1,0:T(8,128)(2,1)}, bf16[2,2,2,2,96,384]{5,4,3,2,1,0:T(8,128)(2,1)S(1)}, u32[]{:S(2)}, u32[]{:S(2)}) collective-permute-start(bf16[2,2,2,2,96,384]{5,4,3,2,1,0:T(8,128)(2,1)} %get-tuple-element.169), channel_id=1, source_target_pairs={{0,4},{4,0},{8,12},{12,8},{16,20},{20,16},{24,28},{28,24},{1,5},{5... | collective-permute-start | bytes 3538952 | tf_op jit(solution)/shard_map/ppermute | solution.py:867
  285.8 38.7 %collective-permute-start.7 = (bf16[2,2,2,2,96,384]{5,4,3,2,1,0:T(8,128)(2,1)}, bf16[2,2,2,2,96,384]{5,4,3,2,1,0:T(8,128)(2,1)S(1)}, u32[]{:S(2)}, u32[]{:S(2)}) collective-permute-start(bf16[2,2,2,2,96,384]{5,4,3,2,1,0:T(8,128)(2,1)} %get-tuple-element.170), channel_id=1, source_target_pairs={{0,8},{4,12},{8,0},{12,4},{16,24},{20,28},{24,16},{28,20},{1,9},{5... | collective-permute-start | bytes 3538952 | tf_op jit(solution)/shard_map/ppermute | solution.py:867
  327.9 14.4 %collective-permute-start.8 = (bf16[2,2,2,96,384]{4,3,2,1,0:T(8,128)(2,1)S(1)}, bf16[2,2,2,96,384]{4,3,2,1,0:T(8,128)(2,1)S(1)}, u32[]{:S(2)}, u32[]{:S(2)}) collective-permute-start(bf16[2,2,2,96,384]{4,3,2,1,0:T(8,128)(2,1)S(1)} %get-tuple-element.183), channel_id=1, source_target_pairs={{0,4},{4,0},{8,12},{12,8},{16,20},{20,16},{24,28},{28,24},{1,5},{5... | collective-permute-start | bytes 1769480 | tf_op jit(solution)/shard_map/ppermute | solution.py:867
  328.5 28.5 %collective-permute-start.9 = (bf16[2,2,2,96,384]{4,3,2,1,0:T(8,128)(2,1)}, bf16[2,2,2,96,384]{4,3,2,1,0:T(8,128)(2,1)S(1)}, u32[]{:S(2)}, u32[]{:S(2)}) collective-permute-start(bf16[2,2,2,96,384]{4,3,2,1,0:T(8,128)(2,1)} %get-tuple-element.184), channel_id=1, source_target_pairs={{0,8},{4,12},{8,0},{12,4},{16,24},{20,28},{24,16},{28,20},{1,9},{5... | collective-permute-start | bytes 1769480 | tf_op jit(solution)/shard_map/ppermute | solution.py:867
  329.9 27.6 %collective-permute-start.10 = (bf16[2,2,2,96,384]{4,3,2,1,0:T(8,128)(2,1)}, bf16[2,2,2,96,384]{4,3,2,1,0:T(8,128)(2,1)S(1)}, u32[]{:S(2)}, u32[]{:S(2)}) collective-permute-start(bf16[2,2,2,96,384]{4,3,2,1,0:T(8,128)(2,1)} %get-tuple-element.185), channel_id=1, source_target_pairs={{0,2},{1,3},{2,0},{3,1},{4,6},{5,7},{6,4},{7,5},{8,10},{9,11},{10,... | collective-permute-start | bytes 1769480 | tf_op jit(solution)/shard_map/ppermute | solution.py:867
  331.3 27.3 %collective-permute-start.14 = (bf16[1024,256]{1,0:T(8,128)(2,1)}, bf16[1024,256]{1,0:T(8,128)(2,1)S(1)}, u32[]{:S(2)}, u32[]{:S(2)}) collective-permute-start(bf16[1024,256]{1,0:T(8,128)(2,1)} %get-tuple-element.203), channel_id=1, source_target_pairs={{0,1},{1,0},{2,3},{3,2},{4,5},{5,4},{6,7},{7,6},{8,9},{9,8},{10,11... | collective-permute-start | bytes 1572872 | tf_op jit(solution)/shard_map/ppermute | solution.py:867
  331.3 29.8 %collective-permute-start.16 = (bf16[1024,384]{1,0:T(8,128)(2,1)}, bf16[1024,384]{1,0:T(8,128)(2,1)S(1)}, u32[]{:S(2)}, u32[]{:S(2)}) collective-permute-start(bf16[1024,384]{1,0:T(8,128)(2,1)} %get-tuple-element.208), channel_id=1, source_target_pairs={{0,1},{1,0},{2,3},{3,2},{4,5},{5,4},{6,7},{7,6},{8,9},{9,8},{10,11... | collective-permute-start | bytes 2359304 | tf_op jit(solution)/shard_map/ppermute | solution.py:867
  342.3 18.8 %collective-permute-start.17 = (bf16[1024,384]{1,0:T(8,128)(2,1)}, bf16[1024,384]{1,0:T(8,128)(2,1)S(1)}, u32[]{:S(2)}, u32[]{:S(2)}) collective-permute-start(bf16[1024,384]{1,0:T(8,128)(2,1)} %get-tuple-element.210), channel_id=1, source_target_pairs={{0,1},{1,0},{2,3},{3,2},{4,5},{5,4},{6,7},{7,6},{8,9},{9,8},{10,11... | collective-permute-start | bytes 2359304 | tf_op jit(solution)/shard_map/ppermute | solution.py:867
  370.6 11.5 %collective-permute-start.23 = (bf16[2,12,96,384]{3,2,1,0:T(8,128)(2,1)}, bf16[2,12,96,384]{3,2,1,0:T(8,128)(2,1)S(1)}, u32[]{:S(2)}, u32[]{:S(2)}) collective-permute-start(bf16[2,12,96,384]{3,2,1,0:T(8,128)(2,1)} %bitcast.173), channel_id=1, source_target_pairs={{0,1},{1,0},{2,3},{3,2},{4,5},{5,4},{6,7},{7,6},{8,9},{9,8},{10,11... | collective-permute-start | bytes 5308424 | tf_op jit(solution)/shard_map/ppermute | solution.py:867
  371.1 9.6 %collective-permute-start.11 = (bf16[2,2,96,384]{3,2,1,0:T(8,128)(2,1)}, bf16[2,2,96,384]{3,2,1,0:T(8,128)(2,1)S(1)}, u32[]{:S(2)}, u32[]{:S(2)}) collective-permute-start(bf16[2,2,96,384]{3,2,1,0:T(8,128)(2,1)} %get-tuple-element.197), channel_id=1, source_target_pairs={{0,8},{4,12},{8,0},{12,4},{16,24},{20,28},{24,16},{28,20},{1,9},{5... | collective-permute-start | bytes 884744 | tf_op jit(solution)/shard_map/ppermute | solution.py:867
  372.5 9.3 %collective-permute-start.12 = (bf16[2,2,96,384]{3,2,1,0:T(8,128)(2,1)}, bf16[2,2,96,384]{3,2,1,0:T(8,128)(2,1)S(1)}, u32[]{:S(2)}, u32[]{:S(2)}) collective-permute-start(bf16[2,2,96,384]{3,2,1,0:T(8,128)(2,1)} %get-tuple-element.198), channel_id=1, source_target_pairs={{0,2},{1,3},{2,0},{3,1},{4,6},{5,7},{6,4},{7,5},{8,10},{9,11},{10,... | collective-permute-start | bytes 884744 | tf_op jit(solution)/shard_map/ppermute | solution.py:867
  383.6 22.3 %collective-permute-start.24 = (bf16[12,96,384]{2,1,0:T(8,128)(2,1)}, bf16[12,96,384]{2,1,0:T(8,128)(2,1)S(1)}, u32[]{:S(2)}, u32[]{:S(2)}) collective-permute-start(bf16[12,96,384]{2,1,0:T(8,128)(2,1)} %fusion.1), channel_id=1, source_target_pairs={{0,2},{1,3},{2,0},{3,1},{4,6},{5,7},{6,4},{7,5},{8,10},{9,11},{10,... | collective-permute-start | bytes 2654216 | tf_op jit(solution)/shard_map/ppermute | solution.py:867
  386.5 19.3 %collective-permute-start.20 = (bf16[2,96,384]{2,1,0:T(8,128)(2,1)}, bf16[2,96,384]{2,1,0:T(8,128)(2,1)S(1)}, u32[]{:S(2)}, u32[]{:S(2)}) collective-permute-start(bf16[2,96,384]{2,1,0:T(8,128)(2,1)} %fusion.24), channel_id=1, source_target_pairs={{0,16},{4,20},{8,24},{12,28},{16,0},{20,4},{24,8},{28,12},{1,17},{... | collective-permute-start | bytes 442376 | tf_op jit(solution)/shard_map/ppermute | solution.py:867
  388.1 17.8 %collective-permute-start.21 = (bf16[2,96,384]{2,1,0:T(8,128)(2,1)}, bf16[2,96,384]{2,1,0:T(8,128)(2,1)S(1)}, u32[]{:S(2)}, u32[]{:S(2)}) collective-permute-start(bf16[2,96,384]{2,1,0:T(8,128)(2,1)} %fusion.25), channel_id=1, source_target_pairs={{0,16},{4,20},{8,24},{12,28},{16,0},{20,4},{24,8},{28,12},{1,17},{... | collective-permute-start | bytes 442376 | tf_op jit(solution)/shard_map/ppermute | solution.py:867
  389.5 18.5 %collective-permute-start.22 = (bf16[2,96,384]{2,1,0:T(8,128)(2,1)S(1)}, bf16[2,96,384]{2,1,0:T(8,128)(2,1)S(1)}, u32[]{:S(2)}, u32[]{:S(2)}) collective-permute-start(bf16[2,96,384]{2,1,0:T(8,128)(2,1)S(1)} %fusion.26), channel_id=1, source_target_pairs={{0,16},{4,20},{8,24},{12,28},{16,0},{20,4},{24,8},{28,12},{1,17},{... | collective-permute-start | bytes 442376 | tf_op jit(solution)/shard_map/ppermute | solution.py:867
  408.2 35.8 %collective-permute-start.25 = (bf16[512,768]{1,0:T(8,128)(2,1)S(1)}, bf16[512,768]{1,0:T(8,128)(2,1)S(1)}, u32[]{:S(2)}, u32[]{:S(2)}) collective-permute-start(bf16[512,768]{1,0:T(8,128)(2,1)S(1)} %get-tuple-element.293), channel_id=1, source_target_pairs={{0,2},{1,3},{2,0},{3,1},{4,6},{5,7},{6,4},{7,5},{8,10},{9,11},{10,... | collective-permute-start | bytes 2359304 | tf_op jit(solution)/shard_map/ppermute | solution.py:867
  411.5 11.2 %collective-permute-start.31 = (bf16[3,48,384]{2,1,0:T(8,128)(2,1)S(1)}, bf16[3,48,384]{2,1,0:T(8,128)(2,1)S(1)}, u32[]{:S(2)}, u32[]{:S(2)}) collective-permute-start(bf16[3,48,384]{2,1,0:T(8,128)(2,1)S(1)} %get-tuple-element.244), channel_id=1, source_target_pairs={{0,24},{4,28},{8,16},{12,20},{16,8},{20,12},{24,0},{28,4},{1,25},{... | collective-permute-start | bytes 331784 | tf_op jit(solution)/shard_map/ppermute | solution.py:867
  413.8 14.5 %collective-permute-start.30 = (bf16[3,48,384]{2,1,0:T(8,128)(2,1)S(1)}, bf16[3,48,384]{2,1,0:T(8,128)(2,1)S(1)}, u32[]{:S(2)}, u32[]{:S(2)}) collective-permute-start(bf16[3,48,384]{2,1,0:T(8,128)(2,1)S(1)} %get-tuple-element.243), channel_id=1, source_target_pairs={{0,20},{4,16},{8,28},{12,24},{16,4},{20,0},{24,12},{28,8},{1,21},{... | collective-permute-start | bytes 331784 | tf_op jit(solution)/shard_map/ppermute | solution.py:867
  413.9 15.9 %collective-permute-start.29 = (bf16[3,48,384]{2,1,0:T(8,128)(2,1)S(1)}, bf16[3,48,384]{2,1,0:T(8,128)(2,1)S(1)}, u32[]{:S(2)}, u32[]{:S(2)}) collective-permute-start(bf16[3,48,384]{2,1,0:T(8,128)(2,1)S(1)} %get-tuple-element.242), channel_id=1, source_target_pairs={{0,16},{4,20},{8,24},{12,28},{16,0},{20,4},{24,8},{28,12},{1,17},{... | collective-permute-start | bytes 331784 | tf_op jit(solution)/shard_map/ppermute | solution.py:867
  418.0 11.9 %collective-permute-start.28 = (bf16[3,48,384]{2,1,0:T(8,128)(2,1)S(1)}, bf16[3,48,384]{2,1,0:T(8,128)(2,1)S(1)}, u32[]{:S(2)}, u32[]{:S(2)}) collective-permute-start(bf16[3,48,384]{2,1,0:T(8,128)(2,1)S(1)} %get-tuple-element.241), channel_id=1, source_target_pairs={{0,12},{4,8},{8,4},{12,0},{16,28},{20,24},{24,20},{28,16},{1,13},{... | collective-permute-start | bytes 331784 | tf_op jit(solution)/shard_map/ppermute | solution.py:867
  434.9 11.2 %collective-permute-start.35 = (bf16[3,48,384]{2,1,0:T(8,128)(2,1)S(1)}, bf16[3,48,384]{2,1,0:T(8,128)(2,1)S(1)}, u32[]{:S(2)}, u32[]{:S(2)}) collective-permute-start(bf16[3,48,384]{2,1,0:T(8,128)(2,1)S(1)} %add_convert_fusion.6.refs_0_), channel_id=1, source_target_pairs={{0,12},{4,8},{8,4},{12,0},{16,28},{20,24},{24,20},{28,16},{1,13},{... | collective-permute-start | bytes 331784 | tf_op jit(solution)/shard_map/ppermute | solution.py:867
  437.1 12.5 %collective-permute-start.36 = (bf16[3,48,384]{2,1,0:T(8,128)(2,1)S(1)}, bf16[3,48,384]{2,1,0:T(8,128)(2,1)S(1)}, u32[]{:S(2)}, u32[]{:S(2)}) collective-permute-start(bf16[3,48,384]{2,1,0:T(8,128)(2,1)S(1)} %add_convert_fusion.6.refs_0_), channel_id=1, source_target_pairs={{0,16},{4,20},{8,24},{12,28},{16,0},{20,4},{24,8},{28,12},{1,17},{... | collective-permute-start | bytes 331784 | tf_op jit(solution)/shard_map/ppermute | solution.py:867
  438.8 14.6 %collective-permute-start.37 = (bf16[3,48,384]{2,1,0:T(8,128)(2,1)S(1)}, bf16[3,48,384]{2,1,0:T(8,128)(2,1)S(1)}, u32[]{:S(2)}, u32[]{:S(2)}) collective-permute-start(bf16[3,48,384]{2,1,0:T(8,128)(2,1)S(1)} %add_convert_fusion.6.refs_0_), channel_id=1, source_target_pairs={{0,20},{4,16},{8,28},{12,24},{16,4},{20,0},{24,12},{28,8},{1,21},{... | collective-permute-start | bytes 331784 | tf_op jit(solution)/shard_map/ppermute | solution.py:867
  440.8 12.6 %collective-permute-start.38 = (bf16[3,48,384]{2,1,0:T(8,128)(2,1)S(1)}, bf16[3,48,384]{2,1,0:T(8,128)(2,1)S(1)}, u32[]{:S(2)}, u32[]{:S(2)}) collective-permute-start(bf16[3,48,384]{2,1,0:T(8,128)(2,1)S(1)} %add_convert_fusion.6.refs_0_), channel_id=1, source_target_pairs={{0,24},{4,28},{8,16},{12,20},{16,8},{20,12},{24,0},{28,4},{1,25},{... | collective-permute-start | bytes 331784 | tf_op jit(solution)/shard_map/ppermute | solution.py:867
  444.0 9.4 %collective-permute-start.39 = (bf16[3,48,384]{2,1,0:T(8,128)(2,1)S(1)}, bf16[3,48,384]{2,1,0:T(8,128)(2,1)S(1)}, u32[]{:S(2)}, u32[]{:S(2)}) collective-permute-start(bf16[3,48,384]{2,1,0:T(8,128)(2,1)S(1)} %add_convert_fusion.6.refs_0_), channel_id=1, source_target_pairs={{0,28},{4,24},{8,20},{12,16},{16,12},{20,8},{24,4},{28,0},{1,29},{... | collective-permute-start | bytes 331784 | tf_op jit(solution)/shard_map/ppermute | solution.py:867
  (74 other events, 868.6 us)
Sparse Core Ops, SparseCore 0:
  11.5 108.4 all-gather.5
  457.7 55.5 all-gather.7

commit v7 on v6

--- a/solution.py
+++ b/solution.py
@@ -248,7 +248,7 @@
 
 def attn_bwd_kernel(
     q_ref, k1, v1, k2, v2, bias_ref, o_ref, lse_ref, do_ref,
-    dq_ref, dk1, dv1, dk2, dv2, ka, kb, va, vb, kt, dk, dv, *, chunk,
+    dq_ref, dk1, dv1, dkv2, ka, kb, va, vb, kt, dk, dv, *, chunk,
 ):
     rows = k1.shape[0]
 
@@ -303,9 +303,9 @@
     @pl.when(pl.program_id(1) == pl.num_programs(1) - 1)
     def _():
         dk1[...] = dk[:rows, :].astype(LOW)
-        dk2[...] = dk[rows:, :].astype(LOW)
         dv1[...] = dv[:rows, :].astype(LOW)
-        dv2[...] = dv[rows:, :].astype(LOW)
+        dkv2[0] = dk[rows:, :].astype(LOW)
+        dkv2[1] = dv[rows:, :].astype(LOW)
 
 
 def attn_backward(q, kv, other, bias, attn, lse, d_attn, first, count, q_rows=512, chunk=1024):
@@ -323,8 +323,9 @@
             q_spec, k_spec, v_spec, k_spec, v_spec, pl.BlockSpec((keys, 128), lambda p, i: (0, 0)),
             q_spec, q_spec, q_spec,
         ],
-        out_specs=[out_spec, k_out, k_out, k_out, k_out],
-        out_shape=[jax.ShapeDtypeStruct((rows, count * 128), LOW)] * 5,
+        out_specs=[out_spec, k_out, k_out, pl.BlockSpec((2, rows, 128), lambda p, i: (0, 0, p))],
+        out_shape=[jax.ShapeDtypeStruct((rows, count * 128), LOW)] * 3
+        + [jax.ShapeDtypeStruct((2, rows, count * 128), LOW)],
         scratch_shapes=[pltpu.VMEM((keys, 128), LOW)] * 4
         + [pltpu.VMEM((128, keys), LOW)]
         + [pltpu.VMEM((keys, 128), F32)] * 2,
@@ -497,18 +498,18 @@
 
 
 def d_columns(step, grads, work):
-    def both(n):
-        return jnp.concatenate([ref[...] for ref in grads[n::5]], axis=1)
+    def joined(n, *at):
+        return jnp.concatenate([ref[at] if at else ref[...] for ref in grads[n::4]], axis=1)
 
     @pl.when(step == 0)
     def _():
-        work(both(0))
-
-    for n in (1, 3):
-
-        @pl.when(step == (n + 1) // 2)
+        work(joined(0))
+
+    for n in (1, 2):
+
+        @pl.when(step == n)
         def _():
-            work((both(n).astype(F32) + both(n + 1).astype(F32)).astype(LOW))
+            work((joined(n).astype(F32) + joined(3, n - 1).astype(F32)).astype(LOW))
 
 
 def qkv_grad_kernel(seq, a_ref, *refs):
@@ -539,7 +540,7 @@
             num_scalar_prefetch=1,
             grid=(3,),
             in_specs=[pl.BlockSpec((rows, D), lambda i, seq: (0, 0))]
-            + [pl.BlockSpec(grad.shape, lambda i, seq: (0, 0)) for grad in grads],
+            + [pl.BlockSpec(grad.shape, lambda i, seq, n=grad.ndim: (0,) * n) for grad in grads],
             out_specs=[tile_out, tile_out, pl.BlockSpec((1, D), lambda i, seq: (0, i))],
             scratch_shapes=[pltpu.VMEM((BLK, D), LOW)],
         ),
@@ -819,7 +820,7 @@
     )(keep, got)
 
 
-def choose_kernel(dp, source, *refs):
+def choose_kernel(dp, source, *refs, blocks):
     parts, early, out, held = refs[:-3], refs[-3], refs[-2], refs[-1]
     per, half = held.shape[1], held.shape[2]
     for k, part in enumerate(parts):
@@ -830,9 +831,13 @@
     def one(i, carry):
         block = source[i]
 
-        @pl.when(2 * block >= units)
+        @pl.when((2 * block >= units) & (block < blocks))
         def _():
             out[i] = early[i]
+
+        @pl.when(block >= blocks)
+        def _():
+            out[i] = jnp.zeros(out.shape[1:], out.dtype)
 
         @pl.when(2 * block < units)
         def _():
@@ -845,9 +850,9 @@
     lax.fori_loop(0, slots, one, 0)
 
 
-def choose(dp, source, parts, early):
+def choose(dp, source, parts, early, blocks):
     return pl.pallas_call(
-        choose_kernel,
+        functools.partial(choose_kernel, blocks=blocks),
         grid_spec=pltpu.PrefetchScalarGridSpec(
             num_scalar_prefetch=2,
             grid=(1,),
@@ -903,8 +908,7 @@
 
 def quarters(piece):
     across = swap(piece, "seq", 2)
-    beside = swap(jnp.stack([piece, across]), "seq", 1)
-    return piece, across, beside[0], beside[1]
+    return piece, across, swap(piece, "seq", 1), swap(across, "seq", 1)
 
 
 def block_places(owners, owner_count, slot_count):
@@ -999,6 +1003,14 @@
     guard = fill
 
     def advance(step, guard):
+        if step == len(names) - 1 and len(groups) > 1:
+            name = plans[0][step]
+            sent = jnp.concatenate([group.take(name, 1) for group in groups], axis=0)
+            kept = jnp.concatenate([group.take(name, 0) for group in groups], axis=0)
+            groups[:] = [Halving(kept, None, [name])]
+            sent, guard = lax.optimization_barrier((groups[0].send(name, (sent, kept)), guard))
+            groups[0].receive(sent)
+            return guard
         ready = [None] * len(plans)
         if step == 0 and len(plans) == 3:
             made = first_halves(keep, groups[0].got, plans)
@@ -1023,8 +1035,8 @@
         )
         for group, array in zip(groups, got, strict=True):
             group.got = array
-        dq, dk, dv, sent_k, sent_v = parts
-        grads += [dq, dk, swap(sent_k, "seq", 1), dv, swap(sent_v, "seq", 1)]
+        dq, dk, dv, sent_kv = parts
+        grads += [dq, dk, dv, swap(sent_kv, "seq", 1)]
     normed = advance(taken, normed)
     taken += 1
     late_keep, late_send, cols = qkv_grad(seq_of, normed, grads)
@@ -1047,7 +1059,7 @@
     late.got, d_x = lax.optimization_barrier((late.got, d_x))
     d_x = after(d_x)
     d_x_other = swap(d_x[part_len:], "seq", 2)
-    early = jnp.concatenate([group.total() for group in groups], axis=0)
+    early = groups[0].total()
     output = to_positions(result[:part_len], result_other)
     d_tokens = to_positions(d_x[:part_len], d_x_other)
     early, output, d_tokens = lax.optimization_barrier((early, output, d_tokens))
@@ -1059,7 +1071,7 @@
         parts = [parts[0]] + [swap(part, "dp", k) for k, part in enumerate(parts) if k]
         total = sum(part.astype(F32) for part in parts).astype(LOW)
         parts = [total] + [swap(total, "dp", k) for k in range(1, owner_count)]
-        piece = choose(dp_of, mine_from, parts, early)
+        piece = choose(dp_of, mine_from, parts, early, owners.shape[0])
     else:
         tiles = jnp.concatenate([late.total(), jnp.zeros((1, quarter, BLK), LOW)], axis=0)
         at = sources.reshape(owner_count, slot_count)[dp_id ^ jnp.arange(owner_count)]
@@ -1069,8 +1081,8 @@
         for bit in range(bits):
             owned.receive(owned.send(bit))
         piece = jnp.where((mine_from < first_blocks)[:, None, None], owned.total(), early)
+        piece = jnp.where((mine_from < owners.shape[0])[:, None, None], piece, jnp.zeros_like(piece))
     state = (master, moment_one, moment_two, left_stats, right_stats, left_basis, right_basis)
-    piece = jnp.where((mine_from < owners.shape[0])[:, None, None], piece, jnp.zeros_like(piece))
     piece, sums_one, sums_two, cols, bias_grad = lax.optimization_barrier(
         (piece, sums_one, sums_two, cols, bias_grad)
     )

time: 567 us -> 558 us (0.984)
  waiting for transfers between devices: 124 us -> 112 us
    ppermute x42 -> x38, waiting for transfers between devices: 42 us -> 30.4 us  [swap(): return lax.ppermute(x, axis, [(i, i ^ bit) for i in range(size)])]
    ppermute x42 -> x38, starting transfers between devices: 54.7 us -> 52.2 us  [swap(): return lax.ppermute(x, axis, [(i, i ^ bit) for i in range(size)])]
    unnamed x127 -> x109, local copies, waits for them, and re-layouts: 15.8 us -> 17.2 us
  transfers between devices with their start and end apart: 44 -> 40, of which waited for: 15 -> 14; matrix products, arithmetic and copies ran while one was open for 4% -> 5% of each run, Pallas kernels for 41% -> 42%
where the time goes in v7:
time: 558 us; the launch traced here: 549 us
  Pallas kernels  316 us (57%)
  waiting for transfers between devices  112 us (20%)
  starting transfers between devices  52.3 us (9%)
  local copies, waits for them, and re-layouts  32.2 us (6%)
  other arithmetic  21.1 us (4%)
  between operations  15 us (3%)
    all_gather x1, waiting for transfers between devices, on_device(): lax.all_gather(mine, AXES, axis=0, tiled=False)  81.9 us
    pallas_call x3, Pallas kernels, attn_backward(): pl.pallas_call(functools.partial(attn_bwd_kernel, chunk=chunk), grid=(cou...  78.9 us
    pallas_call x1, Pallas kernels, soap_update(): pl.pallas_call(soap_kernel, grid_spec=pltpu.PrefetchScalarGridSpec(num_sc...  78.3 us
    pallas_call x1, Pallas kernels, mid_layer(): pl.pallas_call(functools.partial(mid_kernel, chunk=chunk), grid_spec=pltp...  58.3 us
    ppermute x38, starting transfers between devices, swap(): return lax.ppermute(x, axis, [(i, i ^ bit) for i in range(size)])  52.2 us
    pallas_call x1, Pallas kernels, attn_forward(): pl.pallas_call(attn_fwd_kernel, grid=(pairs, rows // q_rows), in_specs=[q...  47.3 us
    ppermute x38, waiting for transfers between devices, swap(): return lax.ppermute(x, axis, [(i, i ^ bit) for i in range(size)])  30.4 us
    unnamed x109, local copies, waits for them, and re-layouts  17.2 us
  transfers between devices with their start and end apart: 40, of which 14 were waited for; matrix products, arithmetic and copies ran while one was open for 5% of the time, Pallas kernels for 42%

profile of v7, /device:TPU:0, one launch (start us, length us, event | category | flops | bytes accessed | tf_op | source)
XLA Modules:
  0.0 549.3 jit_solution(3900421417566446112)
XLA Ops:
  7.2 2.0 dynamic-slice_convert_fusion
  10.9 3.0 collective-permute-start
  14.9 2.0 copy-done.4
  16.8 2.0 copy-done.5
  18.9 2.0 copy-done.6
  20.9 12.1 %stats.1 = (f32[6,384,384]{2,1,0:T(8,128)S(1)}, f32[6,384,384]{2,1,0:T(8,128)S(1)}) custom-call(f32[6,384,384]{2,1,0:T(8,128)S(1)} %copy-done.3, f32[6,384,384]{2,1,0:T(8,128)S(1)} %copy-done.4, f32[6,384,384]{2,1,0:T(8,128)S(1)} %copy-done.5, f32[6,384,384]{2,1,0:T(8,128)S(1)} %copy-done.6), custom_call_target="tpu_custom_call" | custom-call | tf_op jit(solution)/shard_map/stats/pallas_call | solution.py:644
  38.1 81.9 %all-gather.6.cloned.1.call-done = bf16[192,1,96,384]{3,2,1,0:T(8,128)(2,1)} async-done(((bf16[6,1,96,384]{3,2,1,0:T(8,128)(2,1)}), bf16[192,1,96,384]{3,2,1,0:T(8,128)(2,1)}) %all-gather.6.cloned.1.call-update) | async-done | bytes 14155792 | tf_op jit(solution)/shard_map/all_gather | solution.py:952
  120.0 9.1 %qkv.1 = (bf16[1024,768]{1,0:T(8,128)(2,1)S(1)}, bf16[1024,1536]{1,0:T(8,128)(2,1)}, bf16[1024,768]{1,0:T(8,128)(2,1)S(1)}) custom-call(s32[48]{0:T(128)S(1)} %copy-done.24, s32[48]{0:T(128)S(1)} %convert_reduce_fusion.slot, bf16[1024,768]{1,0:T(8,128)(2,1)S(1)} %pad_maximum_fusion.x_ref, f32[12,768]{1,0:T(8,128)S(1)} %copy-done.22, ...), custom_call_target="tpu_custom_call" | custom-call | tf_op jit(solution)/shard_map/qkv/pallas_call | solution.py:130
  136.6 47.3 %attn_fwd.1 = (bf16[1024,768]{1,0:T(8,128)(2,1)S(1)}, f32[1024,768]{1,0:T(8,128)}) custom-call(bf16[1024,768]{1,0:T(8,128)(2,1)S(1)} %get-tuple-element.137.q_ref, bf16[1024,1536]{1,0:T(8,128)(2,1)} %get-tuple-element.138.k1.v1, bf16[1024,1536]{1,0:T(8,128)(2,1)} %get-tuple-element.138.k1.v1, bf16[1024,1536]{1,0:T(8,128)(2,1)} %collective-permute-done.1.k2.v2, ...), custom_call_target="tpu_custom_call" | custom-call | tf_op jit(solution)/shard_map/attn_fwd/pallas_call | solution.py:195
  185.6 58.3 %mid.1 = (bf16[1024,768]{1,0:T(8,128)(2,1)}, f32[1024,768]{1,0:T(8,128)}, bf16[1024,768]{1,0:T(8,128)(2,1)}, bf16[2,8,6,96,384]{4,3,2,1,0:T(8,128)(2,1)}, bf16[2...) custom-call(s32[48]{0:T(128)} %own.5, s32[48]{0:T(128)} %copy-done.25, ...), custom_call_target="tpu_custom_call" | custom-call | tf_op jit(solution)/shard_map/mid/pallas_call | solution.py:465
  244.2 2.4 slice_bitcast_fusion.2
  248.0 26.3 %attn_bwd.3 = (bf16[1024,256]{1,0:T(8,128)(2,1)}, bf16[1024,256]{1,0:T(8,128)(2,1)}, bf16[1024,256]{1,0:T(8,128)(2,1)}, bf16[2,1024,256]{2,1,0:T(8,128)(2,1)}) custom-call(bf16[1024,768]{1,0:T(8,128)(2,1)} %copy-done.2, bf16[1024,1536]{1,0:T(8,128)(2,1)} %get-tuple-element.138.k1.v1, bf16[1024,1536]{1,0:T(8,128)(2,1)} %get-tuple-element.138.k1.v1, ...), custom_call_target="tpu_custom_call" | custom-call | tf_op jit(solution)/shard_map/attn_bwd/pallas_call | solution.py:319
  275.2 9.4 %first_halves.1 = (bf16[2,2,2,2,96,384]{5,4,3,2,1,0:T(8,128)(2,1)}, bf16[2,2,2,2,96,384]{5,4,3,2,1,0:T(8,128)(2,1)}, bf16[2,2,2,2,96,384]{5,4,3,2,1,0:T(8,128)(2...) custom-call(bf16[2,2,2,2,6,96,384]{6,5,4,3,2,1,0:T(8,128)(2,1)} %bit, ...), custom_call_target="tpu_custom_call" | custom-call | tf_op jit(solution)/shard_map/first_halves/pallas_call | solution.py:812
  287.3 38.0 %attn_bwd.4 = (bf16[1024,384]{1,0:T(8,128)(2,1)}, bf16[1024,384]{1,0:T(8,128)(2,1)}, bf16[1024,384]{1,0:T(8,128)(2,1)}, bf16[2,1024,384]{2,1,0:T(8,128)(2,1)}) custom-call(bf16[1024,768]{1,0:T(8,128)(2,1)} %copy-done.2, bf16[1024,1536]{1,0:T(8,128)(2,1)} %get-tuple-element.138.k1.v1, bf16[1024,1536]{1,0:T(8,128)(2,1)} %get-tuple-element.138.k1.v1, ...), custom_call_target="tpu_custom_call" | custom-call | tf_op jit(solution)/shard_map/attn_bwd/pallas_call | solution.py:319
  326.8 2.9 add_convert_fusion.1
  333.6 14.6 %attn_bwd.5 = (bf16[1024,128]{1,0:T(8,128)(2,1)}, bf16[1024,128]{1,0:T(8,128)(2,1)}, bf16[1024,128]{1,0:T(8,128)(2,1)}, bf16[2,1024,128]{2,1,0:T(8,128)(2,1)}) custom-call(bf16[1024,768]{1,0:T(8,128)(2,1)} %copy-done.2, bf16[1024,1536]{1,0:T(8,128)(2,1)} %get-tuple-element.138.k1.v1, bf16[1024,1536]{1,0:T(8,128)(2,1)} %get-tuple-element.138.k1.v1, ...), custom_call_target="tpu_custom_call" | custom-call | tf_op jit(solution)/shard_map/attn_bwd/pallas_call | solution.py:319
  354.0 8.0 %qkv_grad.1 = (bf16[2,2,6,96,384]{4,3,2,1,0:T(8,128)(2,1)}, bf16[2,2,6,96,384]{4,3,2,1,0:T(8,128)(2,1)}, f32[1,2304]{1,0:T(1,128)S(1)}) custom-call(s32[1]{0:T(128)} %bitcast.seq.seq_ref, bf16[1024,768]{1,0:T(8,128)(2,1)} %copy-done.18, bf16[1024,256]{1,0:T(8,128)(2,1)S(1)} %copy-done.13, bf16[1024,256]{1,0:T(8,128)(2,1)S(1)} %copy-done.14, ...), custom_call_target="tpu_custom_call" | custom-call | tf_op jit(solution)/shard_map/qkv_grad/pallas_call | solution.py:537
  365.1 6.3 %collective-permute-done.11 = bf16[2,2,96,384]{3,2,1,0:T(8,128)(2,1)S(1)} collective-permute-done((bf16[2,2,96,384]{3,2,1,0:T(8,128)(2,1)S(1)}, bf16[2,2,96,384]{3,2,1,0:T(8,128)(2,1)S(1)}, u32[]{:S(2)}, u32[]{:S(2)}) %collective-permute-start.11) | collective-permute-done | bytes 294944 | tf_op jit(solution)/shard_map/ppermute | solution.py:872
  378.9 14.0 %qkv_bwd.1 = (bf16[1024,768]{1,0:T(8,128)(2,1)}, f32[8,768]{1,0:T(8,128)}) custom-call(s32[48]{0:T(128)} %own.5, s32[48]{0:T(128)} %copy-done.25, bf16[1024,768]{1,0:T(8,128)(2,1)} %copy-done.1, f32[1024,768]{1,0:T(8,128)} %get-tuple-element.209.dmid_ref, f32[12,768]{1,0:T(8,128)} %vec_ref.5, bf16[1024,256]{1,0:T(8,128)(2,1)} %get-tuple-element.188.refs_0_, ...), custom_call_target="tpu_custom_call" | custom-call | tf_op jit(solution)/shard_map/qkv_bwd/pallas_call | solution.py:579
  394.4 4.0 collective-permute-done.17
  400.2 3.2 collective-permute-start.27
  405.1 2.9 collective-permute-start.24
  408.3 8.2 %collective-permute-start.23 = (bf16[3,48,384]{2,1,0:T(8,128)(2,1)S(1)}, bf16[3,48,384]{2,1,0:T(8,128)(2,1)S(1)}, u32[]{:S(2)}, u32[]{:S(2)}) collective-permute-start(bf16[3,48,384]{2,1,0:T(8,128)(2,1)S(1)} %get-tuple-element.221), channel_id=1, source_target_pairs={{0,12},{4,8},{8,4},{12,0},{16,28},{20,24},{24,20},{28,16},{1,13},{... | collective-permute-start | bytes 331784 | tf_op jit(solution)/shard_map/ppermute | solution.py:872
  421.8 2.8 maximum_select_fusion
  425.2 2.4 collective-permute-start.28
  430.4 4.3 collective-permute-start.32
  434.9 3.2 collective-permute-start.34
  438.0 2.9 maximum_select_fusion.1
  440.9 3.2 collective-permute-done.31.refs_4_
  444.1 2.5 collective-permute-done.32.refs_5_
  452.0 7.1 %collective-permute-done.35.g1 = bf16[6,96,384]{2,1,0:T(8,128)(2,1)S(1)} collective-permute-done((bf16[6,96,384]{2,1,0:T(8,128)(2,1)S(1)}, bf16[6,96,384]{2,1,0:T(8,128)(2,1)S(1)}, u32[]{:S(2)}, u32[]{:S(2)}) %collective-permute-start.35) | collective-permute-done | bytes 442400 | tf_op jit(solution)/shard_map/ppermute | solution.py:872
  461.7 78.3 %soap.1 = (f32[6,384,384]{2,1,0:T(8,128)}, f32[6,384,384]{2,1,0:T(8,128)}, f32[6,384,384]{2,1,0:T(8,128)}, f32[6,384,384]{2,1,0:T(8,128)}, f32[6,384,384]{2,1,0:...) custom-call(s32[1]{0:T(128)} %bitcast.seq.seq_ref, ...), custom_call_target="tpu_custom_call" | custom-call | tf_op jit(solution)/shard_map/soap/pallas_call | solution.py:741
  (225 shorter events, 67.8 us)
Async XLA Ops:
  7.2 112.8 %all-gather.6.cloned.1.call-start = ((), (), s32[]{:S(2)}) async-start(), calls=%async_computation | async-start | bytes 14598144 | tf_op jit(solution)/shard_map/all_gather | solution.py:952
  9.2 530.8 %all-gather.8.cloned.1.call-start = ((), (), s32[]{:S(2)}) async-start(), calls=%async_computation.1 | async-start | bytes 1622016 | tf_op jit(solution)/shard_map/all_gather | solution.py:1102
  10.9 27.0 %collective-permute-start = (bf16[512,768]{1,0:T(8,128)(2,1)S(1)}, bf16[512,768]{1,0:T(8,128)(2,1)S(1)}, u32[]{:S(2)}, u32[]{:S(2)}) collective-permute-start(bf16[512,768]{1,0:T(8,128)(2,1)S(1)} %get-tuple-element.277), channel_id=1, source_target_pairs={{0,2},{1,3},{2,0},{3,1},{4,6},{5,7},{6,4},{7,5},{8,10},{9,11},{10,... | collective-permute-start | bytes 2359304 | tf_op jit(solution)/shard_map/ppermute | solution.py:872
  131.3 52.6 %collective-permute-start.2 = (bf16[512,768]{1,0:T(8,128)(2,1)}, bf16[512,768]{1,0:T(8,128)(2,1)S(1)}, u32[]{:S(2)}, u32[]{:S(2)}) collective-permute-start(bf16[512,768]{1,0:T(8,128)(2,1)} %get-tuple-element.140), channel_id=1, source_target_pairs={{0,2},{1,3},{2,0},{3,1},{4,6},{5,7},{6,4},{7,5},{8,10},{9,11},{10,... | collective-permute-start | bytes 2359304 | tf_op jit(solution)/shard_map/ppermute | solution.py:872
  243.8 31.3 %collective-permute-start.3 = (bf16[2,8,6,96,384]{4,3,2,1,0:T(8,128)(2,1)}, bf16[2,8,6,96,384]{4,3,2,1,0:T(8,128)(2,1)}, u32[]{:S(2)}, u32[]{:S(2)}) collective-permute-start(bf16[2,8,6,96,384]{4,3,2,1,0:T(8,128)(2,1)} %get-tuple-element.144), channel_id=1, source_target_pairs={{0,1},{1,0},{2,3},{3,2},{4,5},{5,4},{6,7},{7,6},{8,9},{9,8},{10,11... | collective-permute-start | bytes 21233672 | tf_op jit(solution)/shard_map/ppermute | solution.py:872
  246.6 27.7 %collective-permute-start.4 = (bf16[512,768]{1,0:T(8,128)(2,1)S(1)}, bf16[512,768]{1,0:T(8,128)(2,1)S(1)}, u32[]{:S(2)}, u32[]{:S(2)}) collective-permute-start(bf16[512,768]{1,0:T(8,128)(2,1)S(1)} %get-tuple-element.273), channel_id=1, source_target_pairs={{0,2},{1,3},{2,0},{3,1},{4,6},{5,7},{6,4},{7,5},{8,10},{9,11},{10,... | collective-permute-start | bytes 2359304 | tf_op jit(solution)/shard_map/ppermute | solution.py:872
  284.6 40.8 %collective-permute-start.5 = (bf16[2,2,2,2,96,384]{5,4,3,2,1,0:T(8,128)(2,1)}, bf16[2,2,2,2,96,384]{5,4,3,2,1,0:T(8,128)(2,1)S(1)}, u32[]{:S(2)}, u32[]{:S(2)}) collective-permute-start(bf16[2,2,2,2,96,384]{5,4,3,2,1,0:T(8,128)(2,1)} %get-tuple-element.157), channel_id=1, source_target_pairs={{0,2},{1,3},{2,0},{3,1},{4,6},{5,7},{6,4},{7,5},{8,10},{9,11},{10,... | collective-permute-start | bytes 3538952 | tf_op jit(solution)/shard_map/ppermute | solution.py:872
  285.3 40.1 %collective-permute-start.6 = (bf16[2,2,2,2,96,384]{5,4,3,2,1,0:T(8,128)(2,1)}, bf16[2,2,2,2,96,384]{5,4,3,2,1,0:T(8,128)(2,1)S(1)}, u32[]{:S(2)}, u32[]{:S(2)}) collective-permute-start(bf16[2,2,2,2,96,384]{5,4,3,2,1,0:T(8,128)(2,1)} %get-tuple-element.158), channel_id=1, source_target_pairs={{0,4},{4,0},{8,12},{12,8},{16,20},{20,16},{24,28},{28,24},{1,5},{5... | collective-permute-start | bytes 3538952 | tf_op jit(solution)/shard_map/ppermute | solution.py:872
  286.7 38.7 %collective-permute-start.7 = (bf16[2,2,2,2,96,384]{5,4,3,2,1,0:T(8,128)(2,1)}, bf16[2,2,2,2,96,384]{5,4,3,2,1,0:T(8,128)(2,1)S(1)}, u32[]{:S(2)}, u32[]{:S(2)}) collective-permute-start(bf16[2,2,2,2,96,384]{5,4,3,2,1,0:T(8,128)(2,1)} %get-tuple-element.159), channel_id=1, source_target_pairs={{0,8},{4,12},{8,0},{12,4},{16,24},{20,28},{24,16},{28,20},{1,9},{5... | collective-permute-start | bytes 3538952 | tf_op jit(solution)/shard_map/ppermute | solution.py:872
  326.8 25.1 %collective-permute-start.15 = (bf16[2,1024,384]{2,1,0:T(8,128)(2,1)}, bf16[2,1024,384]{2,1,0:T(8,128)(2,1)S(1)}, u32[]{:S(2)}, u32[]{:S(2)}) collective-permute-start(bf16[2,1024,384]{2,1,0:T(8,128)(2,1)} %get-tuple-element.195), channel_id=1, source_target_pairs={{0,1},{1,0},{2,3},{3,2},{4,5},{5,4},{6,7},{7,6},{8,9},{9,8},{10,11... | collective-permute-start | bytes 4718600 | tf_op jit(solution)/shard_map/ppermute | solution.py:872
  330.1 18.1 %collective-permute-start.8 = (bf16[2,2,2,96,384]{4,3,2,1,0:T(8,128)(2,1)}, bf16[2,2,2,96,384]{4,3,2,1,0:T(8,128)(2,1)S(1)}, u32[]{:S(2)}, u32[]{:S(2)}) collective-permute-start(bf16[2,2,2,96,384]{4,3,2,1,0:T(8,128)(2,1)} %get-tuple-element.171), channel_id=1, source_target_pairs={{0,4},{4,0},{8,12},{12,8},{16,20},{20,16},{24,28},{28,24},{1,5},{5... | collective-permute-start | bytes 1769480 | tf_op jit(solution)/shard_map/ppermute | solution.py:872
  330.7 17.5 %collective-permute-start.9 = (bf16[2,2,2,96,384]{4,3,2,1,0:T(8,128)(2,1)S(1)}, bf16[2,2,2,96,384]{4,3,2,1,0:T(8,128)(2,1)S(1)}, u32[]{:S(2)}, u32[]{:S(2)}) collective-permute-start(bf16[2,2,2,96,384]{4,3,2,1,0:T(8,128)(2,1)S(1)} %get-tuple-element.172), channel_id=1, source_target_pairs={{0,8},{4,12},{8,0},{12,4},{16,24},{20,28},{24,16},{28,20},{1,9},{5... | collective-permute-start | bytes 1769480 | tf_op jit(solution)/shard_map/ppermute | solution.py:872
  332.2 16.1 %collective-permute-start.10 = (bf16[2,2,2,96,384]{4,3,2,1,0:T(8,128)(2,1)S(1)}, bf16[2,2,2,96,384]{4,3,2,1,0:T(8,128)(2,1)S(1)}, u32[]{:S(2)}, u32[]{:S(2)}) collective-permute-start(bf16[2,2,2,96,384]{4,3,2,1,0:T(8,128)(2,1)S(1)} %get-tuple-element.173), channel_id=1, source_target_pairs={{0,2},{1,3},{2,0},{3,1},{4,6},{5,7},{6,4},{7,5},{8,10},{9,11},{10,... | collective-permute-start | bytes 1769480 | tf_op jit(solution)/shard_map/ppermute | solution.py:872
  333.6 18.2 %collective-permute-start.14 = (bf16[2,1024,256]{2,1,0:T(8,128)(2,1)}, bf16[2,1024,256]{2,1,0:T(8,128)(2,1)S(1)}, u32[]{:S(2)}, u32[]{:S(2)}) collective-permute-start(bf16[2,1024,256]{2,1,0:T(8,128)(2,1)} %get-tuple-element.191), channel_id=1, source_target_pairs={{0,1},{1,0},{2,3},{3,2},{4,5},{5,4},{6,7},{7,6},{8,9},{9,8},{10,11... | collective-permute-start | bytes 3145736 | tf_op jit(solution)/shard_map/ppermute | solution.py:872
  362.0 11.8 %collective-permute-start.18 = (bf16[2,12,96,384]{3,2,1,0:T(8,128)(2,1)}, bf16[2,12,96,384]{3,2,1,0:T(8,128)(2,1)S(1)}, u32[]{:S(2)}, u32[]{:S(2)}) collective-permute-start(bf16[2,12,96,384]{3,2,1,0:T(8,128)(2,1)} %bitcast.155), channel_id=1, source_target_pairs={{0,1},{1,0},{2,3},{3,2},{4,5},{5,4},{6,7},{7,6},{8,9},{9,8},{10,11... | collective-permute-start | bytes 5308424 | tf_op jit(solution)/shard_map/ppermute | solution.py:872
  362.5 9.0 %collective-permute-start.11 = (bf16[2,2,96,384]{3,2,1,0:T(8,128)(2,1)S(1)}, bf16[2,2,96,384]{3,2,1,0:T(8,128)(2,1)S(1)}, u32[]{:S(2)}, u32[]{:S(2)}) collective-permute-start(bf16[2,2,96,384]{3,2,1,0:T(8,128)(2,1)S(1)} %get-tuple-element.184), channel_id=1, source_target_pairs={{0,8},{4,12},{8,0},{12,4},{16,24},{20,28},{24,16},{28,20},{1,9},{5... | collective-permute-start | bytes 884744 | tf_op jit(solution)/shard_map/ppermute | solution.py:872
  363.0 8.7 %collective-permute-start.12 = (bf16[2,2,96,384]{3,2,1,0:T(8,128)(2,1)S(1)}, bf16[2,2,96,384]{3,2,1,0:T(8,128)(2,1)S(1)}, u32[]{:S(2)}, u32[]{:S(2)}) collective-permute-start(bf16[2,2,96,384]{3,2,1,0:T(8,128)(2,1)S(1)} %get-tuple-element.185), channel_id=1, source_target_pairs={{0,2},{1,3},{2,0},{3,1},{4,6},{5,7},{6,4},{7,5},{8,10},{9,11},{10,... | collective-permute-start | bytes 884744 | tf_op jit(solution)/shard_map/ppermute | solution.py:872
  363.6 8.4 %collective-permute-start.13 = (bf16[2,2,96,384]{3,2,1,0:T(8,128)(2,1)S(1)}, bf16[2,2,96,384]{3,2,1,0:T(8,128)(2,1)S(1)}, u32[]{:S(2)}, u32[]{:S(2)}) collective-permute-start(bf16[2,2,96,384]{3,2,1,0:T(8,128)(2,1)S(1)} %get-tuple-element.186), channel_id=1, source_target_pairs={{0,4},{4,0},{8,12},{12,8},{16,20},{20,16},{24,28},{28,24},{1,5},{5... | collective-permute-start | bytes 884744 | tf_op jit(solution)/shard_map/ppermute | solution.py:872
  374.1 20.2 %collective-permute-start.19 = (bf16[12,96,384]{2,1,0:T(8,128)(2,1)S(1)}, bf16[12,96,384]{2,1,0:T(8,128)(2,1)S(1)}, u32[]{:S(2)}, u32[]{:S(2)}) collective-permute-start(bf16[12,96,384]{2,1,0:T(8,128)(2,1)S(1)} %fusion.1), channel_id=1, source_target_pairs={{0,2},{1,3},{2,0},{3,1},{4,6},{5,7},{6,4},{7,5},{8,10},{9,11},{10,... | collective-permute-start | bytes 2654216 | tf_op jit(solution)/shard_map/ppermute | solution.py:872
  377.3 21.1 %collective-permute-start.17 = (bf16[6,96,384]{2,1,0:T(8,128)(2,1)}, bf16[6,96,384]{2,1,0:T(8,128)(2,1)}, u32[]{:S(2)}, u32[]{:S(2)}) collective-permute-start(bf16[6,96,384]{2,1,0:T(8,128)(2,1)} %pad_maximum_fusion.2), channel_id=1, source_target_pairs={{0,16},{4,20},{8,24},{12,28},{16,0},{20,4},{24,8},{28,12},{1,17},{... | collective-permute-start | bytes 1327112 | tf_op jit(solution)/shard_map/ppermute | solution.py:872
  399.3 35.5 %collective-permute-start.20 = (bf16[512,768]{1,0:T(8,128)(2,1)}, bf16[512,768]{1,0:T(8,128)(2,1)}, u32[]{:S(2)}, u32[]{:S(2)}) collective-permute-start(bf16[512,768]{1,0:T(8,128)(2,1)} %get-tuple-element.271), channel_id=1, source_target_pairs={{0,2},{1,3},{2,0},{3,1},{4,6},{5,7},{6,4},{7,5},{8,10},{9,11},{10,... | collective-permute-start | bytes 2359304 | tf_op jit(solution)/shard_map/ppermute | solution.py:872
  403.4 13.1 %collective-permute-start.26 = (bf16[3,48,384]{2,1,0:T(8,128)(2,1)S(1)}, bf16[3,48,384]{2,1,0:T(8,128)(2,1)S(1)}, u32[]{:S(2)}, u32[]{:S(2)}) collective-permute-start(bf16[3,48,384]{2,1,0:T(8,128)(2,1)S(1)} %get-tuple-element.224), channel_id=1, source_target_pairs={{0,24},{4,28},{8,16},{12,20},{16,8},{20,12},{24,0},{28,4},{1,25},{... | collective-permute-start | bytes 331784 | tf_op jit(solution)/shard_map/ppermute | solution.py:872
  405.0 15.4 %collective-permute-start.25 = (bf16[3,48,384]{2,1,0:T(8,128)(2,1)S(1)}, bf16[3,48,384]{2,1,0:T(8,128)(2,1)S(1)}, u32[]{:S(2)}, u32[]{:S(2)}) collective-permute-start(bf16[3,48,384]{2,1,0:T(8,128)(2,1)S(1)} %get-tuple-element.223), channel_id=1, source_target_pairs={{0,20},{4,16},{8,28},{12,24},{16,4},{20,0},{24,12},{28,8},{1,21},{... | collective-permute-start | bytes 331784 | tf_op jit(solution)/shard_map/ppermute | solution.py:872
  405.1 19.6 %collective-permute-start.24 = (bf16[3,48,384]{2,1,0:T(8,128)(2,1)S(1)}, bf16[3,48,384]{2,1,0:T(8,128)(2,1)S(1)}, u32[]{:S(2)}, u32[]{:S(2)}) collective-permute-start(bf16[3,48,384]{2,1,0:T(8,128)(2,1)S(1)} %get-tuple-element.222), channel_id=1, source_target_pairs={{0,16},{4,20},{8,24},{12,28},{16,0},{20,4},{24,8},{28,12},{1,17},{... | collective-permute-start | bytes 331784 | tf_op jit(solution)/shard_map/ppermute | solution.py:872
  408.3 16.4 %collective-permute-start.23 = (bf16[3,48,384]{2,1,0:T(8,128)(2,1)S(1)}, bf16[3,48,384]{2,1,0:T(8,128)(2,1)S(1)}, u32[]{:S(2)}, u32[]{:S(2)}) collective-permute-start(bf16[3,48,384]{2,1,0:T(8,128)(2,1)S(1)} %get-tuple-element.221), channel_id=1, source_target_pairs={{0,12},{4,8},{8,4},{12,0},{16,28},{20,24},{24,20},{28,16},{1,13},{... | collective-permute-start | bytes 331784 | tf_op jit(solution)/shard_map/ppermute | solution.py:872
  416.5 8.1 %collective-permute-start.22 = (bf16[3,48,384]{2,1,0:T(8,128)(2,1)S(1)}, bf16[3,48,384]{2,1,0:T(8,128)(2,1)S(1)}, u32[]{:S(2)}, u32[]{:S(2)}) collective-permute-start(bf16[3,48,384]{2,1,0:T(8,128)(2,1)S(1)} %get-tuple-element.220), channel_id=1, source_target_pairs={{0,8},{4,12},{8,0},{12,4},{16,24},{20,28},{24,16},{28,20},{1,9},{5... | collective-permute-start | bytes 331784 | tf_op jit(solution)/shard_map/ppermute | solution.py:872
  428.8 12.1 %collective-permute-start.30 = (bf16[3,48,384]{2,1,0:T(8,128)(2,1)S(1)}, bf16[3,48,384]{2,1,0:T(8,128)(2,1)S(1)}, u32[]{:S(2)}, u32[]{:S(2)}) collective-permute-start(bf16[3,48,384]{2,1,0:T(8,128)(2,1)S(1)} %add_convert_fusion.7.refs_0_), channel_id=1, source_target_pairs={{0,12},{4,8},{8,4},{12,0},{16,28},{20,24},{24,20},{28,16},{1,13},{... | collective-permute-start | bytes 331784 | tf_op jit(solution)/shard_map/ppermute | solution.py:872
  430.4 13.7 %collective-permute-start.31 = (bf16[3,48,384]{2,1,0:T(8,128)(2,1)S(1)}, bf16[3,48,384]{2,1,0:T(8,128)(2,1)S(1)}, u32[]{:S(2)}, u32[]{:S(2)}) collective-permute-start(bf16[3,48,384]{2,1,0:T(8,128)(2,1)S(1)} %add_convert_fusion.7.refs_0_), channel_id=1, source_target_pairs={{0,16},{4,20},{8,24},{12,28},{16,0},{20,4},{24,8},{28,12},{1,17},{... | collective-permute-start | bytes 331784 | tf_op jit(solution)/shard_map/ppermute | solution.py:872
  430.4 16.2 %collective-permute-start.32 = (bf16[3,48,384]{2,1,0:T(8,128)(2,1)S(1)}, bf16[3,48,384]{2,1,0:T(8,128)(2,1)S(1)}, u32[]{:S(2)}, u32[]{:S(2)}) collective-permute-start(bf16[3,48,384]{2,1,0:T(8,128)(2,1)S(1)} %add_convert_fusion.7.refs_0_), channel_id=1, source_target_pairs={{0,20},{4,16},{8,28},{12,24},{16,4},{20,0},{24,12},{28,8},{1,21},{... | collective-permute-start | bytes 331784 | tf_op jit(solution)/shard_map/ppermute | solution.py:872
  434.7 11.9 %collective-permute-start.33 = (bf16[3,48,384]{2,1,0:T(8,128)(2,1)S(1)}, bf16[3,48,384]{2,1,0:T(8,128)(2,1)S(1)}, u32[]{:S(2)}, u32[]{:S(2)}) collective-permute-start(bf16[3,48,384]{2,1,0:T(8,128)(2,1)S(1)} %add_convert_fusion.7.refs_0_), channel_id=1, source_target_pairs={{0,24},{4,28},{8,16},{12,20},{16,8},{20,12},{24,0},{28,4},{1,25},{... | collective-permute-start | bytes 331784 | tf_op jit(solution)/shard_map/ppermute | solution.py:872
  434.9 11.7 %collective-permute-start.34 = (bf16[3,48,384]{2,1,0:T(8,128)(2,1)S(1)}, bf16[3,48,384]{2,1,0:T(8,128)(2,1)S(1)}, u32[]{:S(2)}, u32[]{:S(2)}) collective-permute-start(bf16[3,48,384]{2,1,0:T(8,128)(2,1)S(1)} %add_convert_fusion.7.refs_0_), channel_id=1, source_target_pairs={{0,28},{4,24},{8,20},{12,16},{16,12},{20,8},{24,4},{28,0},{1,29},{... | collective-permute-start | bytes 331784 | tf_op jit(solution)/shard_map/ppermute | solution.py:872
  450.7 8.4 %collective-permute-start.35 = (bf16[6,96,384]{2,1,0:T(8,128)(2,1)S(1)}, bf16[6,96,384]{2,1,0:T(8,128)(2,1)S(1)}, u32[]{:S(2)}, u32[]{:S(2)}) collective-permute-start(bf16[6,96,384]{2,1,0:T(8,128)(2,1)S(1)} %choose.1.g0), channel_id=1, source_target_pairs={{0,2},{1,3},{2,0},{3,1},{4,6},{5,7},{6,4},{7,5},{8,10},{9,11},{10,... | collective-permute-start | bytes 1327112 | tf_op jit(solution)/shard_map/ppermute | solution.py:872
  (62 other events, 789.4 us)
Sparse Core Ops, SparseCore 0:
  11.5 108.4 all-gather.5
  450.8 55.1 all-gather.7

commit v8 on v7

--- a/solution.py
+++ b/solution.py
@@ -308,7 +308,7 @@
         dkv2[1] = dv[rows:, :].astype(LOW)
 
 
-def attn_backward(q, kv, other, bias, attn, lse, d_attn, first, count, q_rows=512, chunk=1024):
+def attn_backward(q, kv, other, bias, attn, lse, d_attn, first, count, q_rows=1024, chunk=1024):
     rows, pairs = q.shape[0], D // 128
     keys = 2 * rows
     out_spec = pl.BlockSpec((q_rows, 128), lambda p, i: (i, p))
@@ -1049,9 +1049,9 @@
             group.got = array
         return value
 
-    sent_x, d_mid = lax.optimization_barrier((late.send("x"), d_mid))
+    sent_x = late.send("x")
     late.receive(sent_x)
-    cols = after(cols)
+    late.kept, d_mid = after(lax.optimization_barrier((late.kept, d_mid)))
     while taken < len(names):
         advance(taken, fill)
         taken += 1

time: 558 us -> 563 us (level)
  Pallas kernels: 316 us -> 322 us
    pallas_call x1, Pallas kernels: 58.3 us -> 69.6 us  [mid_layer(): pl.pallas_call(functools.partial(mid_kernel, chunk=chunk), grid_spec=pltp...]
    unnamed x109 -> x111, local copies, waits for them, and re-layouts: 17.2 us -> 16.8 us
  transfers between devices with their start and end apart: 40 -> 40, of which waited for: 14 -> 17; matrix products, arithmetic and copies ran while one was open for 5% -> 5% of each run, Pallas kernels for 42% -> 41%
where the time goes in v8:
time: 563 us; the launch traced here: 554 us
  Pallas kernels  322 us (57%)
  waiting for transfers between devices  116 us (21%)
  starting transfers between devices  47.8 us (8%)
  local copies, waits for them, and re-layouts  33.5 us (6%)
  other arithmetic  19.5 us (3%)
  between operations  15 us (3%)
    all_gather x1, waiting for transfers between devices, on_device(): lax.all_gather(mine, AXES, axis=0, tiled=False)  81.8 us
    pallas_call x1, Pallas kernels, soap_update(): pl.pallas_call(soap_kernel, grid_spec=pltpu.PrefetchScalarGridSpec(num_sc...  78.1 us
    pallas_call x3, Pallas kernels, attn_backward(): pl.pallas_call(functools.partial(attn_bwd_kernel, chunk=chunk), grid=(cou...  73.3 us
    pallas_call x1, Pallas kernels, mid_layer(): pl.pallas_call(functools.partial(mid_kernel, chunk=chunk), grid_spec=pltp...  69.6 us
    ppermute x38, starting transfers between devices, swap(): return lax.ppermute(x, axis, [(i, i ^ bit) for i in range(size)])  47.7 us
    pallas_call x1, Pallas kernels, attn_forward(): pl.pallas_call(attn_fwd_kernel, grid=(pairs, rows // q_rows), in_specs=[q...  47.3 us
    ppermute x38, waiting for transfers between devices, swap(): return lax.ppermute(x, axis, [(i, i ^ bit) for i in range(size)])  34.6 us
    unnamed x111, local copies, waits for them, and re-layouts  16.8 us
  transfers between devices with their start and end apart: 40, of which 17 were waited for; matrix products, arithmetic and copies ran while one was open for 5% of the time, Pallas kernels for 41%

profile of v8, /device:TPU:0, one launch (start us, length us, event | category | flops | bytes accessed | tf_op | source)
XLA Modules:
  0.0 554.1 jit_solution(15356580922546121643)
XLA Ops:
  10.9 3.0 collective-permute-start
  16.8 2.0 copy-done.5
  20.9 12.1 %stats.1 = (f32[6,384,384]{2,1,0:T(8,128)S(1)}, f32[6,384,384]{2,1,0:T(8,128)S(1)}) custom-call(f32[6,384,384]{2,1,0:T(8,128)S(1)} %copy-done.3, f32[6,384,384]{2,1,0:T(8,128)S(1)} %copy-done.4, f32[6,384,384]{2,1,0:T(8,128)S(1)} %copy-done.5, f32[6,384,384]{2,1,0:T(8,128)S(1)} %copy-done.6), custom_call_target="tpu_custom_call" | custom-call | tf_op jit(solution)/shard_map/stats/pallas_call | solution.py:644
  38.1 81.8 %all-gather.6.cloned.1.call-done = bf16[192,1,96,384]{3,2,1,0:T(8,128)(2,1)} async-done(((bf16[6,1,96,384]{3,2,1,0:T(8,128)(2,1)}), bf16[192,1,96,384]{3,2,1,0:T(8,128)(2,1)}) %all-gather.6.cloned.1.call-update) | async-done | bytes 14155792 | tf_op jit(solution)/shard_map/all_gather | solution.py:952
  120.0 9.1 %qkv.1 = (bf16[1024,768]{1,0:T(8,128)(2,1)S(1)}, bf16[1024,1536]{1,0:T(8,128)(2,1)}, bf16[1024,768]{1,0:T(8,128)(2,1)S(1)}) custom-call(s32[48]{0:T(128)S(1)} %copy-done.24, s32[48]{0:T(128)S(1)} %convert_reduce_fusion.slot, bf16[1024,768]{1,0:T(8,128)(2,1)S(1)} %pad_maximum_fusion.x_ref, f32[12,768]{1,0:T(8,128)S(1)} %copy-done.22, ...), custom_call_target="tpu_custom_call" | custom-call | tf_op jit(solution)/shard_map/qkv/pallas_call | solution.py:130
  136.6 47.3 %attn_fwd.1 = (bf16[1024,768]{1,0:T(8,128)(2,1)S(1)}, f32[1024,768]{1,0:T(8,128)}) custom-call(bf16[1024,768]{1,0:T(8,128)(2,1)S(1)} %get-tuple-element.138.q_ref, bf16[1024,1536]{1,0:T(8,128)(2,1)} %get-tuple-element.139.k1.v1, bf16[1024,1536]{1,0:T(8,128)(2,1)} %get-tuple-element.139.k1.v1, bf16[1024,1536]{1,0:T(8,128)(2,1)} %collective-permute-done.1.k2.v2, ...), custom_call_target="tpu_custom_call" | custom-call | tf_op jit(solution)/shard_map/attn_fwd/pallas_call | solution.py:195
  185.5 69.6 %mid.1 = (bf16[1024,768]{1,0:T(8,128)(2,1)}, f32[1024,768]{1,0:T(8,128)}, bf16[1024,768]{1,0:T(8,128)(2,1)}, bf16[2,8,6,96,384]{4,3,2,1,0:T(8,128)(2,1)}, bf16[2...) custom-call(s32[48]{0:T(128)} %own.5, s32[48]{0:T(128)} %copy-done.25, ...), custom_call_target="tpu_custom_call" | custom-call | tf_op jit(solution)/shard_map/mid/pallas_call | solution.py:465
  255.5 2.4 slice_bitcast_fusion.3
  259.3 24.5 %attn_bwd.3 = (bf16[1024,256]{1,0:T(8,128)(2,1)}, bf16[1024,256]{1,0:T(8,128)(2,1)}, bf16[1024,256]{1,0:T(8,128)(2,1)}, bf16[2,1024,256]{2,1,0:T(8,128)(2,1)}) custom-call(bf16[1024,768]{1,0:T(8,128)(2,1)} %copy-done.2, bf16[1024,1536]{1,0:T(8,128)(2,1)} %get-tuple-element.139.k1.v1, bf16[1024,1536]{1,0:T(8,128)(2,1)} %get-tuple-element.139.k1.v1, ...), custom_call_target="tpu_custom_call" | custom-call | tf_op jit(solution)/shard_map/attn_bwd/pallas_call | solution.py:319
  284.7 9.4 %first_halves.1 = (bf16[2,2,2,2,96,384]{5,4,3,2,1,0:T(8,128)(2,1)}, bf16[2,2,2,2,96,384]{5,4,3,2,1,0:T(8,128)(2,1)}, bf16[2,2,2,2,96,384]{5,4,3,2,1,0:T(8,128)(2...) custom-call(bf16[2,2,2,2,6,96,384]{6,5,4,3,2,1,0:T(8,128)(2,1)} %bit, ...), custom_call_target="tpu_custom_call" | custom-call | tf_op jit(solution)/shard_map/first_halves/pallas_call | solution.py:812
  296.9 35.6 %attn_bwd.4 = (bf16[1024,384]{1,0:T(8,128)(2,1)}, bf16[1024,384]{1,0:T(8,128)(2,1)}, bf16[1024,384]{1,0:T(8,128)(2,1)}, bf16[2,1024,384]{2,1,0:T(8,128)(2,1)}) custom-call(bf16[1024,768]{1,0:T(8,128)(2,1)} %copy-done.2, bf16[1024,1536]{1,0:T(8,128)(2,1)} %get-tuple-element.139.k1.v1, bf16[1024,1536]{1,0:T(8,128)(2,1)} %get-tuple-element.139.k1.v1, ...), custom_call_target="tpu_custom_call" | custom-call | tf_op jit(solution)/shard_map/attn_bwd/pallas_call | solution.py:319
  334.0 2.9 add_convert_fusion.1
  340.7 13.2 %attn_bwd.5 = (bf16[1024,128]{1,0:T(8,128)(2,1)}, bf16[1024,128]{1,0:T(8,128)(2,1)}, bf16[1024,128]{1,0:T(8,128)(2,1)}, bf16[2,1024,128]{2,1,0:T(8,128)(2,1)}) custom-call(bf16[1024,768]{1,0:T(8,128)(2,1)} %copy-done.2, bf16[1024,1536]{1,0:T(8,128)(2,1)} %get-tuple-element.139.k1.v1, bf16[1024,1536]{1,0:T(8,128)(2,1)} %get-tuple-element.139.k1.v1, ...), custom_call_target="tpu_custom_call" | custom-call | tf_op jit(solution)/shard_map/attn_bwd/pallas_call | solution.py:319
  357.8 8.4 %qkv_grad.1 = (bf16[2,2,6,96,384]{4,3,2,1,0:T(8,128)(2,1)}, bf16[2,2,6,96,384]{4,3,2,1,0:T(8,128)(2,1)}, f32[1,2304]{1,0:T(1,128)S(1)}) custom-call(s32[1]{0:T(128)} %bitcast.seq.seq_ref, bf16[1024,768]{1,0:T(8,128)(2,1)} %copy-done.18, bf16[1024,256]{1,0:T(8,128)(2,1)S(1)} %copy-done.13, bf16[1024,256]{1,0:T(8,128)(2,1)S(1)} %copy-done.14, ...), custom_call_target="tpu_custom_call" | custom-call | tf_op jit(solution)/shard_map/qkv_grad/pallas_call | solution.py:537
  372.1 3.5 collective-permute-done.11
  381.6 13.6 %qkv_bwd.1 = (bf16[1024,768]{1,0:T(8,128)(2,1)}, f32[8,768]{1,0:T(8,128)}) custom-call(s32[48]{0:T(128)} %own.5, s32[48]{0:T(128)} %copy-done.25, bf16[1024,768]{1,0:T(8,128)(2,1)} %copy-done.1, f32[1024,768]{1,0:T(8,128)} %get-tuple-element.210.dmid_ref, f32[12,768]{1,0:T(8,128)} %vec_ref.5, bf16[1024,256]{1,0:T(8,128)(2,1)} %get-tuple-element.189.refs_0_, ...), custom_call_target="tpu_custom_call" | custom-call | tf_op jit(solution)/shard_map/qkv_bwd/pallas_call | solution.py:579
  395.2 2.7 collective-permute-done.19
  397.9 3.3 collective-permute-done.18
  402.0 2.6 slice_bitcast_fusion.2
  406.2 2.5 collective-permute-start.27
  410.3 3.7 collective-permute-start.24
  414.3 7.5 %collective-permute-start.23 = (bf16[3,48,384]{2,1,0:T(8,128)(2,1)S(1)}, bf16[3,48,384]{2,1,0:T(8,128)(2,1)S(1)}, u32[]{:S(2)}, u32[]{:S(2)}) collective-permute-start(bf16[3,48,384]{2,1,0:T(8,128)(2,1)S(1)} %get-tuple-element.223), channel_id=1, source_target_pairs={{0,12},{4,8},{8,4},{12,0},{16,28},{20,24},{24,20},{28,16},{1,13},{... | collective-permute-start | bytes 331784 | tf_op jit(solution)/shard_map/ppermute | solution.py:872
  423.7 2.7 collective-permute-done.25
  427.1 2.9 maximum_select_fusion
  430.0 2.1 collective-permute-done.21
  432.5 3.4 collective-permute-start.30
  439.1 4.5 collective-permute-start.34
  443.6 2.9 maximum_select_fusion.1
  446.5 2.6 collective-permute-done.31.refs_4_
  449.1 2.5 collective-permute-done.32.refs_5_
  456.4 7.7 %collective-permute-done.35.g1 = bf16[6,96,384]{2,1,0:T(8,128)(2,1)S(1)} collective-permute-done((bf16[6,96,384]{2,1,0:T(8,128)(2,1)S(1)}, bf16[6,96,384]{2,1,0:T(8,128)(2,1)S(1)}, u32[]{:S(2)}, u32[]{:S(2)}) %collective-permute-start.35) | collective-permute-done | bytes 442400 | tf_op jit(solution)/shard_map/ppermute | solution.py:872
  466.6 78.1 %soap.1 = (f32[6,384,384]{2,1,0:T(8,128)}, f32[6,384,384]{2,1,0:T(8,128)}, f32[6,384,384]{2,1,0:T(8,128)}, f32[6,384,384]{2,1,0:T(8,128)}, f32[6,384,384]{2,1,0:...) custom-call(s32[1]{0:T(128)} %bitcast.seq.seq_ref, ...), custom_call_target="tpu_custom_call" | custom-call | tf_op jit(solution)/shard_map/soap/pallas_call | solution.py:741
  (224 shorter events, 69.1 us)
Async XLA Ops:
  7.2 112.8 %all-gather.6.cloned.1.call-start = ((), (), s32[]{:S(2)}) async-start(), calls=%async_computation | async-start | bytes 14598144 | tf_op jit(solution)/shard_map/all_gather | solution.py:952
  9.2 535.6 %all-gather.8.cloned.1.call-start = ((), (), s32[]{:S(2)}) async-start(), calls=%async_computation.1 | async-start | bytes 1622016 | tf_op jit(solution)/shard_map/all_gather | solution.py:1102
  10.9 27.1 %collective-permute-start = (bf16[512,768]{1,0:T(8,128)(2,1)S(1)}, bf16[512,768]{1,0:T(8,128)(2,1)S(1)}, u32[]{:S(2)}, u32[]{:S(2)}) collective-permute-start(bf16[512,768]{1,0:T(8,128)(2,1)S(1)} %get-tuple-element.281), channel_id=1, source_target_pairs={{0,2},{1,3},{2,0},{3,1},{4,6},{5,7},{6,4},{7,5},{8,10},{9,11},{10,... | collective-permute-start | bytes 2359304 | tf_op jit(solution)/shard_map/ppermute | solution.py:872
  131.3 52.6 %collective-permute-start.2 = (bf16[512,768]{1,0:T(8,128)(2,1)}, bf16[512,768]{1,0:T(8,128)(2,1)S(1)}, u32[]{:S(2)}, u32[]{:S(2)}) collective-permute-start(bf16[512,768]{1,0:T(8,128)(2,1)} %get-tuple-element.141), channel_id=1, source_target_pairs={{0,2},{1,3},{2,0},{3,1},{4,6},{5,7},{6,4},{7,5},{8,10},{9,11},{10,... | collective-permute-start | bytes 2359304 | tf_op jit(solution)/shard_map/ppermute | solution.py:872
  255.1 29.6 %collective-permute-start.3 = (bf16[2,8,6,96,384]{4,3,2,1,0:T(8,128)(2,1)}, bf16[2,8,6,96,384]{4,3,2,1,0:T(8,128)(2,1)}, u32[]{:S(2)}, u32[]{:S(2)}) collective-permute-start(bf16[2,8,6,96,384]{4,3,2,1,0:T(8,128)(2,1)} %get-tuple-element.145), channel_id=1, source_target_pairs={{0,1},{1,0},{2,3},{3,2},{4,5},{5,4},{6,7},{7,6},{8,9},{9,8},{10,11... | collective-permute-start | bytes 21233672 | tf_op jit(solution)/shard_map/ppermute | solution.py:872
  257.8 25.9 %collective-permute-start.4 = (bf16[512,768]{1,0:T(8,128)(2,1)S(1)}, bf16[512,768]{1,0:T(8,128)(2,1)S(1)}, u32[]{:S(2)}, u32[]{:S(2)}) collective-permute-start(bf16[512,768]{1,0:T(8,128)(2,1)S(1)} %get-tuple-element.277), channel_id=1, source_target_pairs={{0,2},{1,3},{2,0},{3,1},{4,6},{5,7},{6,4},{7,5},{8,10},{9,11},{10,... | collective-permute-start | bytes 2359304 | tf_op jit(solution)/shard_map/ppermute | solution.py:872
  294.1 38.4 %collective-permute-start.5 = (bf16[2,2,2,2,96,384]{5,4,3,2,1,0:T(8,128)(2,1)}, bf16[2,2,2,2,96,384]{5,4,3,2,1,0:T(8,128)(2,1)S(1)}, u32[]{:S(2)}, u32[]{:S(2)}) collective-permute-start(bf16[2,2,2,2,96,384]{5,4,3,2,1,0:T(8,128)(2,1)} %get-tuple-element.158), channel_id=1, source_target_pairs={{0,2},{1,3},{2,0},{3,1},{4,6},{5,7},{6,4},{7,5},{8,10},{9,11},{10,... | collective-permute-start | bytes 3538952 | tf_op jit(solution)/shard_map/ppermute | solution.py:872
  294.7 37.8 %collective-permute-start.6 = (bf16[2,2,2,2,96,384]{5,4,3,2,1,0:T(8,128)(2,1)}, bf16[2,2,2,2,96,384]{5,4,3,2,1,0:T(8,128)(2,1)S(1)}, u32[]{:S(2)}, u32[]{:S(2)}) collective-permute-start(bf16[2,2,2,2,96,384]{5,4,3,2,1,0:T(8,128)(2,1)} %get-tuple-element.159), channel_id=1, source_target_pairs={{0,4},{4,0},{8,12},{12,8},{16,20},{20,16},{24,28},{28,24},{1,5},{5... | collective-permute-start | bytes 3538952 | tf_op jit(solution)/shard_map/ppermute | solution.py:872
  296.3 36.3 %collective-permute-start.7 = (bf16[2,2,2,2,96,384]{5,4,3,2,1,0:T(8,128)(2,1)}, bf16[2,2,2,2,96,384]{5,4,3,2,1,0:T(8,128)(2,1)S(1)}, u32[]{:S(2)}, u32[]{:S(2)}) collective-permute-start(bf16[2,2,2,2,96,384]{5,4,3,2,1,0:T(8,128)(2,1)} %get-tuple-element.160), channel_id=1, source_target_pairs={{0,8},{4,12},{8,0},{12,4},{16,24},{20,28},{24,16},{28,20},{1,9},{5... | collective-permute-start | bytes 3538952 | tf_op jit(solution)/shard_map/ppermute | solution.py:872
  333.9 22.6 %collective-permute-start.15 = (bf16[2,1024,384]{2,1,0:T(8,128)(2,1)}, bf16[2,1024,384]{2,1,0:T(8,128)(2,1)S(1)}, u32[]{:S(2)}, u32[]{:S(2)}) collective-permute-start(bf16[2,1024,384]{2,1,0:T(8,128)(2,1)} %get-tuple-element.196), channel_id=1, source_target_pairs={{0,1},{1,0},{2,3},{3,2},{4,5},{5,4},{6,7},{7,6},{8,9},{9,8},{10,11... | collective-permute-start | bytes 4718600 | tf_op jit(solution)/shard_map/ppermute | solution.py:872
  337.3 16.7 %collective-permute-start.8 = (bf16[2,2,2,96,384]{4,3,2,1,0:T(8,128)(2,1)}, bf16[2,2,2,96,384]{4,3,2,1,0:T(8,128)(2,1)S(1)}, u32[]{:S(2)}, u32[]{:S(2)}) collective-permute-start(bf16[2,2,2,96,384]{4,3,2,1,0:T(8,128)(2,1)} %get-tuple-element.172), channel_id=1, source_target_pairs={{0,4},{4,0},{8,12},{12,8},{16,20},{20,16},{24,28},{28,24},{1,5},{5... | collective-permute-start | bytes 1769480 | tf_op jit(solution)/shard_map/ppermute | solution.py:872
  337.9 16.1 %collective-permute-start.9 = (bf16[2,2,2,96,384]{4,3,2,1,0:T(8,128)(2,1)S(1)}, bf16[2,2,2,96,384]{4,3,2,1,0:T(8,128)(2,1)S(1)}, u32[]{:S(2)}, u32[]{:S(2)}) collective-permute-start(bf16[2,2,2,96,384]{4,3,2,1,0:T(8,128)(2,1)S(1)} %get-tuple-element.173), channel_id=1, source_target_pairs={{0,8},{4,12},{8,0},{12,4},{16,24},{20,28},{24,16},{28,20},{1,9},{5... | collective-permute-start | bytes 1769480 | tf_op jit(solution)/shard_map/ppermute | solution.py:872
  339.3 15.2 %collective-permute-start.10 = (bf16[2,2,2,96,384]{4,3,2,1,0:T(8,128)(2,1)S(1)}, bf16[2,2,2,96,384]{4,3,2,1,0:T(8,128)(2,1)S(1)}, u32[]{:S(2)}, u32[]{:S(2)}) collective-permute-start(bf16[2,2,2,96,384]{4,3,2,1,0:T(8,128)(2,1)S(1)} %get-tuple-element.174), channel_id=1, source_target_pairs={{0,2},{1,3},{2,0},{3,1},{4,6},{5,7},{6,4},{7,5},{8,10},{9,11},{10,... | collective-permute-start | bytes 1769480 | tf_op jit(solution)/shard_map/ppermute | solution.py:872
  340.7 14.4 %collective-permute-start.14 = (bf16[2,1024,256]{2,1,0:T(8,128)(2,1)}, bf16[2,1024,256]{2,1,0:T(8,128)(2,1)S(1)}, u32[]{:S(2)}, u32[]{:S(2)}) collective-permute-start(bf16[2,1024,256]{2,1,0:T(8,128)(2,1)} %get-tuple-element.192), channel_id=1, source_target_pairs={{0,1},{1,0},{2,3},{3,2},{4,5},{5,4},{6,7},{7,6},{8,9},{9,8},{10,11... | collective-permute-start | bytes 3145736 | tf_op jit(solution)/shard_map/ppermute | solution.py:872
  366.3 9.3 %collective-permute-start.11 = (bf16[2,2,96,384]{3,2,1,0:T(8,128)(2,1)S(1)}, bf16[2,2,96,384]{3,2,1,0:T(8,128)(2,1)S(1)}, u32[]{:S(2)}, u32[]{:S(2)}) collective-permute-start(bf16[2,2,96,384]{3,2,1,0:T(8,128)(2,1)S(1)} %get-tuple-element.185), channel_id=1, source_target_pairs={{0,8},{4,12},{8,0},{12,4},{16,24},{20,28},{24,16},{28,20},{1,9},{5... | collective-permute-start | bytes 884744 | tf_op jit(solution)/shard_map/ppermute | solution.py:872
  366.9 9.1 %collective-permute-start.12 = (bf16[2,2,96,384]{3,2,1,0:T(8,128)(2,1)S(1)}, bf16[2,2,96,384]{3,2,1,0:T(8,128)(2,1)S(1)}, u32[]{:S(2)}, u32[]{:S(2)}) collective-permute-start(bf16[2,2,96,384]{3,2,1,0:T(8,128)(2,1)S(1)} %get-tuple-element.186), channel_id=1, source_target_pairs={{0,2},{1,3},{2,0},{3,1},{4,6},{5,7},{6,4},{7,5},{8,10},{9,11},{10,... | collective-permute-start | bytes 884744 | tf_op jit(solution)/shard_map/ppermute | solution.py:872
  368.3 8.8 %collective-permute-start.13 = (bf16[2,2,96,384]{3,2,1,0:T(8,128)(2,1)S(1)}, bf16[2,2,96,384]{3,2,1,0:T(8,128)(2,1)S(1)}, u32[]{:S(2)}, u32[]{:S(2)}) collective-permute-start(bf16[2,2,96,384]{3,2,1,0:T(8,128)(2,1)S(1)} %get-tuple-element.187), channel_id=1, source_target_pairs={{0,4},{4,0},{8,12},{12,8},{16,20},{20,16},{24,28},{28,24},{1,5},{5... | collective-permute-start | bytes 884744 | tf_op jit(solution)/shard_map/ppermute | solution.py:872
  377.1 20.8 %collective-permute-start.19 = (bf16[12,96,384]{2,1,0:T(8,128)(2,1)}, bf16[12,96,384]{2,1,0:T(8,128)(2,1)S(1)}, u32[]{:S(2)}, u32[]{:S(2)}) collective-permute-start(bf16[12,96,384]{2,1,0:T(8,128)(2,1)} %get-tuple-element.270), channel_id=1, source_target_pairs={{0,2},{1,3},{2,0},{3,1},{4,6},{5,7},{6,4},{7,5},{8,10},{9,11},{10,... | collective-permute-start | bytes 2654216 | tf_op jit(solution)/shard_map/ppermute | solution.py:872
  380.0 21.3 %collective-permute-start.18 = (bf16[6,96,384]{2,1,0:T(8,128)(2,1)S(1)}, bf16[6,96,384]{2,1,0:T(8,128)(2,1)S(1)}, u32[]{:S(2)}, u32[]{:S(2)}) collective-permute-start(bf16[6,96,384]{2,1,0:T(8,128)(2,1)S(1)} %pad_maximum_fusion.2), channel_id=1, source_target_pairs={{0,16},{4,20},{8,24},{12,28},{16,0},{20,4},{24,8},{28,12},{1,17},{... | collective-permute-start | bytes 1327112 | tf_op jit(solution)/shard_map/ppermute | solution.py:872
  404.6 34.5 %collective-permute-start.20 = (bf16[512,768]{1,0:T(8,128)(2,1)}, bf16[512,768]{1,0:T(8,128)(2,1)}, u32[]{:S(2)}, u32[]{:S(2)}) collective-permute-start(bf16[512,768]{1,0:T(8,128)(2,1)} %get-tuple-element.275), channel_id=1, source_target_pairs={{0,2},{1,3},{2,0},{3,1},{4,6},{5,7},{6,4},{7,5},{8,10},{9,11},{10,... | collective-permute-start | bytes 2359304 | tf_op jit(solution)/shard_map/ppermute | solution.py:872
  406.2 8.1 %collective-permute-start.27 = (bf16[3,48,384]{2,1,0:T(8,128)(2,1)S(1)}, bf16[3,48,384]{2,1,0:T(8,128)(2,1)S(1)}, u32[]{:S(2)}, u32[]{:S(2)}) collective-permute-start(bf16[3,48,384]{2,1,0:T(8,128)(2,1)S(1)} %get-tuple-element.227), channel_id=1, source_target_pairs={{0,28},{4,24},{8,20},{12,16},{16,12},{20,8},{24,4},{28,0},{1,29},{... | collective-permute-start | bytes 331784 | tf_op jit(solution)/shard_map/ppermute | solution.py:872
  408.7 13.1 %collective-permute-start.26 = (bf16[3,48,384]{2,1,0:T(8,128)(2,1)S(1)}, bf16[3,48,384]{2,1,0:T(8,128)(2,1)S(1)}, u32[]{:S(2)}, u32[]{:S(2)}) collective-permute-start(bf16[3,48,384]{2,1,0:T(8,128)(2,1)S(1)} %get-tuple-element.226), channel_id=1, source_target_pairs={{0,24},{4,28},{8,16},{12,20},{16,8},{20,12},{24,0},{28,4},{1,25},{... | collective-permute-start | bytes 331784 | tf_op jit(solution)/shard_map/ppermute | solution.py:872
  410.2 16.2 %collective-permute-start.25 = (bf16[3,48,384]{2,1,0:T(8,128)(2,1)S(1)}, bf16[3,48,384]{2,1,0:T(8,128)(2,1)S(1)}, u32[]{:S(2)}, u32[]{:S(2)}) collective-permute-start(bf16[3,48,384]{2,1,0:T(8,128)(2,1)S(1)} %get-tuple-element.225), channel_id=1, source_target_pairs={{0,20},{4,16},{8,28},{12,24},{16,4},{20,0},{24,12},{28,8},{1,21},{... | collective-permute-start | bytes 331784 | tf_op jit(solution)/shard_map/ppermute | solution.py:872
  410.3 19.7 %collective-permute-start.24 = (bf16[3,48,384]{2,1,0:T(8,128)(2,1)S(1)}, bf16[3,48,384]{2,1,0:T(8,128)(2,1)S(1)}, u32[]{:S(2)}, u32[]{:S(2)}) collective-permute-start(bf16[3,48,384]{2,1,0:T(8,128)(2,1)S(1)} %get-tuple-element.224), channel_id=1, source_target_pairs={{0,16},{4,20},{8,24},{12,28},{16,0},{20,4},{24,8},{28,12},{1,17},{... | collective-permute-start | bytes 331784 | tf_op jit(solution)/shard_map/ppermute | solution.py:872
  414.3 15.7 %collective-permute-start.23 = (bf16[3,48,384]{2,1,0:T(8,128)(2,1)S(1)}, bf16[3,48,384]{2,1,0:T(8,128)(2,1)S(1)}, u32[]{:S(2)}, u32[]{:S(2)}) collective-permute-start(bf16[3,48,384]{2,1,0:T(8,128)(2,1)S(1)} %get-tuple-element.223), channel_id=1, source_target_pairs={{0,12},{4,8},{8,4},{12,0},{16,28},{20,24},{24,20},{28,16},{1,13},{... | collective-permute-start | bytes 331784 | tf_op jit(solution)/shard_map/ppermute | solution.py:872
  421.8 8.2 %collective-permute-start.22 = (bf16[3,48,384]{2,1,0:T(8,128)(2,1)S(1)}, bf16[3,48,384]{2,1,0:T(8,128)(2,1)S(1)}, u32[]{:S(2)}, u32[]{:S(2)}) collective-permute-start(bf16[3,48,384]{2,1,0:T(8,128)(2,1)S(1)} %get-tuple-element.222), channel_id=1, source_target_pairs={{0,8},{4,12},{8,0},{12,4},{16,24},{20,28},{24,16},{28,20},{1,9},{5... | collective-permute-start | bytes 331784 | tf_op jit(solution)/shard_map/ppermute | solution.py:872
  432.5 14.0 %collective-permute-start.30 = (bf16[3,48,384]{2,1,0:T(8,128)(2,1)S(1)}, bf16[3,48,384]{2,1,0:T(8,128)(2,1)S(1)}, u32[]{:S(2)}, u32[]{:S(2)}) collective-permute-start(bf16[3,48,384]{2,1,0:T(8,128)(2,1)S(1)} %add_convert_fusion.7.refs_0_), channel_id=1, source_target_pairs={{0,12},{4,8},{8,4},{12,0},{16,28},{20,24},{24,20},{28,16},{1,13},{... | collective-permute-start | bytes 331784 | tf_op jit(solution)/shard_map/ppermute | solution.py:872
  435.9 13.2 %collective-permute-start.31 = (bf16[3,48,384]{2,1,0:T(8,128)(2,1)S(1)}, bf16[3,48,384]{2,1,0:T(8,128)(2,1)S(1)}, u32[]{:S(2)}, u32[]{:S(2)}) collective-permute-start(bf16[3,48,384]{2,1,0:T(8,128)(2,1)S(1)} %add_convert_fusion.7.refs_0_), channel_id=1, source_target_pairs={{0,16},{4,20},{8,24},{12,28},{16,0},{20,4},{24,8},{28,12},{1,17},{... | collective-permute-start | bytes 331784 | tf_op jit(solution)/shard_map/ppermute | solution.py:872
  437.0 14.6 %collective-permute-start.32 = (bf16[3,48,384]{2,1,0:T(8,128)(2,1)S(1)}, bf16[3,48,384]{2,1,0:T(8,128)(2,1)S(1)}, u32[]{:S(2)}, u32[]{:S(2)}) collective-permute-start(bf16[3,48,384]{2,1,0:T(8,128)(2,1)S(1)} %add_convert_fusion.7.refs_0_), channel_id=1, source_target_pairs={{0,20},{4,16},{8,28},{12,24},{16,4},{20,0},{24,12},{28,8},{1,21},{... | collective-permute-start | bytes 331784 | tf_op jit(solution)/shard_map/ppermute | solution.py:872
  438.4 13.2 %collective-permute-start.33 = (bf16[3,48,384]{2,1,0:T(8,128)(2,1)S(1)}, bf16[3,48,384]{2,1,0:T(8,128)(2,1)S(1)}, u32[]{:S(2)}, u32[]{:S(2)}) collective-permute-start(bf16[3,48,384]{2,1,0:T(8,128)(2,1)S(1)} %add_convert_fusion.7.refs_0_), channel_id=1, source_target_pairs={{0,24},{4,28},{8,16},{12,20},{16,8},{20,12},{24,0},{28,4},{1,25},{... | collective-permute-start | bytes 331784 | tf_op jit(solution)/shard_map/ppermute | solution.py:872
  439.1 12.5 %collective-permute-start.34 = (bf16[3,48,384]{2,1,0:T(8,128)(2,1)S(1)}, bf16[3,48,384]{2,1,0:T(8,128)(2,1)S(1)}, u32[]{:S(2)}, u32[]{:S(2)}) collective-permute-start(bf16[3,48,384]{2,1,0:T(8,128)(2,1)S(1)} %add_convert_fusion.7.refs_0_), channel_id=1, source_target_pairs={{0,28},{4,24},{8,20},{12,16},{16,12},{20,8},{24,4},{28,0},{1,29},{... | collective-permute-start | bytes 331784 | tf_op jit(solution)/shard_map/ppermute | solution.py:872
  455.7 8.4 %collective-permute-start.35 = (bf16[6,96,384]{2,1,0:T(8,128)(2,1)S(1)}, bf16[6,96,384]{2,1,0:T(8,128)(2,1)S(1)}, u32[]{:S(2)}, u32[]{:S(2)}) collective-permute-start(bf16[6,96,384]{2,1,0:T(8,128)(2,1)S(1)} %choose.1.g0), channel_id=1, source_target_pairs={{0,2},{1,3},{2,0},{3,1},{4,6},{5,7},{6,4},{7,5},{8,10},{9,11},{10,... | collective-permute-start | bytes 1327112 | tf_op jit(solution)/shard_map/ppermute | solution.py:872
  (62 other events, 765.6 us)
Sparse Core Ops, SparseCore 0:
  11.5 108.4 all-gather.5
  455.8 54.5 all-gather.7

commit v9 on v8

--- a/solution.py
+++ b/solution.py
@@ -308,7 +308,7 @@
         dkv2[1] = dv[rows:, :].astype(LOW)
 
 
-def attn_backward(q, kv, other, bias, attn, lse, d_attn, first, count, q_rows=1024, chunk=1024):
+def attn_backward(q, kv, other, bias, attn, lse, d_attn, first, count, q_rows=512, chunk=1024):
     rows, pairs = q.shape[0], D // 128
     keys = 2 * rows
     out_spec = pl.BlockSpec((q_rows, 128), lambda p, i: (i, p))

time: 563 us -> 555 us (0.986)
  Pallas kernels: 322 us -> 316 us
    pallas_call x1, Pallas kernels: 69.6 us -> 58.3 us  [mid_layer(): pl.pallas_call(functools.partial(mid_kernel, chunk=chunk), grid_spec=pltp...]
  transfers between devices with their start and end apart: 40 -> 40, of which waited for: 17 -> 16; matrix products, arithmetic and copies ran while one was open for 5% -> 5% of each run, Pallas kernels for 41% -> 42%
where the time goes in v9:
time: 555 us; the launch traced here: 547 us
  Pallas kernels  316 us (57%)
  waiting for transfers between devices  111 us (20%)
  starting transfers between devices  51.3 us (9%)
  local copies, waits for them, and re-layouts  33.4 us (6%)
  other arithmetic  19.5 us (4%)
  between operations  15 us (3%)
    all_gather x1, waiting for transfers between devices, on_device(): lax.all_gather(mine, AXES, axis=0, tiled=False)  81.9 us
    pallas_call x3, Pallas kernels, attn_backward(): pl.pallas_call(functools.partial(attn_bwd_kernel, chunk=chunk), grid=(cou...  78.9 us
    pallas_call x1, Pallas kernels, soap_update(): pl.pallas_call(soap_kernel, grid_spec=pltpu.PrefetchScalarGridSpec(num_sc...  78.3 us
    pallas_call x1, Pallas kernels, mid_layer(): pl.pallas_call(functools.partial(mid_kernel, chunk=chunk), grid_spec=pltp...  58.3 us
    ppermute x38, starting transfers between devices, swap(): return lax.ppermute(x, axis, [(i, i ^ bit) for i in range(size)])  51.2 us
    pallas_call x1, Pallas kernels, attn_forward(): pl.pallas_call(attn_fwd_kernel, grid=(pairs, rows // q_rows), in_specs=[q...  47.3 us
    ppermute x38, waiting for transfers between devices, swap(): return lax.ppermute(x, axis, [(i, i ^ bit) for i in range(size)])  29.3 us
    unnamed x111, local copies, waits for them, and re-layouts  16.8 us
  transfers between devices with their start and end apart: 40, of which 16 were waited for; matrix products, arithmetic and copies ran while one was open for 5% of the time, Pallas kernels for 42%

profile of v9, /device:TPU:0, one launch (start us, length us, event | category | flops | bytes accessed | tf_op | source)
XLA Modules:
  0.0 546.5 jit_solution(6712830271485179991)
XLA Ops:
  10.9 3.0 collective-permute-start
  14.9 2.0 copy-done.4
  16.8 2.0 copy-done.5
  18.9 2.0 copy-done.6
  20.9 12.1 %stats.1 = (f32[6,384,384]{2,1,0:T(8,128)S(1)}, f32[6,384,384]{2,1,0:T(8,128)S(1)}) custom-call(f32[6,384,384]{2,1,0:T(8,128)S(1)} %copy-done.3, f32[6,384,384]{2,1,0:T(8,128)S(1)} %copy-done.4, f32[6,384,384]{2,1,0:T(8,128)S(1)} %copy-done.5, f32[6,384,384]{2,1,0:T(8,128)S(1)} %copy-done.6), custom_call_target="tpu_custom_call" | custom-call | tf_op jit(solution)/shard_map/stats/pallas_call | solution.py:644
  38.1 81.9 %all-gather.6.cloned.1.call-done = bf16[192,1,96,384]{3,2,1,0:T(8,128)(2,1)} async-done(((bf16[6,1,96,384]{3,2,1,0:T(8,128)(2,1)}), bf16[192,1,96,384]{3,2,1,0:T(8,128)(2,1)}) %all-gather.6.cloned.1.call-update) | async-done | bytes 14155792 | tf_op jit(solution)/shard_map/all_gather | solution.py:952
  120.0 9.1 %qkv.1 = (bf16[1024,768]{1,0:T(8,128)(2,1)S(1)}, bf16[1024,1536]{1,0:T(8,128)(2,1)}, bf16[1024,768]{1,0:T(8,128)(2,1)S(1)}) custom-call(s32[48]{0:T(128)S(1)} %copy-done.24, s32[48]{0:T(128)S(1)} %convert_reduce_fusion.slot, bf16[1024,768]{1,0:T(8,128)(2,1)S(1)} %pad_maximum_fusion.x_ref, f32[12,768]{1,0:T(8,128)S(1)} %copy-done.22, ...), custom_call_target="tpu_custom_call" | custom-call | tf_op jit(solution)/shard_map/qkv/pallas_call | solution.py:130
  136.6 47.3 %attn_fwd.1 = (bf16[1024,768]{1,0:T(8,128)(2,1)S(1)}, f32[1024,768]{1,0:T(8,128)}) custom-call(bf16[1024,768]{1,0:T(8,128)(2,1)S(1)} %get-tuple-element.138.q_ref, bf16[1024,1536]{1,0:T(8,128)(2,1)} %get-tuple-element.139.k1.v1, bf16[1024,1536]{1,0:T(8,128)(2,1)} %get-tuple-element.139.k1.v1, bf16[1024,1536]{1,0:T(8,128)(2,1)} %collective-permute-done.1.k2.v2, ...), custom_call_target="tpu_custom_call" | custom-call | tf_op jit(solution)/shard_map/attn_fwd/pallas_call | solution.py:195
  185.5 58.3 %mid.1 = (bf16[1024,768]{1,0:T(8,128)(2,1)}, f32[1024,768]{1,0:T(8,128)}, bf16[1024,768]{1,0:T(8,128)(2,1)}, bf16[2,8,6,96,384]{4,3,2,1,0:T(8,128)(2,1)}, bf16[2...) custom-call(s32[48]{0:T(128)} %own.5, s32[48]{0:T(128)} %copy-done.25, ...), custom_call_target="tpu_custom_call" | custom-call | tf_op jit(solution)/shard_map/mid/pallas_call | solution.py:465
  244.1 2.4 slice_bitcast_fusion.3
  247.9 26.3 %attn_bwd.3 = (bf16[1024,256]{1,0:T(8,128)(2,1)}, bf16[1024,256]{1,0:T(8,128)(2,1)}, bf16[1024,256]{1,0:T(8,128)(2,1)}, bf16[2,1024,256]{2,1,0:T(8,128)(2,1)}) custom-call(bf16[1024,768]{1,0:T(8,128)(2,1)} %copy-done.2, bf16[1024,1536]{1,0:T(8,128)(2,1)} %get-tuple-element.139.k1.v1, bf16[1024,1536]{1,0:T(8,128)(2,1)} %get-tuple-element.139.k1.v1, ...), custom_call_target="tpu_custom_call" | custom-call | tf_op jit(solution)/shard_map/attn_bwd/pallas_call | solution.py:319
  275.1 9.4 %first_halves.1 = (bf16[2,2,2,2,96,384]{5,4,3,2,1,0:T(8,128)(2,1)}, bf16[2,2,2,2,96,384]{5,4,3,2,1,0:T(8,128)(2,1)}, bf16[2,2,2,2,96,384]{5,4,3,2,1,0:T(8,128)(2...) custom-call(bf16[2,2,2,2,6,96,384]{6,5,4,3,2,1,0:T(8,128)(2,1)} %bit, ...), custom_call_target="tpu_custom_call" | custom-call | tf_op jit(solution)/shard_map/first_halves/pallas_call | solution.py:812
  287.3 38.0 %attn_bwd.4 = (bf16[1024,384]{1,0:T(8,128)(2,1)}, bf16[1024,384]{1,0:T(8,128)(2,1)}, bf16[1024,384]{1,0:T(8,128)(2,1)}, bf16[2,1024,384]{2,1,0:T(8,128)(2,1)}) custom-call(bf16[1024,768]{1,0:T(8,128)(2,1)} %copy-done.2, bf16[1024,1536]{1,0:T(8,128)(2,1)} %get-tuple-element.139.k1.v1, bf16[1024,1536]{1,0:T(8,128)(2,1)} %get-tuple-element.139.k1.v1, ...), custom_call_target="tpu_custom_call" | custom-call | tf_op jit(solution)/shard_map/attn_bwd/pallas_call | solution.py:319
  326.8 2.9 add_convert_fusion.1
  333.5 14.6 %attn_bwd.5 = (bf16[1024,128]{1,0:T(8,128)(2,1)}, bf16[1024,128]{1,0:T(8,128)(2,1)}, bf16[1024,128]{1,0:T(8,128)(2,1)}, bf16[2,1024,128]{2,1,0:T(8,128)(2,1)}) custom-call(bf16[1024,768]{1,0:T(8,128)(2,1)} %copy-done.2, bf16[1024,1536]{1,0:T(8,128)(2,1)} %get-tuple-element.139.k1.v1, bf16[1024,1536]{1,0:T(8,128)(2,1)} %get-tuple-element.139.k1.v1, ...), custom_call_target="tpu_custom_call" | custom-call | tf_op jit(solution)/shard_map/attn_bwd/pallas_call | solution.py:319
  351.7 7.9 %qkv_grad.1 = (bf16[2,2,6,96,384]{4,3,2,1,0:T(8,128)(2,1)}, bf16[2,2,6,96,384]{4,3,2,1,0:T(8,128)(2,1)}, f32[1,2304]{1,0:T(1,128)S(1)}) custom-call(s32[1]{0:T(128)} %bitcast.seq.seq_ref, bf16[1024,768]{1,0:T(8,128)(2,1)} %copy-done.18, bf16[1024,256]{1,0:T(8,128)(2,1)S(1)} %copy-done.13, bf16[1024,256]{1,0:T(8,128)(2,1)S(1)} %copy-done.14, ...), custom_call_target="tpu_custom_call" | custom-call | tf_op jit(solution)/shard_map/qkv_grad/pallas_call | solution.py:537
  365.9 3.1 collective-permute-done.11
  375.1 13.8 %qkv_bwd.1 = (bf16[1024,768]{1,0:T(8,128)(2,1)}, f32[8,768]{1,0:T(8,128)}) custom-call(s32[48]{0:T(128)} %own.5, s32[48]{0:T(128)} %copy-done.25, bf16[1024,768]{1,0:T(8,128)(2,1)} %copy-done.1, f32[1024,768]{1,0:T(8,128)} %get-tuple-element.210.dmid_ref, f32[12,768]{1,0:T(8,128)} %vec_ref.5, bf16[1024,256]{1,0:T(8,128)(2,1)} %get-tuple-element.189.refs_0_, ...), custom_call_target="tpu_custom_call" | custom-call | tf_op jit(solution)/shard_map/qkv_bwd/pallas_call | solution.py:579
  390.1 4.1 collective-permute-done.18
  395.0 2.6 slice_bitcast_fusion.2
  398.5 3.2 collective-permute-start.27
  403.3 2.9 collective-permute-start.24
  406.6 8.2 %collective-permute-start.23 = (bf16[3,48,384]{2,1,0:T(8,128)(2,1)S(1)}, bf16[3,48,384]{2,1,0:T(8,128)(2,1)S(1)}, u32[]{:S(2)}, u32[]{:S(2)}) collective-permute-start(bf16[3,48,384]{2,1,0:T(8,128)(2,1)S(1)} %get-tuple-element.223), channel_id=1, source_target_pairs={{0,12},{4,8},{8,4},{12,0},{16,28},{20,24},{24,20},{28,16},{1,13},{... | collective-permute-start | bytes 331784 | tf_op jit(solution)/shard_map/ppermute | solution.py:872
  420.1 2.9 maximum_select_fusion
  423.5 2.4 collective-permute-start.28
  428.6 3.3 collective-permute-start.32
  432.1 3.2 collective-permute-start.34
  435.3 2.9 maximum_select_fusion.1
  438.2 3.2 collective-permute-done.31.refs_4_
  441.4 2.4 collective-permute-done.32.refs_5_
  449.3 7.0 %collective-permute-done.35.g1 = bf16[6,96,384]{2,1,0:T(8,128)(2,1)S(1)} collective-permute-done((bf16[6,96,384]{2,1,0:T(8,128)(2,1)S(1)}, bf16[6,96,384]{2,1,0:T(8,128)(2,1)S(1)}, u32[]{:S(2)}, u32[]{:S(2)}) %collective-permute-start.35) | collective-permute-done | bytes 442400 | tf_op jit(solution)/shard_map/ppermute | solution.py:872
  458.9 78.3 %soap.1 = (f32[6,384,384]{2,1,0:T(8,128)}, f32[6,384,384]{2,1,0:T(8,128)}, f32[6,384,384]{2,1,0:T(8,128)}, f32[6,384,384]{2,1,0:T(8,128)}, f32[6,384,384]{2,1,0:...) custom-call(s32[1]{0:T(128)} %bitcast.seq.seq_ref, ...), custom_call_target="tpu_custom_call" | custom-call | tf_op jit(solution)/shard_map/soap/pallas_call | solution.py:741
  (224 shorter events, 68.7 us)
Async XLA Ops:
  7.2 112.8 %all-gather.6.cloned.1.call-start = ((), (), s32[]{:S(2)}) async-start(), calls=%async_computation | async-start | bytes 14598144 | tf_op jit(solution)/shard_map/all_gather | solution.py:952
  9.2 528.0 %all-gather.8.cloned.1.call-start = ((), (), s32[]{:S(2)}) async-start(), calls=%async_computation.1 | async-start | bytes 1622016 | tf_op jit(solution)/shard_map/all_gather | solution.py:1102
  10.9 27.0 %collective-permute-start = (bf16[512,768]{1,0:T(8,128)(2,1)S(1)}, bf16[512,768]{1,0:T(8,128)(2,1)S(1)}, u32[]{:S(2)}, u32[]{:S(2)}) collective-permute-start(bf16[512,768]{1,0:T(8,128)(2,1)S(1)} %get-tuple-element.281), channel_id=1, source_target_pairs={{0,2},{1,3},{2,0},{3,1},{4,6},{5,7},{6,4},{7,5},{8,10},{9,11},{10,... | collective-permute-start | bytes 2359304 | tf_op jit(solution)/shard_map/ppermute | solution.py:872
  131.2 52.6 %collective-permute-start.2 = (bf16[512,768]{1,0:T(8,128)(2,1)}, bf16[512,768]{1,0:T(8,128)(2,1)S(1)}, u32[]{:S(2)}, u32[]{:S(2)}) collective-permute-start(bf16[512,768]{1,0:T(8,128)(2,1)} %get-tuple-element.141), channel_id=1, source_target_pairs={{0,2},{1,3},{2,0},{3,1},{4,6},{5,7},{6,4},{7,5},{8,10},{9,11},{10,... | collective-permute-start | bytes 2359304 | tf_op jit(solution)/shard_map/ppermute | solution.py:872
  243.8 31.3 %collective-permute-start.3 = (bf16[2,8,6,96,384]{4,3,2,1,0:T(8,128)(2,1)}, bf16[2,8,6,96,384]{4,3,2,1,0:T(8,128)(2,1)}, u32[]{:S(2)}, u32[]{:S(2)}) collective-permute-start(bf16[2,8,6,96,384]{4,3,2,1,0:T(8,128)(2,1)} %get-tuple-element.145), channel_id=1, source_target_pairs={{0,1},{1,0},{2,3},{3,2},{4,5},{5,4},{6,7},{7,6},{8,9},{9,8},{10,11... | collective-permute-start | bytes 21233672 | tf_op jit(solution)/shard_map/ppermute | solution.py:872
  246.5 27.7 %collective-permute-start.4 = (bf16[512,768]{1,0:T(8,128)(2,1)S(1)}, bf16[512,768]{1,0:T(8,128)(2,1)S(1)}, u32[]{:S(2)}, u32[]{:S(2)}) collective-permute-start(bf16[512,768]{1,0:T(8,128)(2,1)S(1)} %get-tuple-element.277), channel_id=1, source_target_pairs={{0,2},{1,3},{2,0},{3,1},{4,6},{5,7},{6,4},{7,5},{8,10},{9,11},{10,... | collective-permute-start | bytes 2359304 | tf_op jit(solution)/shard_map/ppermute | solution.py:872
  284.5 40.8 %collective-permute-start.5 = (bf16[2,2,2,2,96,384]{5,4,3,2,1,0:T(8,128)(2,1)}, bf16[2,2,2,2,96,384]{5,4,3,2,1,0:T(8,128)(2,1)S(1)}, u32[]{:S(2)}, u32[]{:S(2)}) collective-permute-start(bf16[2,2,2,2,96,384]{5,4,3,2,1,0:T(8,128)(2,1)} %get-tuple-element.158), channel_id=1, source_target_pairs={{0,2},{1,3},{2,0},{3,1},{4,6},{5,7},{6,4},{7,5},{8,10},{9,11},{10,... | collective-permute-start | bytes 3538952 | tf_op jit(solution)/shard_map/ppermute | solution.py:872
  285.2 40.1 %collective-permute-start.6 = (bf16[2,2,2,2,96,384]{5,4,3,2,1,0:T(8,128)(2,1)}, bf16[2,2,2,2,96,384]{5,4,3,2,1,0:T(8,128)(2,1)S(1)}, u32[]{:S(2)}, u32[]{:S(2)}) collective-permute-start(bf16[2,2,2,2,96,384]{5,4,3,2,1,0:T(8,128)(2,1)} %get-tuple-element.159), channel_id=1, source_target_pairs={{0,4},{4,0},{8,12},{12,8},{16,20},{20,16},{24,28},{28,24},{1,5},{5... | collective-permute-start | bytes 3538952 | tf_op jit(solution)/shard_map/ppermute | solution.py:872
  286.7 38.7 %collective-permute-start.7 = (bf16[2,2,2,2,96,384]{5,4,3,2,1,0:T(8,128)(2,1)}, bf16[2,2,2,2,96,384]{5,4,3,2,1,0:T(8,128)(2,1)S(1)}, u32[]{:S(2)}, u32[]{:S(2)}) collective-permute-start(bf16[2,2,2,2,96,384]{5,4,3,2,1,0:T(8,128)(2,1)} %get-tuple-element.160), channel_id=1, source_target_pairs={{0,8},{4,12},{8,0},{12,4},{16,24},{20,28},{24,16},{28,20},{1,9},{5... | collective-permute-start | bytes 3538952 | tf_op jit(solution)/shard_map/ppermute | solution.py:872
  326.7 23.7 %collective-permute-start.15 = (bf16[2,1024,384]{2,1,0:T(8,128)(2,1)}, bf16[2,1024,384]{2,1,0:T(8,128)(2,1)S(1)}, u32[]{:S(2)}, u32[]{:S(2)}) collective-permute-start(bf16[2,1024,384]{2,1,0:T(8,128)(2,1)} %get-tuple-element.196), channel_id=1, source_target_pairs={{0,1},{1,0},{2,3},{3,2},{4,5},{5,4},{6,7},{7,6},{8,9},{9,8},{10,11... | collective-permute-start | bytes 4718600 | tf_op jit(solution)/shard_map/ppermute | solution.py:872
  330.1 18.0 %collective-permute-start.8 = (bf16[2,2,2,96,384]{4,3,2,1,0:T(8,128)(2,1)}, bf16[2,2,2,96,384]{4,3,2,1,0:T(8,128)(2,1)S(1)}, u32[]{:S(2)}, u32[]{:S(2)}) collective-permute-start(bf16[2,2,2,96,384]{4,3,2,1,0:T(8,128)(2,1)} %get-tuple-element.172), channel_id=1, source_target_pairs={{0,4},{4,0},{8,12},{12,8},{16,20},{20,16},{24,28},{28,24},{1,5},{5... | collective-permute-start | bytes 1769480 | tf_op jit(solution)/shard_map/ppermute | solution.py:872
  330.7 17.4 %collective-permute-start.9 = (bf16[2,2,2,96,384]{4,3,2,1,0:T(8,128)(2,1)S(1)}, bf16[2,2,2,96,384]{4,3,2,1,0:T(8,128)(2,1)S(1)}, u32[]{:S(2)}, u32[]{:S(2)}) collective-permute-start(bf16[2,2,2,96,384]{4,3,2,1,0:T(8,128)(2,1)S(1)} %get-tuple-element.173), channel_id=1, source_target_pairs={{0,8},{4,12},{8,0},{12,4},{16,24},{20,28},{24,16},{28,20},{1,9},{5... | collective-permute-start | bytes 1769480 | tf_op jit(solution)/shard_map/ppermute | solution.py:872
  332.1 16.0 %collective-permute-start.10 = (bf16[2,2,2,96,384]{4,3,2,1,0:T(8,128)(2,1)S(1)}, bf16[2,2,2,96,384]{4,3,2,1,0:T(8,128)(2,1)S(1)}, u32[]{:S(2)}, u32[]{:S(2)}) collective-permute-start(bf16[2,2,2,96,384]{4,3,2,1,0:T(8,128)(2,1)S(1)} %get-tuple-element.174), channel_id=1, source_target_pairs={{0,2},{1,3},{2,0},{3,1},{4,6},{5,7},{6,4},{7,5},{8,10},{9,11},{10,... | collective-permute-start | bytes 1769480 | tf_op jit(solution)/shard_map/ppermute | solution.py:872
  333.5 15.7 %collective-permute-start.14 = (bf16[2,1024,256]{2,1,0:T(8,128)(2,1)}, bf16[2,1024,256]{2,1,0:T(8,128)(2,1)S(1)}, u32[]{:S(2)}, u32[]{:S(2)}) collective-permute-start(bf16[2,1024,256]{2,1,0:T(8,128)(2,1)} %get-tuple-element.192), channel_id=1, source_target_pairs={{0,1},{1,0},{2,3},{3,2},{4,5},{5,4},{6,7},{7,6},{8,9},{9,8},{10,11... | collective-permute-start | bytes 3145736 | tf_op jit(solution)/shard_map/ppermute | solution.py:872
  360.0 9.0 %collective-permute-start.11 = (bf16[2,2,96,384]{3,2,1,0:T(8,128)(2,1)S(1)}, bf16[2,2,96,384]{3,2,1,0:T(8,128)(2,1)S(1)}, u32[]{:S(2)}, u32[]{:S(2)}) collective-permute-start(bf16[2,2,96,384]{3,2,1,0:T(8,128)(2,1)S(1)} %get-tuple-element.185), channel_id=1, source_target_pairs={{0,8},{4,12},{8,0},{12,4},{16,24},{20,28},{24,16},{28,20},{1,9},{5... | collective-permute-start | bytes 884744 | tf_op jit(solution)/shard_map/ppermute | solution.py:872
  360.6 8.7 %collective-permute-start.12 = (bf16[2,2,96,384]{3,2,1,0:T(8,128)(2,1)S(1)}, bf16[2,2,96,384]{3,2,1,0:T(8,128)(2,1)S(1)}, u32[]{:S(2)}, u32[]{:S(2)}) collective-permute-start(bf16[2,2,96,384]{3,2,1,0:T(8,128)(2,1)S(1)} %get-tuple-element.186), channel_id=1, source_target_pairs={{0,2},{1,3},{2,0},{3,1},{4,6},{5,7},{6,4},{7,5},{8,10},{9,11},{10,... | collective-permute-start | bytes 884744 | tf_op jit(solution)/shard_map/ppermute | solution.py:872
  361.2 8.5 %collective-permute-start.13 = (bf16[2,2,96,384]{3,2,1,0:T(8,128)(2,1)S(1)}, bf16[2,2,96,384]{3,2,1,0:T(8,128)(2,1)S(1)}, u32[]{:S(2)}, u32[]{:S(2)}) collective-permute-start(bf16[2,2,96,384]{3,2,1,0:T(8,128)(2,1)S(1)} %get-tuple-element.187), channel_id=1, source_target_pairs={{0,4},{4,0},{8,12},{12,8},{16,20},{20,16},{24,28},{28,24},{1,5},{5... | collective-permute-start | bytes 884744 | tf_op jit(solution)/shard_map/ppermute | solution.py:872
  369.7 20.4 %collective-permute-start.19 = (bf16[12,96,384]{2,1,0:T(8,128)(2,1)}, bf16[12,96,384]{2,1,0:T(8,128)(2,1)S(1)}, u32[]{:S(2)}, u32[]{:S(2)}) collective-permute-start(bf16[12,96,384]{2,1,0:T(8,128)(2,1)} %get-tuple-element.270), channel_id=1, source_target_pairs={{0,2},{1,3},{2,0},{3,1},{4,6},{5,7},{6,4},{7,5},{8,10},{9,11},{10,... | collective-permute-start | bytes 2654216 | tf_op jit(solution)/shard_map/ppermute | solution.py:872
  373.4 20.9 %collective-permute-start.18 = (bf16[6,96,384]{2,1,0:T(8,128)(2,1)S(1)}, bf16[6,96,384]{2,1,0:T(8,128)(2,1)S(1)}, u32[]{:S(2)}, u32[]{:S(2)}) collective-permute-start(bf16[6,96,384]{2,1,0:T(8,128)(2,1)S(1)} %pad_maximum_fusion.2), channel_id=1, source_target_pairs={{0,16},{4,20},{8,24},{12,28},{16,0},{20,4},{24,8},{28,12},{1,17},{... | collective-permute-start | bytes 1327112 | tf_op jit(solution)/shard_map/ppermute | solution.py:872
  397.6 34.5 %collective-permute-start.20 = (bf16[512,768]{1,0:T(8,128)(2,1)}, bf16[512,768]{1,0:T(8,128)(2,1)}, u32[]{:S(2)}, u32[]{:S(2)}) collective-permute-start(bf16[512,768]{1,0:T(8,128)(2,1)} %get-tuple-element.275), channel_id=1, source_target_pairs={{0,2},{1,3},{2,0},{3,1},{4,6},{5,7},{6,4},{7,5},{8,10},{9,11},{10,... | collective-permute-start | bytes 2359304 | tf_op jit(solution)/shard_map/ppermute | solution.py:872
  398.5 8.1 %collective-permute-start.27 = (bf16[3,48,384]{2,1,0:T(8,128)(2,1)S(1)}, bf16[3,48,384]{2,1,0:T(8,128)(2,1)S(1)}, u32[]{:S(2)}, u32[]{:S(2)}) collective-permute-start(bf16[3,48,384]{2,1,0:T(8,128)(2,1)S(1)} %get-tuple-element.227), channel_id=1, source_target_pairs={{0,28},{4,24},{8,20},{12,16},{16,12},{20,8},{24,4},{28,0},{1,29},{... | collective-permute-start | bytes 331784 | tf_op jit(solution)/shard_map/ppermute | solution.py:872
  401.7 13.1 %collective-permute-start.26 = (bf16[3,48,384]{2,1,0:T(8,128)(2,1)S(1)}, bf16[3,48,384]{2,1,0:T(8,128)(2,1)S(1)}, u32[]{:S(2)}, u32[]{:S(2)}) collective-permute-start(bf16[3,48,384]{2,1,0:T(8,128)(2,1)S(1)} %get-tuple-element.226), channel_id=1, source_target_pairs={{0,24},{4,28},{8,16},{12,20},{16,8},{20,12},{24,0},{28,4},{1,25},{... | collective-permute-start | bytes 331784 | tf_op jit(solution)/shard_map/ppermute | solution.py:872
  403.2 15.3 %collective-permute-start.25 = (bf16[3,48,384]{2,1,0:T(8,128)(2,1)S(1)}, bf16[3,48,384]{2,1,0:T(8,128)(2,1)S(1)}, u32[]{:S(2)}, u32[]{:S(2)}) collective-permute-start(bf16[3,48,384]{2,1,0:T(8,128)(2,1)S(1)} %get-tuple-element.225), channel_id=1, source_target_pairs={{0,20},{4,16},{8,28},{12,24},{16,4},{20,0},{24,12},{28,8},{1,21},{... | collective-permute-start | bytes 331784 | tf_op jit(solution)/shard_map/ppermute | solution.py:872
  403.3 19.6 %collective-permute-start.24 = (bf16[3,48,384]{2,1,0:T(8,128)(2,1)S(1)}, bf16[3,48,384]{2,1,0:T(8,128)(2,1)S(1)}, u32[]{:S(2)}, u32[]{:S(2)}) collective-permute-start(bf16[3,48,384]{2,1,0:T(8,128)(2,1)S(1)} %get-tuple-element.224), channel_id=1, source_target_pairs={{0,16},{4,20},{8,24},{12,28},{16,0},{20,4},{24,8},{28,12},{1,17},{... | collective-permute-start | bytes 331784 | tf_op jit(solution)/shard_map/ppermute | solution.py:872
  406.6 16.4 %collective-permute-start.23 = (bf16[3,48,384]{2,1,0:T(8,128)(2,1)S(1)}, bf16[3,48,384]{2,1,0:T(8,128)(2,1)S(1)}, u32[]{:S(2)}, u32[]{:S(2)}) collective-permute-start(bf16[3,48,384]{2,1,0:T(8,128)(2,1)S(1)} %get-tuple-element.223), channel_id=1, source_target_pairs={{0,12},{4,8},{8,4},{12,0},{16,28},{20,24},{24,20},{28,16},{1,13},{... | collective-permute-start | bytes 331784 | tf_op jit(solution)/shard_map/ppermute | solution.py:872
  414.7 8.2 %collective-permute-start.22 = (bf16[3,48,384]{2,1,0:T(8,128)(2,1)S(1)}, bf16[3,48,384]{2,1,0:T(8,128)(2,1)S(1)}, u32[]{:S(2)}, u32[]{:S(2)}) collective-permute-start(bf16[3,48,384]{2,1,0:T(8,128)(2,1)S(1)} %get-tuple-element.222), channel_id=1, source_target_pairs={{0,8},{4,12},{8,0},{12,4},{16,24},{20,28},{24,16},{28,20},{1,9},{5... | collective-permute-start | bytes 331784 | tf_op jit(solution)/shard_map/ppermute | solution.py:872
  426.0 12.2 %collective-permute-start.30 = (bf16[3,48,384]{2,1,0:T(8,128)(2,1)S(1)}, bf16[3,48,384]{2,1,0:T(8,128)(2,1)S(1)}, u32[]{:S(2)}, u32[]{:S(2)}) collective-permute-start(bf16[3,48,384]{2,1,0:T(8,128)(2,1)S(1)} %add_convert_fusion.7.refs_0_), channel_id=1, source_target_pairs={{0,12},{4,8},{8,4},{12,0},{16,28},{20,24},{24,20},{28,16},{1,13},{... | collective-permute-start | bytes 331784 | tf_op jit(solution)/shard_map/ppermute | solution.py:872
  427.6 13.8 %collective-permute-start.31 = (bf16[3,48,384]{2,1,0:T(8,128)(2,1)S(1)}, bf16[3,48,384]{2,1,0:T(8,128)(2,1)S(1)}, u32[]{:S(2)}, u32[]{:S(2)}) collective-permute-start(bf16[3,48,384]{2,1,0:T(8,128)(2,1)S(1)} %add_convert_fusion.7.refs_0_), channel_id=1, source_target_pairs={{0,16},{4,20},{8,24},{12,28},{16,0},{20,4},{24,8},{28,12},{1,17},{... | collective-permute-start | bytes 331784 | tf_op jit(solution)/shard_map/ppermute | solution.py:872
  428.6 15.2 %collective-permute-start.32 = (bf16[3,48,384]{2,1,0:T(8,128)(2,1)S(1)}, bf16[3,48,384]{2,1,0:T(8,128)(2,1)S(1)}, u32[]{:S(2)}, u32[]{:S(2)}) collective-permute-start(bf16[3,48,384]{2,1,0:T(8,128)(2,1)S(1)} %add_convert_fusion.7.refs_0_), channel_id=1, source_target_pairs={{0,20},{4,16},{8,28},{12,24},{16,4},{20,0},{24,12},{28,8},{1,21},{... | collective-permute-start | bytes 331784 | tf_op jit(solution)/shard_map/ppermute | solution.py:872
  432.0 11.9 %collective-permute-start.33 = (bf16[3,48,384]{2,1,0:T(8,128)(2,1)S(1)}, bf16[3,48,384]{2,1,0:T(8,128)(2,1)S(1)}, u32[]{:S(2)}, u32[]{:S(2)}) collective-permute-start(bf16[3,48,384]{2,1,0:T(8,128)(2,1)S(1)} %add_convert_fusion.7.refs_0_), channel_id=1, source_target_pairs={{0,24},{4,28},{8,16},{12,20},{16,8},{20,12},{24,0},{28,4},{1,25},{... | collective-permute-start | bytes 331784 | tf_op jit(solution)/shard_map/ppermute | solution.py:872
  432.1 11.8 %collective-permute-start.34 = (bf16[3,48,384]{2,1,0:T(8,128)(2,1)S(1)}, bf16[3,48,384]{2,1,0:T(8,128)(2,1)S(1)}, u32[]{:S(2)}, u32[]{:S(2)}) collective-permute-start(bf16[3,48,384]{2,1,0:T(8,128)(2,1)S(1)} %add_convert_fusion.7.refs_0_), channel_id=1, source_target_pairs={{0,28},{4,24},{8,20},{12,16},{16,12},{20,8},{24,4},{28,0},{1,29},{... | collective-permute-start | bytes 331784 | tf_op jit(solution)/shard_map/ppermute | solution.py:872
  447.9 8.4 %collective-permute-start.35 = (bf16[6,96,384]{2,1,0:T(8,128)(2,1)S(1)}, bf16[6,96,384]{2,1,0:T(8,128)(2,1)S(1)}, u32[]{:S(2)}, u32[]{:S(2)}) collective-permute-start(bf16[6,96,384]{2,1,0:T(8,128)(2,1)S(1)} %choose.1.g0), channel_id=1, source_target_pairs={{0,2},{1,3},{2,0},{3,1},{4,6},{5,7},{6,4},{7,5},{8,10},{9,11},{10,... | collective-permute-start | bytes 1327112 | tf_op jit(solution)/shard_map/ppermute | solution.py:872
  (62 other events, 768.2 us)
Sparse Core Ops, SparseCore 0:
  11.5 108.4 all-gather.5
  448.1 55.1 all-gather.7
